TPU v7x, 256 devices: a whole 4x4x8 slice. The times are simulated.
256 devices in a mesh: mod: 2 (over core), tp: 32 (over y, z), seq: 4 (over x).
Axes of the slice: x: 4, y: 4, z: 8, core: 2. Of those that a mesh axis runs over, the one named last changes fastest.
Arguments:
- tokens: bfloat16 [2048, 8192], P('seq', ('mod', 'tp')), may hold values from -6 to 6
- modality: int32 [2048], P('seq'), may hold values from 0 to 1, as said below
- norm_gain: float32 [2, 8192], P('mod'), may hold values from 0.25 to 1.75
- w_qkv: bfloat16 [2, 8192, 3, 4096], P('mod', None, None, 'tp'), may hold values from -0.0625 to 0.0625
- qk_gain: float32 [2, 4096], P(None, 'tp'), may hold values from 0.48 to 9.6
- w_out: bfloat16 [2, 4096, 8192], P('mod', 'tp'), may hold values from -1.5 to 1.5
Outputs:
- attended: bfloat16 [2048, 8192], P('seq', ('mod', 'tp'))
Inputs may be any that keep to these rules, and one draw needn't show every extreme that they name: `modality`: 1 marks image tokens and 0 text tokens; exactly 1024 tokens are image tokens, those at the 1024 positions from some start on, continuing from position 0 where they pass the end of the sequence.
All inputs are finite; a program needn't handle non-finite values.
Results may differ from a plain program's by a relative error of at most 0.01.
The roundings to bfloat16 on the way count: a program that leaves them out, or rounds other values in their place, can miss the bound.
Values may be sent and summed in bfloat16 or wider, within the bound.
No kernel may reach another device: no remote copies, remote signals or barrier semaphores. Data moves between devices by JAX's collectives and lax.ppermute only.
A program may use at most 128 MiB of HBM per device.

v0:
```python
import math

import jax
import jax.numpy as jnp
from jax import lax
from jax.sharding import PartitionSpec as P

HD = 128


epsilon = 1e-05
masked_score = -1e30


def swapped(x, axis, apart):
    return lax.ppermute(x, axis, [(i, i ^ 1 << apart) for i in range(lax.axis_size(axis))])


def headnorm(projected, gain_row):
    row_count = projected.shape[0]
    by_head = projected.reshape(row_count, -1, HD)
    average = jnp.mean(by_head, axis=2, keepdims=True)
    centred = by_head - average
    variance = jnp.mean(centred * centred, axis=2, keepdims=True)
    return centred * lax.rsqrt(variance + epsilon) * gain_row.reshape(1, -1, HD)


def rotate(by_head, places):
    half_dim = HD // 2
    inverse = 1.0 / 10000.0 ** (jnp.arange(half_dim, dtype=jnp.float32) * (2.0 / HD))
    angles = places.astype(jnp.float32)[:, None] * inverse[None, :]
    cosines = jnp.cos(angles)[:, None, :]
    sines = jnp.sin(angles)[:, None, :]
    lower_half = by_head[:, :, :half_dim]
    upper_half = by_head[:, :, half_dim:]
    return jnp.concatenate(
        [lower_half * cosines - upper_half * sines, upper_half * cosines + lower_half * sines],
        axis=2,
    )


def project(tokens, gain_row, w_section, qk_gain, places):
    row_count = tokens.shape[0]
    as_float = tokens.astype(jnp.float32)
    inv_rms = lax.rsqrt(jnp.mean(as_float * as_float, axis=1, keepdims=True) + epsilon)
    normed = (as_float * inv_rms * gain_row[None, :]).astype(jnp.bfloat16)
    col_width = w_section.shape[2]
    projected = jnp.dot(
        normed,
        w_section.reshape(w_section.shape[0], 3 * col_width),
        preferred_element_type=jnp.float32,
    )
    projected = projected.reshape(row_count, 3, col_width)
    queries = rotate(headnorm(projected[:, 0], qk_gain[0]), places).astype(jnp.bfloat16)
    key_rows = rotate(headnorm(projected[:, 1], qk_gain[1]), places).astype(jnp.bfloat16)
    value_rows = projected[:, 2].reshape(row_count, -1, HD).astype(jnp.bfloat16)
    return (queries, key_rows, value_rows)


def attend(queries, query_places, key_rows, value_rows):
    query_count = queries.shape[0]
    head_count = queries.shape[1]
    inv_root = 1.0 / math.sqrt(HD)
    running = jnp.full((query_count, head_count), masked_score, jnp.float32)
    key_piece = lax.all_gather(key_rows, "seq", axis=0, tiled=True)
    value_piece = lax.all_gather(value_rows, "seq", axis=0, tiled=True)
    scores = (
        jnp.einsum("qhd,khd->qhk", queries, key_piece, preferred_element_type=jnp.float32)
        * inv_root
    )
    key_places = jnp.arange(key_piece.shape[0], dtype=jnp.int32)
    allowed = (key_places[None, :] <= query_places[:, None])[:, None, :]
    scores = jnp.where(allowed, scores, masked_score)
    new_best = jnp.maximum(running, jnp.max(scores, axis=2))
    weights = jnp.where(allowed, jnp.exp(scores - new_best[:, :, None]), 0.0)
    denominator = jnp.sum(weights, axis=2)
    weighted = jnp.einsum(
        "qhk,khd->qhd",
        weights.astype(jnp.bfloat16),
        value_piece,
        preferred_element_type=jnp.float32,
    )
    running, denominator, weighted = (new_best, denominator, weighted)
    return (
        (weighted / denominator[:, :, None])
        .astype(jnp.bfloat16)
        .reshape(query_count, head_count * HD)
    )


def shards(tokens, modality, norm_gain, w_qkv, qk_gain, w_out):
    row_count = tokens.shape[0]
    section = lax.axis_index("mod")
    seq_block = lax.axis_index("seq")
    places = seq_block * row_count + jnp.arange(row_count, dtype=jnp.int32)
    gathered = lax.all_gather(tokens, ("mod", "tp"), axis=1, tiled=True)
    queries, key_rows, value_rows = project(gathered, norm_gain[0], w_qkv[0], qk_gain, places)
    stacked = jnp.stack([queries, key_rows, value_rows], axis=0)
    partner = swapped(stacked, "mod", 0)
    own_rows = (modality == section)[None, :, None, None]
    joined = jnp.where(own_rows, stacked, partner)
    queries, key_rows, value_rows = (joined[0], joined[1], joined[2])
    heads_out = attend(queries, places, key_rows, value_rows)
    masked = jnp.where((modality == section)[:, None], heads_out, jnp.zeros_like(heads_out))
    partial_value = jnp.dot(masked, w_out[0], preferred_element_type=jnp.float32)
    result = lax.psum_scatter(partial_value, ("mod", "tp"), scatter_dimension=1, tiled=True)
    return result.astype(jnp.bfloat16)


def solution(mesh):
    placed = (
        P("seq", ("mod", "tp")),
        P("seq"),
        P("mod", None),
        P("mod", None, None, "tp"),
        P(None, "tp"),
        P("mod", "tp", None),
    )
    return jax.shard_map(
        shards, mesh=mesh, in_specs=placed, out_specs=P("seq", ("mod", "tp")), check_vma=False
    )
```

profile of v0, /device:TPU:1, one launch (start us, length us, event | category | flops | bytes accessed | tf_op | source)
XLA Modules:
  0.0 348.5 jit_solution(6936272427434710083)
XLA Ops:
  6.5 0.0 copy-start
  6.5 0.0 all-gather.4.cloned.1.call-start
  6.5 0.7 all-gather.4.cloned.1.call-update
  7.3 0.0 reduce-scatter.2.cloned.1.call-start
  7.3 0.0 copy-start.4
  7.3 0.0 copy-start.5
  7.3 8.6 %copy.7 = bf16[1,8192,3,128]{1,3,2,0:T(8,128)(2,1)} copy(bf16[1,8192,3,128]{3,1,2,0:T(8,128)(2,1)} %param.9) | data formatting | bytes 12582912 | tf_op args[3]
  16.0 0.0 copy-done.4
  16.0 83.7 %all-gather.4.cloned.1.call-done = bf16[512,8192]{1,0:T(8,128)(2,1)} async-done(((bf16[512,128]{1,0:T(8,128)(2,1)}), bf16[512,8192]{1,0:T(8,128)(2,1)}) %all-gather.4.cloned.1.call-update) | async-done | bytes 8388624 | tf_op jit(solution)/shard_map/all_gather | solution.py:96
  99.7 5.3 %fusion = f32[512]{0:T(512)S(1)} fusion(bf16[512,8192]{1,0:T(8,128)(2,1)} %all-gather.4.cloned.1.call-done), kind=kLoop, calls=%fused_computation.2 | loop fusion | flops 12582400 | bytes 8390656 | tf_op jit(solution)/shard_map/reduce_sum | solution.py:45
  104.9 0.0 copy-done.5
  104.9 0.5 copy-done.2
  105.4 6.7 %fusion.4 = f32[512,3,128]{0,2,1:T(8,128)S(1)} fusion(bf16[512,8192]{1,0:T(8,128)(2,1)S(1)} %copy-done.2, f32[8192]{0:T(1024)S(1)} %bitcast.102, f32[512]{0:T(512)S(1)} %add_rsqrt_fusion.2, bf16[1,8192,3,128]{1,3,2,0:T(8,128)(2,1)} %copy.7), kind=kOutput, calls=%fused_computation.6 | convolution fusion | flops 3238002688 | bytes 15501312 | tf_op jit(solution)/shard_map/dot_general | solution.py:48
  112.2 0.1 slice_reduce_fusion.1
  112.3 0.1 multiply_reduce_fusion.1
  112.4 0.1 multiply_multiply_fusion.1
  112.5 0.6 fusion.61
  113.1 0.3 collective-permute-start
  113.5 0.0 copy-done.3
  113.5 1.5 collective-permute-done
  114.9 0.1 broadcast_select_fusion
  115.1 10.9 %all-gather = bf16[1,2048,1,128]{1,3,2,0:T(8,128)(2,1)S(1)} all-gather(bf16[1,512,1,128]{1,3,2,0:T(8,128)(2,1)S(1)} %get-tuple-element.11), channel_id=2, replica_groups=mesh['mod'=2,'tp'=32,'seq'=4] {'seq'}, dimensions={1}, use_global_device_ids=true | all-gather | bytes 655360 | tf_op jit(solution)/shard_map/all_gather | solution.py:66
  126.0 9.9 %all-gather.1 = bf16[1,2048,1,128]{1,3,2,0:T(8,128)(2,1)S(1)} all-gather(bf16[1,512,1,128]{1,3,2,0:T(8,128)(2,1)S(1)} %get-tuple-element.12), channel_id=3, replica_groups=mesh['mod'=2,'tp'=32,'seq'=4] {'seq'}, dimensions={1}, use_global_device_ids=true | all-gather | bytes 655360 | tf_op jit(solution)/shard_map/all_gather | solution.py:65
  135.9 0.8 fusion.9
  136.7 0.0 copy-start.1
  136.8 1.9 copy-done.1
  138.7 1.2 fusion.10
  139.9 0.0 copy-done
  139.9 10.4 %fusion.13 = f32[512,8192]{1,0:T(8,128)} fusion(bf16[1,128,8192]{2,1,0:T(8,128)(2,1)S(1)} %copy-done, f32[2048,512]{1,0:T(8,128)} %copy-done.1, f32[512]{0:T(512)S(1)} %broadcast_maximum_fusion, s32[512]{0:T(512)S(1)} %iota_add_fusion, bf16[1,2048,1,128]{1,3,2,0:T(8,128)(2,1)S(1)} %all-gather, f32[512]{0:T(512)S(1)} %fusion.10, ...), kind=kOutput, calls=%fused_computation.17 | convolution fusion | flops 1348665344 | bytes 23599616 | tf_op jit(solution)/shard_map/dot_general | solution.py:105
  150.3 0.0 reduce-scatter.2.cloned.1.call-update
  150.3 189.8 %reduce-scatter.2.cloned.1.call-done = f32[512,128]{1,0:T(8,128)} async-done(((f32[512,8192]{1,0:T(8,128)}), f32[512,128]{1,0:T(8,128)}) %reduce-scatter.2.cloned.1.call-update) | async-done | bytes 262160 | tf_op jit(solution)/shard_map/reduce_scatter | solution.py:106
  340.1 1.6 convert_element_type.50
  (15 shorter events, 0.1 us)
Async XLA Ops:
  6.5 133.4 %copy-start = (bf16[1,128,8192]{2,1,0:T(8,128)(2,1)S(1)}, bf16[1,128,8192]{2,1,0:T(8,128)(2,1)}, u32[]{:S(2)}) copy-start(bf16[1,128,8192]{2,1,0:T(8,128)(2,1)} %param.11) | copy-start | bytes 6291460
  6.5 93.1 %all-gather.4.cloned.1.call-start = ((), (), s32[]{:S(2)}) async-start(), calls=%async_computation.1 | async-start | bytes 8519680 | tf_op jit(solution)/shard_map/all_gather | solution.py:96
  7.3 332.8 %reduce-scatter.2.cloned.1.call-start = ((), (), s32[]{:S(2)}) async-start(), calls=%async_computation.2 | async-start | bytes 17039360 | tf_op jit(solution)/shard_map/reduce_scatter | solution.py:106
  7.3 8.7 %copy-start.4 = (f32[2,128]{1,0:T(2,128)S(1)}, f32[2,128]{1,0:T(2,128)}, u32[]{:S(2)}) copy-start(f32[2,128]{1,0:T(2,128)} %param.10) | copy-start | bytes 3076
  7.3 97.6 %copy-start.5 = (f32[1,8192]{1,0:T(1,128)S(1)}, f32[1,8192]{1,0:T(1,128)}, u32[]{:S(2)}) copy-start(f32[1,8192]{1,0:T(1,128)} %param.8) | copy-start | bytes 98308
  99.7 5.8 %copy-start.2 = (bf16[512,8192]{1,0:T(8,128)(2,1)S(1)}, bf16[512,8192]{1,0:T(8,128)(2,1)}, u32[]{:S(2)}) copy-start(bf16[512,8192]{1,0:T(8,128)(2,1)} %all-gather.4.cloned.1.call-done) | copy-start | bytes 25165828
  105.4 8.0 %copy-start.3 = (s32[512]{0:T(512)S(1)}, s32[512]{0:T(512)}, u32[]{:S(2)}) copy-start(s32[512]{0:T(512)} %param.7) | copy-start | bytes 6148
  113.1 1.8 collective-permute-start
  136.7 1.9 copy-start.1
Sparse Core Ops, SparseCore 0:
  9.9 89.7 all-gather.3
  150.4 189.6 reduce-scatter.1
where the time goes:
time: 352 us; the launch traced here: 349 us
  waiting for transfers between devices  276 us (78%)
  blocking collectives  20.8 us (6%)
  matrix products  17.9 us (5%)
  between operations  13.5 us (4%)
  local copies, waits for them, and re-layouts  11.1 us (3%)
  other arithmetic  9.12 us (3%)
    reduce_scatter x1, waiting for transfers between devices, shards(): lax.psum_scatter(partial_value, ('mod', 'tp'), scatter_dimension=1, tiled...  190 us
    all_gather x1, waiting for transfers between devices, shards(): gathered = lax.all_gather(tokens, ('mod', 'tp'), axis=1, tiled=True)  83.7 us
    unnamed x13, local copies, waits for them, and re-layouts  11.1 us
    all_gather x1, blocking collectives, attend(): value_piece = lax.all_gather(value_rows, 'seq', axis=0, tiled=True)  10.9 us
    dot_general x1, matrix products, shards(): jnp.dot(masked, w_out[0], preferred_element_type=jnp.float32)  10.4 us
    all_gather x1, blocking collectives, attend(): key_piece = lax.all_gather(key_rows, 'seq', axis=0, tiled=True)  9.89 us
  transfers between devices with their start and end apart: 3, of which 3 were waited for; matrix products, arithmetic and copies ran while one was open for 2% of the time, Pallas kernels for 0%

commit v1 on v0

v1 whole, which is shorter than its diff:
```python
import math

import jax
import jax.numpy as jnp
from jax import lax
from jax.experimental import pallas as pl
from jax.experimental.pallas import tpu as pltpu
from jax.sharding import Mesh
from jax.sharding import PartitionSpec as P

HD = 128
EPS = 1e-05
MASKED = -1e30
NY = 4
NZ = 8
NX = 4
AXES = ("mod", "y", "z", "seq")
ROWS_A = 256


def pairs(dc, dy, dz, dx, wrap_x=True):
    out = []
    for c in range(2):
        for y in range(NY):
            for z in range(NZ):
                for x in range(NX):
                    if not wrap_x and not 0 <= x - dx < NX:
                        continue
                    source = ((c * NY + y) * NZ + z) * NX + x
                    to = (((c - dc) % 2 * NY + (y - dy) % NY) * NZ + (z - dz) % NZ) * NX + (x - dx) % NX
                    out.append((source, to))
    return out


def take(x, dc=0, dy=0, dz=0, dx=0, wrap_x=True):
    return lax.ppermute(x, AXES, pairs(dc, dy, dz, dx, wrap_x))


def gather_a(rows):
    s1, s3, s2 = take(rows, dy=1), take(rows, dy=-1), take(rows, dy=2)
    own = jnp.stack([rows, s1, s2, s3])
    f1, b1 = take(own, dz=1), take(own, dz=-1)
    f2, b2 = take(f1, dz=1), take(b1, dz=-1)
    f3, b3 = take(f2, dz=1), take(b2, dz=-1)
    f4, b4 = take(f3[:2], dz=1), take(b3[2:], dz=-1)
    return [own, f1, f2, f3, jnp.concatenate([f4, b4]), b3, b2, b1]


def gather_b(rows):
    got = [rows] + [take(rows, dz=d if d < 5 else d - 8) for d in range(1, NZ)]
    own = jnp.stack(got)
    f1, b1 = take(own, dy=1), take(own, dy=-1)
    f2, b2 = take(f1[:4], dy=1), take(b1[4:], dy=-1)
    return [own, f1, jnp.concatenate([f2, b2]), b1]


def qkv_kernel(z_first, at_ref, inv_ref, own_row_ref, gain_ref, gain_other_ref, w_ref, w_other_ref, *rest):
    pieces, out_ref, acc = rest[:-2], rest[-2], rest[-1]
    step = pl.program_id(0)
    inverse = inv_ref[...]
    own_row = own_row_ref[...] > 0
    normed, own_w, other_w = [], [], []
    for k, piece in enumerate(pieces):
        if z_first:
            yi, zi = lax.rem(at_ref[1] + k, NY), lax.rem(at_ref[2] + step, NZ)
            where = (0, yi, 0)
        else:
            yi, zi = lax.rem(at_ref[1] + step, NY), lax.rem(at_ref[2] + k, NZ)
            where = (0, 0, zi)
        gain = jnp.where(own_row, gain_ref[yi, pl.ds(zi, 1), :], gain_other_ref[yi, pl.ds(zi, 1), :])
        normed.append((piece[0].astype(jnp.float32) * inverse * gain).astype(jnp.bfloat16))
        own_w.append(jnp.concatenate([w_ref[(p, *where)] for p in range(3)], axis=1))
        other_w.append(jnp.concatenate([w_other_ref[(p, *where)] for p in range(3)], axis=1))
    left = jnp.concatenate(normed, axis=1)
    right = jnp.concatenate(
        [jnp.concatenate(own_w, axis=0), jnp.concatenate(other_w, axis=0)], axis=1
    )
    part = jnp.dot(left, right, preferred_element_type=jnp.float32)

    @pl.when(step == 0)
    def _():
        acc[...] = part

    @pl.when(step > 0)
    def _():
        acc[...] += part

    @pl.when(step == pl.num_programs(0) - 1)
    def _():
        out_ref[...] = jnp.where(own_row, acc[:, : 3 * HD], acc[:, 3 * HD :])


def qkv_part(at, inverse, own_row, gain, gain_other, w, w_other, pieces, z_first):
    rows = pieces[0].shape[1]
    steps = pieces[0].shape[0]
    if z_first:
        block = (3, 1, NY, 1, HD, HD)
        index = lambda g, at: (0, at[0], 0, lax.rem(at[2] + g, NZ), 0, 0)
        index_other = lambda g, at: (0, 0, 0, lax.rem(at[2] + g, NZ), 0, 0)
    else:
        block = (3, 1, 1, NZ, HD, HD)
        index = lambda g, at: (0, at[0], lax.rem(at[1] + g, NY), 0, 0, 0)
        index_other = lambda g, at: (0, 0, lax.rem(at[1] + g, NY), 0, 0, 0)

    def body(*refs):
        qkv_kernel(z_first, *refs)

    whole = lambda shape: pl.BlockSpec(shape, lambda g, at: (0,) * len(shape))
    return pl.pallas_call(
        body,
        grid_spec=pltpu.PrefetchScalarGridSpec(
            num_scalar_prefetch=1,
            grid=(steps,),
            in_specs=[
                whole((rows, 1)),
                whole((rows, 1)),
                whole((NY, NZ, HD)),
                whole((NY, NZ, HD)),
                pl.BlockSpec(block, index),
                pl.BlockSpec(block, index_other),
            ]
            + [pl.BlockSpec((1, rows, HD), lambda g, at: (g, 0, 0)) for _ in pieces],
            out_specs=whole((rows, 3 * HD)),
            scratch_shapes=[pltpu.VMEM((rows, 6 * HD), jnp.float32)],
        ),
        out_shape=jax.ShapeDtypeStruct((rows, 3 * HD), jnp.float32),
        compiler_params=pltpu.CompilerParams(vmem_limit_bytes=40 * 2**20),
        cost_estimate=pl.CostEstimate(
            flops=2 * rows * 4096 * 6 * HD, bytes_accessed=8 * 2**20, transcendentals=0
        ),
    )(at, inverse, own_row, gain, gain_other, w, w_other, *pieces)


def headnorm(x, gain_row):
    average = jnp.mean(x, axis=1, keepdims=True)
    centred = x - average
    variance = jnp.mean(centred * centred, axis=1, keepdims=True)
    return centred * lax.rsqrt(variance + EPS) * gain_row[None, :]


def rotate(x, cosines, sines):
    lower, upper = x[:, : HD // 2], x[:, HD // 2 :]
    return jnp.concatenate([lower * cosines - upper * sines, upper * cosines + lower * sines], axis=1)


def attention_kernel(base_ref, q_ref, *rest):
    key_refs, out_ref = rest[:-1], rest[-1]
    rows = q_ref.shape[0]
    queries = q_ref[...]
    scale = 1.0 / math.sqrt(HD)
    row = base_ref[0] + lax.broadcasted_iota(jnp.int32, (rows, rows), 0)
    column = lax.broadcasted_iota(jnp.int32, (rows, rows), 1)
    blocks = [(ref, i) for ref in key_refs for i in range(ref.shape[0])]
    scores, seen = [], []
    for n, (ref, i) in enumerate(blocks):
        s = lax.dot_general(queries, ref[i, 0], (((1,), (1,)), ((), ())), preferred_element_type=jnp.float32)
        allowed = column + base_ref[n] <= row
        seen.append(allowed)
        scores.append(jnp.where(allowed, s * scale, MASKED))
    best = scores[0].max(axis=1, keepdims=True)
    for s in scores[1:]:
        best = jnp.maximum(best, s.max(axis=1, keepdims=True))
    total = jnp.zeros((rows, 1), jnp.float32)
    out = jnp.zeros((rows, HD), jnp.float32)
    for n, (ref, i) in enumerate(blocks):
        weights = jnp.where(seen[n], jnp.exp(scores[n] - best), 0.0)
        total += weights.sum(axis=1, keepdims=True)
        out += jnp.dot(weights.astype(jnp.bfloat16), ref[i, 1], preferred_element_type=jnp.float32)
    out_ref[...] = (out / total).astype(jnp.bfloat16)


def attention(bases, queries, keys):
    vmem = pl.BlockSpec(memory_space=pltpu.VMEM)
    return pl.pallas_call(
        attention_kernel,
        in_specs=[pl.BlockSpec(memory_space=pltpu.SMEM)] + [vmem] * (1 + len(keys)),
        out_specs=vmem,
        out_shape=jax.ShapeDtypeStruct(queries.shape, jnp.bfloat16),
        compiler_params=pltpu.CompilerParams(vmem_limit_bytes=40 * 2**20),
        cost_estimate=pl.CostEstimate(flops=2**28, bytes_accessed=2**20, transcendentals=2**19),
    )(bases, queries, *keys)


def out_kernel(own_row_ref, w_ref, w_other_ref, h0, h1, h2, h3, out_ref):
    heads = jnp.concatenate([h0[...], h1[...], h2[...], h3[...]], axis=1)
    sums = []
    for ref in (w_ref, w_other_ref):
        w = jnp.concatenate([ref[x, y] for y in range(NY) for x in range(NX)], axis=0)
        sums.append(jnp.dot(heads, w, preferred_element_type=jnp.float32))
    out_ref[0] = jnp.where(own_row_ref[...] > 0, *sums).astype(jnp.bfloat16)


def out_part(own_row, w, w_other, heads):
    rows = heads[0].shape[0]
    width = w.shape[-1] // NZ
    whole = lambda shape: pl.BlockSpec(shape, lambda g: (0,) * len(shape))
    weights = pl.BlockSpec((NX, NY, HD // NX, width), lambda g: (0, 0, 0, g))
    return pl.pallas_call(
        out_kernel,
        grid=(NZ,),
        in_specs=[whole((rows, 1)), weights, weights] + [whole((rows, HD))] * NY,
        out_specs=pl.BlockSpec((1, rows, width), lambda g: (g, 0, 0)),
        out_shape=jax.ShapeDtypeStruct((NZ, rows, width), jnp.bfloat16),
        compiler_params=pltpu.CompilerParams(vmem_limit_bytes=40 * 2**20),
        cost_estimate=pl.CostEstimate(
            flops=4 * rows * NY * HD * NZ * width, bytes_accessed=5 * 2**20, transcendentals=0
        ),
    )(own_row, w, w_other, *heads)


def spread_w_out(w_out, y, seq):
    quarter = lax.dynamic_slice_in_dim(w_out[0], seq * (HD // NX), HD // NX, axis=0)
    by_y = quarter.reshape(HD // NX, 2, NY, NZ, HD).transpose(2, 0, 3, 1, 4).reshape(NY, HD // NX, 2 * NZ * HD)
    pick = lambda d: lax.dynamic_index_in_dim(by_y, lax.rem(y - d + NY, NY), axis=0, keepdims=False)
    s1, s3, s2 = take(pick(1), dy=1), take(pick(3), dy=-1), take(pick(2), dy=2)
    lines = jnp.stack([pick(0), s1, s2, s3])
    return lax.all_gather(lines, "seq", axis=0)


def shards(tokens, modality, norm_gain, w_qkv, qk_gain, w_out):
    row_count = tokens.shape[0]
    half = row_count // 2
    c, y, z, seq = (lax.axis_index(a) for a in AXES)
    own_row = (modality == c).astype(jnp.int32)[:, None]

    squares = jnp.sum(jnp.square(tokens.astype(jnp.float32)), axis=1)
    pieces_a = gather_a(tokens[:ROWS_A])
    pieces_b = gather_b(tokens[ROWS_A:])
    squares = lax.psum(squares, ("mod", "y", "z"))
    inverse = lax.rsqrt(squares / (2 * NY * NZ * HD) + EPS)[:, None]

    w = w_qkv[0].transpose(1, 0, 2).reshape(3, 2, NY, NZ, HD, HD)
    gains = norm_gain.reshape(2, NY, NZ, HD)
    w_other = take(lax.dynamic_slice_in_dim(w, 1 - c, 1, axis=1), dc=1)
    gain_other = take(lax.dynamic_index_in_dim(gains, 1 - c, axis=0, keepdims=False), dc=1)
    gain = lax.dynamic_index_in_dim(gains, c, axis=0, keepdims=False)
    w_cols = spread_w_out(w_out, y, seq)
    w_cols_other = take(w_cols, dc=1)

    at = jnp.stack([c, y, z]).astype(jnp.int32)
    common = lambda rows: (at, inverse[rows], own_row[rows], gain, gain_other, w, w_other)
    part_a = qkv_part(*common(slice(None, ROWS_A)), pieces_a, False)
    part_b = qkv_part(*common(slice(ROWS_A, None)), pieces_b, True)
    parts = jnp.concatenate([part_a, part_b]).reshape(2, half, 3 * HD)
    mine = lax.dynamic_index_in_dim(parts, c, axis=0, keepdims=False)
    theirs = lax.dynamic_index_in_dim(parts, 1 - c, axis=0, keepdims=False)
    projected = mine + take(theirs, dc=1)

    first = seq * row_count + c * half
    places = first + jnp.arange(half, dtype=jnp.int32)
    rates = 1.0 / 10000.0 ** (jnp.arange(HD // 2, dtype=jnp.float32) * (2.0 / HD))
    angles = places.astype(jnp.float32)[:, None] * rates[None, :]
    cosines, sines = jnp.cos(angles), jnp.sin(angles)
    queries = rotate(headnorm(projected[:, :HD], qk_gain[0]), cosines, sines).astype(jnp.bfloat16)
    keys = rotate(headnorm(projected[:, HD : 2 * HD], qk_gain[1]), cosines, sines).astype(jnp.bfloat16)
    values = projected[:, 2 * HD :].astype(jnp.bfloat16)

    own_keys = jnp.stack([keys, values])
    got = jnp.stack([own_keys] + [take(own_keys, dx=-d, wrap_x=False) for d in (1, 2, 3)])
    sibling = take(got, dc=1)
    never = 1 << 20
    begin = [jnp.where(seq >= d, (seq - d) * row_count, never) for d in range(NX)]
    bases = jnp.stack([b + c * half for b in begin] + [b + (1 - c) * half for b in begin]).astype(jnp.int32)
    heads_out = attention(bases, queries, [got, sibling])

    h1, h3, h2 = take(heads_out, dy=1), take(heads_out, dy=-1), take(heads_out, dy=2)
    own_half = lax.dynamic_slice_in_dim(own_row, c * half, half, axis=0)
    partial = out_part(own_half, w_cols, w_cols_other, [heads_out, h1, h2, h3])
    spread = lax.all_to_all(partial, "z", 0, 0)
    summed = jnp.sum(spread.astype(jnp.float32), axis=0).astype(jnp.bfloat16).reshape(half, 2, HD)
    keep = lax.dynamic_index_in_dim(summed, c, axis=1, keepdims=False)
    other = take(lax.dynamic_index_in_dim(summed, 1 - c, axis=1, keepdims=False), dc=1)
    return jnp.where(c == 0, jnp.concatenate([keep, other]), jnp.concatenate([other, keep]))


def solution(mesh):
    mesh = Mesh(mesh.devices.reshape(2, NY, NZ, NX), AXES)
    tp = ("y", "z")
    placed = (
        P("seq", ("mod", *tp)),
        P("seq"),
        P("mod", None),
        P("mod", None, None, tp),
        P(None, tp),
        P("mod", tp, None),
    )
    return jax.shard_map(shards, mesh=mesh, in_specs=placed, out_specs=P("seq", ("mod", *tp)), check_vma=False)
```

time: 352 us -> 313 us (0.89)
  waiting for transfers between devices: 276 us -> 22 us
  blocking collectives: 20.8 us -> 159 us
  starting transfers between devices: 0.38 us -> 54.2 us
  local copies, waits for them, and re-layouts: 11.1 us -> 34.4 us
  Pallas kernels: 0 us -> 20.3 us
  matrix products: 17.9 us -> 0 us
    reduce_scatter x1 -> x0, waiting for transfers between devices: 190 us -> none  [shards(): lax.psum_scatter(partial_value, ('mod', 'tp'), scatter_dimension=1, tiled...]
    psum x0 -> x1, blocking collectives: none -> 130 us  [shards(): squares = lax.psum(squares, ('mod', 'y', 'z'))]
    all_gather x1, waiting for transfers between devices: 83.7 us -> 0.02 us  [spread_w_out(): return lax.all_gather(lines, 'seq', axis=0)]
    ppermute x1 -> x37, starting transfers between devices: 0.34 us -> 54.2 us  [take(): return lax.ppermute(x, AXES, pairs(dc, dy, dz, dx, wrap_x))]
    all_to_all x0 -> x1, blocking collectives: none -> 29.7 us  [shards(): spread = lax.all_to_all(partial, 'z', 0, 0)]
    all_gather x2 -> x0, blocking collectives: 20.8 us -> none  [the longest x1 10.9 us: attend(): value_piece = lax.all_gather(value_rows, 'seq', axis=0, tiled=True)]
    ppermute x1 -> x37, waiting for transfers between devices: 1.46 us -> 21.9 us  [take(): return lax.ppermute(x, AXES, pairs(dc, dy, dz, dx, wrap_x))]
    pallas_call x0 -> x4, Pallas kernels: none -> 20.3 us  [the longest x2 13 us: qkv_part(): pl.pallas_call(body, grid_spec=pltpu.PrefetchScalarGridSpec(num_scalar_pr...]
  transfers between devices with their start and end apart: 3 -> 38, of which waited for: 3 -> 15; matrix products, arithmetic and copies ran while one was open for 2% -> 10% of each run, Pallas kernels for 0% -> 5%
where the time goes in v1:
time: 313 us; the launch traced here: 312 us
  blocking collectives  159 us (51%)
  starting transfers between devices  54.2 us (17%)
  local copies, waits for them, and re-layouts  34.4 us (11%)
  waiting for transfers between devices  22 us (7%)
  Pallas kernels  20.3 us (6%)
  between operations  13.8 us (4%)
  other arithmetic  7.85 us (3%)
    psum x1, blocking collectives, shards(): squares = lax.psum(squares, ('mod', 'y', 'z'))  130 us
    ppermute x37, starting transfers between devices, take(): return lax.ppermute(x, AXES, pairs(dc, dy, dz, dx, wrap_x))  54.2 us
    all_to_all x1, blocking collectives, shards(): spread = lax.all_to_all(partial, 'z', 0, 0)  29.7 us
    ppermute x37, waiting for transfers between devices, take(): return lax.ppermute(x, AXES, pairs(dc, dy, dz, dx, wrap_x))  21.9 us
    unnamed x33, local copies, waits for them, and re-layouts  14.9 us
    pallas_call x2, Pallas kernels, qkv_part(): pl.pallas_call(body, grid_spec=pltpu.PrefetchScalarGridSpec(num_scalar_pr...  13 us
  transfers between devices with their start and end apart: 38, of which 15 were waited for; matrix products, arithmetic and copies ran while one was open for 10% of the time, Pallas kernels for 5%

profile of v1, /device:TPU:1, one launch (start us, length us, event | category | flops | bytes accessed | tf_op | source)
XLA Modules:
  0.0 312.0 jit_solution(15002598013288222741)
XLA Ops:
  6.5 1.7 slice_bitcast_fusion.2
  8.2 3.6 %collective-permute-start.6 = (bf16[256,128]{1,0:T(8,128)(2,1)S(1)}, bf16[256,128]{1,0:T(8,128)(2,1)}, u32[]{:S(2)}, u32[]{:S(2)}) collective-permute-start(bf16[256,128]{1,0:T(8,128)(2,1)S(1)} %get-tuple-element.23), channel_id=1, source_target_pairs={{0,96},{1,97},{2,98},{3,99},{4,100},{5,101},{6,102},{7,103},{8,104... | collective-permute-start | bytes 196616 | tf_op jit(solution)/shard_map/ppermute | solution.py:36
  12.8 5.6 %collective-permute-start.17 = (bf16[256,128]{1,0:T(8,128)(2,1)}, bf16[256,128]{1,0:T(8,128)(2,1)S(1)}, u32[]{:S(2)}, u32[]{:S(2)}) collective-permute-start(bf16[256,128]{1,0:T(8,128)(2,1)} %get-tuple-element.22), channel_id=1, source_target_pairs={{0,28},{1,29},{2,30},{3,31},{4,0},{5,1},{6,2},{7,3},{8,4},{9,5},{1... | collective-permute-start | bytes 196616 | tf_op jit(solution)/shard_map/ppermute | solution.py:36
  22.8 4.1 %constant_dynamic-slice_fusion.2 = bf16[3,1,4,8,128,128]{5,4,3,2,1,0:T(8,128)(2,1)} fusion(bf16[3,2,4,8,128,128]{5,4,3,2,1,0:T(8,128)(2,1)} %bitcast.87, s32[]{:T(128)S(6)} %select_n.66), kind=kLoop, calls=%fused_computation.58 | loop fusion | bytes 6291460 | tf_op jit(solution)/shard_map/dynamic_slice | solution.py:234
  26.9 2.1 collective-permute-start.5
  30.4 2.0 collective-permute-start
  33.8 1.6 collective-permute-done.19
  35.3 1.6 collective-permute-start.2
  37.6 2.3 collective-permute-start.20
  40.8 4.7 %collective-permute-start.21 = (bf16[256,128]{1,0:T(8,128)(2,1)}, bf16[256,128]{1,0:T(8,128)(2,1)S(1)}, u32[]{:S(2)}, u32[]{:S(2)}) collective-permute-start(bf16[256,128]{1,0:T(8,128)(2,1)} %get-tuple-element.22), channel_id=1, source_target_pairs={{0,12},{1,13},{2,14},{3,15},{4,16},{5,17},{6,18},{7,19},{8,20},{9,... | collective-permute-start | bytes 196616 | tf_op jit(solution)/shard_map/ppermute | solution.py:36
  45.5 1.8 collective-permute-start.22
  48.2 2.9 collective-permute-start.9
  52.5 2.0 collective-permute-done.22
  57.5 129.8 %psum.7 = f32[512]{0:T(512)S(1)} all-reduce(f32[512]{0:T(512)S(1)} %multiply_reduce_fusion), channel_id=1, replica_groups=mesh['mod'=2,'y'=4,'z'=8,'seq'=4] {'mod','y','z'}, use_global_device_ids=true, to_apply=%region_1.0 | all-reduce | flops 512 | bytes 4096 | tf_op jit(solution)/shard_map/psum | solution.py:229
  192.4 1.8 collective-permute-done.10.refs_9_
  197.8 3.9 %collective-permute-done.11.refs_10_ = bf16[4,256,128]{2,1,0:T(8,128)(2,1)} collective-permute-done((bf16[4,256,128]{2,1,0:T(8,128)(2,1)}, bf16[4,256,128]{2,1,0:T(8,128)(2,1)}, u32[]{:S(2)}, u32[]{:S(2)}) %collective-permute-start.11) | collective-permute-done | bytes 262176 | tf_op jit(solution)/shard_map/ppermute | solution.py:36
  201.7 1.6 slice.93
  203.3 1.7 collective-permute-start.12
  205.0 1.6 slice.94
  214.2 2.8 copy-done.1
  219.4 5.5 %shard_map.64 = f32[256,384]{1,0:T(8,128)S(1)} custom-call(s32[3]{0:T(128)S(1)} %copy-done.7, f32[256,1]{1,0:T(8,128)S(1)} %copy-done.6, s32[256,1]{1,0:T(8,128)S(1)} %copy-done.5, f32[4,8,128]{2,1,0:T(8,128)S(1)} %get-tuple-element.25.refs_3_, f32[4,8,128]{2,1,0:T(8,128)S(1)} %collective-permute-done.4.refs_4_, ...), custom_call_target="tpu_custom_call" | custom-call | flops 1610612736 | bytes 8388608 | tf_op jit(solution)/shard_map/pallas_call | solution.py:109
  224.9 2.8 copy-done.2
  227.7 7.5 %shard_map.65 = f32[256,384]{1,0:T(8,128)S(1)} custom-call(s32[3]{0:T(128)S(1)} %copy-done.7, f32[256,1]{1,0:T(8,128)S(1)} %copy-done.4, s32[256,1]{1,0:T(8,128)S(1)} %copy.24.refs_2_, f32[4,8,128]{2,1,0:T(8,128)S(1)} %get-tuple-element.25.refs_3_, f32[4,8,128]{2,1,0:T(8,128)S(1)} %collective-permute-done.4.refs_4_, ...), custom_call_target="tpu_custom_call" | custom-call | flops 1610612736 | bytes 8388608 | tf_op jit(solution)/shard_map/pallas_call | solution.py:109
  239.9 3.1 collective-permute-start.29
  243.0 4.4 %collective-permute-start.30 = (bf16[2,256,128]{2,1,0:T(8,128)(2,1)S(1)}, bf16[2,256,128]{2,1,0:T(8,128)(2,1)S(1)}, u32[]{:S(2)}, u32[]{:S(2)}) collective-permute-start(bf16[2,256,128]{2,1,0:T(8,128)(2,1)S(1)} %pad_maximum_fusion.6), channel_id=1, source_target_pairs={{0,2},{1,3},{4,6},{5,7},{8,10},{9,11},{12,14},{13,15},{16,18},{17,... | collective-permute-start | bytes 393224 | tf_op jit(solution)/shard_map/ppermute | solution.py:36
  250.9 1.6 collective-permute-start.32
  254.1 1.7 shard_map.66.h0
  258.9 2.7 collective-permute-done.34.h2
  263.0 1.6 copy-done.3
  264.6 5.6 %shard_map.67 = bf16[8,256,256]{2,1,0:T(8,128)(2,1)S(1)} custom-call(s32[256,1]{1,0:T(8,128)S(1)} %copy.25.own_row_ref, bf16[4,4,32,2048]{3,2,1,0:T(8,128)(2,1)S(1)} %bitcast.91, bf16[4,4,32,2048]{3,2,1,0:T(8,128)(2,1)} %collective-permute-done.3.w_other_ref, bf16[256,128]{1,0:T(8,128)(2,1)S(1)} %shard_map.66.h0, ...), custom_call_target="tpu_custom_call" | custom-call | flops 1073741824 | bytes 5242880 | tf_op jit(solution)/shard_map/pallas_call | solution.py:198
  270.2 29.7 %all_to_all.5 = bf16[8,256,256]{2,1,0:T(8,128)(2,1)S(1)} all-to-all(bf16[8,256,256]{2,1,0:T(8,128)(2,1)S(1)} %shard_map.67), channel_id=1, replica_groups=mesh['mod'=2,'y'=4,'z'=8,'seq'=4] {'z'}, dimensions={0} | all-to-all | bytes 2097152 | tf_op jit(solution)/shard_map/all_to_all | solution.py:269
  300.3 3.3 %collective-permute-start.36 = (bf16[256,128]{1,0:T(8,128)(2,1)S(1)}, bf16[256,128]{1,0:T(8,128)(2,1)S(1)}, u32[]{:S(2)}, u32[]{:S(2)}) collective-permute-start(bf16[256,128]{1,0:T(8,128)(2,1)S(1)} %bitcast.103), channel_id=1, source_target_pairs={{0,128},{1,129},{2,130},{3,131},{4,132},{5,133},{6,134},{7,135},{8... | collective-permute-start | bytes 196616 | tf_op jit(solution)/shard_map/ppermute | solution.py:36
  (135 shorter events, 49.8 us)
Async XLA Ops:
  6.5 230.4 %all-gather.3.cloned.1.call-start = ((), (), s32[]{:S(2)}) async-start(), calls=%async_computation.1 | async-start | bytes 2621440 | tf_op jit(solution)/shard_map/all_gather | solution.py:217
  8.2 22.1 %collective-permute-start.6 = (bf16[256,128]{1,0:T(8,128)(2,1)S(1)}, bf16[256,128]{1,0:T(8,128)(2,1)}, u32[]{:S(2)}, u32[]{:S(2)}) collective-permute-start(bf16[256,128]{1,0:T(8,128)(2,1)S(1)} %get-tuple-element.23), channel_id=1, source_target_pairs={{0,96},{1,97},{2,98},{3,99},{4,100},{5,101},{6,102},{7,103},{8,104... | collective-permute-start | bytes 196616 | tf_op jit(solution)/shard_map/ppermute | solution.py:36
  11.8 20.6 %collective-permute-start.7 = (bf16[256,128]{1,0:T(8,128)(2,1)S(1)}, bf16[256,128]{1,0:T(8,128)(2,1)}, u32[]{:S(2)}, u32[]{:S(2)}) collective-permute-start(bf16[256,128]{1,0:T(8,128)(2,1)S(1)} %get-tuple-element.23), channel_id=1, source_target_pairs={{0,64},{1,65},{2,66},{3,67},{4,68},{5,69},{6,70},{7,71},{8,72},{9,... | collective-permute-start | bytes 196616 | tf_op jit(solution)/shard_map/ppermute | solution.py:36
  12.1 25.4 %collective-permute-start.8 = (bf16[256,128]{1,0:T(8,128)(2,1)S(1)}, bf16[256,128]{1,0:T(8,128)(2,1)}, u32[]{:S(2)}, u32[]{:S(2)}) collective-permute-start(bf16[256,128]{1,0:T(8,128)(2,1)S(1)} %get-tuple-element.23), channel_id=1, source_target_pairs={{0,32},{1,33},{2,34},{3,35},{4,36},{5,37},{6,38},{7,39},{8,40},{9,... | collective-permute-start | bytes 196616 | tf_op jit(solution)/shard_map/ppermute | solution.py:36
  12.8 14.0 %collective-permute-start.17 = (bf16[256,128]{1,0:T(8,128)(2,1)}, bf16[256,128]{1,0:T(8,128)(2,1)S(1)}, u32[]{:S(2)}, u32[]{:S(2)}) collective-permute-start(bf16[256,128]{1,0:T(8,128)(2,1)} %get-tuple-element.22), channel_id=1, source_target_pairs={{0,28},{1,29},{2,30},{3,31},{4,0},{5,1},{6,2},{7,3},{8,4},{9,5},{1... | collective-permute-start | bytes 196616 | tf_op jit(solution)/shard_map/ppermute | solution.py:36
  18.4 11.2 %collective-permute-start.18 = (bf16[256,128]{1,0:T(8,128)(2,1)}, bf16[256,128]{1,0:T(8,128)(2,1)S(1)}, u32[]{:S(2)}, u32[]{:S(2)}) collective-permute-start(bf16[256,128]{1,0:T(8,128)(2,1)} %get-tuple-element.22), channel_id=1, source_target_pairs={{0,24},{1,25},{2,26},{3,27},{4,28},{5,29},{6,30},{7,31},{8,0},{9,1... | collective-permute-start | bytes 196616 | tf_op jit(solution)/shard_map/ppermute | solution.py:36
  26.9 187.3 %collective-permute-start.5 = (bf16[3,1,4,8,128,128]{5,4,3,2,1,0:T(8,128)(2,1)}, bf16[3,1,4,8,128,128]{5,4,3,2,1,0:T(8,128)(2,1)}, u32[]{:S(2)}, u32[]{:S(2)}) collective-permute-start(bf16[3,1,4,8,128,128]{5,4,3,2,1,0:T(8,128)(2,1)} %constant_dynamic-slice_fusion.2), channel_id=1, source_target_pairs={{0,128},{1,129},{2,130},{3,131},{4,132},{5,133},{6,134},{7,135},{8... | collective-permute-start | bytes 9437192 | tf_op jit(solution)/shard_map/ppermute | solution.py:36
  29.6 5.8 %collective-permute-start.19 = (bf16[256,128]{1,0:T(8,128)(2,1)}, bf16[256,128]{1,0:T(8,128)(2,1)S(1)}, u32[]{:S(2)}, u32[]{:S(2)}) collective-permute-start(bf16[256,128]{1,0:T(8,128)(2,1)} %get-tuple-element.22), channel_id=1, source_target_pairs={{0,20},{1,21},{2,22},{3,23},{4,24},{5,25},{6,26},{7,27},{8,28},{9,... | collective-permute-start | bytes 196616 | tf_op jit(solution)/shard_map/ppermute | solution.py:36
  30.4 10.4 %collective-permute-start = (bf16[32,2048]{1,0:T(8,128)(2,1)S(1)}, bf16[32,2048]{1,0:T(8,128)(2,1)S(1)}, u32[]{:S(2)}, u32[]{:S(2)}) collective-permute-start(bf16[32,2048]{1,0:T(8,128)(2,1)S(1)} %get-tuple-element.12), channel_id=1, source_target_pairs={{0,96},{1,97},{2,98},{3,99},{4,100},{5,101},{6,102},{7,103},{8,104... | collective-permute-start | bytes 393224 | tf_op jit(solution)/shard_map/ppermute | solution.py:36
  32.3 13.2 %collective-permute-start.1 = (bf16[32,2048]{1,0:T(8,128)(2,1)S(1)}, bf16[32,2048]{1,0:T(8,128)(2,1)S(1)}, u32[]{:S(2)}, u32[]{:S(2)}) collective-permute-start(bf16[32,2048]{1,0:T(8,128)(2,1)S(1)} %get-tuple-element.11), channel_id=1, source_target_pairs={{0,64},{1,65},{2,66},{3,67},{4,68},{5,69},{6,70},{7,71},{8,72},{9,... | collective-permute-start | bytes 393224 | tf_op jit(solution)/shard_map/ppermute | solution.py:36
  35.3 12.0 %collective-permute-start.2 = (bf16[32,2048]{1,0:T(8,128)(2,1)S(1)}, bf16[32,2048]{1,0:T(8,128)(2,1)S(1)}, u32[]{:S(2)}, u32[]{:S(2)}) collective-permute-start(bf16[32,2048]{1,0:T(8,128)(2,1)S(1)} %get-tuple-element.10), channel_id=1, source_target_pairs={{0,32},{1,33},{2,34},{3,35},{4,36},{5,37},{6,38},{7,39},{8,40},{9,... | collective-permute-start | bytes 393224 | tf_op jit(solution)/shard_map/ppermute | solution.py:36
  37.6 10.7 %collective-permute-start.20 = (bf16[256,128]{1,0:T(8,128)(2,1)}, bf16[256,128]{1,0:T(8,128)(2,1)S(1)}, u32[]{:S(2)}, u32[]{:S(2)}) collective-permute-start(bf16[256,128]{1,0:T(8,128)(2,1)} %get-tuple-element.22), channel_id=1, source_target_pairs={{0,16},{1,17},{2,18},{3,19},{4,20},{5,21},{6,22},{7,23},{8,24},{9,... | collective-permute-start | bytes 196616 | tf_op jit(solution)/shard_map/ppermute | solution.py:36
  40.8 11.0 %collective-permute-start.21 = (bf16[256,128]{1,0:T(8,128)(2,1)}, bf16[256,128]{1,0:T(8,128)(2,1)S(1)}, u32[]{:S(2)}, u32[]{:S(2)}) collective-permute-start(bf16[256,128]{1,0:T(8,128)(2,1)} %get-tuple-element.22), channel_id=1, source_target_pairs={{0,12},{1,13},{2,14},{3,15},{4,16},{5,17},{6,18},{7,19},{8,20},{9,... | collective-permute-start | bytes 196616 | tf_op jit(solution)/shard_map/ppermute | solution.py:36
  45.5 9.0 %collective-permute-start.22 = (bf16[256,128]{1,0:T(8,128)(2,1)}, bf16[256,128]{1,0:T(8,128)(2,1)S(1)}, u32[]{:S(2)}, u32[]{:S(2)}) collective-permute-start(bf16[256,128]{1,0:T(8,128)(2,1)} %get-tuple-element.22), channel_id=1, source_target_pairs={{0,8},{1,9},{2,10},{3,11},{4,12},{5,13},{6,14},{7,15},{8,16},{9,17... | collective-permute-start | bytes 196616 | tf_op jit(solution)/shard_map/ppermute | solution.py:36
  47.3 7.9 %collective-permute-start.23 = (bf16[256,128]{1,0:T(8,128)(2,1)}, bf16[256,128]{1,0:T(8,128)(2,1)S(1)}, u32[]{:S(2)}, u32[]{:S(2)}) collective-permute-start(bf16[256,128]{1,0:T(8,128)(2,1)} %get-tuple-element.22), channel_id=1, source_target_pairs={{0,4},{1,5},{2,6},{3,7},{4,8},{5,9},{6,10},{7,11},{8,12},{9,13},{1... | collective-permute-start | bytes 196616 | tf_op jit(solution)/shard_map/ppermute | solution.py:36
  48.2 139.0 %collective-permute-start.9 = (bf16[4,256,128]{2,1,0:T(8,128)(2,1)S(1)}, bf16[4,256,128]{2,1,0:T(8,128)(2,1)}, u32[]{:S(2)}, u32[]{:S(2)}) collective-permute-start(bf16[4,256,128]{2,1,0:T(8,128)(2,1)S(1)} %pad_maximum_fusion.4.refs_7_), channel_id=1, source_target_pairs={{0,28},{1,29},{2,30},{3,31},{4,0},{5,1},{6,2},{7,3},{8,4},{9,5},{1... | collective-permute-start | bytes 786440 | tf_op jit(solution)/shard_map/ppermute | solution.py:36
  51.8 135.5 %collective-permute-start.13 = (bf16[4,256,128]{2,1,0:T(8,128)(2,1)S(1)}, bf16[4,256,128]{2,1,0:T(8,128)(2,1)}, u32[]{:S(2)}, u32[]{:S(2)}) collective-permute-start(bf16[4,256,128]{2,1,0:T(8,128)(2,1)S(1)} %pad_maximum_fusion.4.refs_7_), channel_id=1, source_target_pairs={{0,4},{1,5},{2,6},{3,7},{4,8},{5,9},{6,10},{7,11},{8,12},{9,13},{1... | collective-permute-start | bytes 786440 | tf_op jit(solution)/shard_map/ppermute | solution.py:36
  55.9 133.6 %collective-permute-start.24 = (bf16[8,256,128]{2,1,0:T(8,128)(2,1)}, bf16[8,256,128]{2,1,0:T(8,128)(2,1)S(1)}, u32[]{:S(2)}, u32[]{:S(2)}) collective-permute-start(bf16[8,256,128]{2,1,0:T(8,128)(2,1)} %bitcast_dynamic-update-slice_fusion.refs_7_), channel_id=1, source_target_pairs={{0,96},{1,97},{2,98},{3,99},{4,100},{5,101},{6,102},{7,103},{8,104... | collective-permute-start | bytes 1572872 | tf_op jit(solution)/shard_map/ppermute | solution.py:36
  56.8 133.4 %collective-permute-start.26 = (bf16[8,256,128]{2,1,0:T(8,128)(2,1)}, bf16[8,256,128]{2,1,0:T(8,128)(2,1)S(1)}, u32[]{:S(2)}, u32[]{:S(2)}) collective-permute-start(bf16[8,256,128]{2,1,0:T(8,128)(2,1)} %bitcast_dynamic-update-slice_fusion.refs_7_), channel_id=1, source_target_pairs={{0,32},{1,33},{2,34},{3,35},{4,36},{5,37},{6,38},{7,39},{8,40},{9,... | collective-permute-start | bytes 1572872 | tf_op jit(solution)/shard_map/ppermute | solution.py:36
  187.3 6.9 %collective-permute-start.10 = (bf16[4,256,128]{2,1,0:T(8,128)(2,1)}, bf16[4,256,128]{2,1,0:T(8,128)(2,1)}, u32[]{:S(2)}, u32[]{:S(2)}) collective-permute-start(bf16[4,256,128]{2,1,0:T(8,128)(2,1)} %collective-permute-done.9.refs_8_), channel_id=1, source_target_pairs={{0,28},{1,29},{2,30},{3,31},{4,0},{5,1},{6,2},{7,3},{8,4},{9,5},{1... | collective-permute-start | bytes 786440 | tf_op jit(solution)/shard_map/ppermute | solution.py:36
  187.4 8.1 %collective-permute-start.14 = (bf16[4,256,128]{2,1,0:T(8,128)(2,1)}, bf16[4,256,128]{2,1,0:T(8,128)(2,1)}, u32[]{:S(2)}, u32[]{:S(2)}) collective-permute-start(bf16[4,256,128]{2,1,0:T(8,128)(2,1)} %collective-permute-done.13.refs_14_), channel_id=1, source_target_pairs={{0,4},{1,5},{2,6},{3,7},{4,8},{5,9},{6,10},{7,11},{8,12},{9,13},{1... | collective-permute-start | bytes 786440 | tf_op jit(solution)/shard_map/ppermute | solution.py:36
  190.2 20.8 %collective-permute-start.25 = (bf16[4,256,128]{2,1,0:T(8,128)(2,1)}, bf16[4,256,128]{2,1,0:T(8,128)(2,1)}, u32[]{:S(2)}, u32[]{:S(2)}) collective-permute-start(bf16[4,256,128]{2,1,0:T(8,128)(2,1)} %slice.95), channel_id=1, source_target_pairs={{0,96},{1,97},{2,98},{3,99},{4,100},{5,101},{6,102},{7,103},{8,104... | collective-permute-start | bytes 786440 | tf_op jit(solution)/shard_map/ppermute | solution.py:36
  190.9 20.1 %collective-permute-start.27 = (bf16[4,256,128]{2,1,0:T(8,128)(2,1)}, bf16[4,256,128]{2,1,0:T(8,128)(2,1)}, u32[]{:S(2)}, u32[]{:S(2)}) collective-permute-start(bf16[4,256,128]{2,1,0:T(8,128)(2,1)} %slice.96), channel_id=1, source_target_pairs={{0,32},{1,33},{2,34},{3,35},{4,36},{5,37},{6,38},{7,39},{8,40},{9,... | collective-permute-start | bytes 786440 | tf_op jit(solution)/shard_map/ppermute | solution.py:36
  194.1 7.6 %collective-permute-start.11 = (bf16[4,256,128]{2,1,0:T(8,128)(2,1)}, bf16[4,256,128]{2,1,0:T(8,128)(2,1)}, u32[]{:S(2)}, u32[]{:S(2)}) collective-permute-start(bf16[4,256,128]{2,1,0:T(8,128)(2,1)} %collective-permute-done.10.refs_9_), channel_id=1, source_target_pairs={{0,28},{1,29},{2,30},{3,31},{4,0},{5,1},{6,2},{7,3},{8,4},{9,5},{1... | collective-permute-start | bytes 786440 | tf_op jit(solution)/shard_map/ppermute | solution.py:36
  195.5 9.5 %collective-permute-start.15 = (bf16[4,256,128]{2,1,0:T(8,128)(2,1)}, bf16[4,256,128]{2,1,0:T(8,128)(2,1)}, u32[]{:S(2)}, u32[]{:S(2)}) collective-permute-start(bf16[4,256,128]{2,1,0:T(8,128)(2,1)} %collective-permute-done.14.refs_13_), channel_id=1, source_target_pairs={{0,4},{1,5},{2,6},{3,7},{4,8},{5,9},{6,10},{7,11},{8,12},{9,13},{1... | collective-permute-start | bytes 786440 | tf_op jit(solution)/shard_map/ppermute | solution.py:36
  203.3 8.8 %collective-permute-start.12 = (bf16[2,256,128]{2,1,0:T(8,128)(2,1)}, bf16[2,256,128]{2,1,0:T(8,128)(2,1)}, u32[]{:S(2)}, u32[]{:S(2)}) collective-permute-start(bf16[2,256,128]{2,1,0:T(8,128)(2,1)} %slice.93), channel_id=1, source_target_pairs={{0,28},{1,29},{2,30},{3,31},{4,0},{5,1},{6,2},{7,3},{8,4},{9,5},{1... | collective-permute-start | bytes 393224 | tf_op jit(solution)/shard_map/ppermute | solution.py:36
  206.5 6.6 %collective-permute-start.16 = (bf16[2,256,128]{2,1,0:T(8,128)(2,1)}, bf16[2,256,128]{2,1,0:T(8,128)(2,1)}, u32[]{:S(2)}, u32[]{:S(2)}) collective-permute-start(bf16[2,256,128]{2,1,0:T(8,128)(2,1)} %slice.94), channel_id=1, source_target_pairs={{0,4},{1,5},{2,6},{3,7},{4,8},{5,9},{6,10},{7,11},{8,12},{9,13},{1... | collective-permute-start | bytes 393224 | tf_op jit(solution)/shard_map/ppermute | solution.py:36
  237.0 26.0 %collective-permute-start.3 = (bf16[4,4,32,2048]{3,2,1,0:T(8,128)(2,1)}, bf16[4,4,32,2048]{3,2,1,0:T(8,128)(2,1)}, u32[]{:S(2)}, u32[]{:S(2)}) collective-permute-start(bf16[4,4,32,2048]{3,2,1,0:T(8,128)(2,1)} %bitcast.90), channel_id=1, source_target_pairs={{0,128},{1,129},{2,130},{3,131},{4,132},{5,133},{6,134},{7,135},{8... | collective-permute-start | bytes 6291464 | tf_op jit(solution)/shard_map/ppermute | solution.py:36
  239.9 8.9 %collective-permute-start.29 = (bf16[2,256,128]{2,1,0:T(8,128)(2,1)S(1)}, bf16[2,256,128]{2,1,0:T(8,128)(2,1)S(1)}, u32[]{:S(2)}, u32[]{:S(2)}) collective-permute-start(bf16[2,256,128]{2,1,0:T(8,128)(2,1)S(1)} %pad_maximum_fusion.6), channel_id=1, source_target_pairs={{0,1},{1,2},{2,3},{4,5},{5,6},{6,7},{8,9},{9,10},{10,11},{12,13},{... | collective-permute-start | bytes 393224 | tf_op jit(solution)/shard_map/ppermute | solution.py:36
  243.0 6.5 %collective-permute-start.30 = (bf16[2,256,128]{2,1,0:T(8,128)(2,1)S(1)}, bf16[2,256,128]{2,1,0:T(8,128)(2,1)S(1)}, u32[]{:S(2)}, u32[]{:S(2)}) collective-permute-start(bf16[2,256,128]{2,1,0:T(8,128)(2,1)S(1)} %pad_maximum_fusion.6), channel_id=1, source_target_pairs={{0,2},{1,3},{4,6},{5,7},{8,10},{9,11},{12,14},{13,15},{16,18},{17,... | collective-permute-start | bytes 393224 | tf_op jit(solution)/shard_map/ppermute | solution.py:36
  256.9 4.7 %collective-permute-start.34 = (bf16[256,128]{1,0:T(8,128)(2,1)S(1)}, bf16[256,128]{1,0:T(8,128)(2,1)S(1)}, u32[]{:S(2)}, u32[]{:S(2)}) collective-permute-start(bf16[256,128]{1,0:T(8,128)(2,1)S(1)} %shard_map.66.h0), channel_id=1, source_target_pairs={{0,64},{1,65},{2,66},{3,67},{4,68},{5,69},{6,70},{7,71},{8,72},{9,... | collective-permute-start | bytes 196616 | tf_op jit(solution)/shard_map/ppermute | solution.py:36
  256.9 6.1 %collective-permute-start.35 = (bf16[256,128]{1,0:T(8,128)(2,1)S(1)}, bf16[256,128]{1,0:T(8,128)(2,1)S(1)}, u32[]{:S(2)}, u32[]{:S(2)}) collective-permute-start(bf16[256,128]{1,0:T(8,128)(2,1)S(1)} %shard_map.66.h0), channel_id=1, source_target_pairs={{0,32},{1,33},{2,34},{3,35},{4,36},{5,37},{6,38},{7,39},{8,40},{9,... | collective-permute-start | bytes 196616 | tf_op jit(solution)/shard_map/ppermute | solution.py:36
  (18 other events, 131.3 us)
Sparse Core Ops, SparseCore 0:
  48.4 32.5 all-gather.2

commit v2 on v1

--- a/solution.py
+++ b/solution.py
@@ -2,6 +2,7 @@
 
 import jax
 import jax.numpy as jnp
+import numpy as np
 from jax import lax
 from jax.experimental import pallas as pl
 from jax.experimental.pallas import tpu as pltpu
@@ -15,67 +16,90 @@
 NZ = 8
 NX = 4
 AXES = ("mod", "y", "z", "seq")
-ROWS_A = 256
-
-
-def pairs(dc, dy, dz, dx, wrap_x=True):
+
+
+def pairs(moves, wrap_x=True):
     out = []
     for c in range(2):
+        if moves[c] is None:
+            continue
+        dc, dy, dz, dx = moves[c]
         for y in range(NY):
             for z in range(NZ):
                 for x in range(NX):
-                    if not wrap_x and not 0 <= x - dx < NX:
+                    if not wrap_x and not 0 <= x + dx < NX:
                         continue
-                    source = ((c * NY + y) * NZ + z) * NX + x
-                    to = (((c - dc) % 2 * NY + (y - dy) % NY) * NZ + (z - dz) % NZ) * NX + (x - dx) % NX
-                    out.append((source, to))
+                    source = (((c + dc) % 2 * NY + (y + dy) % NY) * NZ + (z + dz) % NZ) * NX + (x + dx) % NX
+                    out.append((source, ((c * NY + y) * NZ + z) * NX + x))
     return out
 
 
 def take(x, dc=0, dy=0, dz=0, dx=0, wrap_x=True):
-    return lax.ppermute(x, AXES, pairs(dc, dy, dz, dx, wrap_x))
-
-
-def gather_a(rows):
-    s1, s3, s2 = take(rows, dy=1), take(rows, dy=-1), take(rows, dy=2)
-    own = jnp.stack([rows, s1, s2, s3])
-    f1, b1 = take(own, dz=1), take(own, dz=-1)
-    f2, b2 = take(f1, dz=1), take(b1, dz=-1)
-    f3, b3 = take(f2, dz=1), take(b2, dz=-1)
-    f4, b4 = take(f3[:2], dz=1), take(b3[2:], dz=-1)
-    return [own, f1, f2, f3, jnp.concatenate([f4, b4]), b3, b2, b1]
-
-
-def gather_b(rows):
-    got = [rows] + [take(rows, dz=d if d < 5 else d - 8) for d in range(1, NZ)]
-    own = jnp.stack(got)
-    f1, b1 = take(own, dy=1), take(own, dy=-1)
-    f2, b2 = take(f1[:4], dy=1), take(b1[4:], dy=-1)
-    return [own, f1, jnp.concatenate([f2, b2]), b1]
-
-
-def qkv_kernel(z_first, at_ref, inv_ref, own_row_ref, gain_ref, gain_other_ref, w_ref, w_other_ref, *rest):
-    pieces, out_ref, acc = rest[:-2], rest[-2], rest[-1]
+    return lax.ppermute(x, AXES, pairs([(dc, dy, dz, dx)] * 2, wrap_x))
+
+
+def take_by_core(x, on_y, on_z):
+    return lax.ppermute(x, AXES, pairs([m and (0, *m, 0) for m in (on_y, on_z)]))
+
+
+FIRST_Y = (0, 1, 3, 2)
+FIRST_Z = (0, 1, 7, 2)
+LATER_Z = (3, 6, 4, 5)
+
+
+def gather(c, rows):
+    k1 = take_by_core(rows, (1, 0), (0, 1))
+    k2 = take_by_core(rows, (-1, 0), (0, -1))
+    k3 = take_by_core(rows, (2, 0), (0, 2))
+    g0 = jnp.stack([rows, k1, k2, k3])
+    x1 = take_by_core(g0, (0, 1), (1, 0))
+    x2 = take_by_core(g0, (0, -1), (-1, 0))
+    k4 = take_by_core(k3, None, (0, 1))
+    k5 = take_by_core(k2, None, (0, -1))
+    k6 = take_by_core(k3, None, (0, 2))
+    k7 = take_by_core(k2, None, (0, -2))
+    g1 = jnp.stack([k4, k5, k6, k7])
+    x3 = take_by_core(x1, (0, 1), (1, 0))
+    x4 = take_by_core(jnp.where(c == 0, x2, g1), (0, -1), (-1, 0))
+    x5 = take_by_core(jnp.where(c == 0, x3, g1), (0, 1), (1, 0))
+    x6 = take_by_core(x4, (0, -1), (-1, 0))
+    x7 = take_by_core(x5, (0, 1), None)
+    return [g0, x1, x2, x3, x4, x5, x6], g1, x7
+
+
+PLACES = np.array(
+    [
+        [[(dy, dz) for dy in FIRST_Y] for dz in (0, 1, 7, 2, 6, 3, 5, 4)],
+        [
+            [(dy, dz) for dz in order]
+            for dy, order in (
+                (0, FIRST_Z), (1, FIRST_Z), (3, FIRST_Z), (2, FIRST_Z),
+                (3, LATER_Z), (1, LATER_Z), (2, LATER_Z), (0, LATER_Z),
+            )
+        ],
+    ],
+    np.int32,
+)
+
+
+def qkv_kernel(table_ref, inv_ref, own_row_ref, gain_ref, gain_other_ref, *rest):
+    own_ws, other_ws, pieces = rest[:8], rest[8:16], rest[16:24]
+    last_ref, out_ref, acc = rest[24:]
     step = pl.program_id(0)
     inverse = inv_ref[...]
     own_row = own_row_ref[...] > 0
-    normed, own_w, other_w = [], [], []
+    on_y = table_ref[0] == 0
+    normed, right = [], []
     for k, piece in enumerate(pieces):
-        if z_first:
-            yi, zi = lax.rem(at_ref[1] + k, NY), lax.rem(at_ref[2] + step, NZ)
-            where = (0, yi, 0)
-        else:
-            yi, zi = lax.rem(at_ref[1] + step, NY), lax.rem(at_ref[2] + k, NZ)
-            where = (0, 0, zi)
+        at = 1 + 2 * (4 * k + step)
+        yi, zi = table_ref[at], table_ref[at + 1]
         gain = jnp.where(own_row, gain_ref[yi, pl.ds(zi, 1), :], gain_other_ref[yi, pl.ds(zi, 1), :])
-        normed.append((piece[0].astype(jnp.float32) * inverse * gain).astype(jnp.bfloat16))
-        own_w.append(jnp.concatenate([w_ref[(p, *where)] for p in range(3)], axis=1))
-        other_w.append(jnp.concatenate([w_other_ref[(p, *where)] for p in range(3)], axis=1))
-    left = jnp.concatenate(normed, axis=1)
-    right = jnp.concatenate(
-        [jnp.concatenate(own_w, axis=0), jnp.concatenate(other_w, axis=0)], axis=1
+        value = piece[0] if k < 7 else jnp.where(on_y, last_ref[0], piece[0])
+        normed.append((value.astype(jnp.float32) * inverse * gain).astype(jnp.bfloat16))
+        right.append(jnp.concatenate([w[p, 0, 0, 0] for w in (own_ws[k], other_ws[k]) for p in range(3)], axis=1))
+    part = jnp.dot(
+        jnp.concatenate(normed, axis=1), jnp.concatenate(right, axis=0), preferred_element_type=jnp.float32
     )
-    part = jnp.dot(left, right, preferred_element_type=jnp.float32)
 
     @pl.when(step == 0)
     def _():
@@ -90,45 +114,32 @@
         out_ref[...] = jnp.where(own_row, acc[:, : 3 * HD], acc[:, 3 * HD :])
 
 
-def qkv_part(at, inverse, own_row, gain, gain_other, w, w_other, pieces, z_first):
-    rows = pieces[0].shape[1]
-    steps = pieces[0].shape[0]
-    if z_first:
-        block = (3, 1, NY, 1, HD, HD)
-        index = lambda g, at: (0, at[0], 0, lax.rem(at[2] + g, NZ), 0, 0)
-        index_other = lambda g, at: (0, 0, 0, lax.rem(at[2] + g, NZ), 0, 0)
-    else:
-        block = (3, 1, 1, NZ, HD, HD)
-        index = lambda g, at: (0, at[0], lax.rem(at[1] + g, NY), 0, 0, 0)
-        index_other = lambda g, at: (0, 0, lax.rem(at[1] + g, NY), 0, 0, 0)
-
-    def body(*refs):
-        qkv_kernel(z_first, *refs)
-
-    whole = lambda shape: pl.BlockSpec(shape, lambda g, at: (0,) * len(shape))
+def project(table, inverse, own_row, gain, gain_other, w, w_other, arrays, g1, x7):
+    rows = g1.shape[1]
+    block = (3, 1, 1, 1, HD, HD)
+    whole = lambda shape: pl.BlockSpec(shape, lambda g, t: (0,) * len(shape))
+    piece = pl.BlockSpec((1, rows, HD), lambda g, t: (g, 0, 0))
+    weights = lambda k, other: pl.BlockSpec(
+        block, lambda g, t: (0, 0 if other else t[0], t[1 + 2 * (4 * k + g)], t[2 + 2 * (4 * k + g)], 0, 0)
+    )
     return pl.pallas_call(
-        body,
+        qkv_kernel,
         grid_spec=pltpu.PrefetchScalarGridSpec(
             num_scalar_prefetch=1,
-            grid=(steps,),
-            in_specs=[
-                whole((rows, 1)),
-                whole((rows, 1)),
-                whole((NY, NZ, HD)),
-                whole((NY, NZ, HD)),
-                pl.BlockSpec(block, index),
-                pl.BlockSpec(block, index_other),
-            ]
-            + [pl.BlockSpec((1, rows, HD), lambda g, at: (g, 0, 0)) for _ in pieces],
+            grid=(4,),
+            in_specs=[whole((rows, 1)), whole((rows, 1)), whole((NY, NZ, HD)), whole((NY, NZ, HD))]
+            + [weights(k, False) for k in range(8)]
+            + [weights(k, True) for k in range(8)]
+            + [piece] * 9,
             out_specs=whole((rows, 3 * HD)),
             scratch_shapes=[pltpu.VMEM((rows, 6 * HD), jnp.float32)],
         ),
         out_shape=jax.ShapeDtypeStruct((rows, 3 * HD), jnp.float32),
         compiler_params=pltpu.CompilerParams(vmem_limit_bytes=40 * 2**20),
         cost_estimate=pl.CostEstimate(
-            flops=2 * rows * 4096 * 6 * HD, bytes_accessed=8 * 2**20, transcendentals=0
+            flops=2 * rows * 4096 * 6 * HD, bytes_accessed=11 * 2**20, transcendentals=0
         ),
-    )(at, inverse, own_row, gain, gain_other, w, w_other, *pieces)
+    )(table, inverse, own_row, gain, gain_other, *[w] * 8, *[w_other] * 8, *arrays, g1, x7)
 
 
 def headnorm(x, gain_row):
@@ -223,25 +234,27 @@
     c, y, z, seq = (lax.axis_index(a) for a in AXES)
     own_row = (modality == c).astype(jnp.int32)[:, None]
 
-    squares = jnp.sum(jnp.square(tokens.astype(jnp.float32)), axis=1)
-    pieces_a = gather_a(tokens[:ROWS_A])
-    pieces_b = gather_b(tokens[ROWS_A:])
-    squares = lax.psum(squares, ("mod", "y", "z"))
-    inverse = lax.rsqrt(squares / (2 * NY * NZ * HD) + EPS)[:, None]
-
     w = w_qkv[0].transpose(1, 0, 2).reshape(3, 2, NY, NZ, HD, HD)
     gains = norm_gain.reshape(2, NY, NZ, HD)
     w_other = take(lax.dynamic_slice_in_dim(w, 1 - c, 1, axis=1), dc=1)
     gain_other = take(lax.dynamic_index_in_dim(gains, 1 - c, axis=0, keepdims=False), dc=1)
     gain = lax.dynamic_index_in_dim(gains, c, axis=0, keepdims=False)
+
+    arrays, g1, x7 = gather(c, tokens)
+    w_out, _ = lax.optimization_barrier((w_out, arrays[1]))
     w_cols = spread_w_out(w_out, y, seq)
     w_cols_other = take(w_cols, dc=1)
 
-    at = jnp.stack([c, y, z]).astype(jnp.int32)
-    common = lambda rows: (at, inverse[rows], own_row[rows], gain, gain_other, w, w_other)
-    part_a = qkv_part(*common(slice(None, ROWS_A)), pieces_a, False)
-    part_b = qkv_part(*common(slice(ROWS_A, None)), pieces_b, True)
-    parts = jnp.concatenate([part_a, part_b]).reshape(2, half, 3 * HD)
+    squared = lambda a: jnp.sum(jnp.square(a.astype(jnp.float32)), axis=(0, 2))
+    squares = sum(squared(a) for a in arrays) + jnp.where(c == 0, squared(x7), squared(g1))
+    squares = squares + take(squares, dc=1)
+    inverse = lax.rsqrt(squares / (2 * NY * NZ * HD) + EPS)[:, None]
+
+    places = jnp.asarray(PLACES)[c].reshape(32, 2)
+    places = lax.rem(places + jnp.stack([y, z]).astype(jnp.int32)[None, :], jnp.array([NY, NZ], jnp.int32)[None, :])
+    table = jnp.concatenate([c.astype(jnp.int32)[None], places.reshape(64)])
+    parts = project(table, inverse, own_row, gain, gain_other, w, w_other, arrays, g1, x7)
+    parts = parts.reshape(2, half, 3 * HD)
     mine = lax.dynamic_index_in_dim(parts, c, axis=0, keepdims=False)
     theirs = lax.dynamic_index_in_dim(parts, 1 - c, axis=0, keepdims=False)
     projected = mine + take(theirs, dc=1)

time: 313 us -> 174 us (0.56)
  blocking collectives: 159 us -> 28.7 us
  local copies, waits for them, and re-layouts: 34.4 us -> 23.2 us
  other arithmetic: 7.85 us -> 15.4 us
  Pallas kernels: 20.3 us -> 16.4 us
    psum x1 -> x0, blocking collectives: 130 us -> none  [shards(): squares = lax.psum(squares, ('mod', 'y', 'z'))]
    slice x10 -> x0, local copies, waits for them, and re-layouts: 9.51 us -> none  [the longest x2 3.13 us: gather_a(): f4, b4 = (take(f3[:2], dz=1), take(b3[2:], dz=-1))]
    reduce_sum x1 -> x8, other arithmetic: 0.15 us -> 7.34 us  [shards(): squared = lambda a: jnp.sum(jnp.square(a.astype(jnp.float32)), axis=(0, 2))]
    unnamed x33 -> x36, local copies, waits for them, and re-layouts: 14.9 us -> 8.27 us
    pallas_call x2 -> x1, Pallas kernels: 13 us -> 9.08 us  [project(): pl.pallas_call(qkv_kernel, grid_spec=pltpu.PrefetchScalarGridSpec(num_sca...]
    ppermute x37 -> x30, starting transfers between devices: 54.2 us -> 53 us  [the longest x14 27.2 us: take_by_core(): lax.ppermute(x, AXES, pairs([m and (0, *m, 0) for m in (on_y, on_z)]))]
    ppermute x37 -> x30, waiting for transfers between devices: 21.9 us -> 22.7 us  [the longest x16 13 us: take(): return lax.ppermute(x, AXES, pairs([(dc, dy, dz, dx)] * 2, wrap_x))]
  transfers between devices with their start and end apart: 38 -> 31, of which waited for: 15 -> 14; matrix products, arithmetic and copies ran while one was open for 10% -> 17% of each run, Pallas kernels for 5% -> 6%
where the time goes in v2:
time: 174 us; the launch traced here: 173 us
  starting transfers between devices  53 us (30%)
  blocking collectives  28.7 us (16%)
  local copies, waits for them, and re-layouts  23.2 us (13%)
  waiting for transfers between devices  22.7 us (13%)
  Pallas kernels  16.4 us (9%)
  other arithmetic  15.4 us (9%)
  between operations  13.8 us (8%)
    all_to_all x1, blocking collectives, shards(): spread = lax.all_to_all(partial, 'z', 0, 0)  28.7 us
    ppermute x14, starting transfers between devices, take_by_core(): lax.ppermute(x, AXES, pairs([m and (0, *m, 0) for m in (on_y, on_z)]))  27.2 us
    ppermute x16, starting transfers between devices, take(): return lax.ppermute(x, AXES, pairs([(dc, dy, dz, dx)] * 2, wrap_x))  25.8 us
    ppermute x16, waiting for transfers between devices, take(): return lax.ppermute(x, AXES, pairs([(dc, dy, dz, dx)] * 2, wrap_x))  13 us
    ppermute x14, waiting for transfers between devices, take_by_core(): lax.ppermute(x, AXES, pairs([m and (0, *m, 0) for m in (on_y, on_z)]))  9.68 us
    pallas_call x1, Pallas kernels, project(): pl.pallas_call(qkv_kernel, grid_spec=pltpu.PrefetchScalarGridSpec(num_sca...  9.08 us
    unnamed x36, local copies, waits for them, and re-layouts  8.27 us
    reduce_sum x8, other arithmetic, shards(): squared = lambda a: jnp.sum(jnp.square(a.astype(jnp.float32)), axis=(0, 2))  7.34 us
  transfers between devices with their start and end apart: 31, of which 14 were waited for; matrix products, arithmetic and copies ran while one was open for 17% of the time, Pallas kernels for 6%

profile of v2, /device:TPU:1, one launch (start us, length us, event | category | flops | bytes accessed | tf_op | source)
XLA Modules:
  0.0 173.2 jit_solution(8874612315876674856)
XLA Ops:
  6.5 2.5 %collective-permute-start.1 = (bf16[512,128]{1,0:T(8,128)(2,1)}, bf16[512,128]{1,0:T(8,128)(2,1)}, u32[]{:S(2)}, u32[]{:S(2)}) collective-permute-start(bf16[512,128]{1,0:T(8,128)(2,1)} %param.8), channel_id=1, source_target_pairs={{96,0},{97,1},{98,2},{99,3},{100,4},{101,5},{102,6},{103,7},{104,8... | collective-permute-start | bytes 393224 | tf_op jit(solution)/shard_map/ppermute | solution.py:42
  9.0 5.1 %collective-permute-start.2 = (bf16[512,128]{1,0:T(8,128)(2,1)}, bf16[512,128]{1,0:T(8,128)(2,1)S(1)}, u32[]{:S(2)}, u32[]{:S(2)}) collective-permute-start(bf16[512,128]{1,0:T(8,128)(2,1)} %param.8), channel_id=1, source_target_pairs={{64,0},{65,1},{66,2},{67,3},{68,4},{69,5},{70,6},{71,7},{72,8},{73... | collective-permute-start | bytes 393224 | tf_op jit(solution)/shard_map/ppermute | solution.py:42
  14.9 4.0 %constant_dynamic-slice_fusion.2 = bf16[3,1,4,8,128,128]{5,4,3,2,1,0:T(8,128)(2,1)} fusion(bf16[3,2,4,8,128,128]{5,4,3,2,1,0:T(8,128)(2,1)} %bitcast.76, s32[]{:T(128)S(6)} %select_n.92), kind=kLoop, calls=%fused_computation.58 | loop fusion | bytes 6291460 | tf_op jit(solution)/shard_map/dynamic_slice | solution.py:239
  19.5 1.8 %multiply_reduce_fusion.8 = (f32[512]{0:T(512)}, bf16[4,512,128]{2,1,0:T(8,128)(2,1)S(1)}) fusion(bf16[1,512,128]{2,1,0:T(8,128)(2,1)S(1)} %bitcast.92, bf16[1,512,128]{2,1,0:T(8,128)(2,1)} %bitcast.3, bf16[1,512,128]{2,1,0:T(8,128)(2,1)S(1)} %bitcast.94, bf16[1,512,128]{2,1,0:T(8,128)(2,1)S(1)} %bitcast.91), kind=kLoop, calls=%fused_computation.8 | loop fusion | flops 1572352 | bytes 1050624 | tf_op jit(solution)/shard_map/reduce_sum | solution.py:248
  22.6 1.4 collective-permute-start.3
  24.9 6.4 %collective-permute-start.10 = (bf16[512,128]{1,0:T(8,128)(2,1)S(1)}, bf16[512,128]{1,0:T(8,128)(2,1)S(1)}, u32[]{:S(2)}, u32[]{:S(2)}) collective-permute-start(bf16[512,128]{1,0:T(8,128)(2,1)S(1)} %collective-permute-done.2), channel_id=1, source_target_pairs={{132,128},{133,129},{134,130},{135,131},{136,132},{137,133},{138,1... | collective-permute-start | bytes 393224 | tf_op jit(solution)/shard_map/ppermute | solution.py:42
  31.3 1.9 %collective-permute-start.11 = (bf16[512,128]{1,0:T(8,128)(2,1)}, bf16[512,128]{1,0:T(8,128)(2,1)S(1)}, u32[]{:S(2)}, u32[]{:S(2)}) collective-permute-start(bf16[512,128]{1,0:T(8,128)(2,1)} %collective-permute-done.1), channel_id=1, source_target_pairs={{156,128},{157,129},{158,130},{159,131},{128,132},{129,133},{130,1... | collective-permute-start | bytes 393224 | tf_op jit(solution)/shard_map/ppermute | solution.py:42
  36.6 3.8 %collective-permute-start.12 = (bf16[512,128]{1,0:T(8,128)(2,1)}, bf16[512,128]{1,0:T(8,128)(2,1)S(1)}, u32[]{:S(2)}, u32[]{:S(2)}) collective-permute-start(bf16[512,128]{1,0:T(8,128)(2,1)} %copy-done.10), channel_id=1, source_target_pairs={{136,128},{137,129},{138,130},{139,131},{140,132},{141,133},{142,1... | collective-permute-start | bytes 393224 | tf_op jit(solution)/shard_map/ppermute | solution.py:42
  40.4 2.4 %collective-permute-start.13 = (bf16[512,128]{1,0:T(8,128)(2,1)}, bf16[512,128]{1,0:T(8,128)(2,1)}, u32[]{:S(2)}, u32[]{:S(2)}) collective-permute-start(bf16[512,128]{1,0:T(8,128)(2,1)} %collective-permute-done.1), channel_id=1, source_target_pairs={{152,128},{153,129},{154,130},{155,131},{156,132},{157,133},{158,1... | collective-permute-start | bytes 393224 | tf_op jit(solution)/shard_map/ppermute | solution.py:42
  42.8 1.3 add_remainder_fusion
  44.1 1.3 dynamic-slice_bitcast_fusion.5
  46.3 4.9 %collective-permute-done.13 = bf16[512,128]{1,0:T(8,128)(2,1)} collective-permute-done((bf16[512,128]{1,0:T(8,128)(2,1)}, bf16[512,128]{1,0:T(8,128)(2,1)}, u32[]{:S(2)}, u32[]{:S(2)}) %collective-permute-start.13) | collective-permute-done | bytes 131104 | tf_op jit(solution)/shard_map/ppermute | solution.py:42
  51.2 1.8 %broadcast_select_fusion.1 = (bf16[4,512,128]{2,1,0:T(8,128)(2,1)}, bf16[4,512,128]{2,1,0:T(8,128)(2,1)S(1)}) fusion(bf16[4,512,128]{2,1,0:T(8,128)(2,1)S(1)} %collective-permute-done.8.rest_18_, pred[]{:T(512)S(6)} %eq.12, bf16[1,512,128]{2,1,0:T(8,128)(2,1)} %bitcast.27, bf16[1,512,128]{2,1,0:T(8,128)(2,1)S(1)} %bitcast.90, ...), kind=kLoop, calls=%fused_computation.15 | loop fusion | flops 1048576 | bytes 2097153 | tf_op jit(solution)/shard_map/jit(_where)/select_n | solution.py:63
  54.4 2.2 %reshape.94 = bf16[4,32,2048]{2,1,0:T(8,128)(2,1)} reshape(bf16[4,32,8,2,128]{4,3,2,1,0:T(2,128)(2,1)} %copy.18) | data formatting | bytes 1048576 | tf_op jit(solution)/shard_map/reshape | solution.py:224
  57.8 2.8 %collective-permute-start.4 = (bf16[32,2048]{1,0:T(8,128)(2,1)S(1)}, bf16[32,2048]{1,0:T(8,128)(2,1)S(1)}, u32[]{:S(2)}, u32[]{:S(2)}) collective-permute-start(bf16[32,2048]{1,0:T(8,128)(2,1)S(1)} %get-tuple-element.18), channel_id=1, source_target_pairs={{32,0},{33,1},{34,2},{35,3},{36,4},{37,5},{38,6},{39,7},{40,8},{41... | collective-permute-start | bytes 393224 | tf_op jit(solution)/shard_map/ppermute | solution.py:38
  62.5 1.3 collective-permute-done.6
  68.5 3.9 %collective-permute-done.15.rest_21_ = bf16[4,512,128]{2,1,0:T(8,128)(2,1)} collective-permute-done((bf16[4,512,128]{2,1,0:T(8,128)(2,1)}, bf16[4,512,128]{2,1,0:T(8,128)(2,1)}, u32[]{:S(2)}, u32[]{:S(2)}) %collective-permute-start.15) | collective-permute-done | bytes 524320 | tf_op jit(solution)/shard_map/ppermute | solution.py:42
  78.8 3.6 %collective-permute-start.18 = (f32[512]{0:T(512)S(1)}, f32[512]{0:T(512)S(1)}, u32[]{:S(2)}, u32[]{:S(2)}) collective-permute-start(f32[512]{0:T(512)S(1)} %select_add_fusion), channel_id=1, source_target_pairs={{128,0},{129,1},{130,2},{131,3},{132,4},{133,5},{134,6},{135,7},{1... | collective-permute-start | bytes 6152 | tf_op jit(solution)/shard_map/ppermute | solution.py:38
  88.2 9.1 %shard_map.82 = f32[512,384]{1,0:T(8,128)S(1)} custom-call(s32[65]{0:T(128)S(1)} %pad_add_fusion.1.table_ref, f32[512,1]{1,0:T(8,128)S(1)} %copy-done.8, s32[512,1]{1,0:T(8,128)S(1)} %copy.20.own_row_ref, f32[4,8,128]{2,1,0:T(8,128)S(1)} %get-tuple-element.28.gain_ref, f32[4,8,128]{2,1,0:T(8,128)S(1)} %collective-permute-done.19.gain_other_ref, ...), custom_call_target="tpu_custom_call" | custom-call | flops 3221225472 | bytes 11534336 | tf_op jit(solution)/shard_map/pallas_call | solution.py:125
  97.8 1.3 collective-permute-done.21
  101.0 3.1 %collective-permute-start.22 = (bf16[2,256,128]{2,1,0:T(8,128)(2,1)S(1)}, bf16[2,256,128]{2,1,0:T(8,128)(2,1)S(1)}, u32[]{:S(2)}, u32[]{:S(2)}) collective-permute-start(bf16[2,256,128]{2,1,0:T(8,128)(2,1)S(1)} %pad_maximum_fusion.4), channel_id=1, source_target_pairs={{0,1},{1,2},{2,3},{4,5},{5,6},{6,7},{8,9},{9,10},{10,11},{12,13},{... | collective-permute-start | bytes 393224 | tf_op jit(solution)/shard_map/ppermute | solution.py:38
  104.1 4.3 %collective-permute-start.23 = (bf16[2,256,128]{2,1,0:T(8,128)(2,1)S(1)}, bf16[2,256,128]{2,1,0:T(8,128)(2,1)S(1)}, u32[]{:S(2)}, u32[]{:S(2)}) collective-permute-start(bf16[2,256,128]{2,1,0:T(8,128)(2,1)S(1)} %pad_maximum_fusion.4), channel_id=1, source_target_pairs={{0,2},{1,3},{4,6},{5,7},{8,10},{9,11},{12,14},{13,15},{16,18},{17,... | collective-permute-start | bytes 393224 | tf_op jit(solution)/shard_map/ppermute | solution.py:38
  112.2 1.4 collective-permute-start.25
  113.8 1.4 collective-permute-done.25.rest_1_
  115.2 1.7 shard_map.83.h0
  117.7 2.1 %collective-permute-start.27 = (bf16[256,128]{1,0:T(8,128)(2,1)S(1)}, bf16[256,128]{1,0:T(8,128)(2,1)S(1)}, u32[]{:S(2)}, u32[]{:S(2)}) collective-permute-start(bf16[256,128]{1,0:T(8,128)(2,1)S(1)} %shard_map.83.h0), channel_id=1, source_target_pairs={{64,0},{65,1},{66,2},{67,3},{68,4},{69,5},{70,6},{71,7},{72,8},{73... | collective-permute-start | bytes 196616 | tf_op jit(solution)/shard_map/ppermute | solution.py:38
  120.0 2.3 %collective-permute-done.27.h2 = bf16[256,128]{1,0:T(8,128)(2,1)S(1)} collective-permute-done((bf16[256,128]{1,0:T(8,128)(2,1)S(1)}, bf16[256,128]{1,0:T(8,128)(2,1)S(1)}, u32[]{:S(2)}, u32[]{:S(2)}) %collective-permute-start.27) | collective-permute-done | bytes 65568 | tf_op jit(solution)/shard_map/ppermute | solution.py:38
  122.3 2.0 %collective-permute-done.28.h3 = bf16[256,128]{1,0:T(8,128)(2,1)S(1)} collective-permute-done((bf16[256,128]{1,0:T(8,128)(2,1)S(1)}, bf16[256,128]{1,0:T(8,128)(2,1)S(1)}, u32[]{:S(2)}, u32[]{:S(2)}) %collective-permute-start.28) | collective-permute-done | bytes 65568 | tf_op jit(solution)/shard_map/ppermute | solution.py:38
  124.3 1.6 copy-done.7
  125.9 5.6 %shard_map.84 = bf16[8,256,256]{2,1,0:T(8,128)(2,1)S(1)} custom-call(s32[256,1]{1,0:T(8,128)S(1)} %copy.21.own_row_ref, bf16[4,4,32,2048]{3,2,1,0:T(8,128)(2,1)S(1)} %bitcast.75, bf16[4,4,32,2048]{3,2,1,0:T(8,128)(2,1)} %collective-permute-done.7.w_other_ref, bf16[256,128]{1,0:T(8,128)(2,1)S(1)} %shard_map.83.h0, ...), custom_call_target="tpu_custom_call" | custom-call | flops 1073741824 | bytes 5242880 | tf_op jit(solution)/shard_map/pallas_call | solution.py:209
  131.5 28.7 %all_to_all.5 = bf16[8,256,256]{2,1,0:T(8,128)(2,1)S(1)} all-to-all(bf16[8,256,256]{2,1,0:T(8,128)(2,1)S(1)} %shard_map.84), channel_id=1, replica_groups=mesh['mod'=2,'y'=4,'z'=8,'seq'=4] {'z'}, dimensions={0} | all-to-all | bytes 2097152 | tf_op jit(solution)/shard_map/all_to_all | solution.py:282
  160.7 4.1 %collective-permute-start.29 = (bf16[256,128]{1,0:T(8,128)(2,1)S(1)}, bf16[256,128]{1,0:T(8,128)(2,1)S(1)}, u32[]{:S(2)}, u32[]{:S(2)}) collective-permute-start(bf16[256,128]{1,0:T(8,128)(2,1)S(1)} %bitcast.100), channel_id=1, source_target_pairs={{128,0},{129,1},{130,2},{131,3},{132,4},{133,5},{134,6},{135,7},{1... | collective-permute-start | bytes 196616 | tf_op jit(solution)/shard_map/ppermute | solution.py:38
  (128 shorter events, 38.3 us)
Async XLA Ops:
  6.5 46.5 %copy-start = (bf16[1,128,8192]{2,1,0:T(8,128)(2,1)S(1)}, bf16[1,128,8192]{2,1,0:T(8,128)(2,1)}, u32[]{:S(2)}) copy-start(bf16[1,128,8192]{2,1,0:T(8,128)(2,1)} %param.13) | copy-start | bytes 6291460
  6.5 93.1 %all-gather.3.cloned.1.call-start = ((), (), s32[]{:S(2)}) async-start(), calls=%async_computation.1 | async-start | bytes 2621440 | tf_op jit(solution)/shard_map/all_gather | solution.py:228
  6.5 13.0 %collective-permute-start.1 = (bf16[512,128]{1,0:T(8,128)(2,1)}, bf16[512,128]{1,0:T(8,128)(2,1)}, u32[]{:S(2)}, u32[]{:S(2)}) collective-permute-start(bf16[512,128]{1,0:T(8,128)(2,1)} %param.8), channel_id=1, source_target_pairs={{96,0},{97,1},{98,2},{99,3},{100,4},{101,5},{102,6},{103,7},{104,8... | collective-permute-start | bytes 393224 | tf_op jit(solution)/shard_map/ppermute | solution.py:42
  9.0 10.5 %collective-permute-start.2 = (bf16[512,128]{1,0:T(8,128)(2,1)}, bf16[512,128]{1,0:T(8,128)(2,1)S(1)}, u32[]{:S(2)}, u32[]{:S(2)}) collective-permute-start(bf16[512,128]{1,0:T(8,128)(2,1)} %param.8), channel_id=1, source_target_pairs={{64,0},{65,1},{66,2},{67,3},{68,4},{69,5},{70,6},{71,7},{72,8},{73... | collective-permute-start | bytes 393224 | tf_op jit(solution)/shard_map/ppermute | solution.py:42
  14.1 5.4 %collective-permute-start = (bf16[512,128]{1,0:T(8,128)(2,1)}, bf16[512,128]{1,0:T(8,128)(2,1)S(1)}, u32[]{:S(2)}, u32[]{:S(2)}) collective-permute-start(bf16[512,128]{1,0:T(8,128)(2,1)} %param.8), channel_id=1, source_target_pairs={{32,0},{33,1},{34,2},{35,3},{36,4},{37,5},{38,6},{39,7},{40,8},{41... | collective-permute-start | bytes 393224 | tf_op jit(solution)/shard_map/ppermute | solution.py:42
  18.9 65.2 %collective-permute-start.20 = (bf16[3,1,4,8,128,128]{5,4,3,2,1,0:T(8,128)(2,1)}, bf16[3,1,4,8,128,128]{5,4,3,2,1,0:T(8,128)(2,1)}, u32[]{:S(2)}, u32[]{:S(2)}) collective-permute-start(bf16[3,1,4,8,128,128]{5,4,3,2,1,0:T(8,128)(2,1)} %constant_dynamic-slice_fusion.2), channel_id=1, source_target_pairs={{128,0},{129,1},{130,2},{131,3},{132,4},{133,5},{134,6},{135,7},{1... | collective-permute-start | bytes 9437192 | tf_op jit(solution)/shard_map/ppermute | solution.py:38
  21.3 29.9 %collective-permute-start.8 = (bf16[4,512,128]{2,1,0:T(8,128)(2,1)S(1)}, bf16[4,512,128]{2,1,0:T(8,128)(2,1)S(1)}, u32[]{:S(2)}, u32[]{:S(2)}) collective-permute-start(bf16[4,512,128]{2,1,0:T(8,128)(2,1)S(1)} %get-tuple-element.12.rest_16_), channel_id=1, source_target_pairs={{28,0},{29,1},{30,2},{31,3},{0,4},{1,5},{2,6},{3,7},{4,8},{5,9},{6... | collective-permute-start | bytes 1572872 | tf_op jit(solution)/shard_map/ppermute | solution.py:42
  22.6 22.9 %collective-permute-start.3 = (bf16[4,512,128]{2,1,0:T(8,128)(2,1)S(1)}, bf16[4,512,128]{2,1,0:T(8,128)(2,1)}, u32[]{:S(2)}, u32[]{:S(2)}) collective-permute-start(bf16[4,512,128]{2,1,0:T(8,128)(2,1)S(1)} %get-tuple-element.12.rest_16_), channel_id=1, source_target_pairs={{4,0},{5,1},{6,2},{7,3},{8,4},{9,5},{10,6},{11,7},{12,8},{13,9},{1... | collective-permute-start | bytes 1572872 | tf_op jit(solution)/shard_map/ppermute | solution.py:42
  24.9 11.8 %collective-permute-start.10 = (bf16[512,128]{1,0:T(8,128)(2,1)S(1)}, bf16[512,128]{1,0:T(8,128)(2,1)S(1)}, u32[]{:S(2)}, u32[]{:S(2)}) collective-permute-start(bf16[512,128]{1,0:T(8,128)(2,1)S(1)} %collective-permute-done.2), channel_id=1, source_target_pairs={{132,128},{133,129},{134,130},{135,131},{136,132},{137,133},{138,1... | collective-permute-start | bytes 393224 | tf_op jit(solution)/shard_map/ppermute | solution.py:42
  31.3 9.1 %collective-permute-start.11 = (bf16[512,128]{1,0:T(8,128)(2,1)}, bf16[512,128]{1,0:T(8,128)(2,1)S(1)}, u32[]{:S(2)}, u32[]{:S(2)}) collective-permute-start(bf16[512,128]{1,0:T(8,128)(2,1)} %collective-permute-done.1), channel_id=1, source_target_pairs={{156,128},{157,129},{158,130},{159,131},{128,132},{129,133},{130,1... | collective-permute-start | bytes 393224 | tf_op jit(solution)/shard_map/ppermute | solution.py:42
  36.6 9.7 %collective-permute-start.12 = (bf16[512,128]{1,0:T(8,128)(2,1)}, bf16[512,128]{1,0:T(8,128)(2,1)S(1)}, u32[]{:S(2)}, u32[]{:S(2)}) collective-permute-start(bf16[512,128]{1,0:T(8,128)(2,1)} %copy-done.10), channel_id=1, source_target_pairs={{136,128},{137,129},{138,130},{139,131},{140,132},{141,133},{142,1... | collective-permute-start | bytes 393224 | tf_op jit(solution)/shard_map/ppermute | solution.py:42
  40.4 10.8 %collective-permute-start.13 = (bf16[512,128]{1,0:T(8,128)(2,1)}, bf16[512,128]{1,0:T(8,128)(2,1)}, u32[]{:S(2)}, u32[]{:S(2)}) collective-permute-start(bf16[512,128]{1,0:T(8,128)(2,1)} %collective-permute-done.1), channel_id=1, source_target_pairs={{152,128},{153,129},{154,130},{155,131},{156,132},{157,133},{158,1... | collective-permute-start | bytes 393224 | tf_op jit(solution)/shard_map/ppermute | solution.py:42
  45.5 15.1 %collective-permute-start.9 = (bf16[4,512,128]{2,1,0:T(8,128)(2,1)}, bf16[4,512,128]{2,1,0:T(8,128)(2,1)}, u32[]{:S(2)}, u32[]{:S(2)}) collective-permute-start(bf16[4,512,128]{2,1,0:T(8,128)(2,1)} %collective-permute-done.3.rest_17_), channel_id=1, source_target_pairs={{4,0},{5,1},{6,2},{7,3},{8,4},{9,5},{10,6},{11,7},{12,8},{13,9},{1... | collective-permute-start | bytes 1572872 | tf_op jit(solution)/shard_map/ppermute | solution.py:42
  53.0 13.8 %collective-permute-start.14 = (bf16[4,512,128]{2,1,0:T(8,128)(2,1)}, bf16[4,512,128]{2,1,0:T(8,128)(2,1)}, u32[]{:S(2)}, u32[]{:S(2)}) collective-permute-start(bf16[4,512,128]{2,1,0:T(8,128)(2,1)} %get-tuple-element.13), channel_id=1, source_target_pairs={{28,0},{29,1},{30,2},{31,3},{0,4},{1,5},{2,6},{3,7},{4,8},{5,9},{6... | collective-permute-start | bytes 1572872 | tf_op jit(solution)/shard_map/ppermute | solution.py:42
  57.7 6.1 %collective-permute-start.6 = (bf16[32,2048]{1,0:T(8,128)(2,1)S(1)}, bf16[32,2048]{1,0:T(8,128)(2,1)S(1)}, u32[]{:S(2)}, u32[]{:S(2)}) collective-permute-start(bf16[32,2048]{1,0:T(8,128)(2,1)S(1)} %get-tuple-element.16), channel_id=1, source_target_pairs={{96,0},{97,1},{98,2},{99,3},{100,4},{101,5},{102,6},{103,7},{104,8... | collective-permute-start | bytes 393224 | tf_op jit(solution)/shard_map/ppermute | solution.py:38
  57.8 6.8 %collective-permute-start.4 = (bf16[32,2048]{1,0:T(8,128)(2,1)S(1)}, bf16[32,2048]{1,0:T(8,128)(2,1)S(1)}, u32[]{:S(2)}, u32[]{:S(2)}) collective-permute-start(bf16[32,2048]{1,0:T(8,128)(2,1)S(1)} %get-tuple-element.18), channel_id=1, source_target_pairs={{32,0},{33,1},{34,2},{35,3},{36,4},{37,5},{38,6},{39,7},{40,8},{41... | collective-permute-start | bytes 393224 | tf_op jit(solution)/shard_map/ppermute | solution.py:38
  60.6 5.3 %collective-permute-start.5 = (bf16[32,2048]{1,0:T(8,128)(2,1)S(1)}, bf16[32,2048]{1,0:T(8,128)(2,1)S(1)}, u32[]{:S(2)}, u32[]{:S(2)}) collective-permute-start(bf16[32,2048]{1,0:T(8,128)(2,1)S(1)} %get-tuple-element.17), channel_id=1, source_target_pairs={{64,0},{65,1},{66,2},{67,3},{68,4},{69,5},{70,6},{71,7},{72,8},{73... | collective-permute-start | bytes 393224 | tf_op jit(solution)/shard_map/ppermute | solution.py:38
  63.9 8.5 %collective-permute-start.15 = (bf16[4,512,128]{2,1,0:T(8,128)(2,1)}, bf16[4,512,128]{2,1,0:T(8,128)(2,1)}, u32[]{:S(2)}, u32[]{:S(2)}) collective-permute-start(bf16[4,512,128]{2,1,0:T(8,128)(2,1)} %broadcast_select_fusion), channel_id=1, source_target_pairs={{4,0},{5,1},{6,2},{7,3},{8,4},{9,5},{10,6},{11,7},{12,8},{13,9},{1... | collective-permute-start | bytes 1572872 | tf_op jit(solution)/shard_map/ppermute | solution.py:42
  64.6 19.5 %collective-permute-start.19 = (f32[4,8,128]{2,1,0:T(8,128)S(1)}, f32[4,8,128]{2,1,0:T(8,128)S(1)}, u32[]{:S(2)}, u32[]{:S(2)}) collective-permute-start(f32[4,8,128]{2,1,0:T(8,128)S(1)} %copy-done.11), channel_id=1, source_target_pairs={{128,0},{129,1},{130,2},{131,3},{132,4},{133,5},{134,6},{135,7},{1... | collective-permute-start | bytes 49160 | tf_op jit(solution)/shard_map/ppermute | solution.py:38
  66.8 10.0 %collective-permute-start.16 = (bf16[4,512,128]{2,1,0:T(8,128)(2,1)}, bf16[4,512,128]{2,1,0:T(8,128)(2,1)S(1)}, u32[]{:S(2)}, u32[]{:S(2)}) collective-permute-start(bf16[4,512,128]{2,1,0:T(8,128)(2,1)} %collective-permute-done.14.rest_20_), channel_id=1, source_target_pairs={{28,0},{29,1},{30,2},{31,3},{0,4},{1,5},{2,6},{3,7},{4,8},{5,9},{6... | collective-permute-start | bytes 1572872 | tf_op jit(solution)/shard_map/ppermute | solution.py:42
  72.4 5.4 %collective-permute-start.17 = (bf16[4,512,128]{2,1,0:T(8,128)(2,1)}, bf16[4,512,128]{2,1,0:T(8,128)(2,1)S(1)}, u32[]{:S(2)}, u32[]{:S(2)}) collective-permute-start(bf16[4,512,128]{2,1,0:T(8,128)(2,1)} %collective-permute-done.15.rest_21_), channel_id=1, source_target_pairs={{4,0},{5,1},{6,2},{7,3},{8,4},{9,5},{10,6},{11,7},{12,8},{13,9},{1... | collective-permute-start | bytes 1572872 | tf_op jit(solution)/shard_map/ppermute | solution.py:42
  78.8 4.4 %collective-permute-start.18 = (f32[512]{0:T(512)S(1)}, f32[512]{0:T(512)S(1)}, u32[]{:S(2)}, u32[]{:S(2)}) collective-permute-start(f32[512]{0:T(512)S(1)} %select_add_fusion), channel_id=1, source_target_pairs={{128,0},{129,1},{130,2},{131,3},{132,4},{133,5},{134,6},{135,7},{1... | collective-permute-start | bytes 6152 | tf_op jit(solution)/shard_map/ppermute | solution.py:38
  97.3 1.8 %collective-permute-start.21 = (f32[256,384]{1,0:T(8,128)S(1)}, f32[256,384]{1,0:T(8,128)S(1)}, u32[]{:S(2)}, u32[]{:S(2)}) collective-permute-start(f32[256,384]{1,0:T(8,128)S(1)} %dynamic-slice_bitcast_fusion.1), channel_id=1, source_target_pairs={{128,0},{129,1},{130,2},{131,3},{132,4},{133,5},{134,6},{135,7},{1... | collective-permute-start | bytes 1179656 | tf_op jit(solution)/shard_map/ppermute | solution.py:38
  99.6 24.7 %collective-permute-start.7 = (bf16[4,4,32,2048]{3,2,1,0:T(8,128)(2,1)}, bf16[4,4,32,2048]{3,2,1,0:T(8,128)(2,1)}, u32[]{:S(2)}, u32[]{:S(2)}) collective-permute-start(bf16[4,4,32,2048]{3,2,1,0:T(8,128)(2,1)} %bitcast.74), channel_id=1, source_target_pairs={{128,0},{129,1},{130,2},{131,3},{132,4},{133,5},{134,6},{135,7},{1... | collective-permute-start | bytes 6291464 | tf_op jit(solution)/shard_map/ppermute | solution.py:38
  101.0 8.9 %collective-permute-start.22 = (bf16[2,256,128]{2,1,0:T(8,128)(2,1)S(1)}, bf16[2,256,128]{2,1,0:T(8,128)(2,1)S(1)}, u32[]{:S(2)}, u32[]{:S(2)}) collective-permute-start(bf16[2,256,128]{2,1,0:T(8,128)(2,1)S(1)} %pad_maximum_fusion.4), channel_id=1, source_target_pairs={{0,1},{1,2},{2,3},{4,5},{5,6},{6,7},{8,9},{9,10},{10,11},{12,13},{... | collective-permute-start | bytes 393224 | tf_op jit(solution)/shard_map/ppermute | solution.py:38
  104.1 6.7 %collective-permute-start.23 = (bf16[2,256,128]{2,1,0:T(8,128)(2,1)S(1)}, bf16[2,256,128]{2,1,0:T(8,128)(2,1)S(1)}, u32[]{:S(2)}, u32[]{:S(2)}) collective-permute-start(bf16[2,256,128]{2,1,0:T(8,128)(2,1)S(1)} %pad_maximum_fusion.4), channel_id=1, source_target_pairs={{0,2},{1,3},{4,6},{5,7},{8,10},{9,11},{12,14},{13,15},{16,18},{17,... | collective-permute-start | bytes 393224 | tf_op jit(solution)/shard_map/ppermute | solution.py:38
  108.5 3.7 %collective-permute-start.24 = (bf16[2,256,128]{2,1,0:T(8,128)(2,1)S(1)}, bf16[2,256,128]{2,1,0:T(8,128)(2,1)S(1)}, u32[]{:S(2)}, u32[]{:S(2)}) collective-permute-start(bf16[2,256,128]{2,1,0:T(8,128)(2,1)S(1)} %pad_maximum_fusion.4), channel_id=1, source_target_pairs={{0,3},{4,7},{8,11},{12,15},{16,19},{20,23},{24,27},{28,31},{32,35}... | collective-permute-start | bytes 393224 | tf_op jit(solution)/shard_map/ppermute | solution.py:38
  112.2 3.0 %collective-permute-start.25 = (bf16[4,2,256,128]{3,2,1,0:T(8,128)(2,1)S(1)}, bf16[4,2,256,128]{3,2,1,0:T(8,128)(2,1)S(1)}, u32[]{:S(2)}, u32[]{:S(2)}) collective-permute-start(bf16[4,2,256,128]{3,2,1,0:T(8,128)(2,1)S(1)} %pad_maximum_fusion.3.rest_0_), channel_id=1, source_target_pairs={{128,0},{129,1},{130,2},{131,3},{132,4},{133,5},{134,6},{135,7},{1... | collective-permute-start | bytes 1572872 | tf_op jit(solution)/shard_map/ppermute | solution.py:38
  116.8 3.2 %collective-permute-start.26 = (bf16[256,128]{1,0:T(8,128)(2,1)S(1)}, bf16[256,128]{1,0:T(8,128)(2,1)S(1)}, u32[]{:S(2)}, u32[]{:S(2)}) collective-permute-start(bf16[256,128]{1,0:T(8,128)(2,1)S(1)} %shard_map.83.h0), channel_id=1, source_target_pairs={{32,0},{33,1},{34,2},{35,3},{36,4},{37,5},{38,6},{39,7},{40,8},{41... | collective-permute-start | bytes 196616 | tf_op jit(solution)/shard_map/ppermute | solution.py:38
  117.7 4.6 %collective-permute-start.27 = (bf16[256,128]{1,0:T(8,128)(2,1)S(1)}, bf16[256,128]{1,0:T(8,128)(2,1)S(1)}, u32[]{:S(2)}, u32[]{:S(2)}) collective-permute-start(bf16[256,128]{1,0:T(8,128)(2,1)S(1)} %shard_map.83.h0), channel_id=1, source_target_pairs={{64,0},{65,1},{66,2},{67,3},{68,4},{69,5},{70,6},{71,7},{72,8},{73... | collective-permute-start | bytes 196616 | tf_op jit(solution)/shard_map/ppermute | solution.py:38
  119.7 4.6 %collective-permute-start.28 = (bf16[256,128]{1,0:T(8,128)(2,1)S(1)}, bf16[256,128]{1,0:T(8,128)(2,1)S(1)}, u32[]{:S(2)}, u32[]{:S(2)}) collective-permute-start(bf16[256,128]{1,0:T(8,128)(2,1)S(1)} %shard_map.83.h0), channel_id=1, source_target_pairs={{96,0},{97,1},{98,2},{99,3},{100,4},{101,5},{102,6},{103,7},{104,8... | collective-permute-start | bytes 196616 | tf_op jit(solution)/shard_map/ppermute | solution.py:38
  160.7 5.0 %collective-permute-start.29 = (bf16[256,128]{1,0:T(8,128)(2,1)S(1)}, bf16[256,128]{1,0:T(8,128)(2,1)S(1)}, u32[]{:S(2)}, u32[]{:S(2)}) collective-permute-start(bf16[256,128]{1,0:T(8,128)(2,1)S(1)} %bitcast.100), channel_id=1, source_target_pairs={{128,0},{129,1},{130,2},{131,3},{132,4},{133,5},{134,6},{135,7},{1... | collective-permute-start | bytes 196616 | tf_op jit(solution)/shard_map/ppermute | solution.py:38
  (16 other events, 110.9 us)
Sparse Core Ops, SparseCore 0:
  66.9 29.5 all-gather.2

commit v3 on v2

--- a/solution.py
+++ b/solution.py
@@ -2,7 +2,6 @@
 
 import jax
 import jax.numpy as jnp
-import numpy as np
 from jax import lax
 from jax.experimental import pallas as pl
 from jax.experimental.pallas import tpu as pltpu
@@ -42,60 +41,43 @@
     return lax.ppermute(x, AXES, pairs([m and (0, *m, 0) for m in (on_y, on_z)]))
 
 
-FIRST_Y = (0, 1, 3, 2)
-FIRST_Z = (0, 1, 7, 2)
-LATER_Z = (3, 6, 4, 5)
-
-
-def gather(c, rows):
-    k1 = take_by_core(rows, (1, 0), (0, 1))
-    k2 = take_by_core(rows, (-1, 0), (0, -1))
-    k3 = take_by_core(rows, (2, 0), (0, 2))
+def gather(rows):
+    k1 = take_by_core(rows, (1, 0), (0, 2))
+    k2 = take_by_core(rows, (-1, 0), (0, -2))
+    k3 = take_by_core(rows, (2, 0), (0, 4))
     g0 = jnp.stack([rows, k1, k2, k3])
-    x1 = take_by_core(g0, (0, 1), (1, 0))
+    g1 = take_by_core(g0, (0, 1), (0, -1))
     x2 = take_by_core(g0, (0, -1), (-1, 0))
-    k4 = take_by_core(k3, None, (0, 1))
-    k5 = take_by_core(k2, None, (0, -1))
-    k6 = take_by_core(k3, None, (0, 2))
-    k7 = take_by_core(k2, None, (0, -2))
-    g1 = jnp.stack([k4, k5, k6, k7])
+    x1 = take_by_core(g1, (0, 1), (1, 0))
+    x4 = take_by_core(x2, (0, -1), (-1, 0))
     x3 = take_by_core(x1, (0, 1), (1, 0))
-    x4 = take_by_core(jnp.where(c == 0, x2, g1), (0, -1), (-1, 0))
-    x5 = take_by_core(jnp.where(c == 0, x3, g1), (0, 1), (1, 0))
     x6 = take_by_core(x4, (0, -1), (-1, 0))
-    x7 = take_by_core(x5, (0, 1), None)
-    return [g0, x1, x2, x3, x4, x5, x6], g1, x7
-
-
-PLACES = np.array(
-    [
-        [[(dy, dz) for dy in FIRST_Y] for dz in (0, 1, 7, 2, 6, 3, 5, 4)],
-        [
-            [(dy, dz) for dz in order]
-            for dy, order in (
-                (0, FIRST_Z), (1, FIRST_Z), (3, FIRST_Z), (2, FIRST_Z),
-                (3, LATER_Z), (1, LATER_Z), (2, LATER_Z), (0, LATER_Z),
-            )
-        ],
-    ],
-    np.int32,
-)
-
-
-def qkv_kernel(table_ref, inv_ref, own_row_ref, gain_ref, gain_other_ref, *rest):
+    x5 = take_by_core(x3, (0, 1), (1, 0))
+    return [g0, g1, x1, x2, x3, x4, x5, x6]
+
+
+OFFSETS = ((0, 0, 0), (1, 0, 7), (2, 1, 7), (7, 3, 0), (3, 2, 7), (6, 2, 0), (4, 3, 7), (5, 1, 0))
+
+
+def place(at, k, step):
+    turn = step ^ (step >> 1)
+    dz0, dy1, dz1 = OFFSETS[k]
+    dy = jnp.where(at[0] == 0, turn, dy1)
+    dz = jnp.where(at[0] == 0, dz0, 2 * turn + dz1)
+    return (at[1] + dy) & (NY - 1), (at[2] + dz) & (NZ - 1)
+
+
+def qkv_kernel(at_ref, inv_ref, own_row_ref, gain_ref, gain_other_ref, *rest):
     own_ws, other_ws, pieces = rest[:8], rest[8:16], rest[16:24]
-    last_ref, out_ref, acc = rest[24:]
+    out_ref, acc = rest[24:]
     step = pl.program_id(0)
     inverse = inv_ref[...]
     own_row = own_row_ref[...] > 0
-    on_y = table_ref[0] == 0
     normed, right = [], []
     for k, piece in enumerate(pieces):
-        at = 1 + 2 * (4 * k + step)
-        yi, zi = table_ref[at], table_ref[at + 1]
+        yi, zi = place(at_ref, k, step)
         gain = jnp.where(own_row, gain_ref[yi, pl.ds(zi, 1), :], gain_other_ref[yi, pl.ds(zi, 1), :])
-        value = piece[0] if k < 7 else jnp.where(on_y, last_ref[0], piece[0])
-        normed.append((value.astype(jnp.float32) * inverse * gain).astype(jnp.bfloat16))
+        normed.append((piece[0].astype(jnp.float32) * inverse * gain).astype(jnp.bfloat16))
         right.append(jnp.concatenate([w[p, 0, 0, 0] for w in (own_ws[k], other_ws[k]) for p in range(3)], axis=1))
     part = jnp.dot(
         jnp.concatenate(normed, axis=1), jnp.concatenate(right, axis=0), preferred_element_type=jnp.float32
@@ -114,13 +96,13 @@
         out_ref[...] = jnp.where(own_row, acc[:, : 3 * HD], acc[:, 3 * HD :])
 
 
-def project(table, inverse, own_row, gain, gain_other, w, w_other, arrays, g1, x7):
-    rows = g1.shape[1]
+def project(at, inverse, own_row, gain, gain_other, w, w_other, arrays):
+    rows = arrays[0].shape[1]
     block = (3, 1, 1, 1, HD, HD)
-    whole = lambda shape: pl.BlockSpec(shape, lambda g, t: (0,) * len(shape))
-    piece = pl.BlockSpec((1, rows, HD), lambda g, t: (g, 0, 0))
+    whole = lambda shape: pl.BlockSpec(shape, lambda g, at: (0,) * len(shape))
+    piece = pl.BlockSpec((1, rows, HD), lambda g, at: (g, 0, 0))
     weights = lambda k, other: pl.BlockSpec(
-        block, lambda g, t: (0, 0 if other else t[0], t[1 + 2 * (4 * k + g)], t[2 + 2 * (4 * k + g)], 0, 0)
+        block, lambda g, at: (0, 0 if other else at[0], *place(at, k, g), 0, 0)
     )
     return pl.pallas_call(
         qkv_kernel,
@@ -130,16 +112,16 @@
             in_specs=[whole((rows, 1)), whole((rows, 1)), whole((NY, NZ, HD)), whole((NY, NZ, HD))]
             + [weights(k, False) for k in range(8)]
             + [weights(k, True) for k in range(8)]
-            + [piece] * 9,
+            + [piece] * 8,
             out_specs=whole((rows, 3 * HD)),
             scratch_shapes=[pltpu.VMEM((rows, 6 * HD), jnp.float32)],
         ),
         out_shape=jax.ShapeDtypeStruct((rows, 3 * HD), jnp.float32),
-        compiler_params=pltpu.CompilerParams(vmem_limit_bytes=40 * 2**20),
+        compiler_params=pltpu.CompilerParams(vmem_limit_bytes=56 * 2**20),
         cost_estimate=pl.CostEstimate(
             flops=2 * rows * 4096 * 6 * HD, bytes_accessed=11 * 2**20, transcendentals=0
         ),
-    )(table, inverse, own_row, gain, gain_other, *[w] * 8, *[w_other] * 8, *arrays, g1, x7)
+    )(at, inverse, own_row, gain, gain_other, *[w] * 8, *[w_other] * 8, *arrays)
 
 
 def headnorm(x, gain_row):
@@ -192,37 +174,48 @@
     )(bases, queries, *keys)
 
 
-def out_kernel(own_row_ref, w_ref, w_other_ref, h0, h1, h2, h3, out_ref):
+def out_kernel(own_row_ref, w0, w1, o0, o1, h0, h1, h2, h3, out_ref):
     heads = jnp.concatenate([h0[...], h1[...], h2[...], h3[...]], axis=1)
-    sums = []
-    for ref in (w_ref, w_other_ref):
-        w = jnp.concatenate([ref[x, y] for y in range(NY) for x in range(NX)], axis=0)
-        sums.append(jnp.dot(heads, w, preferred_element_type=jnp.float32))
-    out_ref[0] = jnp.where(own_row_ref[...] > 0, *sums).astype(jnp.bfloat16)
+    own_row = own_row_ref[...] > 0
+    sections = []
+    for refs in ((w0, w1), (o0, o1)):
+        w = jnp.concatenate(
+            [jnp.concatenate([ref[x, y] for y in range(NY) for x in range(NX)], axis=0) for ref in refs], axis=1
+        )
+        sections.append(jnp.dot(heads, w, preferred_element_type=jnp.float32))
+    both = jnp.where(own_row, *sections).astype(jnp.bfloat16)
+    for i in range(2):
+        out_ref[i, :, :HD] = both[:, i * HD : (i + 1) * HD]
+        out_ref[i, :, HD:] = both[:, (2 + i) * HD : (3 + i) * HD]
 
 
 def out_part(own_row, w, w_other, heads):
     rows = heads[0].shape[0]
-    width = w.shape[-1] // NZ
+    steps = NZ // 2
     whole = lambda shape: pl.BlockSpec(shape, lambda g: (0,) * len(shape))
-    weights = pl.BlockSpec((NX, NY, HD // NX, width), lambda g: (0, 0, 0, g))
+    left = pl.BlockSpec((NX, NY, HD // NX, 2 * HD), lambda g: (0, 0, 0, g))
+    right = pl.BlockSpec((NX, NY, HD // NX, 2 * HD), lambda g: (0, 0, 0, steps + g))
     return pl.pallas_call(
         out_kernel,
-        grid=(NZ,),
-        in_specs=[whole((rows, 1)), weights, weights] + [whole((rows, HD))] * NY,
-        out_specs=pl.BlockSpec((1, rows, width), lambda g: (g, 0, 0)),
-        out_shape=jax.ShapeDtypeStruct((NZ, rows, width), jnp.bfloat16),
-        compiler_params=pltpu.CompilerParams(vmem_limit_bytes=40 * 2**20),
+        grid=(steps,),
+        in_specs=[whole((rows, 1)), left, right, left, right] + [whole((rows, HD))] * NY,
+        out_specs=pl.BlockSpec((2, rows, 2 * HD), lambda g: (g, 0, 0)),
+        out_shape=jax.ShapeDtypeStruct((NZ, rows, 2 * HD), jnp.bfloat16),
+        compiler_params=pltpu.CompilerParams(vmem_limit_bytes=56 * 2**20),
         cost_estimate=pl.CostEstimate(
-            flops=4 * rows * NY * HD * NZ * width, bytes_accessed=5 * 2**20, transcendentals=0
+            flops=8 * rows * NY * HD * NZ * HD, bytes_accessed=5 * 2**20, transcendentals=0
         ),
-    )(own_row, w, w_other, *heads)
+    )(own_row, w, w, w_other, w_other, *heads)
 
 
 def spread_w_out(w_out, y, seq):
-    quarter = lax.dynamic_slice_in_dim(w_out[0], seq * (HD // NX), HD // NX, axis=0)
-    by_y = quarter.reshape(HD // NX, 2, NY, NZ, HD).transpose(2, 0, 3, 1, 4).reshape(NY, HD // NX, 2 * NZ * HD)
-    pick = lambda d: lax.dynamic_index_in_dim(by_y, lax.rem(y - d + NY, NY), axis=0, keepdims=False)
+    rows, width = HD // NX, NZ * HD
+
+    def pick(d):
+        column = ((y - d) & (NY - 1)) * width
+        cut = lambda first: lax.dynamic_slice(w_out[0], (seq * rows, first + column), (rows, width))
+        return jnp.concatenate([cut(0), cut(NY * width)], axis=1)
+
     s1, s3, s2 = take(pick(1), dy=1), take(pick(3), dy=-1), take(pick(2), dy=2)
     lines = jnp.stack([pick(0), s1, s2, s3])
     return lax.all_gather(lines, "seq", axis=0)
@@ -234,26 +227,24 @@
     c, y, z, seq = (lax.axis_index(a) for a in AXES)
     own_row = (modality == c).astype(jnp.int32)[:, None]
 
+    arrays = gather(tokens)
+    w_cols = spread_w_out(w_out, y, seq)
+
     w = w_qkv[0].transpose(1, 0, 2).reshape(3, 2, NY, NZ, HD, HD)
     gains = norm_gain.reshape(2, NY, NZ, HD)
-    w_other = take(lax.dynamic_slice_in_dim(w, 1 - c, 1, axis=1), dc=1)
     gain_other = take(lax.dynamic_index_in_dim(gains, 1 - c, axis=0, keepdims=False), dc=1)
     gain = lax.dynamic_index_in_dim(gains, c, axis=0, keepdims=False)
-
-    arrays, g1, x7 = gather(c, tokens)
-    w_out, _ = lax.optimization_barrier((w_out, arrays[1]))
-    w_cols = spread_w_out(w_out, y, seq)
+    w_send, gain_other = lax.optimization_barrier((lax.dynamic_slice_in_dim(w, 1 - c, 1, axis=1), gain_other))
+    w_other = take(w_send, dc=1)
+
+    squared = [jnp.sum(jnp.square(a.astype(jnp.float32)), axis=(0, 2)) for a in arrays]
+    early, w_cols = lax.optimization_barrier((sum(squared[:6]), w_cols))
     w_cols_other = take(w_cols, dc=1)
-
-    squared = lambda a: jnp.sum(jnp.square(a.astype(jnp.float32)), axis=(0, 2))
-    squares = sum(squared(a) for a in arrays) + jnp.where(c == 0, squared(x7), squared(g1))
+    squares = early + squared[6] + squared[7]
     squares = squares + take(squares, dc=1)
     inverse = lax.rsqrt(squares / (2 * NY * NZ * HD) + EPS)[:, None]
-
-    places = jnp.asarray(PLACES)[c].reshape(32, 2)
-    places = lax.rem(places + jnp.stack([y, z]).astype(jnp.int32)[None, :], jnp.array([NY, NZ], jnp.int32)[None, :])
-    table = jnp.concatenate([c.astype(jnp.int32)[None], places.reshape(64)])
-    parts = project(table, inverse, own_row, gain, gain_other, w, w_other, arrays, g1, x7)
+    at = jnp.stack([c, y, z]).astype(jnp.int32)
+    parts = project(at, inverse, own_row, gain, gain_other, w, w_other, arrays)
     parts = parts.reshape(2, half, 3 * HD)
     mine = lax.dynamic_index_in_dim(parts, c, axis=0, keepdims=False)
     theirs = lax.dynamic_index_in_dim(parts, 1 - c, axis=0, keepdims=False)

time: 174 us -> 175 us (level)
  waiting for transfers between devices: 22.7 us -> 44.7 us
  starting transfers between devices: 53 us -> 39.5 us
  local copies, waits for them, and re-layouts: 23.2 us -> 15.9 us
  other arithmetic: 15.4 us -> 13.2 us
    ppermute x14 -> x10, waiting for transfers between devices: 9.68 us -> 26.5 us  [take_by_core(): lax.ppermute(x, AXES, pairs([m and (0, *m, 0) for m in (on_y, on_z)]))]
    ppermute x14 -> x10, starting transfers between devices: 27.2 us -> 16.3 us  [take_by_core(): lax.ppermute(x, AXES, pairs([m and (0, *m, 0) for m in (on_y, on_z)]))]
    ppermute x16, waiting for transfers between devices: 13 us -> 18.1 us  [take(): return lax.ppermute(x, AXES, pairs([(dc, dy, dz, dx)] * 2, wrap_x))]
    select_n x2 -> x0, other arithmetic: 2.66 us -> none  [the longest x1 1.79 us: gather(): x4 = take_by_core(jnp.where(c == 0, x2, g1), (0, -1), (-1, 0))]
    ppermute x16, starting transfers between devices: 25.8 us -> 23.2 us  [take(): return lax.ppermute(x, AXES, pairs([(dc, dy, dz, dx)] * 2, wrap_x))]
    unnamed x36 -> x32, local copies, waits for them, and re-layouts: 8.27 us -> 6.02 us
    reshape x1 -> x0, local copies, waits for them, and re-layouts: 2.2 us -> none  [spread_w_out(): quarter.reshape(HD // NX, 2, NY, NZ, HD).transpose(2, 0, 3, 1, 4)]
    dynamic_slice x3 -> x2, local copies, waits for them, and re-layouts: 5.89 us -> 5.13 us  [the longest x1 3.98 us: shards(): lax.dynamic_slice_in_dim(w, 1 - c, 1, axis=1)]
  transfers between devices with their start and end apart: 31 -> 27, of which waited for: 14 -> 15; matrix products, arithmetic and copies ran while one was open for 17% -> 11% of each run, Pallas kernels for 6% -> 1%
where the time goes in v3:
time: 175 us; the launch traced here: 174 us
  waiting for transfers between devices  44.7 us (26%)
  starting transfers between devices  39.5 us (23%)
  blocking collectives  30.3 us (17%)
  Pallas kernels  17 us (10%)
  local copies, waits for them, and re-layouts  15.9 us (9%)
  between operations  13.7 us (8%)
  other arithmetic  13.2 us (8%)
    all_to_all x1, blocking collectives, shards(): spread = lax.all_to_all(partial, 'z', 0, 0)  30.3 us
    ppermute x10, waiting for transfers between devices, take_by_core(): lax.ppermute(x, AXES, pairs([m and (0, *m, 0) for m in (on_y, on_z)]))  26.5 us
    ppermute x16, starting transfers between devices, take(): return lax.ppermute(x, AXES, pairs([(dc, dy, dz, dx)] * 2, wrap_x))  23.2 us
    ppermute x16, waiting for transfers between devices, take(): return lax.ppermute(x, AXES, pairs([(dc, dy, dz, dx)] * 2, wrap_x))  18.1 us
    ppermute x10, starting transfers between devices, take_by_core(): lax.ppermute(x, AXES, pairs([m and (0, *m, 0) for m in (on_y, on_z)]))  16.3 us
    pallas_call x1, Pallas kernels, project(): pl.pallas_call(qkv_kernel, grid_spec=pltpu.PrefetchScalarGridSpec(num_sca...  10.4 us
    reduce_sum x8, other arithmetic, shards(): jnp.sum(jnp.square(a.astype(jnp.float32)), axis=(0, 2))  8.19 us
    unnamed x32, local copies, waits for them, and re-layouts  6.02 us
  transfers between devices with their start and end apart: 27, of which 15 were waited for; matrix products, arithmetic and copies ran while one was open for 11% of the time, Pallas kernels for 1%

profile of v3, /device:TPU:1, one launch (start us, length us, event | category | flops | bytes accessed | tf_op | source)
XLA Modules:
  0.0 174.3 jit_solution(1301601655094567897)
XLA Ops:
  7.7 3.6 %collective-permute-start.8 = (bf16[32,2048]{1,0:T(8,128)(2,1)S(1)}, bf16[32,2048]{1,0:T(8,128)(2,1)S(1)}, u32[]{:S(2)}, u32[]{:S(2)}) collective-permute-start(bf16[32,2048]{1,0:T(8,128)(2,1)S(1)} %pad_maximum_fusion.3), channel_id=1, source_target_pairs={{32,0},{33,1},{34,2},{35,3},{36,4},{37,5},{38,6},{39,7},{40,8},{41... | collective-permute-start | bytes 393224 | tf_op jit(solution)/shard_map/ppermute | solution.py:37
  12.6 2.0 %collective-permute-done.8 = bf16[32,2048]{1,0:T(8,128)(2,1)S(1)} collective-permute-done((bf16[32,2048]{1,0:T(8,128)(2,1)S(1)}, bf16[32,2048]{1,0:T(8,128)(2,1)S(1)}, u32[]{:S(2)}, u32[]{:S(2)}) %collective-permute-start.8) | collective-permute-done | bytes 131104 | tf_op jit(solution)/shard_map/ppermute | solution.py:37
  14.6 2.3 %collective-permute-done.9 = bf16[32,2048]{1,0:T(8,128)(2,1)S(1)} collective-permute-done((bf16[32,2048]{1,0:T(8,128)(2,1)S(1)}, bf16[32,2048]{1,0:T(8,128)(2,1)S(1)}, u32[]{:S(2)}, u32[]{:S(2)}) %collective-permute-start.9) | collective-permute-done | bytes 131104 | tf_op jit(solution)/shard_map/ppermute | solution.py:37
  16.9 4.2 %collective-permute-done.10 = bf16[32,2048]{1,0:T(8,128)(2,1)S(1)} collective-permute-done((bf16[32,2048]{1,0:T(8,128)(2,1)S(1)}, bf16[32,2048]{1,0:T(8,128)(2,1)S(1)}, u32[]{:S(2)}, u32[]{:S(2)}) %collective-permute-start.10) | collective-permute-done | bytes 131104 | tf_op jit(solution)/shard_map/ppermute | solution.py:37
  22.0 6.1 %collective-permute-start = (bf16[512,128]{1,0:T(8,128)(2,1)S(1)}, bf16[512,128]{1,0:T(8,128)(2,1)S(1)}, u32[]{:S(2)}, u32[]{:S(2)}) collective-permute-start(bf16[512,128]{1,0:T(8,128)(2,1)S(1)} %copy-done.7), channel_id=1, source_target_pairs={{32,0},{33,1},{34,2},{35,3},{36,4},{37,5},{38,6},{39,7},{40,8},{41... | collective-permute-start | bytes 393224 | tf_op jit(solution)/shard_map/ppermute | solution.py:41
  28.1 3.3 %collective-permute-start.2 = (bf16[512,128]{1,0:T(8,128)(2,1)S(1)}, bf16[512,128]{1,0:T(8,128)(2,1)}, u32[]{:S(2)}, u32[]{:S(2)}) collective-permute-start(bf16[512,128]{1,0:T(8,128)(2,1)S(1)} %copy-done.7), channel_id=1, source_target_pairs={{64,0},{65,1},{66,2},{67,3},{68,4},{69,5},{70,6},{71,7},{72,8},{73... | collective-permute-start | bytes 393224 | tf_op jit(solution)/shard_map/ppermute | solution.py:41
  31.9 4.0 %constant_dynamic-slice_fusion.2 = bf16[3,1,4,8,128,128]{5,4,3,2,1,0:T(8,128)(2,1)} fusion(bf16[3,2,4,8,128,128]{5,4,3,2,1,0:T(8,128)(2,1)} %bitcast.73, s32[]{:T(128)S(6)} %select_n.88), kind=kLoop, calls=%fused_computation.62 | loop fusion | bytes 6291460 | tf_op jit(solution)/shard_map/dynamic_slice | solution.py:237
  36.6 1.7 multiply_reduce_fusion.7
  38.3 2.4 %collective-permute-start.3 = (bf16[4,512,128]{2,1,0:T(8,128)(2,1)S(1)}, bf16[4,512,128]{2,1,0:T(8,128)(2,1)S(1)}, u32[]{:S(2)}, u32[]{:S(2)}) collective-permute-start(bf16[4,512,128]{2,1,0:T(8,128)(2,1)S(1)} %get-tuple-element.18.rest_16_), channel_id=1, source_target_pairs={{4,0},{5,1},{6,2},{7,3},{8,4},{9,5},{10,6},{11,7},{12,8},{13,9},{1... | collective-permute-start | bytes 1572872 | tf_op jit(solution)/shard_map/ppermute | solution.py:41
  40.7 13.0 %collective-permute-done.3.rest_17_ = bf16[4,512,128]{2,1,0:T(8,128)(2,1)S(1)} collective-permute-done((bf16[4,512,128]{2,1,0:T(8,128)(2,1)S(1)}, bf16[4,512,128]{2,1,0:T(8,128)(2,1)S(1)}, u32[]{:S(2)}, u32[]{:S(2)}) %collective-permute-start.3) | collective-permute-done | bytes 524320 | tf_op jit(solution)/shard_map/ppermute | solution.py:41
  55.2 7.0 %collective-permute-done.4.rest_18_ = bf16[4,512,128]{2,1,0:T(8,128)(2,1)} collective-permute-done((bf16[4,512,128]{2,1,0:T(8,128)(2,1)S(1)}, bf16[4,512,128]{2,1,0:T(8,128)(2,1)}, u32[]{:S(2)}, u32[]{:S(2)}) %collective-permute-start.4) | collective-permute-done | bytes 524320 | tf_op jit(solution)/shard_map/ppermute | solution.py:41
  63.4 1.2 multiply_reduce_fusion.4
  66.2 1.2 multiply_reduce_fusion.2
  67.4 3.3 %collective-permute-done.6.rest_20_ = bf16[4,512,128]{2,1,0:T(8,128)(2,1)} collective-permute-done((bf16[4,512,128]{2,1,0:T(8,128)(2,1)}, bf16[4,512,128]{2,1,0:T(8,128)(2,1)}, u32[]{:S(2)}, u32[]{:S(2)}) %collective-permute-start.6) | collective-permute-done | bytes 524320 | tf_op jit(solution)/shard_map/ppermute | solution.py:41
  70.7 2.4 %collective-permute-start.12 = (bf16[4,512,128]{2,1,0:T(8,128)(2,1)}, bf16[4,512,128]{2,1,0:T(8,128)(2,1)S(1)}, u32[]{:S(2)}, u32[]{:S(2)}) collective-permute-start(bf16[4,512,128]{2,1,0:T(8,128)(2,1)} %collective-permute-done.6.rest_20_), channel_id=1, source_target_pairs={{4,0},{5,1},{6,2},{7,3},{8,4},{9,5},{10,6},{11,7},{12,8},{13,9},{1... | collective-permute-start | bytes 1572872 | tf_op jit(solution)/shard_map/ppermute | solution.py:41
  74.3 1.2 multiply_reduce_fusion.3
  76.6 3.0 %collective-permute-done.12.rest_22_ = bf16[4,512,128]{2,1,0:T(8,128)(2,1)S(1)} collective-permute-done((bf16[4,512,128]{2,1,0:T(8,128)(2,1)}, bf16[4,512,128]{2,1,0:T(8,128)(2,1)S(1)}, u32[]{:S(2)}, u32[]{:S(2)}) %collective-permute-start.12) | collective-permute-done | bytes 524320 | tf_op jit(solution)/shard_map/ppermute | solution.py:41
  83.1 1.7 copy-done.1
  84.7 10.4 %shard_map.64 = f32[512,384]{1,0:T(8,128)} custom-call(s32[3]{0:T(128)} %pad_add_fusion.at_ref, f32[512,1]{1,0:T(8,128)} %copy.15.inv_ref, s32[512,1]{1,0:T(8,128)} %copy.16.own_row_ref, f32[4,8,128]{2,1,0:T(8,128)} %get-tuple-element.36.gain_ref, f32[4,8,128]{2,1,0:T(8,128)} %copy-done.12, bf16[3,2,4,8,128,128]{5,4,3,2,1,0:T(8,128)(2,1)} %bitcast.74, ...), custom_call_target="tpu_custom_call" | custom-call | flops 3221225472 | bytes 11534336 | tf_op jit(solution)/shard_map/pallas_call | solution.py:107
  100.5 3.1 %collective-permute-start.18 = (bf16[2,256,128]{2,1,0:T(8,128)(2,1)S(1)}, bf16[2,256,128]{2,1,0:T(8,128)(2,1)S(1)}, u32[]{:S(2)}, u32[]{:S(2)}) collective-permute-start(bf16[2,256,128]{2,1,0:T(8,128)(2,1)S(1)} %pad_maximum_fusion.6), channel_id=1, source_target_pairs={{0,1},{1,2},{2,3},{4,5},{5,6},{6,7},{8,9},{9,10},{10,11},{12,13},{... | collective-permute-start | bytes 393224 | tf_op jit(solution)/shard_map/ppermute | solution.py:37
  103.6 4.4 %collective-permute-start.19 = (bf16[2,256,128]{2,1,0:T(8,128)(2,1)S(1)}, bf16[2,256,128]{2,1,0:T(8,128)(2,1)S(1)}, u32[]{:S(2)}, u32[]{:S(2)}) collective-permute-start(bf16[2,256,128]{2,1,0:T(8,128)(2,1)S(1)} %pad_maximum_fusion.6), channel_id=1, source_target_pairs={{0,2},{1,3},{4,6},{5,7},{8,10},{9,11},{12,14},{13,15},{16,18},{17,... | collective-permute-start | bytes 393224 | tf_op jit(solution)/shard_map/ppermute | solution.py:37
  108.0 1.3 collective-permute-start.20
  110.2 1.3 collective-permute-done.20
  111.5 1.6 collective-permute-start.21
  113.3 1.4 collective-permute-done.21.rest_1_
  114.7 1.7 shard_map.65.h0
  116.4 3.1 %collective-permute-start.22 = (bf16[256,128]{1,0:T(8,128)(2,1)S(1)}, bf16[256,128]{1,0:T(8,128)(2,1)S(1)}, u32[]{:S(2)}, u32[]{:S(2)}) collective-permute-start(bf16[256,128]{1,0:T(8,128)(2,1)S(1)} %shard_map.65.h0), channel_id=1, source_target_pairs={{32,0},{33,1},{34,2},{35,3},{36,4},{37,5},{38,6},{39,7},{40,8},{41... | collective-permute-start | bytes 196616 | tf_op jit(solution)/shard_map/ppermute | solution.py:37
  121.0 3.2 %collective-permute-done.23.h2 = bf16[256,128]{1,0:T(8,128)(2,1)S(1)} collective-permute-done((bf16[256,128]{1,0:T(8,128)(2,1)S(1)}, bf16[256,128]{1,0:T(8,128)(2,1)S(1)}, u32[]{:S(2)}, u32[]{:S(2)}) %collective-permute-start.23) | collective-permute-done | bytes 65568 | tf_op jit(solution)/shard_map/ppermute | solution.py:37
  126.0 1.3 copy-done.2
  127.3 5.0 %shard_map.66 = bf16[8,256,256]{2,1,0:T(8,128)(2,1)} custom-call(s32[256,1]{1,0:T(8,128)} %copy.17.own_row_ref, bf16[4,4,32,2048]{3,2,1,0:T(8,128)(2,1)} %bitcast.17.w0.w1, bf16[4,4,32,2048]{3,2,1,0:T(8,128)(2,1)} %bitcast.17.w0.w1, bf16[4,4,32,2048]{3,2,1,0:T(8,128)(2,1)} %copy-done.2, bf16[4,4,32,2048]{3,2,1,0:T(8,128)(2,1)} %copy-done.2, ...), custom_call_target="tpu_custom_call" | custom-call | flops 1073741824 | bytes 5242880 | tf_op jit(solution)/shard_map/pallas_call | solution.py:198
  132.2 30.3 %all_to_all.5 = bf16[8,256,256]{2,1,0:T(8,128)(2,1)S(1)} all-to-all(bf16[8,256,256]{2,1,0:T(8,128)(2,1)} %shard_map.66), channel_id=1, replica_groups=mesh['mod'=2,'y'=4,'z'=8,'seq'=4] {'z'}, dimensions={0} | all-to-all | bytes 2097152 | tf_op jit(solution)/shard_map/all_to_all | solution.py:273
  162.9 2.9 %collective-permute-start.25 = (bf16[256,128]{1,0:T(8,128)(2,1)S(1)}, bf16[256,128]{1,0:T(8,128)(2,1)S(1)}, u32[]{:S(2)}, u32[]{:S(2)}) collective-permute-start(bf16[256,128]{1,0:T(8,128)(2,1)S(1)} %bitcast.95), channel_id=1, source_target_pairs={{128,0},{129,1},{130,2},{131,3},{132,4},{133,5},{134,6},{135,7},{1... | collective-permute-start | bytes 196616 | tf_op jit(solution)/shard_map/ppermute | solution.py:37
  (108 shorter events, 26.2 us)
Async XLA Ops:
  6.5 15.4 %copy-start.7 = (bf16[512,128]{1,0:T(8,128)(2,1)S(1)}, bf16[512,128]{1,0:T(8,128)(2,1)}, u32[]{:S(2)}) copy-start(bf16[512,128]{1,0:T(8,128)(2,1)} %param.6) | copy-start | bytes 393220
  6.5 24.8 %copy-start.11 = (f32[1,8192]{1,0:T(1,128)S(1)}, f32[1,8192]{1,0:T(1,128)}, u32[]{:S(2)}) copy-start(f32[1,8192]{1,0:T(1,128)} %param.8) | copy-start | bytes 98308
  6.5 74.0 %all-gather.3.cloned.1.call-start = ((), (), s32[]{:S(2)}) async-start(), calls=%async_computation.1 | async-start | bytes 2621440 | tf_op jit(solution)/shard_map/all_gather | solution.py:221
  7.7 6.8 %collective-permute-start.8 = (bf16[32,2048]{1,0:T(8,128)(2,1)S(1)}, bf16[32,2048]{1,0:T(8,128)(2,1)S(1)}, u32[]{:S(2)}, u32[]{:S(2)}) collective-permute-start(bf16[32,2048]{1,0:T(8,128)(2,1)S(1)} %pad_maximum_fusion.3), channel_id=1, source_target_pairs={{32,0},{33,1},{34,2},{35,3},{36,4},{37,5},{38,6},{39,7},{40,8},{41... | collective-permute-start | bytes 393224 | tf_op jit(solution)/shard_map/ppermute | solution.py:37
  11.4 5.5 %collective-permute-start.9 = (bf16[32,2048]{1,0:T(8,128)(2,1)S(1)}, bf16[32,2048]{1,0:T(8,128)(2,1)S(1)}, u32[]{:S(2)}, u32[]{:S(2)}) collective-permute-start(bf16[32,2048]{1,0:T(8,128)(2,1)S(1)} %pad_maximum_fusion.4), channel_id=1, source_target_pairs={{64,0},{65,1},{66,2},{67,3},{68,4},{69,5},{70,6},{71,7},{72,8},{73... | collective-permute-start | bytes 393224 | tf_op jit(solution)/shard_map/ppermute | solution.py:37
  11.8 9.2 %collective-permute-start.10 = (bf16[32,2048]{1,0:T(8,128)(2,1)S(1)}, bf16[32,2048]{1,0:T(8,128)(2,1)S(1)}, u32[]{:S(2)}, u32[]{:S(2)}) collective-permute-start(bf16[32,2048]{1,0:T(8,128)(2,1)S(1)} %pad_maximum_fusion.5), channel_id=1, source_target_pairs={{96,0},{97,1},{98,2},{99,3},{100,4},{101,5},{102,6},{103,7},{104,8... | collective-permute-start | bytes 393224 | tf_op jit(solution)/shard_map/ppermute | solution.py:37
  22.0 14.5 %collective-permute-start = (bf16[512,128]{1,0:T(8,128)(2,1)S(1)}, bf16[512,128]{1,0:T(8,128)(2,1)S(1)}, u32[]{:S(2)}, u32[]{:S(2)}) collective-permute-start(bf16[512,128]{1,0:T(8,128)(2,1)S(1)} %copy-done.7), channel_id=1, source_target_pairs={{32,0},{33,1},{34,2},{35,3},{36,4},{37,5},{38,6},{39,7},{40,8},{41... | collective-permute-start | bytes 393224 | tf_op jit(solution)/shard_map/ppermute | solution.py:41
  28.1 8.4 %collective-permute-start.1 = (bf16[512,128]{1,0:T(8,128)(2,1)S(1)}, bf16[512,128]{1,0:T(8,128)(2,1)S(1)}, u32[]{:S(2)}, u32[]{:S(2)}) collective-permute-start(bf16[512,128]{1,0:T(8,128)(2,1)S(1)} %copy-done.7), channel_id=1, source_target_pairs={{96,0},{97,1},{98,2},{99,3},{100,4},{101,5},{102,6},{103,7},{104,8... | collective-permute-start | bytes 393224 | tf_op jit(solution)/shard_map/ppermute | solution.py:41
  28.1 8.5 %collective-permute-start.2 = (bf16[512,128]{1,0:T(8,128)(2,1)S(1)}, bf16[512,128]{1,0:T(8,128)(2,1)}, u32[]{:S(2)}, u32[]{:S(2)}) collective-permute-start(bf16[512,128]{1,0:T(8,128)(2,1)S(1)} %copy-done.7), channel_id=1, source_target_pairs={{64,0},{65,1},{66,2},{67,3},{68,4},{69,5},{70,6},{71,7},{72,8},{73... | collective-permute-start | bytes 393224 | tf_op jit(solution)/shard_map/ppermute | solution.py:41
  31.9 4.0 %collective-permute-start.15 = (f32[4,8,128]{2,1,0:T(8,128)S(1)}, f32[4,8,128]{2,1,0:T(8,128)S(1)}, u32[]{:S(2)}, u32[]{:S(2)}) collective-permute-start(f32[4,8,128]{2,1,0:T(8,128)S(1)} %get-tuple-element.35), channel_id=1, source_target_pairs={{128,0},{129,1},{130,2},{131,3},{132,4},{133,5},{134,6},{135,7},{1... | collective-permute-start | bytes 49160 | tf_op jit(solution)/shard_map/ppermute | solution.py:37
  31.9 31.4 %copy-start.14 = (s32[512]{0:T(512)S(1)}, s32[512]{0:T(512)}, u32[]{:S(2)}) copy-start(s32[512]{0:T(512)} %param.7) | copy-start | bytes 6148
  35.9 47.2 %copy-start.12 = (f32[4,8,128]{2,1,0:T(8,128)}, f32[4,8,128]{2,1,0:T(8,128)S(1)}, u32[]{:S(2)}) copy-start(f32[4,8,128]{2,1,0:T(8,128)S(1)} %collective-permute-done.15.gain_other_ref) | copy-start | bytes 49156
  35.9 47.2 %collective-permute-start.16 = (bf16[3,1,4,8,128,128]{5,4,3,2,1,0:T(8,128)(2,1)}, bf16[3,1,4,8,128,128]{5,4,3,2,1,0:T(8,128)(2,1)S(1)}, u32[]{:S(2)}, u32[]{:S(2)}) collective-permute-start(bf16[3,1,4,8,128,128]{5,4,3,2,1,0:T(8,128)(2,1)} %constant_dynamic-slice_fusion.2), channel_id=1, source_target_pairs={{128,0},{129,1},{130,2},{131,3},{132,4},{133,5},{134,6},{135,7},{1... | collective-permute-start | bytes 9437192 | tf_op jit(solution)/shard_map/ppermute | solution.py:37
  38.3 38.2 %copy-start.13 = (f32[512]{0:T(512)S(1)}, f32[512]{0:T(512)}, u32[]{:S(2)}) copy-start(f32[512]{0:T(512)} %get-tuple-element.17) | copy-start | bytes 6148
  38.3 15.4 %collective-permute-start.3 = (bf16[4,512,128]{2,1,0:T(8,128)(2,1)S(1)}, bf16[4,512,128]{2,1,0:T(8,128)(2,1)S(1)}, u32[]{:S(2)}, u32[]{:S(2)}) collective-permute-start(bf16[4,512,128]{2,1,0:T(8,128)(2,1)S(1)} %get-tuple-element.18.rest_16_), channel_id=1, source_target_pairs={{4,0},{5,1},{6,2},{7,3},{8,4},{9,5},{10,6},{11,7},{12,8},{13,9},{1... | collective-permute-start | bytes 1572872 | tf_op jit(solution)/shard_map/ppermute | solution.py:41
  40.7 13.0 %collective-permute-start.5 = (bf16[4,512,128]{2,1,0:T(8,128)(2,1)S(1)}, bf16[4,512,128]{2,1,0:T(8,128)(2,1)}, u32[]{:S(2)}, u32[]{:S(2)}) collective-permute-start(bf16[4,512,128]{2,1,0:T(8,128)(2,1)S(1)} %get-tuple-element.18.rest_16_), channel_id=1, source_target_pairs={{28,0},{29,1},{30,2},{31,3},{0,4},{1,5},{2,6},{3,7},{4,8},{5,9},{6... | collective-permute-start | bytes 1572872 | tf_op jit(solution)/shard_map/ppermute | solution.py:41
  53.7 8.4 %collective-permute-start.4 = (bf16[4,512,128]{2,1,0:T(8,128)(2,1)S(1)}, bf16[4,512,128]{2,1,0:T(8,128)(2,1)}, u32[]{:S(2)}, u32[]{:S(2)}) collective-permute-start(bf16[4,512,128]{2,1,0:T(8,128)(2,1)S(1)} %collective-permute-done.3.rest_17_), channel_id=1, source_target_pairs={{4,0},{5,1},{6,2},{7,3},{8,4},{9,5},{10,6},{11,7},{12,8},{13,9},{1... | collective-permute-start | bytes 1572872 | tf_op jit(solution)/shard_map/ppermute | solution.py:41
  54.6 10.0 %collective-permute-start.7 = (bf16[4,512,128]{2,1,0:T(8,128)(2,1)}, bf16[4,512,128]{2,1,0:T(8,128)(2,1)}, u32[]{:S(2)}, u32[]{:S(2)}) collective-permute-start(bf16[4,512,128]{2,1,0:T(8,128)(2,1)} %collective-permute-done.5.rest_19_), channel_id=1, source_target_pairs={{28,0},{29,1},{30,2},{31,3},{0,4},{1,5},{2,6},{3,7},{4,8},{5,9},{6... | collective-permute-start | bytes 1572872 | tf_op jit(solution)/shard_map/ppermute | solution.py:41
  62.2 8.5 %collective-permute-start.6 = (bf16[4,512,128]{2,1,0:T(8,128)(2,1)}, bf16[4,512,128]{2,1,0:T(8,128)(2,1)}, u32[]{:S(2)}, u32[]{:S(2)}) collective-permute-start(bf16[4,512,128]{2,1,0:T(8,128)(2,1)} %collective-permute-done.4.rest_18_), channel_id=1, source_target_pairs={{4,0},{5,1},{6,2},{7,3},{8,4},{9,5},{10,6},{11,7},{12,8},{13,9},{1... | collective-permute-start | bytes 1572872 | tf_op jit(solution)/shard_map/ppermute | solution.py:41
  64.6 11.0 %collective-permute-start.13 = (bf16[4,512,128]{2,1,0:T(8,128)(2,1)}, bf16[4,512,128]{2,1,0:T(8,128)(2,1)S(1)}, u32[]{:S(2)}, u32[]{:S(2)}) collective-permute-start(bf16[4,512,128]{2,1,0:T(8,128)(2,1)} %collective-permute-done.7.rest_21_), channel_id=1, source_target_pairs={{28,0},{29,1},{30,2},{31,3},{0,4},{1,5},{2,6},{3,7},{4,8},{5,9},{6... | collective-permute-start | bytes 1572872 | tf_op jit(solution)/shard_map/ppermute | solution.py:41
  70.7 8.9 %collective-permute-start.12 = (bf16[4,512,128]{2,1,0:T(8,128)(2,1)}, bf16[4,512,128]{2,1,0:T(8,128)(2,1)S(1)}, u32[]{:S(2)}, u32[]{:S(2)}) collective-permute-start(bf16[4,512,128]{2,1,0:T(8,128)(2,1)} %collective-permute-done.6.rest_20_), channel_id=1, source_target_pairs={{4,0},{5,1},{6,2},{7,3},{8,4},{9,5},{10,6},{11,7},{12,8},{13,9},{1... | collective-permute-start | bytes 1572872 | tf_op jit(solution)/shard_map/ppermute | solution.py:41
  80.6 1.6 collective-permute-start.14
  96.1 1.9 %collective-permute-start.17 = (f32[256,384]{1,0:T(8,128)S(1)}, f32[256,384]{1,0:T(8,128)S(1)}, u32[]{:S(2)}, u32[]{:S(2)}) collective-permute-start(f32[256,384]{1,0:T(8,128)S(1)} %dynamic-slice_bitcast_fusion), channel_id=1, source_target_pairs={{128,0},{129,1},{130,2},{131,3},{132,4},{133,5},{134,6},{135,7},{1... | collective-permute-start | bytes 1179656 | tf_op jit(solution)/shard_map/ppermute | solution.py:37
  96.8 28.6 %collective-permute-start.11 = (bf16[4,4,32,2048]{3,2,1,0:T(8,128)(2,1)}, bf16[4,4,32,2048]{3,2,1,0:T(8,128)(2,1)S(1)}, u32[]{:S(2)}, u32[]{:S(2)}) collective-permute-start(bf16[4,4,32,2048]{3,2,1,0:T(8,128)(2,1)} %bitcast.17.w0.w1), channel_id=1, source_target_pairs={{128,0},{129,1},{130,2},{131,3},{132,4},{133,5},{134,6},{135,7},{1... | collective-permute-start | bytes 6291464 | tf_op jit(solution)/shard_map/ppermute | solution.py:37
  100.5 8.9 %collective-permute-start.18 = (bf16[2,256,128]{2,1,0:T(8,128)(2,1)S(1)}, bf16[2,256,128]{2,1,0:T(8,128)(2,1)S(1)}, u32[]{:S(2)}, u32[]{:S(2)}) collective-permute-start(bf16[2,256,128]{2,1,0:T(8,128)(2,1)S(1)} %pad_maximum_fusion.6), channel_id=1, source_target_pairs={{0,1},{1,2},{2,3},{4,5},{5,6},{6,7},{8,9},{9,10},{10,11},{12,13},{... | collective-permute-start | bytes 393224 | tf_op jit(solution)/shard_map/ppermute | solution.py:37
  103.6 6.5 %collective-permute-start.19 = (bf16[2,256,128]{2,1,0:T(8,128)(2,1)S(1)}, bf16[2,256,128]{2,1,0:T(8,128)(2,1)S(1)}, u32[]{:S(2)}, u32[]{:S(2)}) collective-permute-start(bf16[2,256,128]{2,1,0:T(8,128)(2,1)S(1)} %pad_maximum_fusion.6), channel_id=1, source_target_pairs={{0,2},{1,3},{4,6},{5,7},{8,10},{9,11},{12,14},{13,15},{16,18},{17,... | collective-permute-start | bytes 393224 | tf_op jit(solution)/shard_map/ppermute | solution.py:37
  108.0 3.5 %collective-permute-start.20 = (bf16[2,256,128]{2,1,0:T(8,128)(2,1)S(1)}, bf16[2,256,128]{2,1,0:T(8,128)(2,1)S(1)}, u32[]{:S(2)}, u32[]{:S(2)}) collective-permute-start(bf16[2,256,128]{2,1,0:T(8,128)(2,1)S(1)} %pad_maximum_fusion.6), channel_id=1, source_target_pairs={{0,3},{4,7},{8,11},{12,15},{16,19},{20,23},{24,27},{28,31},{32,35}... | collective-permute-start | bytes 393224 | tf_op jit(solution)/shard_map/ppermute | solution.py:37
  111.5 3.1 %collective-permute-start.21 = (bf16[4,2,256,128]{3,2,1,0:T(8,128)(2,1)S(1)}, bf16[4,2,256,128]{3,2,1,0:T(8,128)(2,1)S(1)}, u32[]{:S(2)}, u32[]{:S(2)}) collective-permute-start(bf16[4,2,256,128]{3,2,1,0:T(8,128)(2,1)S(1)} %pad_maximum_fusion.2.rest_0_), channel_id=1, source_target_pairs={{128,0},{129,1},{130,2},{131,3},{132,4},{133,5},{134,6},{135,7},{1... | collective-permute-start | bytes 1572872 | tf_op jit(solution)/shard_map/ppermute | solution.py:37
  116.4 4.6 %collective-permute-start.22 = (bf16[256,128]{1,0:T(8,128)(2,1)S(1)}, bf16[256,128]{1,0:T(8,128)(2,1)S(1)}, u32[]{:S(2)}, u32[]{:S(2)}) collective-permute-start(bf16[256,128]{1,0:T(8,128)(2,1)S(1)} %shard_map.65.h0), channel_id=1, source_target_pairs={{32,0},{33,1},{34,2},{35,3},{36,4},{37,5},{38,6},{39,7},{40,8},{41... | collective-permute-start | bytes 196616 | tf_op jit(solution)/shard_map/ppermute | solution.py:37
  119.5 4.7 %collective-permute-start.23 = (bf16[256,128]{1,0:T(8,128)(2,1)S(1)}, bf16[256,128]{1,0:T(8,128)(2,1)S(1)}, u32[]{:S(2)}, u32[]{:S(2)}) collective-permute-start(bf16[256,128]{1,0:T(8,128)(2,1)S(1)} %shard_map.65.h0), channel_id=1, source_target_pairs={{64,0},{65,1},{66,2},{67,3},{68,4},{69,5},{70,6},{71,7},{72,8},{73... | collective-permute-start | bytes 196616 | tf_op jit(solution)/shard_map/ppermute | solution.py:37
  119.5 5.9 %collective-permute-start.24 = (bf16[256,128]{1,0:T(8,128)(2,1)S(1)}, bf16[256,128]{1,0:T(8,128)(2,1)S(1)}, u32[]{:S(2)}, u32[]{:S(2)}) collective-permute-start(bf16[256,128]{1,0:T(8,128)(2,1)S(1)} %shard_map.65.h0), channel_id=1, source_target_pairs={{96,0},{97,1},{98,2},{99,3},{100,4},{101,5},{102,6},{103,7},{104,8... | collective-permute-start | bytes 196616 | tf_op jit(solution)/shard_map/ppermute | solution.py:37
  162.9 3.8 %collective-permute-start.25 = (bf16[256,128]{1,0:T(8,128)(2,1)S(1)}, bf16[256,128]{1,0:T(8,128)(2,1)S(1)}, u32[]{:S(2)}, u32[]{:S(2)}) collective-permute-start(bf16[256,128]{1,0:T(8,128)(2,1)S(1)} %bitcast.95), channel_id=1, source_target_pairs={{128,0},{129,1},{130,2},{131,3},{132,4},{133,5},{134,6},{135,7},{1... | collective-permute-start | bytes 196616 | tf_op jit(solution)/shard_map/ppermute | solution.py:37
  (11 other events, 34.9 us)
Sparse Core Ops, SparseCore 0:
  22.1 33.7 all-gather.2

commit v4 on v3

--- a/solution.py
+++ b/solution.py
@@ -14,7 +14,7 @@
 NY = 4
 NZ = 8
 NX = 4
-AXES = ("mod", "y", "z", "seq")
+AXES = ("mod", "y", "zh", "zl", "seq")
 
 
 def pairs(moves, wrap_x=True):
@@ -28,7 +28,8 @@
                 for x in range(NX):
                     if not wrap_x and not 0 <= x + dx < NX:
                         continue
-                    source = (((c + dc) % 2 * NY + (y + dy) % NY) * NZ + (z + dz) % NZ) * NX + (x + dx) % NX
+                    from_z = z ^ 1 if dz == "pair" else (z + dz) % NZ
+                    source = (((c + dc) % 2 * NY + (y + dy) % NY) * NZ + from_z) * NX + (x + dx) % NX
                     out.append((source, ((c * NY + y) * NZ + z) * NX + x))
     return out
 
@@ -53,7 +54,7 @@
     x3 = take_by_core(x1, (0, 1), (1, 0))
     x6 = take_by_core(x4, (0, -1), (-1, 0))
     x5 = take_by_core(x3, (0, 1), (1, 0))
-    return [g0, g1, x1, x2, x3, x4, x5, x6]
+    return [g0, g1, x1, x2, x3, x4, x5, x6], [k1, k2, k3]
 
 
 OFFSETS = ((0, 0, 0), (1, 0, 7), (2, 1, 7), (7, 3, 0), (3, 2, 7), (6, 2, 0), (4, 3, 7), (5, 1, 0))
@@ -67,12 +68,22 @@
     return (at[1] + dy) & (NY - 1), (at[2] + dz) & (NZ - 1)
 
 
-def qkv_kernel(at_ref, inv_ref, own_row_ref, gain_ref, gain_other_ref, *rest):
+def columns(row):
+    return jnp.broadcast_to(row, (HD, row.shape[1])).T
+
+
+def qkv_kernel(at_ref, squares_ref, modality_ref, gain_ref, gain_other_ref, *rest):
     own_ws, other_ws, pieces = rest[:8], rest[8:16], rest[16:24]
-    out_ref, acc = rest[24:]
+    out_ref, acc, inv, own = rest[24:]
     step = pl.program_id(0)
-    inverse = inv_ref[...]
-    own_row = own_row_ref[...] > 0
+
+    @pl.when(step == 0)
+    def _():
+        inv[...] = columns(lax.rsqrt(squares_ref[...] / (2 * NY * NZ * HD) + EPS))
+        own[...] = columns((modality_ref[...] == at_ref[0]).astype(jnp.float32))
+
+    inverse = inv[...]
+    own_row = own[...] > 0
     normed, right = [], []
     for k, piece in enumerate(pieces):
         yi, zi = place(at_ref, k, step)
@@ -93,10 +104,12 @@
 
     @pl.when(step == pl.num_programs(0) - 1)
     def _():
-        out_ref[...] = jnp.where(own_row, acc[:, : 3 * HD], acc[:, 3 * HD :])
-
-
-def project(at, inverse, own_row, gain, gain_other, w, w_other, arrays):
+        for p in range(3):
+            low, high = acc[:, p * HD : (p + 1) * HD], acc[:, (3 + p) * HD : (4 + p) * HD]
+            out_ref[:, p * HD : (p + 1) * HD] = jnp.where(own_row, low, high)
+
+
+def project(at, squares, modality, gain, gain_other, w, w_other, arrays):
     rows = arrays[0].shape[1]
     block = (3, 1, 1, 1, HD, HD)
     whole = lambda shape: pl.BlockSpec(shape, lambda g, at: (0,) * len(shape))
@@ -109,19 +122,19 @@
         grid_spec=pltpu.PrefetchScalarGridSpec(
             num_scalar_prefetch=1,
             grid=(4,),
-            in_specs=[whole((rows, 1)), whole((rows, 1)), whole((NY, NZ, HD)), whole((NY, NZ, HD))]
+            in_specs=[whole((1, rows)), whole((1, rows)), whole((NY, NZ, HD)), whole((NY, NZ, HD))]
             + [weights(k, False) for k in range(8)]
             + [weights(k, True) for k in range(8)]
             + [piece] * 8,
             out_specs=whole((rows, 3 * HD)),
-            scratch_shapes=[pltpu.VMEM((rows, 6 * HD), jnp.float32)],
+            scratch_shapes=[pltpu.VMEM((rows, w), jnp.float32) for w in (6 * HD, HD, HD)],
         ),
         out_shape=jax.ShapeDtypeStruct((rows, 3 * HD), jnp.float32),
         compiler_params=pltpu.CompilerParams(vmem_limit_bytes=56 * 2**20),
         cost_estimate=pl.CostEstimate(
             flops=2 * rows * 4096 * 6 * HD, bytes_accessed=11 * 2**20, transcendentals=0
         ),
-    )(at, inverse, own_row, gain, gain_other, *[w] * 8, *[w_other] * 8, *arrays)
+    )(at, squares, modality, gain, gain_other, *[w] * 8, *[w_other] * 8, *arrays)
 
 
 def headnorm(x, gain_row):
@@ -174,77 +187,100 @@
     )(bases, queries, *keys)
 
 
-def out_kernel(own_row_ref, w0, w1, o0, o1, h0, h1, h2, h3, out_ref):
-    heads = jnp.concatenate([h0[...], h1[...], h2[...], h3[...]], axis=1)
-    own_row = own_row_ref[...] > 0
-    sections = []
-    for refs in ((w0, w1), (o0, o1)):
-        w = jnp.concatenate(
-            [jnp.concatenate([ref[x, y] for y in range(NY) for x in range(NX)], axis=0) for ref in refs], axis=1
-        )
-        sections.append(jnp.dot(heads, w, preferred_element_type=jnp.float32))
-    both = jnp.where(own_row, *sections).astype(jnp.bfloat16)
-    for i in range(2):
-        out_ref[i, :, :HD] = both[:, i * HD : (i + 1) * HD]
-        out_ref[i, :, HD:] = both[:, (2 + i) * HD : (3 + i) * HD]
-
-
-def out_part(own_row, w, w_other, heads):
-    rows = heads[0].shape[0]
+def out_kernel(at_ref, modality_ref, w0, w1, o0, o1, h0, h1, h2, h3, out_ref):
+    heads = jnp.concatenate([h[e] for h in (h0, h1, h2, h3) for e in range(2)], axis=1)
+    own_row = columns((modality_ref[...] == at_ref[0]).astype(jnp.float32)) > 0
+    for i, refs in enumerate(((w0, o0), (w1, o1))):
+        sections = []
+        for ref in refs:
+            w = jnp.concatenate(
+                [ref[x, y, e] for y in range(NY) for e in range(2) for x in range(NX)], axis=0
+            )
+            sections.append(jnp.dot(heads, w, preferred_element_type=jnp.float32))
+        out_ref[0, :, i * HD : (i + 1) * HD] = jnp.where(own_row, *sections).astype(jnp.bfloat16)
+
+
+def out_part(at, modality, w, w_other, heads):
+    rows = heads[0].shape[1]
     steps = NZ // 2
-    whole = lambda shape: pl.BlockSpec(shape, lambda g: (0,) * len(shape))
-    left = pl.BlockSpec((NX, NY, HD // NX, 2 * HD), lambda g: (0, 0, 0, g))
-    right = pl.BlockSpec((NX, NY, HD // NX, 2 * HD), lambda g: (0, 0, 0, steps + g))
+    whole = lambda shape: pl.BlockSpec(shape, lambda g, at: (0,) * len(shape))
+    left = pl.BlockSpec((NX, NY, 2, HD // NX, HD), lambda g, at: (0, 0, 0, 0, g))
+    right = pl.BlockSpec((NX, NY, 2, HD // NX, HD), lambda g, at: (0, 0, 0, 0, steps + g))
     return pl.pallas_call(
         out_kernel,
-        grid=(steps,),
-        in_specs=[whole((rows, 1)), left, right, left, right] + [whole((rows, HD))] * NY,
-        out_specs=pl.BlockSpec((2, rows, 2 * HD), lambda g: (g, 0, 0)),
-        out_shape=jax.ShapeDtypeStruct((NZ, rows, 2 * HD), jnp.bfloat16),
+        grid_spec=pltpu.PrefetchScalarGridSpec(
+            num_scalar_prefetch=1,
+            grid=(steps,),
+            in_specs=[whole((1, rows)), left, right, left, right] + [whole((2, rows, HD))] * NY,
+            out_specs=pl.BlockSpec((1, rows, 2 * HD), lambda g, at: (g, 0, 0)),
+        ),
+        out_shape=jax.ShapeDtypeStruct((steps, rows, 2 * HD), jnp.bfloat16),
         compiler_params=pltpu.CompilerParams(vmem_limit_bytes=56 * 2**20),
         cost_estimate=pl.CostEstimate(
             flops=8 * rows * NY * HD * NZ * HD, bytes_accessed=5 * 2**20, transcendentals=0
         ),
-    )(own_row, w, w, w_other, w_other, *heads)
-
-
-def spread_w_out(w_out, y, seq):
+    )(at, modality, w, w, w_other, w_other, *heads)
+
+
+def cut_kernel(at_ref, w_ref, keep_ref, send_ref):
+    odd = at_ref[2] & 1
+    for d in range(NY):
+        to_y = (at_ref[1] - d) & (NY - 1)
+        for c in range(2):
+            for zh in range(NZ // 2):
+                first = (c * NY + to_y) * NZ * HD + 2 * zh * HD
+                lanes = pl.ds((c * (NZ // 2) + zh) * HD, HD)
+                keep_ref[d, :, lanes] = w_ref[:, pl.ds(pl.multiple_of(first + odd * HD, HD), HD)]
+                send_ref[d, :, lanes] = w_ref[:, pl.ds(pl.multiple_of(first + (1 - odd) * HD, HD), HD)]
+
+
+def after(x, *others):
+    return lax.optimization_barrier((x, *others))[0]
+
+
+def spread_w_out(at, w_out, first, second, third):
     rows, width = HD // NX, NZ * HD
-
-    def pick(d):
-        column = ((y - d) & (NY - 1)) * width
-        cut = lambda first: lax.dynamic_slice(w_out[0], (seq * rows, first + column), (rows, width))
-        return jnp.concatenate([cut(0), cut(NY * width)], axis=1)
-
-    s1, s3, s2 = take(pick(1), dy=1), take(pick(3), dy=-1), take(pick(2), dy=2)
-    lines = jnp.stack([pick(0), s1, s2, s3])
+    piece = jax.ShapeDtypeStruct((NY, rows, width), jnp.bfloat16)
+    whole = pl.BlockSpec((NY, rows, width), lambda g, at: (0, 0, 0))
+    keep, send = pl.pallas_call(
+        cut_kernel,
+        grid_spec=pltpu.PrefetchScalarGridSpec(
+            num_scalar_prefetch=1,
+            grid=(1,),
+            in_specs=[pl.BlockSpec((rows, w_out.shape[1]), lambda g, at: (at[3], 0))],
+            out_specs=[whole, whole],
+        ),
+        out_shape=[piece, piece],
+        cost_estimate=pl.CostEstimate(flops=0, bytes_accessed=2**20, transcendentals=0),
+    )(at, after(w_out, *first))
+    both = after(jnp.stack([keep, take(send, dz="pair")], axis=1), second)
+    s1, s3, s2 = take(both[1], dy=1), take(both[3], dy=-1), take(both[2], dy=2)
+    lines = after(jnp.stack([both[0], s1, s2, s3]), third)
     return lax.all_gather(lines, "seq", axis=0)
 
 
 def shards(tokens, modality, norm_gain, w_qkv, qk_gain, w_out):
     row_count = tokens.shape[0]
     half = row_count // 2
-    c, y, z, seq = (lax.axis_index(a) for a in AXES)
-    own_row = (modality == c).astype(jnp.int32)[:, None]
-
-    arrays = gather(tokens)
-    w_cols = spread_w_out(w_out, y, seq)
+    c, y, zh, zl, seq = (lax.axis_index(a) for a in AXES)
+    z = 2 * zh + zl
+    at = jnp.stack([c, y, z, seq]).astype(jnp.int32)
+    modality = modality[None, :]
+
+    arrays, direct = gather(tokens)
+    w_cols = spread_w_out(at, w_out[0], direct, arrays[1], arrays[2])
+    w_cols_other = take(w_cols, dc=1)
 
     w = w_qkv[0].transpose(1, 0, 2).reshape(3, 2, NY, NZ, HD, HD)
     gains = norm_gain.reshape(2, NY, NZ, HD)
     gain_other = take(lax.dynamic_index_in_dim(gains, 1 - c, axis=0, keepdims=False), dc=1)
     gain = lax.dynamic_index_in_dim(gains, c, axis=0, keepdims=False)
-    w_send, gain_other = lax.optimization_barrier((lax.dynamic_slice_in_dim(w, 1 - c, 1, axis=1), gain_other))
-    w_other = take(w_send, dc=1)
+    w_other = take(lax.dynamic_slice_in_dim(after(w, direct[0]), 1 - c, 1, axis=1), dc=1)
 
     squared = [jnp.sum(jnp.square(a.astype(jnp.float32)), axis=(0, 2)) for a in arrays]
-    early, w_cols = lax.optimization_barrier((sum(squared[:6]), w_cols))
-    w_cols_other = take(w_cols, dc=1)
-    squares = early + squared[6] + squared[7]
+    squares = sum(squared)
     squares = squares + take(squares, dc=1)
-    inverse = lax.rsqrt(squares / (2 * NY * NZ * HD) + EPS)[:, None]
-    at = jnp.stack([c, y, z]).astype(jnp.int32)
-    parts = project(at, inverse, own_row, gain, gain_other, w, w_other, arrays)
+    parts = project(at, squares[None, :], modality, gain, gain_other, w, w_other, arrays)
     parts = parts.reshape(2, half, 3 * HD)
     mine = lax.dynamic_index_in_dim(parts, c, axis=0, keepdims=False)
     theirs = lax.dynamic_index_in_dim(parts, 1 - c, axis=0, keepdims=False)
@@ -267,10 +303,11 @@
     bases = jnp.stack([b + c * half for b in begin] + [b + (1 - c) * half for b in begin]).astype(jnp.int32)
     heads_out = attention(bases, queries, [got, sibling])
 
-    h1, h3, h2 = take(heads_out, dy=1), take(heads_out, dy=-1), take(heads_out, dy=2)
-    own_half = lax.dynamic_slice_in_dim(own_row, c * half, half, axis=0)
-    partial = out_part(own_half, w_cols, w_cols_other, [heads_out, h1, h2, h3])
-    spread = lax.all_to_all(partial, "z", 0, 0)
+    line = jnp.stack([heads_out, take(heads_out, dz="pair")])
+    h1, h3, h2 = take(line, dy=1), take(line, dy=-1), take(line, dy=2)
+    own_half = lax.dynamic_slice_in_dim(modality, c * half, half, axis=1)
+    partial = out_part(at, own_half, w_cols, w_cols_other, [line, h1, h2, h3])
+    spread = lax.all_to_all(partial, "zh", 0, 0)
     summed = jnp.sum(spread.astype(jnp.float32), axis=0).astype(jnp.bfloat16).reshape(half, 2, HD)
     keep = lax.dynamic_index_in_dim(summed, c, axis=1, keepdims=False)
     other = take(lax.dynamic_index_in_dim(summed, 1 - c, axis=1, keepdims=False), dc=1)
@@ -278,8 +315,8 @@
 
 
 def solution(mesh):
-    mesh = Mesh(mesh.devices.reshape(2, NY, NZ, NX), AXES)
-    tp = ("y", "z")
+    mesh = Mesh(mesh.devices.reshape(2, NY, NZ // 2, 2, NX), AXES)
+    tp = ("y", "zh", "zl")
     placed = (
         P("seq", ("mod", *tp)),
         P("seq"),

time: 175 us -> 178 us (1.017)
  blocking collectives: 30.3 us -> 17.5 us
  starting transfers between devices: 39.5 us -> 47.5 us
  waiting for transfers between devices: 44.7 us -> 50.2 us
  Pallas kernels: 17 us -> 20.8 us
  local copies, waits for them, and re-layouts: 15.9 us -> 12.7 us
    ppermute x16 -> x18, waiting for transfers between devices: 18.1 us -> 38 us  [take(): return lax.ppermute(x, AXES, pairs([(dc, dy, dz, dx)] * 2, wrap_x))]
    ppermute x10, waiting for transfers between devices: 26.5 us -> 12.1 us  [take_by_core(): lax.ppermute(x, AXES, pairs([m and (0, *m, 0) for m in (on_y, on_z)]))]
    all_to_all x1, blocking collectives: 30.3 us -> 17.5 us  [shards(): spread = lax.all_to_all(partial, 'zh', 0, 0)]
    ppermute x10, starting transfers between devices: 16.3 us -> 26.1 us  [take_by_core(): lax.ppermute(x, AXES, pairs([m and (0, *m, 0) for m in (on_y, on_z)]))]
    pallas_call x1 -> x2, Pallas kernels: 4.97 us -> 8.93 us  [the longest x1 6.3 us: out_part(): pl.pallas_call(out_kernel, grid_spec=pltpu.PrefetchScalarGridSpec(num_sca...]
    another operation x3 -> x4, other arithmetic: 1.52 us -> 3.5 us  [the longest x1 1.88 us: spread_w_out(): lines = after(jnp.stack([both[0], s1, s2, s3]), third)]
    dynamic_slice x3 -> x1, local copies, waits for them, and re-layouts: 5.93 us -> 4 us  [shards(): lax.dynamic_slice_in_dim(after(w, direct[0]), 1 - c, 1, axis=1)]
    ppermute x16 -> x18, starting transfers between devices: 23.2 us -> 21.4 us  [take(): return lax.ppermute(x, AXES, pairs([(dc, dy, dz, dx)] * 2, wrap_x))]
  transfers between devices with their start and end apart: 27 -> 29, of which waited for: 15 -> 17; matrix products, arithmetic and copies ran while one was open for 11% -> 10% of each run, Pallas kernels for 1% -> 8%
where the time goes in v4:
time: 178 us; the launch traced here: 177 us
  waiting for transfers between devices  50.2 us (28%)
  starting transfers between devices  47.5 us (27%)
  Pallas kernels  20.8 us (12%)
  blocking collectives  17.5 us (10%)
  other arithmetic  14.9 us (8%)
  between operations  13.7 us (8%)
  local copies, waits for them, and re-layouts  12.7 us (7%)
    ppermute x18, waiting for transfers between devices, take(): return lax.ppermute(x, AXES, pairs([(dc, dy, dz, dx)] * 2, wrap_x))  38 us
    ppermute x10, starting transfers between devices, take_by_core(): lax.ppermute(x, AXES, pairs([m and (0, *m, 0) for m in (on_y, on_z)]))  26.1 us
    ppermute x18, starting transfers between devices, take(): return lax.ppermute(x, AXES, pairs([(dc, dy, dz, dx)] * 2, wrap_x))  21.4 us
    all_to_all x1, blocking collectives, shards(): spread = lax.all_to_all(partial, 'zh', 0, 0)  17.5 us
    ppermute x10, waiting for transfers between devices, take_by_core(): lax.ppermute(x, AXES, pairs([m and (0, *m, 0) for m in (on_y, on_z)]))  12.1 us
    pallas_call x1, Pallas kernels, project(): pl.pallas_call(qkv_kernel, grid_spec=pltpu.PrefetchScalarGridSpec(num_sca...  10.2 us
    reduce_sum x8, other arithmetic, shards(): jnp.sum(jnp.square(a.astype(jnp.float32)), axis=(0, 2))  7.4 us
    pallas_call x1, Pallas kernels, out_part(): pl.pallas_call(out_kernel, grid_spec=pltpu.PrefetchScalarGridSpec(num_sca...  6.3 us
  transfers between devices with their start and end apart: 29, of which 17 were waited for; matrix products, arithmetic and copies ran while one was open for 10% of the time, Pallas kernels for 8%

profile of v4, /device:TPU:1, one launch (start us, length us, event | category | flops | bytes accessed | tf_op | source)
XLA Modules:
  0.0 177.4 jit_solution(15299803234973585584)
XLA Ops:
  6.5 6.8 %collective-permute-start = (bf16[512,128]{1,0:T(8,128)(2,1)}, bf16[512,128]{1,0:T(8,128)(2,1)S(1)}, u32[]{:S(2)}, u32[]{:S(2)}) collective-permute-start(bf16[512,128]{1,0:T(8,128)(2,1)} %param.6), channel_id=1, source_target_pairs={{32,0},{33,1},{34,2},{35,3},{36,4},{37,5},{38,6},{39,7},{40,8},{41... | collective-permute-start | bytes 393224 | tf_op jit(solution)/shard_map/ppermute | solution.py:42
  13.4 3.7 %collective-permute-done = bf16[512,128]{1,0:T(8,128)(2,1)S(1)} collective-permute-done((bf16[512,128]{1,0:T(8,128)(2,1)}, bf16[512,128]{1,0:T(8,128)(2,1)S(1)}, u32[]{:S(2)}, u32[]{:S(2)}) %collective-permute-start) | collective-permute-done | bytes 131104 | tf_op jit(solution)/shard_map/ppermute | solution.py:42
  17.1 4.0 %constant_dynamic-slice_fusion.2 = bf16[3,1,4,8,128,128]{5,4,3,2,1,0:T(8,128)(2,1)} fusion(bf16[3,2,4,8,128,128]{5,4,3,2,1,0:T(8,128)(2,1)} %bitcast.68, s32[]{:T(128)S(6)} %select_n.45), kind=kLoop, calls=%fused_computation.56 | loop fusion | bytes 6291460 | tf_op jit(solution)/shard_map/dynamic_slice | solution.py:278
  21.1 1.5 collective-permute-start.1
  22.5 4.5 %collective-permute-start.2 = (bf16[512,128]{1,0:T(8,128)(2,1)S(1)}, bf16[512,128]{1,0:T(8,128)(2,1)S(1)}, u32[]{:S(2)}, u32[]{:S(2)}) collective-permute-start(bf16[512,128]{1,0:T(8,128)(2,1)S(1)} %copy-done.8), channel_id=1, source_target_pairs={{64,0},{65,1},{66,2},{67,3},{68,4},{69,5},{70,6},{71,7},{72,8},{73... | collective-permute-start | bytes 393224 | tf_op jit(solution)/shard_map/ppermute | solution.py:42
  27.0 2.0 %collective-permute-done.1 = bf16[512,128]{1,0:T(8,128)(2,1)S(1)} collective-permute-done((bf16[512,128]{1,0:T(8,128)(2,1)S(1)}, bf16[512,128]{1,0:T(8,128)(2,1)S(1)}, u32[]{:S(2)}, u32[]{:S(2)}) %collective-permute-start.1) | collective-permute-done | bytes 131104 | tf_op jit(solution)/shard_map/ppermute | solution.py:42
  29.0 4.6 %collective-permute-done.2 = bf16[512,128]{1,0:T(8,128)(2,1)S(1)} collective-permute-done((bf16[512,128]{1,0:T(8,128)(2,1)S(1)}, bf16[512,128]{1,0:T(8,128)(2,1)S(1)}, u32[]{:S(2)}, u32[]{:S(2)}) %collective-permute-start.2) | collective-permute-done | bytes 131104 | tf_op jit(solution)/shard_map/ppermute | solution.py:42
  35.1 2.6 %shard_map.64 = (bf16[4,32,1024]{2,1,0:T(8,128)(2,1)}, bf16[4,32,1024]{2,1,0:T(8,128)(2,1)}) custom-call(s32[4]{0:T(128)} %pad_add_fusion.at_ref, bf16[128,8192]{1,0:T(8,128)(2,1)} %bitcast.82), custom_call_target="tpu_custom_call" | custom-call | bytes 1048576 | tf_op jit(solution)/shard_map/pallas_call | solution.py:245
  39.0 10.2 %collective-permute-done.3 = bf16[4,32,1024]{2,1,0:T(8,128)(2,1)S(1)} collective-permute-done((bf16[4,32,1024]{2,1,0:T(8,128)(2,1)}, bf16[4,32,1024]{2,1,0:T(8,128)(2,1)S(1)}, u32[]{:S(2)}, u32[]{:S(2)}) %collective-permute-start.3) | collective-permute-done | bytes 262176 | tf_op jit(solution)/shard_map/ppermute | solution.py:38
  50.2 4.7 %collective-permute-start.8 = (bf16[4,512,128]{2,1,0:T(8,128)(2,1)}, bf16[4,512,128]{2,1,0:T(8,128)(2,1)}, u32[]{:S(2)}, u32[]{:S(2)}) collective-permute-start(bf16[4,512,128]{2,1,0:T(8,128)(2,1)} %collective-permute-done.4.rest_17_), channel_id=1, source_target_pairs={{4,0},{5,1},{6,2},{7,3},{8,4},{9,5},{10,6},{11,7},{12,8},{13,9},{1... | collective-permute-start | bytes 1572872 | tf_op jit(solution)/shard_map/ppermute | solution.py:42
  55.0 1.4 collective-permute-start.12
  56.6 8.9 %collective-permute-done.5 = bf16[2,32,1024]{2,1,0:T(8,128)(2,1)S(1)} collective-permute-done((bf16[2,32,1024]{2,1,0:T(8,128)(2,1)S(1)}, bf16[2,32,1024]{2,1,0:T(8,128)(2,1)S(1)}, u32[]{:S(2)}, u32[]{:S(2)}) %collective-permute-start.5) | collective-permute-done | bytes 131104 | tf_op jit(solution)/shard_map/ppermute | solution.py:38
  66.1 3.1 %collective-permute-start.11 = (bf16[4,512,128]{2,1,0:T(8,128)(2,1)}, bf16[4,512,128]{2,1,0:T(8,128)(2,1)}, u32[]{:S(2)}, u32[]{:S(2)}) collective-permute-start(bf16[4,512,128]{2,1,0:T(8,128)(2,1)} %collective-permute-done.8.rest_18_), channel_id=1, source_target_pairs={{4,0},{5,1},{6,2},{7,3},{8,4},{9,5},{10,6},{11,7},{12,8},{13,9},{1... | collective-permute-start | bytes 1572872 | tf_op jit(solution)/shard_map/ppermute | solution.py:42
  69.2 2.4 %collective-permute-done.7 = bf16[2,32,1024]{2,1,0:T(8,128)(2,1)} collective-permute-done((bf16[2,32,1024]{2,1,0:T(8,128)(2,1)S(1)}, bf16[2,32,1024]{2,1,0:T(8,128)(2,1)}, u32[]{:S(2)}, u32[]{:S(2)}) %collective-permute-start.7) | collective-permute-done | bytes 131104 | tf_op jit(solution)/shard_map/ppermute | solution.py:38
  71.6 1.9 %pad_maximum_fusion.2 = bf16[4,2,32,1024]{3,2,1,0:T(8,128)(2,1)} fusion(bf16[1,2,32,1024]{3,2,1,0:T(8,128)(2,1)} %bitcast.17, bf16[1,2,32,1024]{3,2,1,0:T(8,128)(2,1)} %bitcast.15, bf16[1,2,32,1024]{3,2,1,0:T(8,128)(2,1)} %bitcast.88, bf16[1,2,32,1024]{3,2,1,0:T(8,128)(2,1)S(1)} %get-tuple-element.23), kind=kLoop, calls=%fused_computation.10 | loop fusion | flops 786432 | bytes 1048576 | tf_op jit(solution)/shard_map/stack | solution.py:258
  77.5 2.9 %collective-permute-start.13 = (bf16[4,512,128]{2,1,0:T(8,128)(2,1)}, bf16[4,512,128]{2,1,0:T(8,128)(2,1)S(1)}, u32[]{:S(2)}, u32[]{:S(2)}) collective-permute-start(bf16[4,512,128]{2,1,0:T(8,128)(2,1)} %collective-permute-done.11.rest_20_), channel_id=1, source_target_pairs={{4,0},{5,1},{6,2},{7,3},{8,4},{9,5},{10,6},{11,7},{12,8},{13,9},{1... | collective-permute-start | bytes 1572872 | tf_op jit(solution)/shard_map/ppermute | solution.py:42
  84.1 1.9 %collective-permute-done.14.rest_23_ = bf16[4,512,128]{2,1,0:T(8,128)(2,1)S(1)} collective-permute-done((bf16[4,512,128]{2,1,0:T(8,128)(2,1)}, bf16[4,512,128]{2,1,0:T(8,128)(2,1)S(1)}, u32[]{:S(2)}, u32[]{:S(2)}) %collective-permute-start.14) | collective-permute-done | bytes 524320 | tf_op jit(solution)/shard_map/ppermute | solution.py:42
  88.0 3.2 %collective-permute-start.15 = (f32[512]{0:T(512)S(1)}, f32[512]{0:T(512)S(1)}, u32[]{:S(2)}, u32[]{:S(2)}) collective-permute-start(f32[512]{0:T(512)S(1)} %add_add_fusion), channel_id=1, source_target_pairs={{128,0},{129,1},{130,2},{131,3},{132,4},{133,5},{134,6},{135,7},{1... | collective-permute-start | bytes 6152 | tf_op jit(solution)/shard_map/ppermute | solution.py:38
  94.2 10.2 %shard_map.65 = f32[512,384]{1,0:T(8,128)} custom-call(s32[4]{0:T(128)} %pad_add_fusion.at_ref, f32[1,512]{1,0:T(1,128)} %bitcast.98, s32[1,512]{1,0:T(1,128)} %bitcast.99, f32[4,8,128]{2,1,0:T(8,128)} %get-tuple-element.35.gain_ref, f32[4,8,128]{2,1,0:T(8,128)} %copy-done.10, bf16[3,2,4,8,128,128]{5,4,3,2,1,0:T(8,128)(2,1)} %bitcast.69, ...), custom_call_target="tpu_custom_call" | custom-call | flops 3221225472 | bytes 11534336 | tf_op jit(solution)/shard_map/pallas_call | solution.py:120
  106.0 1.4 collective-permute-done.18
  110.2 3.1 %collective-permute-start.19 = (bf16[2,256,128]{2,1,0:T(8,128)(2,1)S(1)}, bf16[2,256,128]{2,1,0:T(8,128)(2,1)S(1)}, u32[]{:S(2)}, u32[]{:S(2)}) collective-permute-start(bf16[2,256,128]{2,1,0:T(8,128)(2,1)S(1)} %pad_maximum_fusion.4), channel_id=1, source_target_pairs={{0,1},{1,2},{2,3},{4,5},{5,6},{6,7},{8,9},{9,10},{10,11},{12,13},{... | collective-permute-start | bytes 393224 | tf_op jit(solution)/shard_map/ppermute | solution.py:38
  113.3 4.4 %collective-permute-start.20 = (bf16[2,256,128]{2,1,0:T(8,128)(2,1)S(1)}, bf16[2,256,128]{2,1,0:T(8,128)(2,1)S(1)}, u32[]{:S(2)}, u32[]{:S(2)}) collective-permute-start(bf16[2,256,128]{2,1,0:T(8,128)(2,1)S(1)} %pad_maximum_fusion.4), channel_id=1, source_target_pairs={{0,2},{1,3},{4,6},{5,7},{8,10},{9,11},{12,14},{13,15},{16,18},{17,... | collective-permute-start | bytes 393224 | tf_op jit(solution)/shard_map/ppermute | solution.py:38
  121.5 1.4 collective-permute-start.22
  123.0 1.4 collective-permute-done.22.rest_1_
  124.4 1.7 shard_map.66
  126.7 2.6 %collective-permute-done.23 = bf16[256,128]{1,0:T(8,128)(2,1)S(1)} collective-permute-done((bf16[256,128]{1,0:T(8,128)(2,1)S(1)}, bf16[256,128]{1,0:T(8,128)(2,1)S(1)}, u32[]{:S(2)}, u32[]{:S(2)}) %collective-permute-start.23) | collective-permute-done | bytes 65568 | tf_op jit(solution)/shard_map/ppermute | solution.py:38
  129.3 1.5 collective-permute-start.24
  133.2 3.1 %collective-permute-done.25.h2 = bf16[2,256,128]{2,1,0:T(8,128)(2,1)S(1)} collective-permute-done((bf16[2,256,128]{2,1,0:T(8,128)(2,1)S(1)}, bf16[2,256,128]{2,1,0:T(8,128)(2,1)S(1)}, u32[]{:S(2)}, u32[]{:S(2)}) %collective-permute-start.25) | collective-permute-done | bytes 131104 | tf_op jit(solution)/shard_map/ppermute | solution.py:38
  136.2 3.2 %collective-permute-done.26.h3 = bf16[2,256,128]{2,1,0:T(8,128)(2,1)S(1)} collective-permute-done((bf16[2,256,128]{2,1,0:T(8,128)(2,1)S(1)}, bf16[2,256,128]{2,1,0:T(8,128)(2,1)S(1)}, u32[]{:S(2)}, u32[]{:S(2)}) %collective-permute-start.26) | collective-permute-done | bytes 131104 | tf_op jit(solution)/shard_map/ppermute | solution.py:38
  140.8 6.3 %shard_map.67 = bf16[4,256,256]{2,1,0:T(8,128)(2,1)} custom-call(s32[4]{0:T(128)} %pad_add_fusion.at_ref, s32[1,256]{1,0:T(1,128)} %bitcast.100, bf16[4,4,2,32,1024]{4,3,2,1,0:T(8,128)(2,1)} %bitcast.78, bf16[4,4,2,32,1024]{4,3,2,1,0:T(8,128)(2,1)} %bitcast.79, bf16[4,4,2,32,1024]{4,3,2,1,0:T(8,128)(2,1)} %copy-done.1, ...), custom_call_target="tpu_custom_call" | custom-call | flops 1073741824 | bytes 5242880 | tf_op jit(solution)/shard_map/pallas_call | solution.py:209
  147.1 17.5 %all_to_all.5 = bf16[4,256,256]{2,1,0:T(8,128)(2,1)S(1)} all-to-all(bf16[4,256,256]{2,1,0:T(8,128)(2,1)} %shard_map.67), channel_id=1, replica_groups=mesh['mod'=2,'y'=4,'zh'=4,'zl'=2,'seq'=4] {'zh'}, dimensions={0} | all-to-all | bytes 1048576 | tf_op jit(solution)/shard_map/all_to_all | solution.py:310
  164.9 4.0 %collective-permute-start.27 = (bf16[256,128]{1,0:T(8,128)(2,1)S(1)}, bf16[256,128]{1,0:T(8,128)(2,1)S(1)}, u32[]{:S(2)}, u32[]{:S(2)}) collective-permute-start(bf16[256,128]{1,0:T(8,128)(2,1)S(1)} %bitcast.95), channel_id=1, source_target_pairs={{128,0},{129,1},{130,2},{131,3},{132,4},{133,5},{134,6},{135,7},{1... | collective-permute-start | bytes 196616 | tf_op jit(solution)/shard_map/ppermute | solution.py:38
  (101 shorter events, 31.7 us)
Async XLA Ops:
  6.5 102.3 %all-gather.3.cloned.1.call-start = ((), (), s32[]{:S(2)}) async-start(), calls=%async_computation.1 | async-start | bytes 2621440 | tf_op jit(solution)/shard_map/all_gather | solution.py:259
  6.5 10.5 %collective-permute-start = (bf16[512,128]{1,0:T(8,128)(2,1)}, bf16[512,128]{1,0:T(8,128)(2,1)S(1)}, u32[]{:S(2)}, u32[]{:S(2)}) collective-permute-start(bf16[512,128]{1,0:T(8,128)(2,1)} %param.6), channel_id=1, source_target_pairs={{32,0},{33,1},{34,2},{35,3},{36,4},{37,5},{38,6},{39,7},{40,8},{41... | collective-permute-start | bytes 393224 | tf_op jit(solution)/shard_map/ppermute | solution.py:42
  21.1 71.5 %collective-permute-start.17 = (bf16[3,1,4,8,128,128]{5,4,3,2,1,0:T(8,128)(2,1)}, bf16[3,1,4,8,128,128]{5,4,3,2,1,0:T(8,128)(2,1)S(1)}, u32[]{:S(2)}, u32[]{:S(2)}) collective-permute-start(bf16[3,1,4,8,128,128]{5,4,3,2,1,0:T(8,128)(2,1)} %constant_dynamic-slice_fusion.2), channel_id=1, source_target_pairs={{128,0},{129,1},{130,2},{131,3},{132,4},{133,5},{134,6},{135,7},{1... | collective-permute-start | bytes 9437192 | tf_op jit(solution)/shard_map/ppermute | solution.py:38
  21.1 7.9 %collective-permute-start.1 = (bf16[512,128]{1,0:T(8,128)(2,1)S(1)}, bf16[512,128]{1,0:T(8,128)(2,1)S(1)}, u32[]{:S(2)}, u32[]{:S(2)}) collective-permute-start(bf16[512,128]{1,0:T(8,128)(2,1)S(1)} %copy-done.8), channel_id=1, source_target_pairs={{96,0},{97,1},{98,2},{99,3},{100,4},{101,5},{102,6},{103,7},{104,8... | collective-permute-start | bytes 393224 | tf_op jit(solution)/shard_map/ppermute | solution.py:42
  22.5 11.0 %collective-permute-start.2 = (bf16[512,128]{1,0:T(8,128)(2,1)S(1)}, bf16[512,128]{1,0:T(8,128)(2,1)S(1)}, u32[]{:S(2)}, u32[]{:S(2)}) collective-permute-start(bf16[512,128]{1,0:T(8,128)(2,1)S(1)} %copy-done.8), channel_id=1, source_target_pairs={{64,0},{65,1},{66,2},{67,3},{68,4},{69,5},{70,6},{71,7},{72,8},{73... | collective-permute-start | bytes 393224 | tf_op jit(solution)/shard_map/ppermute | solution.py:42
  34.5 15.7 %collective-permute-start.4 = (bf16[4,512,128]{2,1,0:T(8,128)(2,1)}, bf16[4,512,128]{2,1,0:T(8,128)(2,1)}, u32[]{:S(2)}, u32[]{:S(2)}) collective-permute-start(bf16[4,512,128]{2,1,0:T(8,128)(2,1)} %get-tuple-element.22.rest_16_), channel_id=1, source_target_pairs={{4,0},{5,1},{6,2},{7,3},{8,4},{9,5},{10,6},{11,7},{12,8},{13,9},{1... | collective-permute-start | bytes 1572872 | tf_op jit(solution)/shard_map/ppermute | solution.py:42
  37.7 11.4 %collective-permute-start.3 = (bf16[4,32,1024]{2,1,0:T(8,128)(2,1)}, bf16[4,32,1024]{2,1,0:T(8,128)(2,1)S(1)}, u32[]{:S(2)}, u32[]{:S(2)}) collective-permute-start(bf16[4,32,1024]{2,1,0:T(8,128)(2,1)} %get-tuple-element.13), channel_id=1, source_target_pairs={{4,0},{5,1},{6,2},{7,3},{0,4},{1,5},{2,6},{3,7},{12,8},{13,9},{14,... | collective-permute-start | bytes 786440 | tf_op jit(solution)/shard_map/ppermute | solution.py:38
  38.0 17.0 %collective-permute-start.10 = (bf16[4,512,128]{2,1,0:T(8,128)(2,1)}, bf16[4,512,128]{2,1,0:T(8,128)(2,1)}, u32[]{:S(2)}, u32[]{:S(2)}) collective-permute-start(bf16[4,512,128]{2,1,0:T(8,128)(2,1)} %get-tuple-element.22.rest_16_), channel_id=1, source_target_pairs={{28,0},{29,1},{30,2},{31,3},{0,4},{1,5},{2,6},{3,7},{4,8},{5,9},{6... | collective-permute-start | bytes 1572872 | tf_op jit(solution)/shard_map/ppermute | solution.py:42
  50.2 15.9 %collective-permute-start.8 = (bf16[4,512,128]{2,1,0:T(8,128)(2,1)}, bf16[4,512,128]{2,1,0:T(8,128)(2,1)}, u32[]{:S(2)}, u32[]{:S(2)}) collective-permute-start(bf16[4,512,128]{2,1,0:T(8,128)(2,1)} %collective-permute-done.4.rest_17_), channel_id=1, source_target_pairs={{4,0},{5,1},{6,2},{7,3},{8,4},{9,5},{10,6},{11,7},{12,8},{13,9},{1... | collective-permute-start | bytes 1572872 | tf_op jit(solution)/shard_map/ppermute | solution.py:42
  54.9 10.5 %collective-permute-start.5 = (bf16[2,32,1024]{2,1,0:T(8,128)(2,1)S(1)}, bf16[2,32,1024]{2,1,0:T(8,128)(2,1)S(1)}, u32[]{:S(2)}, u32[]{:S(2)}) collective-permute-start(bf16[2,32,1024]{2,1,0:T(8,128)(2,1)S(1)} %get-tuple-element.25), channel_id=1, source_target_pairs={{32,0},{33,1},{34,2},{35,3},{36,4},{37,5},{38,6},{39,7},{40,8},{41... | collective-permute-start | bytes 393224 | tf_op jit(solution)/shard_map/ppermute | solution.py:38
  55.0 21.1 %collective-permute-start.12 = (bf16[4,512,128]{2,1,0:T(8,128)(2,1)}, bf16[4,512,128]{2,1,0:T(8,128)(2,1)}, u32[]{:S(2)}, u32[]{:S(2)}) collective-permute-start(bf16[4,512,128]{2,1,0:T(8,128)(2,1)} %collective-permute-done.10.rest_19_), channel_id=1, source_target_pairs={{28,0},{29,1},{30,2},{31,3},{0,4},{1,5},{2,6},{3,7},{4,8},{5,9},{6... | collective-permute-start | bytes 1572872 | tf_op jit(solution)/shard_map/ppermute | solution.py:42
  56.5 12.7 %collective-permute-start.6 = (bf16[2,32,1024]{2,1,0:T(8,128)(2,1)S(1)}, bf16[2,32,1024]{2,1,0:T(8,128)(2,1)}, u32[]{:S(2)}, u32[]{:S(2)}) collective-permute-start(bf16[2,32,1024]{2,1,0:T(8,128)(2,1)S(1)} %get-tuple-element.24), channel_id=1, source_target_pairs={{64,0},{65,1},{66,2},{67,3},{68,4},{69,5},{70,6},{71,7},{72,8},{73... | collective-permute-start | bytes 393224 | tf_op jit(solution)/shard_map/ppermute | solution.py:38
  66.1 5.6 %collective-permute-start.7 = (bf16[2,32,1024]{2,1,0:T(8,128)(2,1)S(1)}, bf16[2,32,1024]{2,1,0:T(8,128)(2,1)}, u32[]{:S(2)}, u32[]{:S(2)}) collective-permute-start(bf16[2,32,1024]{2,1,0:T(8,128)(2,1)S(1)} %slice_bitcast_fusion.2), channel_id=1, source_target_pairs={{96,0},{97,1},{98,2},{99,3},{100,4},{101,5},{102,6},{103,7},{104,8... | collective-permute-start | bytes 393224 | tf_op jit(solution)/shard_map/ppermute | solution.py:38
  66.1 11.4 %collective-permute-start.11 = (bf16[4,512,128]{2,1,0:T(8,128)(2,1)}, bf16[4,512,128]{2,1,0:T(8,128)(2,1)}, u32[]{:S(2)}, u32[]{:S(2)}) collective-permute-start(bf16[4,512,128]{2,1,0:T(8,128)(2,1)} %collective-permute-done.8.rest_18_), channel_id=1, source_target_pairs={{4,0},{5,1},{6,2},{7,3},{8,4},{9,5},{10,6},{11,7},{12,8},{13,9},{1... | collective-permute-start | bytes 1572872 | tf_op jit(solution)/shard_map/ppermute | solution.py:42
  74.9 17.7 %collective-permute-start.16 = (f32[4,8,128]{2,1,0:T(8,128)S(1)}, f32[4,8,128]{2,1,0:T(8,128)S(1)}, u32[]{:S(2)}, u32[]{:S(2)}) collective-permute-start(f32[4,8,128]{2,1,0:T(8,128)S(1)} %get-tuple-element.34), channel_id=1, source_target_pairs={{128,0},{129,1},{130,2},{131,3},{132,4},{133,5},{134,6},{135,7},{1... | collective-permute-start | bytes 49160 | tf_op jit(solution)/shard_map/ppermute | solution.py:38
  76.1 9.8 %collective-permute-start.14 = (bf16[4,512,128]{2,1,0:T(8,128)(2,1)}, bf16[4,512,128]{2,1,0:T(8,128)(2,1)S(1)}, u32[]{:S(2)}, u32[]{:S(2)}) collective-permute-start(bf16[4,512,128]{2,1,0:T(8,128)(2,1)} %collective-permute-done.12.rest_21_), channel_id=1, source_target_pairs={{28,0},{29,1},{30,2},{31,3},{0,4},{1,5},{2,6},{3,7},{4,8},{5,9},{6... | collective-permute-start | bytes 1572872 | tf_op jit(solution)/shard_map/ppermute | solution.py:42
  77.5 9.5 %collective-permute-start.13 = (bf16[4,512,128]{2,1,0:T(8,128)(2,1)}, bf16[4,512,128]{2,1,0:T(8,128)(2,1)S(1)}, u32[]{:S(2)}, u32[]{:S(2)}) collective-permute-start(bf16[4,512,128]{2,1,0:T(8,128)(2,1)} %collective-permute-done.11.rest_20_), channel_id=1, source_target_pairs={{4,0},{5,1},{6,2},{7,3},{8,4},{9,5},{10,6},{11,7},{12,8},{13,9},{1... | collective-permute-start | bytes 1572872 | tf_op jit(solution)/shard_map/ppermute | solution.py:42
  88.0 4.0 %collective-permute-start.15 = (f32[512]{0:T(512)S(1)}, f32[512]{0:T(512)S(1)}, u32[]{:S(2)}, u32[]{:S(2)}) collective-permute-start(f32[512]{0:T(512)S(1)} %add_add_fusion), channel_id=1, source_target_pairs={{128,0},{129,1},{130,2},{131,3},{132,4},{133,5},{134,6},{135,7},{1... | collective-permute-start | bytes 6152 | tf_op jit(solution)/shard_map/ppermute | solution.py:38
  94.2 11.7 %copy-start.12 = (f32[2,128]{1,0:T(2,128)S(1)}, f32[2,128]{1,0:T(2,128)}, u32[]{:S(2)}) copy-start(f32[2,128]{1,0:T(2,128)} %param.10) | copy-start | bytes 3076
  105.5 1.8 %collective-permute-start.18 = (f32[256,384]{1,0:T(8,128)S(1)}, f32[256,384]{1,0:T(8,128)S(1)}, u32[]{:S(2)}, u32[]{:S(2)}) collective-permute-start(f32[256,384]{1,0:T(8,128)S(1)} %dynamic-slice_bitcast_fusion), channel_id=1, source_target_pairs={{128,0},{129,1},{130,2},{131,3},{132,4},{133,5},{134,6},{135,7},{1... | collective-permute-start | bytes 1179656 | tf_op jit(solution)/shard_map/ppermute | solution.py:38
  106.0 25.5 %copy-start.11 = (s32[512]{0:T(512)S(1)}, s32[512]{0:T(512)}, u32[]{:S(2)}) copy-start(s32[512]{0:T(512)} %param.7) | copy-start | bytes 6148
  108.8 30.6 %collective-permute-start.9 = (bf16[4,4,2,32,1024]{4,3,2,1,0:T(8,128)(2,1)}, bf16[4,4,2,32,1024]{4,3,2,1,0:T(8,128)(2,1)S(1)}, u32[]{:S(2)}, u32[]{:S(2)}) collective-permute-start(bf16[4,4,2,32,1024]{4,3,2,1,0:T(8,128)(2,1)} %bitcast.77), channel_id=1, source_target_pairs={{128,0},{129,1},{130,2},{131,3},{132,4},{133,5},{134,6},{135,7},{1... | collective-permute-start | bytes 6291464 | tf_op jit(solution)/shard_map/ppermute | solution.py:38
  110.2 8.9 %collective-permute-start.19 = (bf16[2,256,128]{2,1,0:T(8,128)(2,1)S(1)}, bf16[2,256,128]{2,1,0:T(8,128)(2,1)S(1)}, u32[]{:S(2)}, u32[]{:S(2)}) collective-permute-start(bf16[2,256,128]{2,1,0:T(8,128)(2,1)S(1)} %pad_maximum_fusion.4), channel_id=1, source_target_pairs={{0,1},{1,2},{2,3},{4,5},{5,6},{6,7},{8,9},{9,10},{10,11},{12,13},{... | collective-permute-start | bytes 393224 | tf_op jit(solution)/shard_map/ppermute | solution.py:38
  113.3 6.8 %collective-permute-start.20 = (bf16[2,256,128]{2,1,0:T(8,128)(2,1)S(1)}, bf16[2,256,128]{2,1,0:T(8,128)(2,1)S(1)}, u32[]{:S(2)}, u32[]{:S(2)}) collective-permute-start(bf16[2,256,128]{2,1,0:T(8,128)(2,1)S(1)} %pad_maximum_fusion.4), channel_id=1, source_target_pairs={{0,2},{1,3},{4,6},{5,7},{8,10},{9,11},{12,14},{13,15},{16,18},{17,... | collective-permute-start | bytes 393224 | tf_op jit(solution)/shard_map/ppermute | solution.py:38
  117.7 3.7 %collective-permute-start.21 = (bf16[2,256,128]{2,1,0:T(8,128)(2,1)S(1)}, bf16[2,256,128]{2,1,0:T(8,128)(2,1)S(1)}, u32[]{:S(2)}, u32[]{:S(2)}) collective-permute-start(bf16[2,256,128]{2,1,0:T(8,128)(2,1)S(1)} %pad_maximum_fusion.4), channel_id=1, source_target_pairs={{0,3},{4,7},{8,11},{12,15},{16,19},{20,23},{24,27},{28,31},{32,35}... | collective-permute-start | bytes 393224 | tf_op jit(solution)/shard_map/ppermute | solution.py:38
  121.5 2.9 %collective-permute-start.22 = (bf16[4,2,256,128]{3,2,1,0:T(8,128)(2,1)S(1)}, bf16[4,2,256,128]{3,2,1,0:T(8,128)(2,1)S(1)}, u32[]{:S(2)}, u32[]{:S(2)}) collective-permute-start(bf16[4,2,256,128]{3,2,1,0:T(8,128)(2,1)S(1)} %pad_maximum_fusion.3.rest_0_), channel_id=1, source_target_pairs={{128,0},{129,1},{130,2},{131,3},{132,4},{133,5},{134,6},{135,7},{1... | collective-permute-start | bytes 1572872 | tf_op jit(solution)/shard_map/ppermute | solution.py:38
  126.0 3.2 %collective-permute-start.23 = (bf16[256,128]{1,0:T(8,128)(2,1)S(1)}, bf16[256,128]{1,0:T(8,128)(2,1)S(1)}, u32[]{:S(2)}, u32[]{:S(2)}) collective-permute-start(bf16[256,128]{1,0:T(8,128)(2,1)S(1)} %shard_map.66), channel_id=1, source_target_pairs={{4,0},{5,1},{6,2},{7,3},{0,4},{1,5},{2,6},{3,7},{12,8},{13,9},{14,... | collective-permute-start | bytes 196616 | tf_op jit(solution)/shard_map/ppermute | solution.py:38
  129.3 10.2 %copy-start.4 = (bf16[2,256,128]{2,1,0:T(8,128)(2,1)}, bf16[2,256,128]{2,1,0:T(8,128)(2,1)S(1)}, u32[]{:S(2)}) copy-start(bf16[2,256,128]{2,1,0:T(8,128)(2,1)S(1)} %pad_maximum_fusion.5.h0) | copy-start | bytes 393220
  129.3 3.9 %collective-permute-start.24 = (bf16[2,256,128]{2,1,0:T(8,128)(2,1)S(1)}, bf16[2,256,128]{2,1,0:T(8,128)(2,1)S(1)}, u32[]{:S(2)}, u32[]{:S(2)}) collective-permute-start(bf16[2,256,128]{2,1,0:T(8,128)(2,1)S(1)} %pad_maximum_fusion.5.h0), channel_id=1, source_target_pairs={{32,0},{33,1},{34,2},{35,3},{36,4},{37,5},{38,6},{39,7},{40,8},{41... | collective-permute-start | bytes 393224 | tf_op jit(solution)/shard_map/ppermute | solution.py:38
  130.8 5.4 %collective-permute-start.25 = (bf16[2,256,128]{2,1,0:T(8,128)(2,1)S(1)}, bf16[2,256,128]{2,1,0:T(8,128)(2,1)S(1)}, u32[]{:S(2)}, u32[]{:S(2)}) collective-permute-start(bf16[2,256,128]{2,1,0:T(8,128)(2,1)S(1)} %pad_maximum_fusion.5.h0), channel_id=1, source_target_pairs={{64,0},{65,1},{66,2},{67,3},{68,4},{69,5},{70,6},{71,7},{72,8},{73... | collective-permute-start | bytes 393224 | tf_op jit(solution)/shard_map/ppermute | solution.py:38
  130.8 8.6 %collective-permute-start.26 = (bf16[2,256,128]{2,1,0:T(8,128)(2,1)S(1)}, bf16[2,256,128]{2,1,0:T(8,128)(2,1)S(1)}, u32[]{:S(2)}, u32[]{:S(2)}) collective-permute-start(bf16[2,256,128]{2,1,0:T(8,128)(2,1)S(1)} %pad_maximum_fusion.5.h0), channel_id=1, source_target_pairs={{96,0},{97,1},{98,2},{99,3},{100,4},{101,5},{102,6},{103,7},{104,8... | collective-permute-start | bytes 393224 | tf_op jit(solution)/shard_map/ppermute | solution.py:38
  164.9 4.9 %collective-permute-start.27 = (bf16[256,128]{1,0:T(8,128)(2,1)S(1)}, bf16[256,128]{1,0:T(8,128)(2,1)S(1)}, u32[]{:S(2)}, u32[]{:S(2)}) collective-permute-start(bf16[256,128]{1,0:T(8,128)(2,1)S(1)} %bitcast.95), channel_id=1, source_target_pairs={{128,0},{129,1},{130,2},{131,3},{132,4},{133,5},{134,6},{135,7},{1... | collective-permute-start | bytes 196616 | tf_op jit(solution)/shard_map/ppermute | solution.py:38
  (10 other events, 20.0 us)
Sparse Core Ops, SparseCore 0:
  73.7 31.3 all-gather.2

commit v5 on v4

--- a/solution.py
+++ b/solution.py
@@ -74,7 +74,7 @@
 
 def qkv_kernel(at_ref, squares_ref, modality_ref, gain_ref, gain_other_ref, *rest):
     own_ws, other_ws, pieces = rest[:8], rest[8:16], rest[16:24]
-    out_ref, acc, inv, own = rest[24:]
+    mine_ref, theirs_ref, acc, inv, own = rest[24:]
     step = pl.program_id(0)
 
     @pl.when(step == 0)
@@ -104,9 +104,13 @@
 
     @pl.when(step == pl.num_programs(0) - 1)
     def _():
-        for p in range(3):
-            low, high = acc[:, p * HD : (p + 1) * HD], acc[:, (3 + p) * HD : (4 + p) * HD]
-            out_ref[:, p * HD : (p + 1) * HD] = jnp.where(own_row, low, high)
+        half = acc.shape[0] // 2
+        for ref, first in ((mine_ref, at_ref[0] * half), (theirs_ref, (1 - at_ref[0]) * half)):
+            rows = pl.ds(pl.multiple_of(first, half), half)
+            own_here = own[rows, :] > 0
+            for p in range(3):
+                low, high = acc[rows, p * HD : (p + 1) * HD], acc[rows, (3 + p) * HD : (4 + p) * HD]
+                ref[:, p * HD : (p + 1) * HD] = jnp.where(own_here, low, high)
 
 
 def project(at, squares, modality, gain, gain_other, w, w_other, arrays):
@@ -126,10 +130,10 @@
             + [weights(k, False) for k in range(8)]
             + [weights(k, True) for k in range(8)]
             + [piece] * 8,
-            out_specs=whole((rows, 3 * HD)),
+            out_specs=[whole((rows // 2, 3 * HD))] * 2,
             scratch_shapes=[pltpu.VMEM((rows, w), jnp.float32) for w in (6 * HD, HD, HD)],
         ),
-        out_shape=jax.ShapeDtypeStruct((rows, 3 * HD), jnp.float32),
+        out_shape=[jax.ShapeDtypeStruct((rows // 2, 3 * HD), jnp.float32)] * 2,
         compiler_params=pltpu.CompilerParams(vmem_limit_bytes=56 * 2**20),
         cost_estimate=pl.CostEstimate(
             flops=2 * rows * 4096 * 6 * HD, bytes_accessed=11 * 2**20, transcendentals=0
@@ -137,16 +141,66 @@
     )(at, squares, modality, gain, gain_other, *[w] * 8, *[w_other] * 8, *arrays)
 
 
-def headnorm(x, gain_row):
-    average = jnp.mean(x, axis=1, keepdims=True)
-    centred = x - average
-    variance = jnp.mean(centred * centred, axis=1, keepdims=True)
-    return centred * lax.rsqrt(variance + EPS) * gain_row[None, :]
-
-
-def rotate(x, cosines, sines):
-    lower, upper = x[:, : HD // 2], x[:, HD // 2 :]
-    return jnp.concatenate([lower * cosines - upper * sines, upper * cosines + lower * sines], axis=1)
+def squares_kernel(x_ref, y_ref, early_ref, out_ref, acc):
+    step = pl.program_id(0)
+    both = jnp.square(x_ref[0].astype(jnp.float32)) + jnp.square(y_ref[0].astype(jnp.float32))
+
+    @pl.when(step == 0)
+    def _():
+        acc[...] = both
+
+    @pl.when(step > 0)
+    def _():
+        acc[...] += both
+
+    @pl.when(step == pl.num_programs(0) - 1)
+    def _():
+        out_ref[...] = early_ref[...] + jnp.sum(acc[...].T, axis=0, keepdims=True)
+
+
+def last_squares(x, y, early):
+    rows = x.shape[1]
+    piece = pl.BlockSpec((1, rows, HD), lambda g: (g, 0, 0))
+    row = pl.BlockSpec((1, rows), lambda g: (0, 0))
+    return pl.pallas_call(
+        squares_kernel,
+        grid=(x.shape[0],),
+        in_specs=[piece, piece, row],
+        out_specs=row,
+        scratch_shapes=[pltpu.VMEM((rows, HD), jnp.float32)],
+        out_shape=jax.ShapeDtypeStruct((1, rows), jnp.float32),
+        compiler_params=pltpu.CompilerParams(vmem_limit_bytes=56 * 2**20),
+    )(x, y, early)
+
+
+def finish_kernel(mine_ref, got_ref, gain_ref, cos_ref, sin_ref, q_ref, kv_ref):
+    projected = mine_ref[...] + got_ref[...]
+    half = HD // 2
+    turned = []
+    for p in range(2):
+        x = projected[:, p * HD : (p + 1) * HD]
+        centred = x - jnp.mean(x, axis=1, keepdims=True)
+        variance = jnp.mean(centred * centred, axis=1, keepdims=True)
+        x = centred * lax.rsqrt(variance + EPS) * gain_ref[p : p + 1, :]
+        swapped = jnp.concatenate([x[:, half:], x[:, :half]], axis=1)
+        turned.append((x * cos_ref[...] + swapped * sin_ref[...]).astype(jnp.bfloat16))
+    q_ref[...] = turned[0]
+    kv_ref[0] = turned[1]
+    kv_ref[1] = projected[:, 2 * HD :].astype(jnp.bfloat16)
+
+
+def finish(mine, got, qk_gain, cosines, sines):
+    rows = mine.shape[0]
+    vmem = pl.BlockSpec(memory_space=pltpu.VMEM)
+    return pl.pallas_call(
+        finish_kernel,
+        in_specs=[vmem] * 5,
+        out_specs=[vmem] * 2,
+        out_shape=[
+            jax.ShapeDtypeStruct((rows, HD), jnp.bfloat16),
+            jax.ShapeDtypeStruct((2, rows, HD), jnp.bfloat16),
+        ],
+    )(mine, got, qk_gain, cosines, sines)
 
 
 def attention_kernel(base_ref, q_ref, *rest):
@@ -187,31 +241,29 @@
     )(bases, queries, *keys)
 
 
-def out_kernel(at_ref, modality_ref, w0, w1, o0, o1, h0, h1, h2, h3, out_ref):
-    heads = jnp.concatenate([h[e] for h in (h0, h1, h2, h3) for e in range(2)], axis=1)
+def out_kernel(at_ref, modality_ref, w_ref, other_ref, heads_ref, out_ref):
+    heads = jnp.concatenate([heads_ref[i] for i in range(2 * NY)], axis=1)
     own_row = columns((modality_ref[...] == at_ref[0]).astype(jnp.float32)) > 0
-    for i, refs in enumerate(((w0, o0), (w1, o1))):
-        sections = []
-        for ref in refs:
-            w = jnp.concatenate(
-                [ref[x, y, e] for y in range(NY) for e in range(2) for x in range(NX)], axis=0
-            )
-            sections.append(jnp.dot(heads, w, preferred_element_type=jnp.float32))
-        out_ref[0, :, i * HD : (i + 1) * HD] = jnp.where(own_row, *sections).astype(jnp.bfloat16)
+    sections = []
+    for ref in (w_ref, other_ref):
+        w = jnp.concatenate([ref[x, i, 0] for i in range(2 * NY) for x in range(NX)], axis=0)
+        sections.append(jnp.dot(heads, w, preferred_element_type=jnp.float32))
+    for i in range(2):
+        lanes = slice(i * HD, (i + 1) * HD)
+        out_ref[0, :, lanes] = jnp.where(own_row, sections[0][:, lanes], sections[1][:, lanes]).astype(jnp.bfloat16)
 
 
 def out_part(at, modality, w, w_other, heads):
-    rows = heads[0].shape[1]
+    rows = heads.shape[1]
     steps = NZ // 2
     whole = lambda shape: pl.BlockSpec(shape, lambda g, at: (0,) * len(shape))
-    left = pl.BlockSpec((NX, NY, 2, HD // NX, HD), lambda g, at: (0, 0, 0, 0, g))
-    right = pl.BlockSpec((NX, NY, 2, HD // NX, HD), lambda g, at: (0, 0, 0, 0, steps + g))
+    weights = pl.BlockSpec((NX, 2 * NY, 1, HD // NX, 2 * HD), lambda g, at: (0, 0, g, 0, 0))
     return pl.pallas_call(
         out_kernel,
         grid_spec=pltpu.PrefetchScalarGridSpec(
             num_scalar_prefetch=1,
             grid=(steps,),
-            in_specs=[whole((1, rows)), left, right, left, right] + [whole((2, rows, HD))] * NY,
+            in_specs=[whole((1, rows)), weights, weights, whole(heads.shape)],
             out_specs=pl.BlockSpec((1, rows, 2 * HD), lambda g, at: (g, 0, 0)),
         ),
         out_shape=jax.ShapeDtypeStruct((steps, rows, 2 * HD), jnp.bfloat16),
@@ -219,43 +271,33 @@
         cost_estimate=pl.CostEstimate(
             flops=8 * rows * NY * HD * NZ * HD, bytes_accessed=5 * 2**20, transcendentals=0
         ),
-    )(at, modality, w, w, w_other, w_other, *heads)
-
-
-def cut_kernel(at_ref, w_ref, keep_ref, send_ref):
-    odd = at_ref[2] & 1
-    for d in range(NY):
-        to_y = (at_ref[1] - d) & (NY - 1)
-        for c in range(2):
+    )(at, modality, w, w_other, heads)
+
+
+def cut_kernel(at_ref, w_ref, out_ref):
+    for y in range(NY):
+        for odd in range(2):
             for zh in range(NZ // 2):
-                first = (c * NY + to_y) * NZ * HD + 2 * zh * HD
-                lanes = pl.ds((c * (NZ // 2) + zh) * HD, HD)
-                keep_ref[d, :, lanes] = w_ref[:, pl.ds(pl.multiple_of(first + odd * HD, HD), HD)]
-                send_ref[d, :, lanes] = w_ref[:, pl.ds(pl.multiple_of(first + (1 - odd) * HD, HD), HD)]
-
-
-def after(x, *others):
-    return lax.optimization_barrier((x, *others))[0]
-
-
-def spread_w_out(at, w_out, first, second, third):
-    rows, width = HD // NX, NZ * HD
-    piece = jax.ShapeDtypeStruct((NY, rows, width), jnp.bfloat16)
-    whole = pl.BlockSpec((NY, rows, width), lambda g, at: (0, 0, 0))
-    keep, send = pl.pallas_call(
+                for c in range(2):
+                    first = ((c * NY + y) * NZ + 2 * zh + odd) * HD
+                    out_ref[2 * y + odd, zh, :, c * HD : (c + 1) * HD] = w_ref[:, first : first + HD]
+
+
+def spread_w_out(at, w_out):
+    rows = HD // NX
+    shape = (2 * NY, NZ // 2, rows, 2 * HD)
+    pieces = pl.pallas_call(
         cut_kernel,
         grid_spec=pltpu.PrefetchScalarGridSpec(
             num_scalar_prefetch=1,
             grid=(1,),
             in_specs=[pl.BlockSpec((rows, w_out.shape[1]), lambda g, at: (at[3], 0))],
-            out_specs=[whole, whole],
-        ),
-        out_shape=[piece, piece],
+            out_specs=pl.BlockSpec(shape, lambda g, at: (0,) * 4),
+        ),
+        out_shape=jax.ShapeDtypeStruct(shape, jnp.bfloat16),
         cost_estimate=pl.CostEstimate(flops=0, bytes_accessed=2**20, transcendentals=0),
-    )(at, after(w_out, *first))
-    both = after(jnp.stack([keep, take(send, dz="pair")], axis=1), second)
-    s1, s3, s2 = take(both[1], dy=1), take(both[3], dy=-1), take(both[2], dy=2)
-    lines = after(jnp.stack([both[0], s1, s2, s3]), third)
+    )(at, w_out)
+    lines = lax.all_to_all(pieces, ("y", "zl"), 0, 0)
     return lax.all_gather(lines, "seq", axis=0)
 
 
@@ -267,46 +309,41 @@
     at = jnp.stack([c, y, z, seq]).astype(jnp.int32)
     modality = modality[None, :]
 
+    w_cols = spread_w_out(at, w_out[0])
     arrays, direct = gather(tokens)
-    w_cols = spread_w_out(at, w_out[0], direct, arrays[1], arrays[2])
     w_cols_other = take(w_cols, dc=1)
-
-    w = w_qkv[0].transpose(1, 0, 2).reshape(3, 2, NY, NZ, HD, HD)
-    gains = norm_gain.reshape(2, NY, NZ, HD)
-    gain_other = take(lax.dynamic_index_in_dim(gains, 1 - c, axis=0, keepdims=False), dc=1)
-    gain = lax.dynamic_index_in_dim(gains, c, axis=0, keepdims=False)
-    w_other = take(lax.dynamic_slice_in_dim(after(w, direct[0]), 1 - c, 1, axis=1), dc=1)
-
-    squared = [jnp.sum(jnp.square(a.astype(jnp.float32)), axis=(0, 2)) for a in arrays]
-    squares = sum(squared)
-    squares = squares + take(squares, dc=1)
-    parts = project(at, squares[None, :], modality, gain, gain_other, w, w_other, arrays)
-    parts = parts.reshape(2, half, 3 * HD)
-    mine = lax.dynamic_index_in_dim(parts, c, axis=0, keepdims=False)
-    theirs = lax.dynamic_index_in_dim(parts, 1 - c, axis=0, keepdims=False)
-    projected = mine + take(theirs, dc=1)
 
     first = seq * row_count + c * half
     places = first + jnp.arange(half, dtype=jnp.int32)
     rates = 1.0 / 10000.0 ** (jnp.arange(HD // 2, dtype=jnp.float32) * (2.0 / HD))
     angles = places.astype(jnp.float32)[:, None] * rates[None, :]
     cosines, sines = jnp.cos(angles), jnp.sin(angles)
-    queries = rotate(headnorm(projected[:, :HD], qk_gain[0]), cosines, sines).astype(jnp.bfloat16)
-    keys = rotate(headnorm(projected[:, HD : 2 * HD], qk_gain[1]), cosines, sines).astype(jnp.bfloat16)
-    values = projected[:, 2 * HD :].astype(jnp.bfloat16)
-
-    own_keys = jnp.stack([keys, values])
-    got = jnp.stack([own_keys] + [take(own_keys, dx=-d, wrap_x=False) for d in (1, 2, 3)])
+    cosines, sines = jnp.concatenate([cosines, cosines], axis=1), jnp.concatenate([-sines, sines], axis=1)
+
+    w = w_qkv[0].transpose(1, 0, 2).reshape(3, 2, NY, NZ, HD, HD)
+    w_other = take(lax.dynamic_slice_in_dim(w, 1 - c, 1, axis=1), dc=1)
+    gains = norm_gain.reshape(2, NY * NZ * HD)
+    gain_send = lax.dynamic_slice_in_dim(gains, 1 - c, 1, axis=0)
+    gain = lax.dynamic_slice_in_dim(gains, c, 1, axis=0).reshape(NY, NZ, HD)
+
+    early = sum(jnp.sum(jnp.square(a.astype(jnp.float32)), axis=(0, 2)) for a in arrays[:6])
+    squares = last_squares(arrays[6], arrays[7], early[None, :])
+    got = take(jnp.concatenate([squares, gain_send], axis=1), dc=1)
+    squares, gain_other = squares + got[:, :row_count], got[:, row_count:].reshape(NY, NZ, HD)
+    mine, theirs = project(at, squares, modality, gain, gain_other, w, w_other, arrays)
+    queries, own_keys = finish(mine, take(theirs, dc=1), qk_gain, cosines, sines)
+
+    moved = {d: take(own_keys, dx=-d, wrap_x=False) for d in (2, 3, 1)}
+    got = jnp.stack([own_keys] + [moved[d] for d in (1, 2, 3)])
     sibling = take(got, dc=1)
     never = 1 << 20
     begin = [jnp.where(seq >= d, (seq - d) * row_count, never) for d in range(NX)]
     bases = jnp.stack([b + c * half for b in begin] + [b + (1 - c) * half for b in begin]).astype(jnp.int32)
     heads_out = attention(bases, queries, [got, sibling])
 
-    line = jnp.stack([heads_out, take(heads_out, dz="pair")])
-    h1, h3, h2 = take(line, dy=1), take(line, dy=-1), take(line, dy=2)
+    heads = lax.all_to_all(jnp.broadcast_to(heads_out[None], (2 * NY, half, HD)), ("y", "zl"), 0, 0)
     own_half = lax.dynamic_slice_in_dim(modality, c * half, half, axis=1)
-    partial = out_part(at, own_half, w_cols, w_cols_other, [line, h1, h2, h3])
+    partial = out_part(at, own_half, w_cols, w_cols_other, heads)
     spread = lax.all_to_all(partial, "zh", 0, 0)
     summed = jnp.sum(spread.astype(jnp.float32), axis=0).astype(jnp.bfloat16).reshape(half, 2, HD)
     keep = lax.dynamic_index_in_dim(summed, c, axis=1, keepdims=False)

time: 178 us -> 169 us (0.949)
  waiting for transfers between devices: 50.2 us -> 39.2 us
  Pallas kernels: 20.8 us -> 25.1 us
  other arithmetic: 14.9 us -> 11.9 us
    ppermute x18 -> x9, waiting for transfers between devices: 38 us -> 5.62 us  [take(): return lax.ppermute(x, AXES, pairs([(dc, dy, dz, dx)] * 2, wrap_x))]
    ppermute x10, waiting for transfers between devices: 12.1 us -> 24.7 us  [take_by_core(): lax.ppermute(x, AXES, pairs([m and (0, *m, 0) for m in (on_y, on_z)]))]
    all_to_all x0 -> x2, starting transfers between devices: none -> 9.87 us  [the longest x1 6.37 us: spread_w_out(): lines = lax.all_to_all(pieces, ('y', 'zl'), 0, 0)]
    all_to_all x0 -> x2, waiting for transfers between devices: none -> 8.83 us  [the longest x1 8.83 us: shards(): lax.all_to_all(jnp.broadcast_to(heads_out[None], (2 * NY, half, HD)), ('y...]
    ppermute x10, starting transfers between devices: 26.1 us -> 19.7 us  [take_by_core(): lax.ppermute(x, AXES, pairs([m and (0, *m, 0) for m in (on_y, on_z)]))]
    pallas_call x0 -> x2, Pallas kernels: none -> 5.27 us  [the longest x1 2.97 us: last_squares(): pl.pallas_call(squares_kernel, grid=(x.shape[0],), in_specs=[piece, piece...]
    ppermute x18 -> x9, starting transfers between devices: 21.4 us -> 17.8 us  [take(): return lax.ppermute(x, AXES, pairs([(dc, dy, dz, dx)] * 2, wrap_x))]
    reduce_sum x8 -> x6, other arithmetic: 7.4 us -> 4.95 us  [shards(): jnp.sum(jnp.square(a.astype(jnp.float32)), axis=(0, 2))]
  transfers between devices with their start and end apart: 29 -> 22, of which waited for: 17 -> 15; matrix products, arithmetic and copies ran while one was open for 10% -> 11% of each run, Pallas kernels for 8% -> 10%
where the time goes in v5:
time: 169 us; the launch traced here: 168 us
  starting transfers between devices  47.4 us (28%)
  waiting for transfers between devices  39.2 us (23%)
  Pallas kernels  25.1 us (15%)
  blocking collectives  17.8 us (11%)
  between operations  13.6 us (8%)
  local copies, waits for them, and re-layouts  13.3 us (8%)
  other arithmetic  11.9 us (7%)
    ppermute x10, waiting for transfers between devices, take_by_core(): lax.ppermute(x, AXES, pairs([m and (0, *m, 0) for m in (on_y, on_z)]))  24.7 us
    ppermute x10, starting transfers between devices, take_by_core(): lax.ppermute(x, AXES, pairs([m and (0, *m, 0) for m in (on_y, on_z)]))  19.7 us
    all_to_all x1, blocking collectives, shards(): spread = lax.all_to_all(partial, 'zh', 0, 0)  17.8 us
    ppermute x9, starting transfers between devices, take(): return lax.ppermute(x, AXES, pairs([(dc, dy, dz, dx)] * 2, wrap_x))  17.8 us
    pallas_call x1, Pallas kernels, project(): pl.pallas_call(qkv_kernel, grid_spec=pltpu.PrefetchScalarGridSpec(num_sca...  10.1 us
    all_to_all x1, waiting for transfers between devices, shards(): lax.all_to_all(jnp.broadcast_to(heads_out[None], (2 * NY, half, HD)), ('y...  8.83 us
    all_to_all x1, starting transfers between devices, spread_w_out(): lines = lax.all_to_all(pieces, ('y', 'zl'), 0, 0)  6.37 us
    unnamed x25, local copies, waits for them, and re-layouts  6.1 us
  transfers between devices with their start and end apart: 22, of which 15 were waited for; matrix products, arithmetic and copies ran while one was open for 11% of the time, Pallas kernels for 10%

profile of v5, /device:TPU:1, one launch (start us, length us, event | category | flops | bytes accessed | tf_op | source)
XLA Modules:
  0.0 168.3 jit_solution(5429375253584439782)
XLA Ops:
  7.2 2.6 %shard_map.64 = bf16[8,4,32,256]{3,2,1,0:T(8,128)(2,1)} custom-call(s32[4]{0:T(128)} %pad_add_fusion.at_ref, bf16[128,8192]{1,0:T(8,128)(2,1)} %bitcast.44), custom_call_target="tpu_custom_call" | custom-call | bytes 1048576 | tf_op jit(solution)/shard_map/pallas_call | solution.py:289
  9.8 6.4 %all-to-all-start = ((bf16[8,4,32,256]{3,2,1,0:T(8,128)(2,1)}), bf16[8,4,32,256]{3,2,1,0:T(8,128)(2,1)}, u32[]{:S(2)}, u32[]{:S(2)}) async-start(bf16[8,4,32,256]{3,2,1,0:T(8,128)(2,1)} %shard_map.64), calls=%async_computation | async-start | bytes 1048576 | tf_op jit(solution)/shard_map/all_to_all | solution.py:300
  16.2 5.2 %collective-permute-start.1 = (bf16[512,128]{1,0:T(8,128)(2,1)S(1)}, bf16[512,128]{1,0:T(8,128)(2,1)S(1)}, u32[]{:S(2)}, u32[]{:S(2)}) collective-permute-start(bf16[512,128]{1,0:T(8,128)(2,1)S(1)} %copy-done.9), channel_id=1, source_target_pairs={{32,0},{33,1},{34,2},{35,3},{36,4},{37,5},{38,6},{39,7},{40,8},{41... | collective-permute-start | bytes 393224 | tf_op jit(solution)/shard_map/ppermute | solution.py:42
  21.4 3.3 %collective-permute-start.3 = (bf16[512,128]{1,0:T(8,128)(2,1)S(1)}, bf16[512,128]{1,0:T(8,128)(2,1)S(1)}, u32[]{:S(2)}, u32[]{:S(2)}) collective-permute-start(bf16[512,128]{1,0:T(8,128)(2,1)S(1)} %copy-done.9), channel_id=1, source_target_pairs={{64,0},{65,1},{66,2},{67,3},{68,4},{69,5},{70,6},{71,7},{72,8},{73... | collective-permute-start | bytes 393224 | tf_op jit(solution)/shard_map/ppermute | solution.py:42
  24.7 6.2 %collective-permute-done.2 = bf16[512,128]{1,0:T(8,128)(2,1)S(1)} collective-permute-done((bf16[512,128]{1,0:T(8,128)(2,1)S(1)}, bf16[512,128]{1,0:T(8,128)(2,1)S(1)}, u32[]{:S(2)}, u32[]{:S(2)}) %collective-permute-start.2) | collective-permute-done | bytes 131104 | tf_op jit(solution)/shard_map/ppermute | solution.py:42
  30.8 2.8 %collective-permute-done.3 = bf16[512,128]{1,0:T(8,128)(2,1)S(1)} collective-permute-done((bf16[512,128]{1,0:T(8,128)(2,1)S(1)}, bf16[512,128]{1,0:T(8,128)(2,1)S(1)}, u32[]{:S(2)}, u32[]{:S(2)}) %collective-permute-start.3) | collective-permute-done | bytes 131104 | tf_op jit(solution)/shard_map/ppermute | solution.py:42
  35.5 4.0 %constant_dynamic-slice_fusion.2 = bf16[3,1,4,8,128,128]{5,4,3,2,1,0:T(8,128)(2,1)} fusion(bf16[3,2,4,8,128,128]{5,4,3,2,1,0:T(8,128)(2,1)} %bitcast.35, s32[]{:T(128)S(6)} %select_n.40), kind=kLoop, calls=%fused_computation.19 | loop fusion | bytes 6291460 | tf_op jit(solution)/shard_map/dynamic_slice | solution.py:324
  40.8 3.3 %collective-permute-done.4.rest_17_ = bf16[4,512,128]{2,1,0:T(8,128)(2,1)} collective-permute-done((bf16[4,512,128]{2,1,0:T(8,128)(2,1)}, bf16[4,512,128]{2,1,0:T(8,128)(2,1)}, u32[]{:S(2)}, u32[]{:S(2)}) %collective-permute-start.4) | collective-permute-done | bytes 524320 | tf_op jit(solution)/shard_map/ppermute | solution.py:42
  44.1 2.6 %collective-permute-start.5 = (bf16[4,512,128]{2,1,0:T(8,128)(2,1)}, bf16[4,512,128]{2,1,0:T(8,128)(2,1)}, u32[]{:S(2)}, u32[]{:S(2)}) collective-permute-start(bf16[4,512,128]{2,1,0:T(8,128)(2,1)} %collective-permute-done.4.rest_17_), channel_id=1, source_target_pairs={{4,0},{5,1},{6,2},{7,3},{8,4},{9,5},{10,6},{11,7},{12,8},{13,9},{1... | collective-permute-start | bytes 1572872 | tf_op jit(solution)/shard_map/ppermute | solution.py:42
  48.0 1.6 collective-permute-done.8.rest_19_
  49.7 3.5 %collective-permute-done.5.rest_18_ = bf16[4,512,128]{2,1,0:T(8,128)(2,1)} collective-permute-done((bf16[4,512,128]{2,1,0:T(8,128)(2,1)}, bf16[4,512,128]{2,1,0:T(8,128)(2,1)}, u32[]{:S(2)}, u32[]{:S(2)}) %collective-permute-start.5) | collective-permute-done | bytes 524320 | tf_op jit(solution)/shard_map/ppermute | solution.py:42
  53.2 3.1 %collective-permute-start.6 = (bf16[4,512,128]{2,1,0:T(8,128)(2,1)}, bf16[4,512,128]{2,1,0:T(8,128)(2,1)S(1)}, u32[]{:S(2)}, u32[]{:S(2)}) collective-permute-start(bf16[4,512,128]{2,1,0:T(8,128)(2,1)} %collective-permute-done.5.rest_18_), channel_id=1, source_target_pairs={{4,0},{5,1},{6,2},{7,3},{8,4},{9,5},{10,6},{11,7},{12,8},{13,9},{1... | collective-permute-start | bytes 1572872 | tf_op jit(solution)/shard_map/ppermute | solution.py:42
  59.5 3.2 %collective-permute-done.6.rest_20_ = bf16[4,512,128]{2,1,0:T(8,128)(2,1)S(1)} collective-permute-done((bf16[4,512,128]{2,1,0:T(8,128)(2,1)}, bf16[4,512,128]{2,1,0:T(8,128)(2,1)S(1)}, u32[]{:S(2)}, u32[]{:S(2)}) %collective-permute-start.6) | collective-permute-done | bytes 524320 | tf_op jit(solution)/shard_map/ppermute | solution.py:42
  62.7 3.4 %collective-permute-start.7 = (bf16[4,512,128]{2,1,0:T(8,128)(2,1)S(1)}, bf16[4,512,128]{2,1,0:T(8,128)(2,1)S(1)}, u32[]{:S(2)}, u32[]{:S(2)}) collective-permute-start(bf16[4,512,128]{2,1,0:T(8,128)(2,1)S(1)} %collective-permute-done.6.rest_20_), channel_id=1, source_target_pairs={{4,0},{5,1},{6,2},{7,3},{8,4},{9,5},{10,6},{11,7},{12,8},{13,9},{1... | collective-permute-start | bytes 1572872 | tf_op jit(solution)/shard_map/ppermute | solution.py:42
  69.2 3.1 %collective-permute-done.7.x_ref.rest_22_ = bf16[4,512,128]{2,1,0:T(8,128)(2,1)S(1)} collective-permute-done((bf16[4,512,128]{2,1,0:T(8,128)(2,1)S(1)}, bf16[4,512,128]{2,1,0:T(8,128)(2,1)S(1)}, u32[]{:S(2)}, u32[]{:S(2)}) %collective-permute-start.7) | collective-permute-done | bytes 524320 | tf_op jit(solution)/shard_map/ppermute | solution.py:42
  73.1 3.0 %shard_map.65 = f32[1,512]{1,0:T(1,128)} custom-call(bf16[4,512,128]{2,1,0:T(8,128)(2,1)} %copy-done.5, bf16[4,512,128]{2,1,0:T(8,128)(2,1)} %copy-done.4, f32[1,512]{1,0:T(1,128)} %bitcast.60), custom_call_target="tpu_custom_call" | custom-call | tf_op jit(solution)/shard_map/pallas_call | solution.py:165
  76.8 2.5 %collective-permute-start.11 = (f32[1,4608]{1,0:T(1,128)S(1)}, f32[1,4608]{1,0:T(1,128)S(1)}, u32[]{:S(2)}, u32[]{:S(2)}) collective-permute-start(f32[1,4608]{1,0:T(1,128)S(1)} %pad_maximum_fusion.4), channel_id=1, source_target_pairs={{128,0},{129,1},{130,2},{131,3},{132,4},{133,5},{134,6},{135,7},{1... | collective-permute-start | bytes 55304 | tf_op jit(solution)/shard_map/ppermute | solution.py:38
  81.9 1.6 copy-done.1
  83.5 10.1 %shard_map.66 = (f32[256,384]{1,0:T(8,128)}, f32[256,384]{1,0:T(8,128)}) custom-call(s32[4]{0:T(128)} %pad_add_fusion.at_ref, f32[1,512]{1,0:T(1,128)} %slice_add_fusion.squares_ref, s32[1,512]{1,0:T(1,128)} %bitcast.61, f32[4,8,128]{2,1,0:T(8,128)} %bitcast.59, f32[4,8,128]{2,1,0:T(8,128)} %bitcast.58, bf16[3,2,4,8,128,128]{5,4,3,2,1,0:T(8,128)(2,1)} %bitcast.36, ...), custom_call_target="tpu_custom_call" | custom-call | flops 3221225472 | bytes 11534336 | tf_op jit(solution)/shard_map/pallas_call | solution.py:124
  96.4 2.3 %shard_map.67 = (bf16[256,128]{1,0:T(8,128)(2,1)}, bf16[2,256,128]{2,1,0:T(8,128)(2,1)}) custom-call(f32[256,384]{1,0:T(8,128)} %get-tuple-element.9.mine_ref, f32[256,384]{1,0:T(8,128)} %copy-done.8, f32[2,128]{1,0:T(2,128)} %gain_ref.1, f32[256,128]{1,0:T(8,128)} %get-tuple-element.22.cos_ref, f32[256,128]{1,0:T(8,128)} %get-tuple-element.23.sin_ref), custom_call_target="tpu_custom_call" | custom-call | tf_op jit(solution)/shard_map/pallas_call | solution.py:195
  98.7 3.1 %collective-permute-start.14 = (bf16[2,256,128]{2,1,0:T(8,128)(2,1)}, bf16[2,256,128]{2,1,0:T(8,128)(2,1)S(1)}, u32[]{:S(2)}, u32[]{:S(2)}) collective-permute-start(bf16[2,256,128]{2,1,0:T(8,128)(2,1)} %get-tuple-element.12), channel_id=1, source_target_pairs={{0,1},{1,2},{2,3},{4,5},{5,6},{6,7},{8,9},{9,10},{10,11},{12,13},{... | collective-permute-start | bytes 393224 | tf_op jit(solution)/shard_map/ppermute | solution.py:38
  101.8 4.4 %collective-permute-start.15 = (bf16[2,256,128]{2,1,0:T(8,128)(2,1)}, bf16[2,256,128]{2,1,0:T(8,128)(2,1)S(1)}, u32[]{:S(2)}, u32[]{:S(2)}) collective-permute-start(bf16[2,256,128]{2,1,0:T(8,128)(2,1)} %get-tuple-element.12), channel_id=1, source_target_pairs={{0,2},{1,3},{4,6},{5,7},{8,10},{9,11},{12,14},{13,15},{16,18},{17,... | collective-permute-start | bytes 393224 | tf_op jit(solution)/shard_map/ppermute | solution.py:38
  106.2 1.3 collective-permute-start.16
  108.7 1.3 collective-permute-done.16
  111.0 1.6 collective-permute-start.17
  112.6 1.5 collective-permute-done.17.rest_1_
  114.9 1.7 shard_map.68
  117.5 3.5 %all-to-all-start.1 = ((bf16[8,256,128]{2,1,0:T(8,128)(2,1)}), bf16[8,256,128]{2,1,0:T(8,128)(2,1)S(1)}, u32[]{:S(2)}, u32[]{:S(2)}) async-start(bf16[8,256,128]{2,1,0:T(8,128)(2,1)} %broadcast_in_dim.5), calls=%async_computation.1 | async-start | bytes 1048576 | tf_op jit(solution)/shard_map/all_to_all | solution.py:344
  121.6 8.8 %all-to-all-done.1.heads_ref = bf16[8,256,128]{2,1,0:T(8,128)(2,1)S(1)} async-done(((bf16[8,256,128]{2,1,0:T(8,128)(2,1)}), bf16[8,256,128]{2,1,0:T(8,128)(2,1)S(1)}, u32[]{:S(2)}, u32[]{:S(2)}) %all-to-all-start.1) | async-done | bytes 524320 | tf_op jit(solution)/shard_map/all_to_all | solution.py:344
  132.0 5.5 %shard_map.69 = bf16[4,256,256]{2,1,0:T(8,128)(2,1)} custom-call(s32[4]{0:T(128)} %pad_add_fusion.at_ref, s32[1,256]{1,0:T(1,128)} %bitcast.62, bf16[4,8,4,32,256]{4,3,2,1,0:T(8,128)(2,1)} %bitcast.46, bf16[4,8,4,32,256]{4,3,2,1,0:T(8,128)(2,1)} %copy-done.7, bf16[8,256,128]{2,1,0:T(8,128)(2,1)} %copy-done.6), custom_call_target="tpu_custom_call" | custom-call | flops 1073741824 | bytes 5242880 | tf_op jit(solution)/shard_map/pallas_call | solution.py:261
  137.5 17.8 %all_to_all.15 = bf16[4,256,256]{2,1,0:T(8,128)(2,1)S(1)} all-to-all(bf16[4,256,256]{2,1,0:T(8,128)(2,1)} %shard_map.69), channel_id=1, replica_groups=mesh['mod'=2,'y'=4,'zh'=4,'zl'=2,'seq'=4] {'zh'}, dimensions={0} | all-to-all | bytes 1048576 | tf_op jit(solution)/shard_map/all_to_all | solution.py:347
  155.6 4.2 %collective-permute-start.18 = (bf16[256,128]{1,0:T(8,128)(2,1)S(1)}, bf16[256,128]{1,0:T(8,128)(2,1)S(1)}, u32[]{:S(2)}, u32[]{:S(2)}) collective-permute-start(bf16[256,128]{1,0:T(8,128)(2,1)S(1)} %bitcast.57), channel_id=1, source_target_pairs={{128,0},{129,1},{130,2},{131,3},{132,4},{133,5},{134,6},{135,7},{1... | collective-permute-start | bytes 196616 | tf_op jit(solution)/shard_map/ppermute | solution.py:38
  (74 shorter events, 26.4 us)
Async XLA Ops:
  6.5 9.7 %copy-start.9 = (bf16[512,128]{1,0:T(8,128)(2,1)S(1)}, bf16[512,128]{1,0:T(8,128)(2,1)}, u32[]{:S(2)}) copy-start(bf16[512,128]{1,0:T(8,128)(2,1)} %param.6) | copy-start | bytes 393220
  9.8 29.9 %all-to-all-start = ((bf16[8,4,32,256]{3,2,1,0:T(8,128)(2,1)}), bf16[8,4,32,256]{3,2,1,0:T(8,128)(2,1)}, u32[]{:S(2)}, u32[]{:S(2)}) async-start(bf16[8,4,32,256]{3,2,1,0:T(8,128)(2,1)} %shard_map.64), calls=%async_computation | async-start | bytes 1048576 | tf_op jit(solution)/shard_map/all_to_all | solution.py:300
  16.1 77.9 %all-gather.3.cloned.1.call-start = ((), (), s32[]{:S(2)}) async-start(), calls=%async_computation.3 | async-start | bytes 2621440 | tf_op jit(solution)/shard_map/all_gather | solution.py:301
  16.2 8.5 %collective-permute-start.1 = (bf16[512,128]{1,0:T(8,128)(2,1)S(1)}, bf16[512,128]{1,0:T(8,128)(2,1)S(1)}, u32[]{:S(2)}, u32[]{:S(2)}) collective-permute-start(bf16[512,128]{1,0:T(8,128)(2,1)S(1)} %copy-done.9), channel_id=1, source_target_pairs={{32,0},{33,1},{34,2},{35,3},{36,4},{37,5},{38,6},{39,7},{40,8},{41... | collective-permute-start | bytes 393224 | tf_op jit(solution)/shard_map/ppermute | solution.py:42
  21.4 9.4 %collective-permute-start.2 = (bf16[512,128]{1,0:T(8,128)(2,1)S(1)}, bf16[512,128]{1,0:T(8,128)(2,1)S(1)}, u32[]{:S(2)}, u32[]{:S(2)}) collective-permute-start(bf16[512,128]{1,0:T(8,128)(2,1)S(1)} %copy-done.9), channel_id=1, source_target_pairs={{96,0},{97,1},{98,2},{99,3},{100,4},{101,5},{102,6},{103,7},{104,8... | collective-permute-start | bytes 393224 | tf_op jit(solution)/shard_map/ppermute | solution.py:42
  21.4 12.2 %collective-permute-start.3 = (bf16[512,128]{1,0:T(8,128)(2,1)S(1)}, bf16[512,128]{1,0:T(8,128)(2,1)S(1)}, u32[]{:S(2)}, u32[]{:S(2)}) collective-permute-start(bf16[512,128]{1,0:T(8,128)(2,1)S(1)} %copy-done.9), channel_id=1, source_target_pairs={{64,0},{65,1},{66,2},{67,3},{68,4},{69,5},{70,6},{71,7},{72,8},{73... | collective-permute-start | bytes 393224 | tf_op jit(solution)/shard_map/ppermute | solution.py:42
  34.6 9.6 %collective-permute-start.4 = (bf16[4,512,128]{2,1,0:T(8,128)(2,1)}, bf16[4,512,128]{2,1,0:T(8,128)(2,1)}, u32[]{:S(2)}, u32[]{:S(2)}) collective-permute-start(bf16[4,512,128]{2,1,0:T(8,128)(2,1)} %get-tuple-element.14.rest_16_), channel_id=1, source_target_pairs={{4,0},{5,1},{6,2},{7,3},{8,4},{9,5},{10,6},{11,7},{12,8},{13,9},{1... | collective-permute-start | bytes 1572872 | tf_op jit(solution)/shard_map/ppermute | solution.py:42
  35.5 11.7 %copy-start.10 = (f32[1,8192]{1,0:T(1,128)S(1)}, f32[1,8192]{1,0:T(1,128)}, u32[]{:S(2)}) copy-start(f32[1,8192]{1,0:T(1,128)} %param.8) | copy-start | bytes 98308
  39.5 42.4 %collective-permute-start.12 = (bf16[3,1,4,8,128,128]{5,4,3,2,1,0:T(8,128)(2,1)}, bf16[3,1,4,8,128,128]{5,4,3,2,1,0:T(8,128)(2,1)S(1)}, u32[]{:S(2)}, u32[]{:S(2)}) collective-permute-start(bf16[3,1,4,8,128,128]{5,4,3,2,1,0:T(8,128)(2,1)} %constant_dynamic-slice_fusion.2), channel_id=1, source_target_pairs={{128,0},{129,1},{130,2},{131,3},{132,4},{133,5},{134,6},{135,7},{1... | collective-permute-start | bytes 9437192 | tf_op jit(solution)/shard_map/ppermute | solution.py:38
  39.7 9.9 %collective-permute-start.8 = (bf16[4,512,128]{2,1,0:T(8,128)(2,1)}, bf16[4,512,128]{2,1,0:T(8,128)(2,1)}, u32[]{:S(2)}, u32[]{:S(2)}) collective-permute-start(bf16[4,512,128]{2,1,0:T(8,128)(2,1)} %get-tuple-element.14.rest_16_), channel_id=1, source_target_pairs={{28,0},{29,1},{30,2},{31,3},{0,4},{1,5},{2,6},{3,7},{4,8},{5,9},{6... | collective-permute-start | bytes 1572872 | tf_op jit(solution)/shard_map/ppermute | solution.py:42
  44.1 9.1 %collective-permute-start.5 = (bf16[4,512,128]{2,1,0:T(8,128)(2,1)}, bf16[4,512,128]{2,1,0:T(8,128)(2,1)}, u32[]{:S(2)}, u32[]{:S(2)}) collective-permute-start(bf16[4,512,128]{2,1,0:T(8,128)(2,1)} %collective-permute-done.4.rest_17_), channel_id=1, source_target_pairs={{4,0},{5,1},{6,2},{7,3},{8,4},{9,5},{10,6},{11,7},{12,8},{13,9},{1... | collective-permute-start | bytes 1572872 | tf_op jit(solution)/shard_map/ppermute | solution.py:42
  49.7 9.9 %collective-permute-start.9 = (bf16[4,512,128]{2,1,0:T(8,128)(2,1)}, bf16[4,512,128]{2,1,0:T(8,128)(2,1)S(1)}, u32[]{:S(2)}, u32[]{:S(2)}) collective-permute-start(bf16[4,512,128]{2,1,0:T(8,128)(2,1)} %collective-permute-done.8.rest_19_), channel_id=1, source_target_pairs={{28,0},{29,1},{30,2},{31,3},{0,4},{1,5},{2,6},{3,7},{4,8},{5,9},{6... | collective-permute-start | bytes 1572872 | tf_op jit(solution)/shard_map/ppermute | solution.py:42
  53.2 9.6 %collective-permute-start.6 = (bf16[4,512,128]{2,1,0:T(8,128)(2,1)}, bf16[4,512,128]{2,1,0:T(8,128)(2,1)S(1)}, u32[]{:S(2)}, u32[]{:S(2)}) collective-permute-start(bf16[4,512,128]{2,1,0:T(8,128)(2,1)} %collective-permute-done.5.rest_18_), channel_id=1, source_target_pairs={{4,0},{5,1},{6,2},{7,3},{8,4},{9,5},{10,6},{11,7},{12,8},{13,9},{1... | collective-permute-start | bytes 1572872 | tf_op jit(solution)/shard_map/ppermute | solution.py:42
  59.5 22.4 %copy-start.2 = (bf16[4,512,128]{2,1,0:T(8,128)(2,1)}, bf16[4,512,128]{2,1,0:T(8,128)(2,1)S(1)}, u32[]{:S(2)}) copy-start(bf16[4,512,128]{2,1,0:T(8,128)(2,1)S(1)} %collective-permute-done.9.rest_21_) | copy-start | bytes 1572868
  59.5 9.6 %collective-permute-start.10 = (bf16[4,512,128]{2,1,0:T(8,128)(2,1)S(1)}, bf16[4,512,128]{2,1,0:T(8,128)(2,1)S(1)}, u32[]{:S(2)}, u32[]{:S(2)}) collective-permute-start(bf16[4,512,128]{2,1,0:T(8,128)(2,1)S(1)} %collective-permute-done.9.rest_21_), channel_id=1, source_target_pairs={{28,0},{29,1},{30,2},{31,3},{0,4},{1,5},{2,6},{3,7},{4,8},{5,9},{6... | collective-permute-start | bytes 1572872 | tf_op jit(solution)/shard_map/ppermute | solution.py:42
  62.7 19.2 %copy-start.3 = (bf16[4,512,128]{2,1,0:T(8,128)(2,1)}, bf16[4,512,128]{2,1,0:T(8,128)(2,1)S(1)}, u32[]{:S(2)}) copy-start(bf16[4,512,128]{2,1,0:T(8,128)(2,1)S(1)} %collective-permute-done.6.rest_20_) | copy-start | bytes 1572868
  62.7 9.5 %collective-permute-start.7 = (bf16[4,512,128]{2,1,0:T(8,128)(2,1)S(1)}, bf16[4,512,128]{2,1,0:T(8,128)(2,1)S(1)}, u32[]{:S(2)}, u32[]{:S(2)}) collective-permute-start(bf16[4,512,128]{2,1,0:T(8,128)(2,1)S(1)} %collective-permute-done.6.rest_20_), channel_id=1, source_target_pairs={{4,0},{5,1},{6,2},{7,3},{8,4},{9,5},{10,6},{11,7},{12,8},{13,9},{1... | collective-permute-start | bytes 1572872 | tf_op jit(solution)/shard_map/ppermute | solution.py:42
  69.2 3.1 %copy-start.4 = (bf16[4,512,128]{2,1,0:T(8,128)(2,1)}, bf16[4,512,128]{2,1,0:T(8,128)(2,1)S(1)}, u32[]{:S(2)}) copy-start(bf16[4,512,128]{2,1,0:T(8,128)(2,1)S(1)} %collective-permute-done.10.y_ref.rest_23_) | copy-start | bytes 1572868
  72.3 0.8 copy-start.5
  76.8 3.3 %collective-permute-start.11 = (f32[1,4608]{1,0:T(1,128)S(1)}, f32[1,4608]{1,0:T(1,128)S(1)}, u32[]{:S(2)}, u32[]{:S(2)}) collective-permute-start(f32[1,4608]{1,0:T(1,128)S(1)} %pad_maximum_fusion.4), channel_id=1, source_target_pairs={{128,0},{129,1},{130,2},{131,3},{132,4},{133,5},{134,6},{135,7},{1... | collective-permute-start | bytes 55304 | tf_op jit(solution)/shard_map/ppermute | solution.py:38
  81.9 1.7 copy-start.1
  93.6 27.4 %copy-start.11 = (s32[512]{0:T(512)S(1)}, s32[512]{0:T(512)}, u32[]{:S(2)}) copy-start(s32[512]{0:T(512)} %param.7) | copy-start | bytes 6148
  93.6 2.0 %collective-permute-start.13 = (f32[256,384]{1,0:T(8,128)}, f32[256,384]{1,0:T(8,128)S(1)}, u32[]{:S(2)}, u32[]{:S(2)}) collective-permute-start(f32[256,384]{1,0:T(8,128)} %get-tuple-element.10), channel_id=1, source_target_pairs={{128,0},{129,1},{130,2},{131,3},{132,4},{133,5},{134,6},{135,7},{1... | collective-permute-start | bytes 1179656 | tf_op jit(solution)/shard_map/ppermute | solution.py:38
  94.0 36.4 %collective-permute-start = (bf16[4,8,4,32,256]{4,3,2,1,0:T(8,128)(2,1)}, bf16[4,8,4,32,256]{4,3,2,1,0:T(8,128)(2,1)S(1)}, u32[]{:S(2)}, u32[]{:S(2)}) collective-permute-start(bf16[4,8,4,32,256]{4,3,2,1,0:T(8,128)(2,1)} %bitcast.45), channel_id=1, source_target_pairs={{128,0},{129,1},{130,2},{131,3},{132,4},{133,5},{134,6},{135,7},{1... | collective-permute-start | bytes 6291464 | tf_op jit(solution)/shard_map/ppermute | solution.py:38
  98.7 8.8 %collective-permute-start.14 = (bf16[2,256,128]{2,1,0:T(8,128)(2,1)}, bf16[2,256,128]{2,1,0:T(8,128)(2,1)S(1)}, u32[]{:S(2)}, u32[]{:S(2)}) collective-permute-start(bf16[2,256,128]{2,1,0:T(8,128)(2,1)} %get-tuple-element.12), channel_id=1, source_target_pairs={{0,1},{1,2},{2,3},{4,5},{5,6},{6,7},{8,9},{9,10},{10,11},{12,13},{... | collective-permute-start | bytes 393224 | tf_op jit(solution)/shard_map/ppermute | solution.py:38
  101.8 6.9 %collective-permute-start.15 = (bf16[2,256,128]{2,1,0:T(8,128)(2,1)}, bf16[2,256,128]{2,1,0:T(8,128)(2,1)S(1)}, u32[]{:S(2)}, u32[]{:S(2)}) collective-permute-start(bf16[2,256,128]{2,1,0:T(8,128)(2,1)} %get-tuple-element.12), channel_id=1, source_target_pairs={{0,2},{1,3},{4,6},{5,7},{8,10},{9,11},{12,14},{13,15},{16,18},{17,... | collective-permute-start | bytes 393224 | tf_op jit(solution)/shard_map/ppermute | solution.py:38
  106.2 3.8 %collective-permute-start.16 = (bf16[2,256,128]{2,1,0:T(8,128)(2,1)}, bf16[2,256,128]{2,1,0:T(8,128)(2,1)S(1)}, u32[]{:S(2)}, u32[]{:S(2)}) collective-permute-start(bf16[2,256,128]{2,1,0:T(8,128)(2,1)} %get-tuple-element.12), channel_id=1, source_target_pairs={{0,3},{4,7},{8,11},{12,15},{16,19},{20,23},{24,27},{28,31},{32,35}... | collective-permute-start | bytes 393224 | tf_op jit(solution)/shard_map/ppermute | solution.py:38
  111.0 3.1 %collective-permute-start.17 = (bf16[4,2,256,128]{3,2,1,0:T(8,128)(2,1)S(1)}, bf16[4,2,256,128]{3,2,1,0:T(8,128)(2,1)S(1)}, u32[]{:S(2)}, u32[]{:S(2)}) collective-permute-start(bf16[4,2,256,128]{3,2,1,0:T(8,128)(2,1)S(1)} %pad_maximum_fusion.1.rest_0_), channel_id=1, source_target_pairs={{128,0},{129,1},{130,2},{131,3},{132,4},{133,5},{134,6},{135,7},{1... | collective-permute-start | bytes 1572872 | tf_op jit(solution)/shard_map/ppermute | solution.py:38
  114.1 0.8 copy-start
  117.5 13.0 %all-to-all-start.1 = ((bf16[8,256,128]{2,1,0:T(8,128)(2,1)}), bf16[8,256,128]{2,1,0:T(8,128)(2,1)S(1)}, u32[]{:S(2)}, u32[]{:S(2)}) async-start(bf16[8,256,128]{2,1,0:T(8,128)(2,1)} %broadcast_in_dim.5), calls=%async_computation.1 | async-start | bytes 1048576 | tf_op jit(solution)/shard_map/all_to_all | solution.py:344
  130.4 1.5 copy-start.7
  155.6 5.1 %collective-permute-start.18 = (bf16[256,128]{1,0:T(8,128)(2,1)S(1)}, bf16[256,128]{1,0:T(8,128)(2,1)S(1)}, u32[]{:S(2)}, u32[]{:S(2)}) collective-permute-start(bf16[256,128]{1,0:T(8,128)(2,1)S(1)} %bitcast.57), channel_id=1, source_target_pairs={{128,0},{129,1},{130,2},{131,3},{132,4},{133,5},{134,6},{135,7},{1... | collective-permute-start | bytes 196616 | tf_op jit(solution)/shard_map/ppermute | solution.py:38
  (2 other events, 1.5 us)
Sparse Core Ops, SparseCore 0:
  39.9 31.5 all-gather.2

commit v6 on v5

--- a/solution.py
+++ b/solution.py
@@ -72,9 +72,14 @@
     return jnp.broadcast_to(row, (HD, row.shape[1])).T
 
 
-def qkv_kernel(at_ref, squares_ref, modality_ref, gain_ref, gain_other_ref, *rest):
-    own_ws, other_ws, pieces = rest[:8], rest[8:16], rest[16:24]
-    mine_ref, theirs_ref, acc, inv, own = rest[24:]
+def qkv_kernel(ks, last, at_ref, squares_ref, modality_ref, gain_ref, gain_other_ref, *rest):
+    n = len(ks)
+    own_ws, other_ws, pieces = rest[:n], rest[n : 2 * n], rest[2 * n : 3 * n]
+    rest = rest[3 * n :]
+    if last:
+        before_ref, mine_ref, theirs_ref, acc, inv, own = rest
+    else:
+        acc, inv, own = rest
     step = pl.program_id(0)
 
     @pl.when(step == 0)
@@ -85,92 +90,71 @@
     inverse = inv[...]
     own_row = own[...] > 0
     normed, right = [], []
-    for k, piece in enumerate(pieces):
-        yi, zi = place(at_ref, k, step)
+    for i, piece in enumerate(pieces):
+        yi, zi = place(at_ref, ks[i], step)
         gain = jnp.where(own_row, gain_ref[yi, pl.ds(zi, 1), :], gain_other_ref[yi, pl.ds(zi, 1), :])
         normed.append((piece[0].astype(jnp.float32) * inverse * gain).astype(jnp.bfloat16))
-        right.append(jnp.concatenate([w[p, 0, 0, 0] for w in (own_ws[k], other_ws[k]) for p in range(3)], axis=1))
+        right.append(jnp.concatenate([w[p, 0, 0, 0] for w in (own_ws[i], other_ws[i]) for p in range(3)], axis=1))
     part = jnp.dot(
         jnp.concatenate(normed, axis=1), jnp.concatenate(right, axis=0), preferred_element_type=jnp.float32
     )
 
     @pl.when(step == 0)
     def _():
-        acc[...] = part
+        acc[...] = part + before_ref[...] if last else part
 
     @pl.when(step > 0)
     def _():
         acc[...] += part
 
-    @pl.when(step == pl.num_programs(0) - 1)
-    def _():
-        half = acc.shape[0] // 2
-        for ref, first in ((mine_ref, at_ref[0] * half), (theirs_ref, (1 - at_ref[0]) * half)):
-            rows = pl.ds(pl.multiple_of(first, half), half)
-            own_here = own[rows, :] > 0
-            for p in range(3):
-                low, high = acc[rows, p * HD : (p + 1) * HD], acc[rows, (3 + p) * HD : (4 + p) * HD]
-                ref[:, p * HD : (p + 1) * HD] = jnp.where(own_here, low, high)
-
-
-def project(at, squares, modality, gain, gain_other, w, w_other, arrays):
-    rows = arrays[0].shape[1]
+    if last:
+
+        @pl.when(step == pl.num_programs(0) - 1)
+        def _():
+            half = acc.shape[0] // 2
+            for ref, first in ((mine_ref, at_ref[0] * half), (theirs_ref, (1 - at_ref[0]) * half)):
+                rows = pl.ds(pl.multiple_of(first, half), half)
+                own_here = own[rows, :] > 0
+                for p in range(3):
+                    low, high = acc[rows, p * HD : (p + 1) * HD], acc[rows, (3 + p) * HD : (4 + p) * HD]
+                    ref[:, p * HD : (p + 1) * HD] = jnp.where(own_here, low, high)
+
+
+def project(ks, before, at, squares, modality, gain, gain_other, w, w_other, arrays):
+    last = before is not None
+    rows, n = arrays[0].shape[1], len(ks)
     block = (3, 1, 1, 1, HD, HD)
     whole = lambda shape: pl.BlockSpec(shape, lambda g, at: (0,) * len(shape))
     piece = pl.BlockSpec((1, rows, HD), lambda g, at: (g, 0, 0))
     weights = lambda k, other: pl.BlockSpec(
         block, lambda g, at: (0, 0 if other else at[0], *place(at, k, g), 0, 0)
     )
+    wide = (rows, 6 * HD)
+    narrow = jax.ShapeDtypeStruct((rows // 2, 3 * HD), jnp.float32)
+    vectors = [pltpu.VMEM((rows, HD), jnp.float32)] * 2
+
+    def body(*refs):
+        qkv_kernel(ks, last, *refs)
+
     return pl.pallas_call(
-        qkv_kernel,
+        body,
         grid_spec=pltpu.PrefetchScalarGridSpec(
             num_scalar_prefetch=1,
             grid=(4,),
             in_specs=[whole((1, rows)), whole((1, rows)), whole((NY, NZ, HD)), whole((NY, NZ, HD))]
-            + [weights(k, False) for k in range(8)]
-            + [weights(k, True) for k in range(8)]
-            + [piece] * 8,
-            out_specs=[whole((rows // 2, 3 * HD))] * 2,
-            scratch_shapes=[pltpu.VMEM((rows, w), jnp.float32) for w in (6 * HD, HD, HD)],
-        ),
-        out_shape=[jax.ShapeDtypeStruct((rows // 2, 3 * HD), jnp.float32)] * 2,
+            + [weights(k, False) for k in ks]
+            + [weights(k, True) for k in ks]
+            + [piece] * n
+            + [whole(wide)] * last,
+            out_specs=[whole(narrow.shape)] * 2 if last else whole(wide),
+            scratch_shapes=[pltpu.VMEM(wide, jnp.float32)] * last + vectors,
+        ),
+        out_shape=[narrow] * 2 if last else jax.ShapeDtypeStruct(wide, jnp.float32),
         compiler_params=pltpu.CompilerParams(vmem_limit_bytes=56 * 2**20),
         cost_estimate=pl.CostEstimate(
-            flops=2 * rows * 4096 * 6 * HD, bytes_accessed=11 * 2**20, transcendentals=0
-        ),
-    )(at, squares, modality, gain, gain_other, *[w] * 8, *[w_other] * 8, *arrays)
-
-
-def squares_kernel(x_ref, y_ref, early_ref, out_ref, acc):
-    step = pl.program_id(0)
-    both = jnp.square(x_ref[0].astype(jnp.float32)) + jnp.square(y_ref[0].astype(jnp.float32))
-
-    @pl.when(step == 0)
-    def _():
-        acc[...] = both
-
-    @pl.when(step > 0)
-    def _():
-        acc[...] += both
-
-    @pl.when(step == pl.num_programs(0) - 1)
-    def _():
-        out_ref[...] = early_ref[...] + jnp.sum(acc[...].T, axis=0, keepdims=True)
-
-
-def last_squares(x, y, early):
-    rows = x.shape[1]
-    piece = pl.BlockSpec((1, rows, HD), lambda g: (g, 0, 0))
-    row = pl.BlockSpec((1, rows), lambda g: (0, 0))
-    return pl.pallas_call(
-        squares_kernel,
-        grid=(x.shape[0],),
-        in_specs=[piece, piece, row],
-        out_specs=row,
-        scratch_shapes=[pltpu.VMEM((rows, HD), jnp.float32)],
-        out_shape=jax.ShapeDtypeStruct((1, rows), jnp.float32),
-        compiler_params=pltpu.CompilerParams(vmem_limit_bytes=56 * 2**20),
-    )(x, y, early)
+            flops=2 * rows * n * 4 * HD * 6 * HD, bytes_accessed=n * 3 * 2**19, transcendentals=0
+        ),
+    )(at, squares, modality, gain, gain_other, *[w] * n, *[w_other] * n, *[arrays[k] for k in ks], *[before] * last)
 
 
 def finish_kernel(mine_ref, got_ref, gain_ref, cos_ref, sin_ref, q_ref, kv_ref):
@@ -226,7 +210,9 @@
         weights = jnp.where(seen[n], jnp.exp(scores[n] - best), 0.0)
         total += weights.sum(axis=1, keepdims=True)
         out += jnp.dot(weights.astype(jnp.bfloat16), ref[i, 1], preferred_element_type=jnp.float32)
-    out_ref[...] = (out / total).astype(jnp.bfloat16)
+    result = (out / total).astype(jnp.bfloat16)
+    for i in range(out_ref.shape[0]):
+        out_ref[i] = result
 
 
 def attention(bases, queries, keys):
@@ -235,7 +221,7 @@
         attention_kernel,
         in_specs=[pl.BlockSpec(memory_space=pltpu.SMEM)] + [vmem] * (1 + len(keys)),
         out_specs=vmem,
-        out_shape=jax.ShapeDtypeStruct(queries.shape, jnp.bfloat16),
+        out_shape=jax.ShapeDtypeStruct((2 * NY, *queries.shape), jnp.bfloat16),
         compiler_params=pltpu.CompilerParams(vmem_limit_bytes=40 * 2**20),
         cost_estimate=pl.CostEstimate(flops=2**28, bytes_accessed=2**20, transcendentals=2**19),
     )(bases, queries, *keys)
@@ -283,7 +269,7 @@
                     out_ref[2 * y + odd, zh, :, c * HD : (c + 1) * HD] = w_ref[:, first : first + HD]
 
 
-def spread_w_out(at, w_out):
+def spread_w_out(at, w_out, *ahead):
     rows = HD // NX
     shape = (2 * NY, NZ // 2, rows, 2 * HD)
     pieces = pl.pallas_call(
@@ -298,7 +284,19 @@
         cost_estimate=pl.CostEstimate(flops=0, bytes_accessed=2**20, transcendentals=0),
     )(at, w_out)
     lines = lax.all_to_all(pieces, ("y", "zl"), 0, 0)
+    lines, *_ = lax.optimization_barrier((lines, *ahead))
     return lax.all_gather(lines, "seq", axis=0)
+
+
+def share_vectors(tokens, norm_gain, at_tp):
+    devices, rows = 2 * NY * NZ, tokens.shape[0] // HD
+    squares = jnp.sum(jnp.square(tokens.astype(jnp.float32)), axis=1).reshape(1, rows, HD)
+    own = lax.dynamic_index_in_dim(norm_gain.reshape(2, NY * NZ, HD), at_tp, axis=1, keepdims=True)
+    own = jnp.broadcast_to(own[:, :, None], (2, NY * NZ, 1, HD)).reshape(devices, 1, HD)
+    sent = jnp.concatenate([jnp.broadcast_to(squares, (devices, rows, HD)), own], axis=1)
+    sent = jnp.pad(sent, ((0, 0), (0, 7 - rows), (0, 0)))
+    got = lax.all_to_all(sent, AXES[:4], 0, 0)
+    return jnp.sum(got[:, :rows], axis=0).reshape(1, rows * HD), got[:, rows].reshape(2, NY, NZ, HD)
 
 
 def shards(tokens, modality, norm_gain, w_qkv, qk_gain, w_out):
@@ -309,8 +307,11 @@
     at = jnp.stack([c, y, z, seq]).astype(jnp.int32)
     modality = modality[None, :]
 
-    w_cols = spread_w_out(at, w_out[0])
     arrays, direct = gather(tokens)
+    squares, gains = share_vectors(tokens, norm_gain, y * NZ + z)
+    gain, gain_other = (lax.dynamic_index_in_dim(gains, i, axis=0, keepdims=False) for i in (c, 1 - c))
+    w_qkv, w_out, squares, *_ = lax.optimization_barrier((w_qkv, w_out, squares, *direct))
+    w_cols = spread_w_out(at, w_out[0], arrays[1], arrays[3])
     w_cols_other = take(w_cols, dc=1)
 
     first = seq * row_count + c * half
@@ -322,15 +323,10 @@
 
     w = w_qkv[0].transpose(1, 0, 2).reshape(3, 2, NY, NZ, HD, HD)
     w_other = take(lax.dynamic_slice_in_dim(w, 1 - c, 1, axis=1), dc=1)
-    gains = norm_gain.reshape(2, NY * NZ * HD)
-    gain_send = lax.dynamic_slice_in_dim(gains, 1 - c, 1, axis=0)
-    gain = lax.dynamic_slice_in_dim(gains, c, 1, axis=0).reshape(NY, NZ, HD)
-
-    early = sum(jnp.sum(jnp.square(a.astype(jnp.float32)), axis=(0, 2)) for a in arrays[:6])
-    squares = last_squares(arrays[6], arrays[7], early[None, :])
-    got = take(jnp.concatenate([squares, gain_send], axis=1), dc=1)
-    squares, gain_other = squares + got[:, :row_count], got[:, row_count:].reshape(NY, NZ, HD)
-    mine, theirs = project(at, squares, modality, gain, gain_other, w, w_other, arrays)
+
+    common = (at, squares, modality, gain, gain_other, w, w_other, arrays)
+    before = project(range(6), None, *common)
+    mine, theirs = project(range(6, 8), before, *common)
     queries, own_keys = finish(mine, take(theirs, dc=1), qk_gain, cosines, sines)
 
     moved = {d: take(own_keys, dx=-d, wrap_x=False) for d in (2, 3, 1)}
@@ -341,7 +337,7 @@
     bases = jnp.stack([b + c * half for b in begin] + [b + (1 - c) * half for b in begin]).astype(jnp.int32)
     heads_out = attention(bases, queries, [got, sibling])
 
-    heads = lax.all_to_all(jnp.broadcast_to(heads_out[None], (2 * NY, half, HD)), ("y", "zl"), 0, 0)
+    heads = lax.all_to_all(heads_out, ("y", "zl"), 0, 0)
     own_half = lax.dynamic_slice_in_dim(modality, c * half, half, axis=1)
     partial = out_part(at, own_half, w_cols, w_cols_other, heads)
     spread = lax.all_to_all(partial, "zh", 0, 0)

time: 169 us -> 179 us (1.059)
  starting transfers between devices: 47.4 us -> 57 us
  other arithmetic: 11.9 us -> 7.19 us
  Pallas kernels: 25.1 us -> 28.4 us
  waiting for transfers between devices: 39.2 us -> 42.1 us
  local copies, waits for them, and re-layouts: 13.3 us -> 11.2 us
    all_to_all x1 -> x2, starting transfers between devices: 3.49 us -> 16.8 us  [the longest x1 13.3 us: share_vectors(): got = lax.all_to_all(sent, AXES[:4], 0, 0)]
    all_to_all x1 -> x2, waiting for transfers between devices: 8.83 us -> 13.9 us  [the longest x1 8.6 us: shards(): heads = lax.all_to_all(heads_out, ('y', 'zl'), 0, 0)]
    reduce_sum x6 -> x2, other arithmetic: 4.95 us -> 1.78 us  [the longest x1 1.12 us: share_vectors(): jnp.sum(jnp.square(tokens.astype(jnp.float32)), axis=1).reshape(1, rows, HD)]
    ppermute x9 -> x8, starting transfers between devices: 17.8 us -> 14.9 us  [take(): return lax.ppermute(x, AXES, pairs([(dc, dy, dz, dx)] * 2, wrap_x))]
    pallas_call x2, Pallas kernels: 13 us -> 15.5 us  [project(): pl.pallas_call(body, grid_spec=pltpu.PrefetchScalarGridSpec(num_scalar_pr...]
    ppermute x9 -> x8, waiting for transfers between devices: 5.62 us -> 4.97 us  [take(): return lax.ppermute(x, AXES, pairs([(dc, dy, dz, dx)] * 2, wrap_x))]
    unnamed x25 -> x18, local copies, waits for them, and re-layouts: 6.1 us -> 5.51 us
  transfers between devices with their start and end apart: 22 -> 22, of which waited for: 15 -> 10; matrix products, arithmetic and copies ran while one was open for 11% -> 6% of each run, Pallas kernels for 10% -> 11%
where the time goes in v6:
time: 179 us; the launch traced here: 178 us
  starting transfers between devices  57 us (32%)
  waiting for transfers between devices  42.1 us (24%)
  Pallas kernels  28.4 us (16%)
  blocking collectives  18.3 us (10%)
  between operations  13.6 us (8%)
  local copies, waits for them, and re-layouts  11.2 us (6%)
  other arithmetic  7.19 us (4%)
    ppermute x10, waiting for transfers between devices, take_by_core(): lax.ppermute(x, AXES, pairs([m and (0, *m, 0) for m in (on_y, on_z)]))  23.2 us
    ppermute x10, starting transfers between devices, take_by_core(): lax.ppermute(x, AXES, pairs([m and (0, *m, 0) for m in (on_y, on_z)]))  20.3 us
    all_to_all x1, blocking collectives, shards(): spread = lax.all_to_all(partial, 'zh', 0, 0)  18.3 us
    pallas_call x2, Pallas kernels, project(): pl.pallas_call(body, grid_spec=pltpu.PrefetchScalarGridSpec(num_scalar_pr...  15.5 us
    ppermute x8, starting transfers between devices, take(): return lax.ppermute(x, AXES, pairs([(dc, dy, dz, dx)] * 2, wrap_x))  14.9 us
    all_to_all x1, starting transfers between devices, share_vectors(): got = lax.all_to_all(sent, AXES[:4], 0, 0)  13.3 us
    all_to_all x1, waiting for transfers between devices, shards(): heads = lax.all_to_all(heads_out, ('y', 'zl'), 0, 0)  8.6 us
    unnamed x18, local copies, waits for them, and re-layouts  5.51 us
  transfers between devices with their start and end apart: 22, of which 10 were waited for; matrix products, arithmetic and copies ran while one was open for 6% of the time, Pallas kernels for 11%

profile of v6, /device:TPU:1, one launch (start us, length us, event | category | flops | bytes accessed | tf_op | source)
XLA Modules:
  0.0 177.8 jit_solution(1704673218261827669)
XLA Ops:
  8.5 13.3 %all-to-all-start = ((f32[64,8,128]{2,1,0:T(8,128)}), f32[64,8,128]{2,1,0:T(8,128)S(1)}, u32[]{:S(2)}, u32[]{:S(2)}) async-start(f32[64,8,128]{2,1,0:T(8,128)} %select_maximum_fusion), calls=%async_computation | async-start | bytes 524288 | tf_op jit(solution)/shard_map/all_to_all | solution.py:298
  21.8 3.6 %collective-permute-start = (bf16[512,128]{1,0:T(8,128)(2,1)}, bf16[512,128]{1,0:T(8,128)(2,1)S(1)}, u32[]{:S(2)}, u32[]{:S(2)}) collective-permute-start(bf16[512,128]{1,0:T(8,128)(2,1)} %param.6), channel_id=1, source_target_pairs={{32,0},{33,1},{34,2},{35,3},{36,4},{37,5},{38,6},{39,7},{40,8},{41... | collective-permute-start | bytes 393224 | tf_op jit(solution)/shard_map/ppermute | solution.py:42
  25.3 4.1 %collective-permute-start.2 = (bf16[512,128]{1,0:T(8,128)(2,1)}, bf16[512,128]{1,0:T(8,128)(2,1)S(1)}, u32[]{:S(2)}, u32[]{:S(2)}) collective-permute-start(bf16[512,128]{1,0:T(8,128)(2,1)} %param.6), channel_id=1, source_target_pairs={{64,0},{65,1},{66,2},{67,3},{68,4},{69,5},{70,6},{71,7},{72,8},{73... | collective-permute-start | bytes 393224 | tf_op jit(solution)/shard_map/ppermute | solution.py:42
  30.1 5.3 %all-to-all-done = f32[64,8,128]{2,1,0:T(8,128)S(1)} async-done(((f32[64,8,128]{2,1,0:T(8,128)}), f32[64,8,128]{2,1,0:T(8,128)S(1)}, u32[]{:S(2)}, u32[]{:S(2)}) %all-to-all-start) | async-done | bytes 262176 | tf_op jit(solution)/shard_map/all_to_all | solution.py:298
  36.1 2.1 %collective-permute-done.2 = bf16[512,128]{1,0:T(8,128)(2,1)S(1)} collective-permute-done((bf16[512,128]{1,0:T(8,128)(2,1)}, bf16[512,128]{1,0:T(8,128)(2,1)S(1)}, u32[]{:S(2)}, u32[]{:S(2)}) %collective-permute-start.2) | collective-permute-done | bytes 131104 | tf_op jit(solution)/shard_map/ppermute | solution.py:42
  38.1 2.6 %shard_map.64 = bf16[8,4,32,256]{3,2,1,0:T(8,128)(2,1)} custom-call(s32[4]{0:T(128)} %pad_add_fusion.at_ref.refs_0_, bf16[128,8192]{1,0:T(8,128)(2,1)} %bitcast.52), custom_call_target="tpu_custom_call" | custom-call | bytes 1048576 | tf_op jit(solution)/shard_map/pallas_call | solution.py:275
  40.8 5.0 %all-to-all-start.1 = ((bf16[8,4,32,256]{3,2,1,0:T(8,128)(2,1)}), bf16[8,4,32,256]{3,2,1,0:T(8,128)(2,1)}, u32[]{:S(2)}, u32[]{:S(2)}) async-start(bf16[8,4,32,256]{3,2,1,0:T(8,128)(2,1)} %shard_map.64), calls=%async_computation.1 | async-start | bytes 1048576 | tf_op jit(solution)/shard_map/all_to_all | solution.py:286
  46.7 1.4 collective-permute-start.3
  49.3 3.9 %constant_dynamic-slice_fusion.2 = bf16[3,1,4,8,128,128]{5,4,3,2,1,0:T(8,128)(2,1)} fusion(bf16[3,2,4,8,128,128]{5,4,3,2,1,0:T(8,128)(2,1)} %bitcast.43, s32[]{:T(128)S(6)} %select_n.47), kind=kLoop, calls=%fused_computation.16 | loop fusion | bytes 6291460 | tf_op jit(solution)/shard_map/dynamic_slice | solution.py:325
  53.3 8.6 %collective-permute-done.3.refs_18_ = bf16[4,512,128]{2,1,0:T(8,128)(2,1)} collective-permute-done((bf16[4,512,128]{2,1,0:T(8,128)(2,1)}, bf16[4,512,128]{2,1,0:T(8,128)(2,1)}, u32[]{:S(2)}, u32[]{:S(2)}) %collective-permute-start.3) | collective-permute-done | bytes 524320 | tf_op jit(solution)/shard_map/ppermute | solution.py:42
  61.9 3.0 %collective-permute-start.7 = (bf16[4,512,128]{2,1,0:T(8,128)(2,1)}, bf16[4,512,128]{2,1,0:T(8,128)(2,1)S(1)}, u32[]{:S(2)}, u32[]{:S(2)}) collective-permute-start(bf16[4,512,128]{2,1,0:T(8,128)(2,1)} %collective-permute-done.3.refs_18_), channel_id=1, source_target_pairs={{4,0},{5,1},{6,2},{7,3},{8,4},{9,5},{10,6},{11,7},{12,8},{13,9},{1... | collective-permute-start | bytes 1572872 | tf_op jit(solution)/shard_map/ppermute | solution.py:42
  64.9 6.4 %collective-permute-done.7.refs_19_ = bf16[4,512,128]{2,1,0:T(8,128)(2,1)S(1)} collective-permute-done((bf16[4,512,128]{2,1,0:T(8,128)(2,1)}, bf16[4,512,128]{2,1,0:T(8,128)(2,1)S(1)}, u32[]{:S(2)}, u32[]{:S(2)}) %collective-permute-start.7) | collective-permute-done | bytes 524320 | tf_op jit(solution)/shard_map/ppermute | solution.py:42
  72.1 3.4 %collective-permute-start.8 = (bf16[4,512,128]{2,1,0:T(8,128)(2,1)S(1)}, bf16[4,512,128]{2,1,0:T(8,128)(2,1)}, u32[]{:S(2)}, u32[]{:S(2)}) collective-permute-start(bf16[4,512,128]{2,1,0:T(8,128)(2,1)S(1)} %collective-permute-done.7.refs_19_), channel_id=1, source_target_pairs={{4,0},{5,1},{6,2},{7,3},{8,4},{9,5},{10,6},{11,7},{12,8},{13,9},{1... | collective-permute-start | bytes 1572872 | tf_op jit(solution)/shard_map/ppermute | solution.py:42
  75.5 6.1 %collective-permute-done.8.refs_21_ = bf16[4,512,128]{2,1,0:T(8,128)(2,1)} collective-permute-done((bf16[4,512,128]{2,1,0:T(8,128)(2,1)S(1)}, bf16[4,512,128]{2,1,0:T(8,128)(2,1)}, u32[]{:S(2)}, u32[]{:S(2)}) %collective-permute-start.8) | collective-permute-done | bytes 524320 | tf_op jit(solution)/shard_map/ppermute | solution.py:42
  81.6 3.5 %collective-permute-start.9 = (bf16[4,512,128]{2,1,0:T(8,128)(2,1)}, bf16[4,512,128]{2,1,0:T(8,128)(2,1)}, u32[]{:S(2)}, u32[]{:S(2)}) collective-permute-start(bf16[4,512,128]{2,1,0:T(8,128)(2,1)} %collective-permute-done.8.refs_21_), channel_id=1, source_target_pairs={{4,0},{5,1},{6,2},{7,3},{8,4},{9,5},{10,6},{11,7},{12,8},{13,9},{1... | collective-permute-start | bytes 1572872 | tf_op jit(solution)/shard_map/ppermute | solution.py:42
  85.8 1.6 copy-done.2
  87.5 8.8 %shard_map.65.refs_11_ = f32[512,768]{1,0:T(8,128)} custom-call(s32[4]{0:T(128)} %pad_add_fusion.at_ref.refs_0_, f32[1,512]{1,0:T(1,128)} %bitcast.68, s32[1,512]{1,0:T(1,128)} %bitcast.70, f32[4,8,128]{2,1,0:T(8,128)} %get-tuple-element.24.refs_3_, f32[4,8,128]{2,1,0:T(8,128)} %get-tuple-element.23.refs_4_, bf16[3,2,4,8,128,128]{5,4,3,2,1,0:T(8,128)(2,1)} %bitcast.44, ...), custom_call_target="tpu_custom_call" | custom-call | flops 2415919104 | bytes 9437184 | tf_op jit(solution)/shard_map/pallas_call | solution.py:139
  96.3 6.7 %shard_map.66 = (f32[256,384]{1,0:T(8,128)}, f32[256,384]{1,0:T(8,128)}) custom-call(s32[4]{0:T(128)} %pad_add_fusion.at_ref.refs_0_, f32[1,512]{1,0:T(1,128)} %bitcast.69, s32[1,512]{1,0:T(1,128)} %bitcast.71, f32[4,8,128]{2,1,0:T(8,128)} %get-tuple-element.24.refs_3_, f32[4,8,128]{2,1,0:T(8,128)} %get-tuple-element.23.refs_4_, ...), custom_call_target="tpu_custom_call" | custom-call | flops 805306368 | bytes 3145728 | tf_op jit(solution)/shard_map/pallas_call | solution.py:139
  105.8 2.3 %shard_map.67 = (bf16[256,128]{1,0:T(8,128)(2,1)}, bf16[2,256,128]{2,1,0:T(8,128)(2,1)}) custom-call(f32[256,384]{1,0:T(8,128)} %get-tuple-element.17.mine_ref, f32[256,384]{1,0:T(8,128)} %copy-done.7, f32[2,128]{1,0:T(2,128)} %gain_ref.1, f32[256,128]{1,0:T(8,128)} %get-tuple-element.28.cos_ref, f32[256,128]{1,0:T(8,128)} %get-tuple-element.29.sin_ref), custom_call_target="tpu_custom_call" | custom-call | tf_op jit(solution)/shard_map/pallas_call | solution.py:179
  108.1 3.1 %collective-permute-start.13 = (bf16[2,256,128]{2,1,0:T(8,128)(2,1)}, bf16[2,256,128]{2,1,0:T(8,128)(2,1)S(1)}, u32[]{:S(2)}, u32[]{:S(2)}) collective-permute-start(bf16[2,256,128]{2,1,0:T(8,128)(2,1)} %get-tuple-element.20), channel_id=1, source_target_pairs={{0,1},{1,2},{2,3},{4,5},{5,6},{6,7},{8,9},{9,10},{10,11},{12,13},{... | collective-permute-start | bytes 393224 | tf_op jit(solution)/shard_map/ppermute | solution.py:38
  111.2 4.4 %collective-permute-start.14 = (bf16[2,256,128]{2,1,0:T(8,128)(2,1)}, bf16[2,256,128]{2,1,0:T(8,128)(2,1)S(1)}, u32[]{:S(2)}, u32[]{:S(2)}) collective-permute-start(bf16[2,256,128]{2,1,0:T(8,128)(2,1)} %get-tuple-element.20), channel_id=1, source_target_pairs={{0,2},{1,3},{4,6},{5,7},{8,10},{9,11},{12,14},{13,15},{16,18},{17,... | collective-permute-start | bytes 393224 | tf_op jit(solution)/shard_map/ppermute | solution.py:38
  115.5 1.3 collective-permute-start.15
  116.9 1.4 collective-permute-done.14
  118.3 1.3 collective-permute-done.15
  120.6 1.4 collective-permute-start.16
  122.0 1.5 collective-permute-done.16.rest_1_
  124.3 2.5 %shard_map.68 = bf16[8,256,128]{2,1,0:T(8,128)(2,1)} custom-call(s32[8]{0:T(128)S(1)} %stack.90.base_ref, bf16[256,128]{1,0:T(8,128)(2,1)S(1)} %copy-done.1, bf16[4,2,256,128]{3,2,1,0:T(8,128)(2,1)S(1)} %pad_maximum_fusion.1.rest_0_, bf16[4,2,256,128]{3,2,1,0:T(8,128)(2,1)S(1)} %collective-permute-done.16.rest_1_), custom_call_target="tpu_custom_call" | custom-call | flops 268435456 | bytes 1048576 | tf_op jit(solution)/shard_map/pallas_call | solution.py:220
  126.7 3.5 %all-to-all-start.2 = ((bf16[8,256,128]{2,1,0:T(8,128)(2,1)}), bf16[8,256,128]{2,1,0:T(8,128)(2,1)S(1)}, u32[]{:S(2)}, u32[]{:S(2)}) async-start(bf16[8,256,128]{2,1,0:T(8,128)(2,1)} %shard_map.68), calls=%async_computation.2 | async-start | bytes 1048576 | tf_op jit(solution)/shard_map/all_to_all | solution.py:340
  130.9 8.6 %all-to-all-done.2.heads_ref = bf16[8,256,128]{2,1,0:T(8,128)(2,1)S(1)} async-done(((bf16[8,256,128]{2,1,0:T(8,128)(2,1)}), bf16[8,256,128]{2,1,0:T(8,128)(2,1)S(1)}, u32[]{:S(2)}, u32[]{:S(2)}) %all-to-all-start.2) | async-done | bytes 524320 | tf_op jit(solution)/shard_map/all_to_all | solution.py:340
  141.0 5.5 %shard_map.69 = bf16[4,256,256]{2,1,0:T(8,128)(2,1)} custom-call(s32[4]{0:T(128)} %pad_add_fusion.at_ref.refs_0_, s32[1,256]{1,0:T(1,128)} %bitcast.73, bf16[4,8,4,32,256]{4,3,2,1,0:T(8,128)(2,1)} %bitcast.54, bf16[4,8,4,32,256]{4,3,2,1,0:T(8,128)(2,1)} %copy-done.4, bf16[8,256,128]{2,1,0:T(8,128)(2,1)} %copy-done.3), custom_call_target="tpu_custom_call" | custom-call | flops 1073741824 | bytes 5242880 | tf_op jit(solution)/shard_map/pallas_call | solution.py:247
  146.5 18.3 %all_to_all.20 = bf16[4,256,256]{2,1,0:T(8,128)(2,1)S(1)} all-to-all(bf16[4,256,256]{2,1,0:T(8,128)(2,1)} %shard_map.69), channel_id=1, replica_groups=mesh['mod'=2,'y'=4,'zh'=4,'zl'=2,'seq'=4] {'zh'}, dimensions={0} | all-to-all | bytes 1048576 | tf_op jit(solution)/shard_map/all_to_all | solution.py:343
  165.1 4.2 %collective-permute-start.17 = (bf16[256,128]{1,0:T(8,128)(2,1)S(1)}, bf16[256,128]{1,0:T(8,128)(2,1)S(1)}, u32[]{:S(2)}, u32[]{:S(2)}) collective-permute-start(bf16[256,128]{1,0:T(8,128)(2,1)S(1)} %bitcast.67), channel_id=1, source_target_pairs={{128,0},{129,1},{130,2},{131,3},{132,4},{133,5},{134,6},{135,7},{1... | collective-permute-start | bytes 196616 | tf_op jit(solution)/shard_map/ppermute | solution.py:38
  (62 shorter events, 15.5 us)
Async XLA Ops:
  6.5 1.1 copy-start
  6.5 39.3 %copy-start.6 = (bf16[512,128]{1,0:T(8,128)(2,1)S(1)}, bf16[512,128]{1,0:T(8,128)(2,1)}, u32[]{:S(2)}) copy-start(bf16[512,128]{1,0:T(8,128)(2,1)} %param.6) | copy-start | bytes 393220
  8.5 26.9 %all-to-all-start = ((f32[64,8,128]{2,1,0:T(8,128)}), f32[64,8,128]{2,1,0:T(8,128)S(1)}, u32[]{:S(2)}, u32[]{:S(2)}) async-start(f32[64,8,128]{2,1,0:T(8,128)} %select_maximum_fusion), calls=%async_computation | async-start | bytes 524288 | tf_op jit(solution)/shard_map/all_to_all | solution.py:298
  21.8 14.3 %collective-permute-start = (bf16[512,128]{1,0:T(8,128)(2,1)}, bf16[512,128]{1,0:T(8,128)(2,1)S(1)}, u32[]{:S(2)}, u32[]{:S(2)}) collective-permute-start(bf16[512,128]{1,0:T(8,128)(2,1)} %param.6), channel_id=1, source_target_pairs={{32,0},{33,1},{34,2},{35,3},{36,4},{37,5},{38,6},{39,7},{40,8},{41... | collective-permute-start | bytes 393224 | tf_op jit(solution)/shard_map/ppermute | solution.py:42
  25.3 10.7 %collective-permute-start.1 = (bf16[512,128]{1,0:T(8,128)(2,1)}, bf16[512,128]{1,0:T(8,128)(2,1)S(1)}, u32[]{:S(2)}, u32[]{:S(2)}) collective-permute-start(bf16[512,128]{1,0:T(8,128)(2,1)} %param.6), channel_id=1, source_target_pairs={{96,0},{97,1},{98,2},{99,3},{100,4},{101,5},{102,6},{103,7},{104,8... | collective-permute-start | bytes 393224 | tf_op jit(solution)/shard_map/ppermute | solution.py:42
  25.3 12.8 %collective-permute-start.2 = (bf16[512,128]{1,0:T(8,128)(2,1)}, bf16[512,128]{1,0:T(8,128)(2,1)S(1)}, u32[]{:S(2)}, u32[]{:S(2)}) collective-permute-start(bf16[512,128]{1,0:T(8,128)(2,1)} %param.6), channel_id=1, source_target_pairs={{64,0},{65,1},{66,2},{67,3},{68,4},{69,5},{70,6},{71,7},{72,8},{73... | collective-permute-start | bytes 393224 | tf_op jit(solution)/shard_map/ppermute | solution.py:42
  40.8 21.1 %all-to-all-start.1 = ((bf16[8,4,32,256]{3,2,1,0:T(8,128)(2,1)}), bf16[8,4,32,256]{3,2,1,0:T(8,128)(2,1)}, u32[]{:S(2)}, u32[]{:S(2)}) async-start(bf16[8,4,32,256]{3,2,1,0:T(8,128)(2,1)} %shard_map.64), calls=%async_computation.1 | async-start | bytes 1048576 | tf_op jit(solution)/shard_map/all_to_all | solution.py:286
  45.8 57.4 %all-gather.3.cloned.1.call-start = ((), (), s32[]{:S(2)}) async-start(), calls=%async_computation.4 | async-start | bytes 2621440 | tf_op jit(solution)/shard_map/all_gather | solution.py:288
  46.7 15.1 %collective-permute-start.3 = (bf16[4,512,128]{2,1,0:T(8,128)(2,1)}, bf16[4,512,128]{2,1,0:T(8,128)(2,1)}, u32[]{:S(2)}, u32[]{:S(2)}) collective-permute-start(bf16[4,512,128]{2,1,0:T(8,128)(2,1)} %pad_maximum_fusion.refs_17_), channel_id=1, source_target_pairs={{4,0},{5,1},{6,2},{7,3},{8,4},{9,5},{10,6},{11,7},{12,8},{13,9},{1... | collective-permute-start | bytes 1572872 | tf_op jit(solution)/shard_map/ppermute | solution.py:42
  48.1 13.7 %collective-permute-start.4 = (bf16[4,512,128]{2,1,0:T(8,128)(2,1)}, bf16[4,512,128]{2,1,0:T(8,128)(2,1)}, u32[]{:S(2)}, u32[]{:S(2)}) collective-permute-start(bf16[4,512,128]{2,1,0:T(8,128)(2,1)} %pad_maximum_fusion.refs_17_), channel_id=1, source_target_pairs={{28,0},{29,1},{30,2},{31,3},{0,4},{1,5},{2,6},{3,7},{4,8},{5,9},{6... | collective-permute-start | bytes 1572872 | tf_op jit(solution)/shard_map/ppermute | solution.py:42
  53.3 32.6 %collective-permute-start.6 = (bf16[3,1,4,8,128,128]{5,4,3,2,1,0:T(8,128)(2,1)}, bf16[3,1,4,8,128,128]{5,4,3,2,1,0:T(8,128)(2,1)S(1)}, u32[]{:S(2)}, u32[]{:S(2)}) collective-permute-start(bf16[3,1,4,8,128,128]{5,4,3,2,1,0:T(8,128)(2,1)} %constant_dynamic-slice_fusion.2), channel_id=1, source_target_pairs={{128,0},{129,1},{130,2},{131,3},{132,4},{133,5},{134,6},{135,7},{1... | collective-permute-start | bytes 9437192 | tf_op jit(solution)/shard_map/ppermute | solution.py:38
  61.9 9.4 %collective-permute-start.7 = (bf16[4,512,128]{2,1,0:T(8,128)(2,1)}, bf16[4,512,128]{2,1,0:T(8,128)(2,1)S(1)}, u32[]{:S(2)}, u32[]{:S(2)}) collective-permute-start(bf16[4,512,128]{2,1,0:T(8,128)(2,1)} %collective-permute-done.3.refs_18_), channel_id=1, source_target_pairs={{4,0},{5,1},{6,2},{7,3},{8,4},{9,5},{10,6},{11,7},{12,8},{13,9},{1... | collective-permute-start | bytes 1572872 | tf_op jit(solution)/shard_map/ppermute | solution.py:42
  64.9 10.6 %collective-permute-start.10 = (bf16[4,512,128]{2,1,0:T(8,128)(2,1)}, bf16[4,512,128]{2,1,0:T(8,128)(2,1)}, u32[]{:S(2)}, u32[]{:S(2)}) collective-permute-start(bf16[4,512,128]{2,1,0:T(8,128)(2,1)} %collective-permute-done.4.refs_20_), channel_id=1, source_target_pairs={{28,0},{29,1},{30,2},{31,3},{0,4},{1,5},{2,6},{3,7},{4,8},{5,9},{6... | collective-permute-start | bytes 1572872 | tf_op jit(solution)/shard_map/ppermute | solution.py:42
  71.3 0.8 copy-start.5
  72.1 9.5 %collective-permute-start.8 = (bf16[4,512,128]{2,1,0:T(8,128)(2,1)S(1)}, bf16[4,512,128]{2,1,0:T(8,128)(2,1)}, u32[]{:S(2)}, u32[]{:S(2)}) collective-permute-start(bf16[4,512,128]{2,1,0:T(8,128)(2,1)S(1)} %collective-permute-done.7.refs_19_), channel_id=1, source_target_pairs={{4,0},{5,1},{6,2},{7,3},{8,4},{9,5},{10,6},{11,7},{12,8},{13,9},{1... | collective-permute-start | bytes 1572872 | tf_op jit(solution)/shard_map/ppermute | solution.py:42
  75.5 20.8 %collective-permute-start.11 = (bf16[4,512,128]{2,1,0:T(8,128)(2,1)}, bf16[4,512,128]{2,1,0:T(8,128)(2,1)}, u32[]{:S(2)}, u32[]{:S(2)}) collective-permute-start(bf16[4,512,128]{2,1,0:T(8,128)(2,1)} %collective-permute-done.10.refs_22_), channel_id=1, source_target_pairs={{28,0},{29,1},{30,2},{31,3},{0,4},{1,5},{2,6},{3,7},{4,8},{5,9},{6... | collective-permute-start | bytes 1572872 | tf_op jit(solution)/shard_map/ppermute | solution.py:42
  81.6 14.7 %collective-permute-start.9 = (bf16[4,512,128]{2,1,0:T(8,128)(2,1)}, bf16[4,512,128]{2,1,0:T(8,128)(2,1)}, u32[]{:S(2)}, u32[]{:S(2)}) collective-permute-start(bf16[4,512,128]{2,1,0:T(8,128)(2,1)} %collective-permute-done.8.refs_21_), channel_id=1, source_target_pairs={{4,0},{5,1},{6,2},{7,3},{8,4},{9,5},{10,6},{11,7},{12,8},{13,9},{1... | collective-permute-start | bytes 1572872 | tf_op jit(solution)/shard_map/ppermute | solution.py:42
  85.8 1.6 copy-start.2
  103.0 27.3 %copy-start.8 = (s32[512]{0:T(512)S(1)}, s32[512]{0:T(512)}, u32[]{:S(2)}) copy-start(s32[512]{0:T(512)} %param.7) | copy-start | bytes 6148
  103.0 2.0 %collective-permute-start.12 = (f32[256,384]{1,0:T(8,128)}, f32[256,384]{1,0:T(8,128)S(1)}, u32[]{:S(2)}, u32[]{:S(2)}) collective-permute-start(f32[256,384]{1,0:T(8,128)} %get-tuple-element.18), channel_id=1, source_target_pairs={{128,0},{129,1},{130,2},{131,3},{132,4},{133,5},{134,6},{135,7},{1... | collective-permute-start | bytes 1179656 | tf_op jit(solution)/shard_map/ppermute | solution.py:38
  103.2 36.4 %collective-permute-start.5 = (bf16[4,8,4,32,256]{4,3,2,1,0:T(8,128)(2,1)}, bf16[4,8,4,32,256]{4,3,2,1,0:T(8,128)(2,1)S(1)}, u32[]{:S(2)}, u32[]{:S(2)}) collective-permute-start(bf16[4,8,4,32,256]{4,3,2,1,0:T(8,128)(2,1)} %bitcast.53), channel_id=1, source_target_pairs={{128,0},{129,1},{130,2},{131,3},{132,4},{133,5},{134,6},{135,7},{1... | collective-permute-start | bytes 6291464 | tf_op jit(solution)/shard_map/ppermute | solution.py:38
  105.0 0.7 copy-start.7
  108.1 8.8 %collective-permute-start.13 = (bf16[2,256,128]{2,1,0:T(8,128)(2,1)}, bf16[2,256,128]{2,1,0:T(8,128)(2,1)S(1)}, u32[]{:S(2)}, u32[]{:S(2)}) collective-permute-start(bf16[2,256,128]{2,1,0:T(8,128)(2,1)} %get-tuple-element.20), channel_id=1, source_target_pairs={{0,1},{1,2},{2,3},{4,5},{5,6},{6,7},{8,9},{9,10},{10,11},{12,13},{... | collective-permute-start | bytes 393224 | tf_op jit(solution)/shard_map/ppermute | solution.py:38
  111.2 7.1 %collective-permute-start.14 = (bf16[2,256,128]{2,1,0:T(8,128)(2,1)}, bf16[2,256,128]{2,1,0:T(8,128)(2,1)S(1)}, u32[]{:S(2)}, u32[]{:S(2)}) collective-permute-start(bf16[2,256,128]{2,1,0:T(8,128)(2,1)} %get-tuple-element.20), channel_id=1, source_target_pairs={{0,2},{1,3},{4,6},{5,7},{8,10},{9,11},{12,14},{13,15},{16,18},{17,... | collective-permute-start | bytes 393224 | tf_op jit(solution)/shard_map/ppermute | solution.py:38
  115.5 4.0 %collective-permute-start.15 = (bf16[2,256,128]{2,1,0:T(8,128)(2,1)}, bf16[2,256,128]{2,1,0:T(8,128)(2,1)S(1)}, u32[]{:S(2)}, u32[]{:S(2)}) collective-permute-start(bf16[2,256,128]{2,1,0:T(8,128)(2,1)} %get-tuple-element.20), channel_id=1, source_target_pairs={{0,3},{4,7},{8,11},{12,15},{16,19},{20,23},{24,27},{28,31},{32,35}... | collective-permute-start | bytes 393224 | tf_op jit(solution)/shard_map/ppermute | solution.py:38
  120.6 2.9 %collective-permute-start.16 = (bf16[4,2,256,128]{3,2,1,0:T(8,128)(2,1)S(1)}, bf16[4,2,256,128]{3,2,1,0:T(8,128)(2,1)S(1)}, u32[]{:S(2)}, u32[]{:S(2)}) collective-permute-start(bf16[4,2,256,128]{3,2,1,0:T(8,128)(2,1)S(1)} %pad_maximum_fusion.1.rest_0_), channel_id=1, source_target_pairs={{128,0},{129,1},{130,2},{131,3},{132,4},{133,5},{134,6},{135,7},{1... | collective-permute-start | bytes 1572872 | tf_op jit(solution)/shard_map/ppermute | solution.py:38
  123.5 0.8 copy-start.1
  126.7 12.8 %all-to-all-start.2 = ((bf16[8,256,128]{2,1,0:T(8,128)(2,1)}), bf16[8,256,128]{2,1,0:T(8,128)(2,1)S(1)}, u32[]{:S(2)}, u32[]{:S(2)}) async-start(bf16[8,256,128]{2,1,0:T(8,128)(2,1)} %shard_map.68), calls=%async_computation.2 | async-start | bytes 1048576 | tf_op jit(solution)/shard_map/all_to_all | solution.py:340
  139.5 0.8 copy-start.3
  139.5 1.5 copy-start.4
  165.1 5.1 %collective-permute-start.17 = (bf16[256,128]{1,0:T(8,128)(2,1)S(1)}, bf16[256,128]{1,0:T(8,128)(2,1)S(1)}, u32[]{:S(2)}, u32[]{:S(2)}) collective-permute-start(bf16[256,128]{1,0:T(8,128)(2,1)S(1)} %bitcast.67), channel_id=1, source_target_pairs={{128,0},{129,1},{130,2},{131,3},{132,4},{133,5},{134,6},{135,7},{1... | collective-permute-start | bytes 196616 | tf_op jit(solution)/shard_map/ppermute | solution.py:38
Sparse Core Ops, SparseCore 0:
  62.0 31.5 all-gather.2

commit v7 on v5

--- a/solution.py
+++ b/solution.py
@@ -72,14 +72,16 @@
     return jnp.broadcast_to(row, (HD, row.shape[1])).T
 
 
-def qkv_kernel(at_ref, squares_ref, modality_ref, gain_ref, gain_other_ref, *rest):
+def qkv_kernel(at_ref, row_ref, got_ref, modality_ref, gain_ref, *rest):
     own_ws, other_ws, pieces = rest[:8], rest[8:16], rest[16:24]
     mine_ref, theirs_ref, acc, inv, own = rest[24:]
     step = pl.program_id(0)
 
     @pl.when(step == 0)
     def _():
-        inv[...] = columns(lax.rsqrt(squares_ref[...] / (2 * NY * NZ * HD) + EPS))
+        count = inv.shape[0]
+        squares = row_ref[:, :count] + got_ref[:, :count]
+        inv[...] = columns(lax.rsqrt(squares / (2 * NY * NZ * HD) + EPS))
         own[...] = columns((modality_ref[...] == at_ref[0]).astype(jnp.float32))
 
     inverse = inv[...]
@@ -87,7 +89,8 @@
     normed, right = [], []
     for k, piece in enumerate(pieces):
         yi, zi = place(at_ref, k, step)
-        gain = jnp.where(own_row, gain_ref[yi, pl.ds(zi, 1), :], gain_other_ref[yi, pl.ds(zi, 1), :])
+        first = pl.multiple_of(inv.shape[0] + (yi * NZ + zi) * HD, HD)
+        gain = jnp.where(own_row, gain_ref[yi, pl.ds(zi, 1), :], got_ref[:, pl.ds(first, HD)])
         normed.append((piece[0].astype(jnp.float32) * inverse * gain).astype(jnp.bfloat16))
         right.append(jnp.concatenate([w[p, 0, 0, 0] for w in (own_ws[k], other_ws[k]) for p in range(3)], axis=1))
     part = jnp.dot(
@@ -113,7 +116,7 @@
                 ref[:, p * HD : (p + 1) * HD] = jnp.where(own_here, low, high)
 
 
-def project(at, squares, modality, gain, gain_other, w, w_other, arrays):
+def project(at, row, got, modality, gain, w, w_other, arrays):
     rows = arrays[0].shape[1]
     block = (3, 1, 1, 1, HD, HD)
     whole = lambda shape: pl.BlockSpec(shape, lambda g, at: (0,) * len(shape))
@@ -126,7 +129,7 @@
         grid_spec=pltpu.PrefetchScalarGridSpec(
             num_scalar_prefetch=1,
             grid=(4,),
-            in_specs=[whole((1, rows)), whole((1, rows)), whole((NY, NZ, HD)), whole((NY, NZ, HD))]
+            in_specs=[whole(row.shape), whole(got.shape), whole((1, rows)), whole((NY, NZ, HD))]
             + [weights(k, False) for k in range(8)]
             + [weights(k, True) for k in range(8)]
             + [piece] * 8,
@@ -134,43 +137,11 @@
             scratch_shapes=[pltpu.VMEM((rows, w), jnp.float32) for w in (6 * HD, HD, HD)],
         ),
         out_shape=[jax.ShapeDtypeStruct((rows // 2, 3 * HD), jnp.float32)] * 2,
-        compiler_params=pltpu.CompilerParams(vmem_limit_bytes=56 * 2**20),
+        compiler_params=pltpu.CompilerParams(vmem_limit_bytes=61 * 2**20),
         cost_estimate=pl.CostEstimate(
             flops=2 * rows * 4096 * 6 * HD, bytes_accessed=11 * 2**20, transcendentals=0
         ),
-    )(at, squares, modality, gain, gain_other, *[w] * 8, *[w_other] * 8, *arrays)
-
-
-def squares_kernel(x_ref, y_ref, early_ref, out_ref, acc):
-    step = pl.program_id(0)
-    both = jnp.square(x_ref[0].astype(jnp.float32)) + jnp.square(y_ref[0].astype(jnp.float32))
-
-    @pl.when(step == 0)
-    def _():
-        acc[...] = both
-
-    @pl.when(step > 0)
-    def _():
-        acc[...] += both
-
-    @pl.when(step == pl.num_programs(0) - 1)
-    def _():
-        out_ref[...] = early_ref[...] + jnp.sum(acc[...].T, axis=0, keepdims=True)
-
-
-def last_squares(x, y, early):
-    rows = x.shape[1]
-    piece = pl.BlockSpec((1, rows, HD), lambda g: (g, 0, 0))
-    row = pl.BlockSpec((1, rows), lambda g: (0, 0))
-    return pl.pallas_call(
-        squares_kernel,
-        grid=(x.shape[0],),
-        in_specs=[piece, piece, row],
-        out_specs=row,
-        scratch_shapes=[pltpu.VMEM((rows, HD), jnp.float32)],
-        out_shape=jax.ShapeDtypeStruct((1, rows), jnp.float32),
-        compiler_params=pltpu.CompilerParams(vmem_limit_bytes=56 * 2**20),
-    )(x, y, early)
+    )(at, row, got, modality, gain, *[w] * 8, *[w_other] * 8, *arrays)
 
 
 def finish_kernel(mine_ref, got_ref, gain_ref, cos_ref, sin_ref, q_ref, kv_ref):
@@ -226,7 +197,9 @@
         weights = jnp.where(seen[n], jnp.exp(scores[n] - best), 0.0)
         total += weights.sum(axis=1, keepdims=True)
         out += jnp.dot(weights.astype(jnp.bfloat16), ref[i, 1], preferred_element_type=jnp.float32)
-    out_ref[...] = (out / total).astype(jnp.bfloat16)
+    result = (out / total).astype(jnp.bfloat16)
+    for i in range(out_ref.shape[0]):
+        out_ref[i] = result
 
 
 def attention(bases, queries, keys):
@@ -235,7 +208,7 @@
         attention_kernel,
         in_specs=[pl.BlockSpec(memory_space=pltpu.SMEM)] + [vmem] * (1 + len(keys)),
         out_specs=vmem,
-        out_shape=jax.ShapeDtypeStruct(queries.shape, jnp.bfloat16),
+        out_shape=jax.ShapeDtypeStruct((2 * NY, *queries.shape), jnp.bfloat16),
         compiler_params=pltpu.CompilerParams(vmem_limit_bytes=40 * 2**20),
         cost_estimate=pl.CostEstimate(flops=2**28, bytes_accessed=2**20, transcendentals=2**19),
     )(bases, queries, *keys)
@@ -267,7 +240,7 @@
             out_specs=pl.BlockSpec((1, rows, 2 * HD), lambda g, at: (g, 0, 0)),
         ),
         out_shape=jax.ShapeDtypeStruct((steps, rows, 2 * HD), jnp.bfloat16),
-        compiler_params=pltpu.CompilerParams(vmem_limit_bytes=56 * 2**20),
+        compiler_params=pltpu.CompilerParams(vmem_limit_bytes=61 * 2**20),
         cost_estimate=pl.CostEstimate(
             flops=8 * rows * NY * HD * NZ * HD, bytes_accessed=5 * 2**20, transcendentals=0
         ),
@@ -283,7 +256,7 @@
                     out_ref[2 * y + odd, zh, :, c * HD : (c + 1) * HD] = w_ref[:, first : first + HD]
 
 
-def spread_w_out(at, w_out):
+def spread_w_out(at, w_out, *ahead):
     rows = HD // NX
     shape = (2 * NY, NZ // 2, rows, 2 * HD)
     pieces = pl.pallas_call(
@@ -298,6 +271,7 @@
         cost_estimate=pl.CostEstimate(flops=0, bytes_accessed=2**20, transcendentals=0),
     )(at, w_out)
     lines = lax.all_to_all(pieces, ("y", "zl"), 0, 0)
+    lines, *_ = lax.optimization_barrier((lines, *ahead))
     return lax.all_gather(lines, "seq", axis=0)
 
 
@@ -309,8 +283,9 @@
     at = jnp.stack([c, y, z, seq]).astype(jnp.int32)
     modality = modality[None, :]
 
-    w_cols = spread_w_out(at, w_out[0])
     arrays, direct = gather(tokens)
+    w_out, *_ = lax.optimization_barrier((w_out, *direct))
+    w_cols = spread_w_out(at, w_out[0], arrays[2], arrays[5])
     w_cols_other = take(w_cols, dc=1)
 
     first = seq * row_count + c * half
@@ -326,11 +301,9 @@
     gain_send = lax.dynamic_slice_in_dim(gains, 1 - c, 1, axis=0)
     gain = lax.dynamic_slice_in_dim(gains, c, 1, axis=0).reshape(NY, NZ, HD)
 
-    early = sum(jnp.sum(jnp.square(a.astype(jnp.float32)), axis=(0, 2)) for a in arrays[:6])
-    squares = last_squares(arrays[6], arrays[7], early[None, :])
-    got = take(jnp.concatenate([squares, gain_send], axis=1), dc=1)
-    squares, gain_other = squares + got[:, :row_count], got[:, row_count:].reshape(NY, NZ, HD)
-    mine, theirs = project(at, squares, modality, gain, gain_other, w, w_other, arrays)
+    squares = sum(jnp.sum(jnp.square(a.astype(jnp.float32)), axis=(0, 2)) for a in arrays)
+    row = jnp.concatenate([squares[None, :], gain_send], axis=1)
+    mine, theirs = project(at, row, take(row, dc=1), modality, gain, w, w_other, arrays)
     queries, own_keys = finish(mine, take(theirs, dc=1), qk_gain, cosines, sines)
 
     moved = {d: take(own_keys, dx=-d, wrap_x=False) for d in (2, 3, 1)}
@@ -341,7 +314,7 @@
     bases = jnp.stack([b + c * half for b in begin] + [b + (1 - c) * half for b in begin]).astype(jnp.int32)
     heads_out = attention(bases, queries, [got, sibling])
 
-    heads = lax.all_to_all(jnp.broadcast_to(heads_out[None], (2 * NY, half, HD)), ("y", "zl"), 0, 0)
+    heads = lax.all_to_all(heads_out, ("y", "zl"), 0, 0)
     own_half = lax.dynamic_slice_in_dim(modality, c * half, half, axis=1)
     partial = out_part(at, own_half, w_cols, w_cols_other, heads)
     spread = lax.all_to_all(partial, "zh", 0, 0)

time: 169 us -> 160 us (0.947)
  local copies, waits for them, and re-layouts: 13.3 us -> 8.04 us
  waiting for transfers between devices: 39.2 us -> 37 us
  Pallas kernels: 25.1 us -> 23 us
    ppermute x10, waiting for transfers between devices: 24.7 us -> 20.7 us  [take_by_core(): lax.ppermute(x, AXES, pairs([m and (0, *m, 0) for m in (on_y, on_z)]))]
    pallas_call x1 -> x0, Pallas kernels: 2.97 us -> none  [last_squares(): pl.pallas_call(squares_kernel, grid=(x.shape[0],), in_specs=[piece, piece...]
    all_to_all x1, waiting for transfers between devices: 0.01 us -> 2.22 us  [spread_w_out(): lines = lax.all_to_all(pieces, ('y', 'zl'), 0, 0)]
    unnamed x25, local copies, waits for them, and re-layouts: 6.1 us -> 4.2 us
    dynamic_slice x1, local copies, waits for them, and re-layouts: 3.96 us -> 2.12 us  [shards(): w_other = take(lax.dynamic_slice_in_dim(w, 1 - c, 1, axis=1), dc=1)]
    all_to_all x1, starting transfers between devices: 6.37 us -> 4.66 us  [spread_w_out(): lines = lax.all_to_all(pieces, ('y', 'zl'), 0, 0)]
    reduce_sum x6 -> x8, other arithmetic: 4.95 us -> 6.54 us  [shards(): jnp.sum(jnp.square(a.astype(jnp.float32)), axis=(0, 2))]
  transfers between devices with their start and end apart: 22 -> 22, of which waited for: 15 -> 15; matrix products, arithmetic and copies ran while one was open for 11% -> 8% of each run, Pallas kernels for 10% -> 11%
where the time goes in v7:
time: 160 us; the launch traced here: 159 us
  starting transfers between devices  47.2 us (30%)
  waiting for transfers between devices  37 us (23%)
  Pallas kernels  23 us (14%)
  blocking collectives  19.4 us (12%)
  between operations  13.6 us (8%)
  other arithmetic  11 us (7%)
  local copies, waits for them, and re-layouts  8.04 us (5%)
    ppermute x10, starting transfers between devices, take_by_core(): lax.ppermute(x, AXES, pairs([m and (0, *m, 0) for m in (on_y, on_z)]))  21.2 us
    ppermute x10, waiting for transfers between devices, take_by_core(): lax.ppermute(x, AXES, pairs([m and (0, *m, 0) for m in (on_y, on_z)]))  20.7 us
    all_to_all x1, blocking collectives, shards(): spread = lax.all_to_all(partial, 'zh', 0, 0)  19.4 us
    ppermute x9, starting transfers between devices, take(): return lax.ppermute(x, AXES, pairs([(dc, dy, dz, dx)] * 2, wrap_x))  17.9 us
    pallas_call x1, Pallas kernels, project(): pl.pallas_call(qkv_kernel, grid_spec=pltpu.PrefetchScalarGridSpec(num_sca...  10.1 us
    all_to_all x1, waiting for transfers between devices, shards(): heads = lax.all_to_all(heads_out, ('y', 'zl'), 0, 0)  8.53 us
    reduce_sum x8, other arithmetic, shards(): jnp.sum(jnp.square(a.astype(jnp.float32)), axis=(0, 2))  6.54 us
    ppermute x9, waiting for transfers between devices, take(): return lax.ppermute(x, AXES, pairs([(dc, dy, dz, dx)] * 2, wrap_x))  5.62 us
  transfers between devices with their start and end apart: 22, of which 15 were waited for; matrix products, arithmetic and copies ran while one was open for 8% of the time, Pallas kernels for 11%

profile of v7, /device:TPU:1, one launch (start us, length us, event | category | flops | bytes accessed | tf_op | source)
XLA Modules:
  0.0 159.4 jit_solution(11666012763254885792)
XLA Ops:
  6.5 6.8 %collective-permute-start = (bf16[512,128]{1,0:T(8,128)(2,1)}, bf16[512,128]{1,0:T(8,128)(2,1)S(1)}, u32[]{:S(2)}, u32[]{:S(2)}) collective-permute-start(bf16[512,128]{1,0:T(8,128)(2,1)} %param.6), channel_id=1, source_target_pairs={{32,0},{33,1},{34,2},{35,3},{36,4},{37,5},{38,6},{39,7},{40,8},{41... | collective-permute-start | bytes 393224 | tf_op jit(solution)/shard_map/ppermute | solution.py:42
  13.4 3.3 %collective-permute-start.2 = (bf16[512,128]{1,0:T(8,128)(2,1)}, bf16[512,128]{1,0:T(8,128)(2,1)S(1)}, u32[]{:S(2)}, u32[]{:S(2)}) collective-permute-start(bf16[512,128]{1,0:T(8,128)(2,1)} %param.6), channel_id=1, source_target_pairs={{64,0},{65,1},{66,2},{67,3},{68,4},{69,5},{70,6},{71,7},{72,8},{73... | collective-permute-start | bytes 393224 | tf_op jit(solution)/shard_map/ppermute | solution.py:42
  17.1 4.2 %collective-permute-done.1 = bf16[512,128]{1,0:T(8,128)(2,1)S(1)} collective-permute-done((bf16[512,128]{1,0:T(8,128)(2,1)}, bf16[512,128]{1,0:T(8,128)(2,1)S(1)}, u32[]{:S(2)}, u32[]{:S(2)}) %collective-permute-start.1) | collective-permute-done | bytes 131104 | tf_op jit(solution)/shard_map/ppermute | solution.py:42
  23.2 2.5 %collective-permute-start.3 = (bf16[4,512,128]{2,1,0:T(8,128)(2,1)S(1)}, bf16[4,512,128]{2,1,0:T(8,128)(2,1)}, u32[]{:S(2)}, u32[]{:S(2)}) collective-permute-start(bf16[4,512,128]{2,1,0:T(8,128)(2,1)S(1)} %get-tuple-element.18.rest_16_), channel_id=1, source_target_pairs={{4,0},{5,1},{6,2},{7,3},{8,4},{9,5},{10,6},{11,7},{12,8},{13,9},{1... | collective-permute-start | bytes 1572872 | tf_op jit(solution)/shard_map/ppermute | solution.py:42
  25.7 1.3 collective-permute-start.5
  27.7 2.6 %shard_map.64 = bf16[8,4,32,256]{3,2,1,0:T(8,128)(2,1)} custom-call(s32[4]{0:T(128)} %pad_add_fusion.at_ref, bf16[128,8192]{1,0:T(8,128)(2,1)} %bitcast.43), custom_call_target="tpu_custom_call" | custom-call | bytes 1048576 | tf_op jit(solution)/shard_map/pallas_call | solution.py:262
  30.2 4.7 %all-to-all-start = ((bf16[8,4,32,256]{3,2,1,0:T(8,128)(2,1)}), bf16[8,4,32,256]{3,2,1,0:T(8,128)(2,1)}, u32[]{:S(2)}, u32[]{:S(2)}) async-start(bf16[8,4,32,256]{3,2,1,0:T(8,128)(2,1)} %shard_map.64), calls=%async_computation | async-start | bytes 1048576 | tf_op jit(solution)/shard_map/all_to_all | solution.py:273
  35.0 2.2 %collective-permute-done.3.rest_17_ = bf16[4,512,128]{2,1,0:T(8,128)(2,1)} collective-permute-done((bf16[4,512,128]{2,1,0:T(8,128)(2,1)S(1)}, bf16[4,512,128]{2,1,0:T(8,128)(2,1)}, u32[]{:S(2)}, u32[]{:S(2)}) %collective-permute-start.3) | collective-permute-done | bytes 524320 | tf_op jit(solution)/shard_map/ppermute | solution.py:42
  37.1 3.8 %collective-permute-start.4 = (bf16[4,512,128]{2,1,0:T(8,128)(2,1)}, bf16[4,512,128]{2,1,0:T(8,128)(2,1)}, u32[]{:S(2)}, u32[]{:S(2)}) collective-permute-start(bf16[4,512,128]{2,1,0:T(8,128)(2,1)} %collective-permute-done.3.rest_17_), channel_id=1, source_target_pairs={{4,0},{5,1},{6,2},{7,3},{8,4},{9,5},{10,6},{11,7},{12,8},{13,9},{1... | collective-permute-start | bytes 1572872 | tf_op jit(solution)/shard_map/ppermute | solution.py:42
  41.0 2.1 %constant_dynamic-slice_fusion.2 = bf16[3,1,4,8,128,128]{5,4,3,2,1,0:T(8,128)(2,1)S(1)} fusion(bf16[3,2,4,8,128,128]{5,4,3,2,1,0:T(8,128)(2,1)} %bitcast.34, s32[]{:T(128)S(6)} %select_n.40), kind=kLoop, calls=%fused_computation.20 | loop fusion | bytes 6291460 | tf_op jit(solution)/shard_map/dynamic_slice | solution.py:299
  43.2 2.2 %all-to-all-done = bf16[8,4,32,256]{3,2,1,0:T(8,128)(2,1)} async-done(((bf16[8,4,32,256]{3,2,1,0:T(8,128)(2,1)}), bf16[8,4,32,256]{3,2,1,0:T(8,128)(2,1)}, u32[]{:S(2)}, u32[]{:S(2)}) %all-to-all-start) | async-done | bytes 524320 | tf_op jit(solution)/shard_map/all_to_all | solution.py:273
  45.4 2.9 %collective-permute-done.4.rest_18_ = bf16[4,512,128]{2,1,0:T(8,128)(2,1)} collective-permute-done((bf16[4,512,128]{2,1,0:T(8,128)(2,1)}, bf16[4,512,128]{2,1,0:T(8,128)(2,1)}, u32[]{:S(2)}, u32[]{:S(2)}) %collective-permute-start.4) | collective-permute-done | bytes 524320 | tf_op jit(solution)/shard_map/ppermute | solution.py:42
  48.3 2.4 %collective-permute-done.6.rest_21_ = bf16[4,512,128]{2,1,0:T(8,128)(2,1)} collective-permute-done((bf16[4,512,128]{2,1,0:T(8,128)(2,1)}, bf16[4,512,128]{2,1,0:T(8,128)(2,1)}, u32[]{:S(2)}, u32[]{:S(2)}) %collective-permute-start.6) | collective-permute-done | bytes 524320 | tf_op jit(solution)/shard_map/ppermute | solution.py:42
  56.8 3.9 %collective-permute-done.8.rest_20_ = bf16[4,512,128]{2,1,0:T(8,128)(2,1)S(1)} collective-permute-done((bf16[4,512,128]{2,1,0:T(8,128)(2,1)}, bf16[4,512,128]{2,1,0:T(8,128)(2,1)S(1)}, u32[]{:S(2)}, u32[]{:S(2)}) %collective-permute-start.8) | collective-permute-done | bytes 524320 | tf_op jit(solution)/shard_map/ppermute | solution.py:42
  60.7 1.8 %collective-permute-start.9 = (bf16[4,512,128]{2,1,0:T(8,128)(2,1)S(1)}, bf16[4,512,128]{2,1,0:T(8,128)(2,1)S(1)}, u32[]{:S(2)}, u32[]{:S(2)}) collective-permute-start(bf16[4,512,128]{2,1,0:T(8,128)(2,1)S(1)} %collective-permute-done.8.rest_20_), channel_id=1, source_target_pairs={{4,0},{5,1},{6,2},{7,3},{8,4},{9,5},{10,6},{11,7},{12,8},{13,9},{1... | collective-permute-start | bytes 1572872 | tf_op jit(solution)/shard_map/ppermute | solution.py:42
  63.7 1.2 multiply_reduce_fusion.5
  65.3 3.8 %collective-permute-done.9.rest_22_ = bf16[4,512,128]{2,1,0:T(8,128)(2,1)S(1)} collective-permute-done((bf16[4,512,128]{2,1,0:T(8,128)(2,1)S(1)}, bf16[4,512,128]{2,1,0:T(8,128)(2,1)S(1)}, u32[]{:S(2)}, u32[]{:S(2)}) %collective-permute-start.9) | collective-permute-done | bytes 524320 | tf_op jit(solution)/shard_map/ppermute | solution.py:42
  69.3 2.6 %collective-permute-start.11 = (f32[1,4608]{1,0:T(1,128)S(1)}, f32[1,4608]{1,0:T(1,128)S(1)}, u32[]{:S(2)}, u32[]{:S(2)}) collective-permute-start(f32[1,4608]{1,0:T(1,128)S(1)} %pad_maximum_fusion.4.row_ref), channel_id=1, source_target_pairs={{128,0},{129,1},{130,2},{131,3},{132,4},{133,5},{134,6},{135,7},{1... | collective-permute-start | bytes 55304 | tf_op jit(solution)/shard_map/ppermute | solution.py:38
  73.4 10.1 %shard_map.65 = (f32[256,384]{1,0:T(8,128)}, f32[256,384]{1,0:T(8,128)}) custom-call(s32[4]{0:T(128)} %pad_add_fusion.at_ref, f32[1,4608]{1,0:T(1,128)} %copy-done.8, f32[1,4608]{1,0:T(1,128)} %copy-done.10, s32[1,512]{1,0:T(1,128)} %bitcast.59, f32[4,8,128]{2,1,0:T(8,128)} %bitcast.57, bf16[3,2,4,8,128,128]{5,4,3,2,1,0:T(8,128)(2,1)} %bitcast.35, ...), custom_call_target="tpu_custom_call" | custom-call | flops 3221225472 | bytes 11534336 | tf_op jit(solution)/shard_map/pallas_call | solution.py:127
  86.3 2.3 %shard_map.66 = (bf16[256,128]{1,0:T(8,128)(2,1)}, bf16[2,256,128]{2,1,0:T(8,128)(2,1)}) custom-call(f32[256,384]{1,0:T(8,128)} %get-tuple-element.13.mine_ref, f32[256,384]{1,0:T(8,128)} %copy-done.7, f32[2,128]{1,0:T(2,128)} %gain_ref.1, f32[256,128]{1,0:T(8,128)} %get-tuple-element.26.cos_ref, f32[256,128]{1,0:T(8,128)} %get-tuple-element.27.sin_ref), custom_call_target="tpu_custom_call" | custom-call | tf_op jit(solution)/shard_map/pallas_call | solution.py:166
  88.6 3.1 %collective-permute-start.14 = (bf16[2,256,128]{2,1,0:T(8,128)(2,1)}, bf16[2,256,128]{2,1,0:T(8,128)(2,1)S(1)}, u32[]{:S(2)}, u32[]{:S(2)}) collective-permute-start(bf16[2,256,128]{2,1,0:T(8,128)(2,1)} %get-tuple-element.16), channel_id=1, source_target_pairs={{0,1},{1,2},{2,3},{4,5},{5,6},{6,7},{8,9},{9,10},{10,11},{12,13},{... | collective-permute-start | bytes 393224 | tf_op jit(solution)/shard_map/ppermute | solution.py:38
  91.7 4.4 %collective-permute-start.15 = (bf16[2,256,128]{2,1,0:T(8,128)(2,1)}, bf16[2,256,128]{2,1,0:T(8,128)(2,1)S(1)}, u32[]{:S(2)}, u32[]{:S(2)}) collective-permute-start(bf16[2,256,128]{2,1,0:T(8,128)(2,1)} %get-tuple-element.16), channel_id=1, source_target_pairs={{0,2},{1,3},{4,6},{5,7},{8,10},{9,11},{12,14},{13,15},{16,18},{17,... | collective-permute-start | bytes 393224 | tf_op jit(solution)/shard_map/ppermute | solution.py:38
  96.1 1.3 collective-permute-start.16
  98.6 1.3 collective-permute-done.16
  100.9 1.6 collective-permute-start.17
  102.6 1.5 collective-permute-done.17.rest_1_
  104.9 2.5 %shard_map.67 = bf16[8,256,128]{2,1,0:T(8,128)(2,1)} custom-call(s32[8]{0:T(128)S(1)} %stack.90.base_ref, bf16[256,128]{1,0:T(8,128)(2,1)S(1)} %copy-done, bf16[4,2,256,128]{3,2,1,0:T(8,128)(2,1)S(1)} %pad_maximum_fusion.1.rest_0_, bf16[4,2,256,128]{3,2,1,0:T(8,128)(2,1)S(1)} %collective-permute-done.17.rest_1_), custom_call_target="tpu_custom_call" | custom-call | flops 268435456 | bytes 1048576 | tf_op jit(solution)/shard_map/pallas_call | solution.py:207
  107.3 3.5 %all-to-all-start.1 = ((bf16[8,256,128]{2,1,0:T(8,128)(2,1)}), bf16[8,256,128]{2,1,0:T(8,128)(2,1)S(1)}, u32[]{:S(2)}, u32[]{:S(2)}) async-start(bf16[8,256,128]{2,1,0:T(8,128)(2,1)} %shard_map.67), calls=%async_computation.1 | async-start | bytes 1048576 | tf_op jit(solution)/shard_map/all_to_all | solution.py:317
  111.5 8.5 %all-to-all-done.1.heads_ref = bf16[8,256,128]{2,1,0:T(8,128)(2,1)S(1)} async-done(((bf16[8,256,128]{2,1,0:T(8,128)(2,1)}), bf16[8,256,128]{2,1,0:T(8,128)(2,1)S(1)}, u32[]{:S(2)}, u32[]{:S(2)}) %all-to-all-start.1) | async-done | bytes 524320 | tf_op jit(solution)/shard_map/all_to_all | solution.py:317
  121.5 5.5 %shard_map.68 = bf16[4,256,256]{2,1,0:T(8,128)(2,1)} custom-call(s32[4]{0:T(128)} %pad_add_fusion.at_ref, s32[1,256]{1,0:T(1,128)} %bitcast.60, bf16[4,8,4,32,256]{4,3,2,1,0:T(8,128)(2,1)} %bitcast.45, bf16[4,8,4,32,256]{4,3,2,1,0:T(8,128)(2,1)} %copy-done.6, bf16[8,256,128]{2,1,0:T(8,128)(2,1)} %copy-done.5), custom_call_target="tpu_custom_call" | custom-call | flops 1073741824 | bytes 5242880 | tf_op jit(solution)/shard_map/pallas_call | solution.py:234
  127.0 19.4 %all_to_all.15 = bf16[4,256,256]{2,1,0:T(8,128)(2,1)S(1)} all-to-all(bf16[4,256,256]{2,1,0:T(8,128)(2,1)} %shard_map.68), channel_id=1, replica_groups=mesh['mod'=2,'y'=4,'zh'=4,'zl'=2,'seq'=4] {'zh'}, dimensions={0} | all-to-all | bytes 1048576 | tf_op jit(solution)/shard_map/all_to_all | solution.py:320
  146.7 4.2 %collective-permute-start.18 = (bf16[256,128]{1,0:T(8,128)(2,1)S(1)}, bf16[256,128]{1,0:T(8,128)(2,1)S(1)}, u32[]{:S(2)}, u32[]{:S(2)}) collective-permute-start(bf16[256,128]{1,0:T(8,128)(2,1)S(1)} %bitcast.56), channel_id=1, source_target_pairs={{128,0},{129,1},{130,2},{131,3},{132,4},{133,5},{134,6},{135,7},{1... | collective-permute-start | bytes 196616 | tf_op jit(solution)/shard_map/ppermute | solution.py:38
  (72 shorter events, 22.1 us)
Async XLA Ops:
  6.5 10.5 %collective-permute-start = (bf16[512,128]{1,0:T(8,128)(2,1)}, bf16[512,128]{1,0:T(8,128)(2,1)S(1)}, u32[]{:S(2)}, u32[]{:S(2)}) collective-permute-start(bf16[512,128]{1,0:T(8,128)(2,1)} %param.6), channel_id=1, source_target_pairs={{32,0},{33,1},{34,2},{35,3},{36,4},{37,5},{38,6},{39,7},{40,8},{41... | collective-permute-start | bytes 393224 | tf_op jit(solution)/shard_map/ppermute | solution.py:42
  13.4 7.9 %collective-permute-start.1 = (bf16[512,128]{1,0:T(8,128)(2,1)}, bf16[512,128]{1,0:T(8,128)(2,1)S(1)}, u32[]{:S(2)}, u32[]{:S(2)}) collective-permute-start(bf16[512,128]{1,0:T(8,128)(2,1)} %param.6), channel_id=1, source_target_pairs={{96,0},{97,1},{98,2},{99,3},{100,4},{101,5},{102,6},{103,7},{104,8... | collective-permute-start | bytes 393224 | tf_op jit(solution)/shard_map/ppermute | solution.py:42
  13.4 8.6 %collective-permute-start.2 = (bf16[512,128]{1,0:T(8,128)(2,1)}, bf16[512,128]{1,0:T(8,128)(2,1)S(1)}, u32[]{:S(2)}, u32[]{:S(2)}) collective-permute-start(bf16[512,128]{1,0:T(8,128)(2,1)} %param.6), channel_id=1, source_target_pairs={{64,0},{65,1},{66,2},{67,3},{68,4},{69,5},{70,6},{71,7},{72,8},{73... | collective-permute-start | bytes 393224 | tf_op jit(solution)/shard_map/ppermute | solution.py:42
  23.2 17.8 %copy-start.1 = (bf16[4,512,128]{2,1,0:T(8,128)(2,1)}, bf16[4,512,128]{2,1,0:T(8,128)(2,1)S(1)}, u32[]{:S(2)}) copy-start(bf16[4,512,128]{2,1,0:T(8,128)(2,1)S(1)} %get-tuple-element.18.rest_16_) | copy-start | bytes 1572868
  23.2 14.0 %collective-permute-start.3 = (bf16[4,512,128]{2,1,0:T(8,128)(2,1)S(1)}, bf16[4,512,128]{2,1,0:T(8,128)(2,1)}, u32[]{:S(2)}, u32[]{:S(2)}) collective-permute-start(bf16[4,512,128]{2,1,0:T(8,128)(2,1)S(1)} %get-tuple-element.18.rest_16_), channel_id=1, source_target_pairs={{4,0},{5,1},{6,2},{7,3},{8,4},{9,5},{10,6},{11,7},{12,8},{13,9},{1... | collective-permute-start | bytes 1572872 | tf_op jit(solution)/shard_map/ppermute | solution.py:42
  25.7 15.2 %collective-permute-start.5 = (bf16[4,512,128]{2,1,0:T(8,128)(2,1)S(1)}, bf16[4,512,128]{2,1,0:T(8,128)(2,1)}, u32[]{:S(2)}, u32[]{:S(2)}) collective-permute-start(bf16[4,512,128]{2,1,0:T(8,128)(2,1)S(1)} %get-tuple-element.18.rest_16_), channel_id=1, source_target_pairs={{28,0},{29,1},{30,2},{31,3},{0,4},{1,5},{2,6},{3,7},{4,8},{5,9},{6... | collective-permute-start | bytes 1572872 | tf_op jit(solution)/shard_map/ppermute | solution.py:42
  30.2 15.1 %all-to-all-start = ((bf16[8,4,32,256]{3,2,1,0:T(8,128)(2,1)}), bf16[8,4,32,256]{3,2,1,0:T(8,128)(2,1)}, u32[]{:S(2)}, u32[]{:S(2)}) async-start(bf16[8,4,32,256]{3,2,1,0:T(8,128)(2,1)} %shard_map.64), calls=%async_computation | async-start | bytes 1048576 | tf_op jit(solution)/shard_map/all_to_all | solution.py:273
  34.9 49.1 %all-gather.3.cloned.1.call-start = ((), (), s32[]{:S(2)}) async-start(), calls=%async_computation.3 | async-start | bytes 2621440 | tf_op jit(solution)/shard_map/all_gather | solution.py:275
  37.1 11.2 %collective-permute-start.4 = (bf16[4,512,128]{2,1,0:T(8,128)(2,1)}, bf16[4,512,128]{2,1,0:T(8,128)(2,1)}, u32[]{:S(2)}, u32[]{:S(2)}) collective-permute-start(bf16[4,512,128]{2,1,0:T(8,128)(2,1)} %collective-permute-done.3.rest_17_), channel_id=1, source_target_pairs={{4,0},{5,1},{6,2},{7,3},{8,4},{9,5},{10,6},{11,7},{12,8},{13,9},{1... | collective-permute-start | bytes 1572872 | tf_op jit(solution)/shard_map/ppermute | solution.py:42
  40.9 9.8 %collective-permute-start.6 = (bf16[4,512,128]{2,1,0:T(8,128)(2,1)}, bf16[4,512,128]{2,1,0:T(8,128)(2,1)}, u32[]{:S(2)}, u32[]{:S(2)}) collective-permute-start(bf16[4,512,128]{2,1,0:T(8,128)(2,1)} %collective-permute-done.5.rest_19_), channel_id=1, source_target_pairs={{28,0},{29,1},{30,2},{31,3},{0,4},{1,5},{2,6},{3,7},{4,8},{5,9},{6... | collective-permute-start | bytes 1572872 | tf_op jit(solution)/shard_map/ppermute | solution.py:42
  40.9 10.4 %copy-start.9 = (f32[1,8192]{1,0:T(1,128)S(1)}, f32[1,8192]{1,0:T(1,128)}, u32[]{:S(2)}) copy-start(f32[1,8192]{1,0:T(1,128)} %param.8) | copy-start | bytes 98308
  43.1 29.7 %collective-permute-start.12 = (bf16[3,1,4,8,128,128]{5,4,3,2,1,0:T(8,128)(2,1)S(1)}, bf16[3,1,4,8,128,128]{5,4,3,2,1,0:T(8,128)(2,1)}, u32[]{:S(2)}, u32[]{:S(2)}) collective-permute-start(bf16[3,1,4,8,128,128]{5,4,3,2,1,0:T(8,128)(2,1)S(1)} %constant_dynamic-slice_fusion.2), channel_id=1, source_target_pairs={{128,0},{129,1},{130,2},{131,3},{132,4},{133,5},{134,6},{135,7},{1... | collective-permute-start | bytes 9437192 | tf_op jit(solution)/shard_map/ppermute | solution.py:38
  52.1 8.6 %collective-permute-start.8 = (bf16[4,512,128]{2,1,0:T(8,128)(2,1)}, bf16[4,512,128]{2,1,0:T(8,128)(2,1)S(1)}, u32[]{:S(2)}, u32[]{:S(2)}) collective-permute-start(bf16[4,512,128]{2,1,0:T(8,128)(2,1)} %collective-permute-done.4.rest_18_), channel_id=1, source_target_pairs={{4,0},{5,1},{6,2},{7,3},{8,4},{9,5},{10,6},{11,7},{12,8},{13,9},{1... | collective-permute-start | bytes 1572872 | tf_op jit(solution)/shard_map/ppermute | solution.py:42
  54.9 10.2 %collective-permute-start.10 = (bf16[4,512,128]{2,1,0:T(8,128)(2,1)}, bf16[4,512,128]{2,1,0:T(8,128)(2,1)S(1)}, u32[]{:S(2)}, u32[]{:S(2)}) collective-permute-start(bf16[4,512,128]{2,1,0:T(8,128)(2,1)} %collective-permute-done.6.rest_21_), channel_id=1, source_target_pairs={{28,0},{29,1},{30,2},{31,3},{0,4},{1,5},{2,6},{3,7},{4,8},{5,9},{6... | collective-permute-start | bytes 1572872 | tf_op jit(solution)/shard_map/ppermute | solution.py:42
  60.7 12.2 %copy-start.2 = (bf16[4,512,128]{2,1,0:T(8,128)(2,1)}, bf16[4,512,128]{2,1,0:T(8,128)(2,1)S(1)}, u32[]{:S(2)}) copy-start(bf16[4,512,128]{2,1,0:T(8,128)(2,1)S(1)} %collective-permute-done.8.rest_20_) | copy-start | bytes 1572868
  60.7 8.4 %collective-permute-start.9 = (bf16[4,512,128]{2,1,0:T(8,128)(2,1)S(1)}, bf16[4,512,128]{2,1,0:T(8,128)(2,1)S(1)}, u32[]{:S(2)}, u32[]{:S(2)}) collective-permute-start(bf16[4,512,128]{2,1,0:T(8,128)(2,1)S(1)} %collective-permute-done.8.rest_20_), channel_id=1, source_target_pairs={{4,0},{5,1},{6,2},{7,3},{8,4},{9,5},{10,6},{11,7},{12,8},{13,9},{1... | collective-permute-start | bytes 1572872 | tf_op jit(solution)/shard_map/ppermute | solution.py:42
  65.1 7.7 %copy-start.3 = (bf16[4,512,128]{2,1,0:T(8,128)(2,1)}, bf16[4,512,128]{2,1,0:T(8,128)(2,1)S(1)}, u32[]{:S(2)}) copy-start(bf16[4,512,128]{2,1,0:T(8,128)(2,1)S(1)} %collective-permute-done.10.rest_23_) | copy-start | bytes 1572868
  69.1 3.7 %copy-start.4 = (bf16[4,512,128]{2,1,0:T(8,128)(2,1)}, bf16[4,512,128]{2,1,0:T(8,128)(2,1)S(1)}, u32[]{:S(2)}) copy-start(bf16[4,512,128]{2,1,0:T(8,128)(2,1)S(1)} %collective-permute-done.9.rest_22_) | copy-start | bytes 1572868
  69.3 3.5 %copy-start.8 = (f32[1,4608]{1,0:T(1,128)}, f32[1,4608]{1,0:T(1,128)S(1)}, u32[]{:S(2)}) copy-start(f32[1,4608]{1,0:T(1,128)S(1)} %pad_maximum_fusion.4.row_ref) | copy-start | bytes 55300
  69.3 3.5 %collective-permute-start.11 = (f32[1,4608]{1,0:T(1,128)S(1)}, f32[1,4608]{1,0:T(1,128)S(1)}, u32[]{:S(2)}, u32[]{:S(2)}) collective-permute-start(f32[1,4608]{1,0:T(1,128)S(1)} %pad_maximum_fusion.4.row_ref), channel_id=1, source_target_pairs={{128,0},{129,1},{130,2},{131,3},{132,4},{133,5},{134,6},{135,7},{1... | collective-permute-start | bytes 55304 | tf_op jit(solution)/shard_map/ppermute | solution.py:38
  83.6 27.3 %copy-start.11 = (s32[512]{0:T(512)S(1)}, s32[512]{0:T(512)}, u32[]{:S(2)}) copy-start(s32[512]{0:T(512)} %param.7) | copy-start | bytes 6148
  83.6 2.0 %collective-permute-start.13 = (f32[256,384]{1,0:T(8,128)}, f32[256,384]{1,0:T(8,128)S(1)}, u32[]{:S(2)}, u32[]{:S(2)}) collective-permute-start(f32[256,384]{1,0:T(8,128)} %get-tuple-element.14), channel_id=1, source_target_pairs={{128,0},{129,1},{130,2},{131,3},{132,4},{133,5},{134,6},{135,7},{1... | collective-permute-start | bytes 1179656 | tf_op jit(solution)/shard_map/ppermute | solution.py:38
  84.0 36.0 %collective-permute-start.7 = (bf16[4,8,4,32,256]{4,3,2,1,0:T(8,128)(2,1)}, bf16[4,8,4,32,256]{4,3,2,1,0:T(8,128)(2,1)S(1)}, u32[]{:S(2)}, u32[]{:S(2)}) collective-permute-start(bf16[4,8,4,32,256]{4,3,2,1,0:T(8,128)(2,1)} %bitcast.44), channel_id=1, source_target_pairs={{128,0},{129,1},{130,2},{131,3},{132,4},{133,5},{134,6},{135,7},{1... | collective-permute-start | bytes 6291464 | tf_op jit(solution)/shard_map/ppermute | solution.py:38
  88.6 8.8 %collective-permute-start.14 = (bf16[2,256,128]{2,1,0:T(8,128)(2,1)}, bf16[2,256,128]{2,1,0:T(8,128)(2,1)S(1)}, u32[]{:S(2)}, u32[]{:S(2)}) collective-permute-start(bf16[2,256,128]{2,1,0:T(8,128)(2,1)} %get-tuple-element.16), channel_id=1, source_target_pairs={{0,1},{1,2},{2,3},{4,5},{5,6},{6,7},{8,9},{9,10},{10,11},{12,13},{... | collective-permute-start | bytes 393224 | tf_op jit(solution)/shard_map/ppermute | solution.py:38
  91.7 6.9 %collective-permute-start.15 = (bf16[2,256,128]{2,1,0:T(8,128)(2,1)}, bf16[2,256,128]{2,1,0:T(8,128)(2,1)S(1)}, u32[]{:S(2)}, u32[]{:S(2)}) collective-permute-start(bf16[2,256,128]{2,1,0:T(8,128)(2,1)} %get-tuple-element.16), channel_id=1, source_target_pairs={{0,2},{1,3},{4,6},{5,7},{8,10},{9,11},{12,14},{13,15},{16,18},{17,... | collective-permute-start | bytes 393224 | tf_op jit(solution)/shard_map/ppermute | solution.py:38
  96.1 3.8 %collective-permute-start.16 = (bf16[2,256,128]{2,1,0:T(8,128)(2,1)}, bf16[2,256,128]{2,1,0:T(8,128)(2,1)S(1)}, u32[]{:S(2)}, u32[]{:S(2)}) collective-permute-start(bf16[2,256,128]{2,1,0:T(8,128)(2,1)} %get-tuple-element.16), channel_id=1, source_target_pairs={{0,3},{4,7},{8,11},{12,15},{16,19},{20,23},{24,27},{28,31},{32,35}... | collective-permute-start | bytes 393224 | tf_op jit(solution)/shard_map/ppermute | solution.py:38
  100.9 3.1 %collective-permute-start.17 = (bf16[4,2,256,128]{3,2,1,0:T(8,128)(2,1)S(1)}, bf16[4,2,256,128]{3,2,1,0:T(8,128)(2,1)S(1)}, u32[]{:S(2)}, u32[]{:S(2)}) collective-permute-start(bf16[4,2,256,128]{3,2,1,0:T(8,128)(2,1)S(1)} %pad_maximum_fusion.1.rest_0_), channel_id=1, source_target_pairs={{128,0},{129,1},{130,2},{131,3},{132,4},{133,5},{134,6},{135,7},{1... | collective-permute-start | bytes 1572872 | tf_op jit(solution)/shard_map/ppermute | solution.py:38
  104.0 0.8 copy-start
  107.3 12.7 %all-to-all-start.1 = ((bf16[8,256,128]{2,1,0:T(8,128)(2,1)}), bf16[8,256,128]{2,1,0:T(8,128)(2,1)S(1)}, u32[]{:S(2)}, u32[]{:S(2)}) async-start(bf16[8,256,128]{2,1,0:T(8,128)(2,1)} %shard_map.67), calls=%async_computation.1 | async-start | bytes 1048576 | tf_op jit(solution)/shard_map/all_to_all | solution.py:317
  120.0 0.8 copy-start.5
  120.0 1.5 copy-start.6
  146.7 5.1 %collective-permute-start.18 = (bf16[256,128]{1,0:T(8,128)(2,1)S(1)}, bf16[256,128]{1,0:T(8,128)(2,1)S(1)}, u32[]{:S(2)}, u32[]{:S(2)}) collective-permute-start(bf16[256,128]{1,0:T(8,128)(2,1)S(1)} %bitcast.56), channel_id=1, source_target_pairs={{128,0},{129,1},{130,2},{131,3},{132,4},{133,5},{134,6},{135,7},{1... | collective-permute-start | bytes 196616 | tf_op jit(solution)/shard_map/ppermute | solution.py:38
  (2 other events, 1.3 us)
Sparse Core Ops, SparseCore 0:
  50.9 30.6 all-gather.2

commit v8 on v7

--- a/solution.py
+++ b/solution.py
@@ -2,6 +2,7 @@
 
 import jax
 import jax.numpy as jnp
+import numpy as np
 from jax import lax
 from jax.experimental import pallas as pl
 from jax.experimental.pallas import tpu as pltpu
@@ -42,10 +43,11 @@
     return lax.ppermute(x, AXES, pairs([m and (0, *m, 0) for m in (on_y, on_z)]))
 
 
-def gather(rows):
+def gather(rows, beside):
     k1 = take_by_core(rows, (1, 0), (0, 2))
     k2 = take_by_core(rows, (-1, 0), (0, -2))
     k3 = take_by_core(rows, (2, 0), (0, 4))
+    k1, k2, k3, beside = lax.optimization_barrier((k1, k2, k3, beside))
     g0 = jnp.stack([rows, k1, k2, k3])
     g1 = take_by_core(g0, (0, 1), (0, -1))
     x2 = take_by_core(g0, (0, -1), (-1, 0))
@@ -54,25 +56,25 @@
     x3 = take_by_core(x1, (0, 1), (1, 0))
     x6 = take_by_core(x4, (0, -1), (-1, 0))
     x5 = take_by_core(x3, (0, 1), (1, 0))
-    return [g0, g1, x1, x2, x3, x4, x5, x6], [k1, k2, k3]
+    return [g0, g1, x1, x2, x3, x4, x5, x6], beside
 
 
 OFFSETS = ((0, 0, 0), (1, 0, 7), (2, 1, 7), (7, 3, 0), (3, 2, 7), (6, 2, 0), (4, 3, 7), (5, 1, 0))
 
 
-def place(at, k, step):
-    turn = step ^ (step >> 1)
-    dz0, dy1, dz1 = OFFSETS[k]
-    dy = jnp.where(at[0] == 0, turn, dy1)
-    dz = jnp.where(at[0] == 0, dz0, 2 * turn + dz1)
-    return (at[1] + dy) & (NY - 1), (at[2] + dz) & (NZ - 1)
+def piece_places(c, y, z):
+    turn = np.tile(np.array([0, 1, 3, 2], np.int32), len(OFFSETS))
+    dz0, dy1, dz1 = (np.repeat(np.array(o, np.int32), 4) for o in zip(*OFFSETS))
+    dy = jnp.where(c == 0, turn, dy1)
+    dz = jnp.where(c == 0, dz0, 2 * turn + dz1)
+    return (y + dy) & (NY - 1), (z + dz) & (NZ - 1)
 
 
 def columns(row):
     return jnp.broadcast_to(row, (HD, row.shape[1])).T
 
 
-def qkv_kernel(at_ref, row_ref, got_ref, modality_ref, gain_ref, *rest):
+def qkv_kernel(at_ref, y_ref, z_ref, row_ref, got_ref, modality_ref, gain_ref, *rest):
     own_ws, other_ws, pieces = rest[:8], rest[8:16], rest[16:24]
     mine_ref, theirs_ref, acc, inv, own = rest[24:]
     step = pl.program_id(0)
@@ -88,7 +90,7 @@
     own_row = own[...] > 0
     normed, right = [], []
     for k, piece in enumerate(pieces):
-        yi, zi = place(at_ref, k, step)
+        yi, zi = y_ref[4 * k + step], z_ref[4 * k + step]
         first = pl.multiple_of(inv.shape[0] + (yi * NZ + zi) * HD, HD)
         gain = jnp.where(own_row, gain_ref[yi, pl.ds(zi, 1), :], got_ref[:, pl.ds(first, HD)])
         normed.append((piece[0].astype(jnp.float32) * inverse * gain).astype(jnp.bfloat16))
@@ -116,18 +118,18 @@
                 ref[:, p * HD : (p + 1) * HD] = jnp.where(own_here, low, high)
 
 
-def project(at, row, got, modality, gain, w, w_other, arrays):
+def project(at, ys, zs, row, got, modality, gain, w, w_other, arrays):
     rows = arrays[0].shape[1]
     block = (3, 1, 1, 1, HD, HD)
-    whole = lambda shape: pl.BlockSpec(shape, lambda g, at: (0,) * len(shape))
-    piece = pl.BlockSpec((1, rows, HD), lambda g, at: (g, 0, 0))
+    whole = lambda shape: pl.BlockSpec(shape, lambda g, *_: (0,) * len(shape))
+    piece = pl.BlockSpec((1, rows, HD), lambda g, *_: (g, 0, 0))
     weights = lambda k, other: pl.BlockSpec(
-        block, lambda g, at: (0, 0 if other else at[0], *place(at, k, g), 0, 0)
+        block, lambda g, at, ys, zs: (0, 0 if other else at[0], ys[4 * k + g], zs[4 * k + g], 0, 0)
     )
     return pl.pallas_call(
         qkv_kernel,
         grid_spec=pltpu.PrefetchScalarGridSpec(
-            num_scalar_prefetch=1,
+            num_scalar_prefetch=3,
             grid=(4,),
             in_specs=[whole(row.shape), whole(got.shape), whole((1, rows)), whole((NY, NZ, HD))]
             + [weights(k, False) for k in range(8)]
@@ -141,7 +143,7 @@
         cost_estimate=pl.CostEstimate(
             flops=2 * rows * 4096 * 6 * HD, bytes_accessed=11 * 2**20, transcendentals=0
         ),
-    )(at, row, got, modality, gain, *[w] * 8, *[w_other] * 8, *arrays)
+    )(at, ys, zs, row, got, modality, gain, *[w] * 8, *[w_other] * 8, *arrays)
 
 
 def finish_kernel(mine_ref, got_ref, gain_ref, cos_ref, sin_ref, q_ref, kv_ref):
@@ -217,29 +219,34 @@
 def out_kernel(at_ref, modality_ref, w_ref, other_ref, heads_ref, out_ref):
     heads = jnp.concatenate([heads_ref[i] for i in range(2 * NY)], axis=1)
     own_row = columns((modality_ref[...] == at_ref[0]).astype(jnp.float32)) > 0
-    sections = []
+    n = out_ref.shape[0]
+    parts = []
     for ref in (w_ref, other_ref):
-        w = jnp.concatenate([ref[x, i, 0] for i in range(2 * NY) for x in range(NX)], axis=0)
-        sections.append(jnp.dot(heads, w, preferred_element_type=jnp.float32))
-    for i in range(2):
-        lanes = slice(i * HD, (i + 1) * HD)
-        out_ref[0, :, lanes] = jnp.where(own_row, sections[0][:, lanes], sections[1][:, lanes]).astype(jnp.bfloat16)
+        for j in range(n):
+            parts.append(jnp.concatenate([ref[x, i, j] for i in range(2 * NY) for x in range(NX)], axis=0))
+    sums = jnp.dot(heads, jnp.concatenate(parts, axis=1), preferred_element_type=jnp.float32)
+    for j in range(n):
+        for i in range(2):
+            own, other = ((2 * (n * m + j) + i) * HD for m in range(2))
+            chosen = jnp.where(own_row, sums[:, own : own + HD], sums[:, other : other + HD])
+            out_ref[j, :, i * HD : (i + 1) * HD] = chosen.astype(jnp.bfloat16)
 
 
 def out_part(at, modality, w, w_other, heads):
     rows = heads.shape[1]
-    steps = NZ // 2
+    steps = 2
+    each = NZ // 2 // steps
     whole = lambda shape: pl.BlockSpec(shape, lambda g, at: (0,) * len(shape))
-    weights = pl.BlockSpec((NX, 2 * NY, 1, HD // NX, 2 * HD), lambda g, at: (0, 0, g, 0, 0))
+    weights = pl.BlockSpec((NX, 2 * NY, each, HD // NX, 2 * HD), lambda g, at: (0, 0, g, 0, 0))
     return pl.pallas_call(
         out_kernel,
         grid_spec=pltpu.PrefetchScalarGridSpec(
             num_scalar_prefetch=1,
             grid=(steps,),
             in_specs=[whole((1, rows)), weights, weights, whole(heads.shape)],
-            out_specs=pl.BlockSpec((1, rows, 2 * HD), lambda g, at: (g, 0, 0)),
-        ),
-        out_shape=jax.ShapeDtypeStruct((steps, rows, 2 * HD), jnp.bfloat16),
+            out_specs=pl.BlockSpec((each, rows, 2 * HD), lambda g, at: (g, 0, 0)),
+        ),
+        out_shape=jax.ShapeDtypeStruct((NZ // 2, rows, 2 * HD), jnp.bfloat16),
         compiler_params=pltpu.CompilerParams(vmem_limit_bytes=61 * 2**20),
         cost_estimate=pl.CostEstimate(
             flops=8 * rows * NY * HD * NZ * HD, bytes_accessed=5 * 2**20, transcendentals=0
@@ -256,10 +263,10 @@
                     out_ref[2 * y + odd, zh, :, c * HD : (c + 1) * HD] = w_ref[:, first : first + HD]
 
 
-def spread_w_out(at, w_out, *ahead):
+def cut_w_out(at, w_out):
     rows = HD // NX
     shape = (2 * NY, NZ // 2, rows, 2 * HD)
-    pieces = pl.pallas_call(
+    return pl.pallas_call(
         cut_kernel,
         grid_spec=pltpu.PrefetchScalarGridSpec(
             num_scalar_prefetch=1,
@@ -270,6 +277,9 @@
         out_shape=jax.ShapeDtypeStruct(shape, jnp.bfloat16),
         cost_estimate=pl.CostEstimate(flops=0, bytes_accessed=2**20, transcendentals=0),
     )(at, w_out)
+
+
+def spread_w_out(pieces, *ahead):
     lines = lax.all_to_all(pieces, ("y", "zl"), 0, 0)
     lines, *_ = lax.optimization_barrier((lines, *ahead))
     return lax.all_gather(lines, "seq", axis=0)
@@ -282,10 +292,10 @@
     z = 2 * zh + zl
     at = jnp.stack([c, y, z, seq]).astype(jnp.int32)
     modality = modality[None, :]
-
-    arrays, direct = gather(tokens)
-    w_out, *_ = lax.optimization_barrier((w_out, *direct))
-    w_cols = spread_w_out(at, w_out[0], arrays[2], arrays[5])
+    ys, zs = piece_places(c.astype(jnp.int32), y.astype(jnp.int32), z.astype(jnp.int32))
+
+    arrays, pieces = gather(tokens, cut_w_out(at, w_out[0]))
+    w_cols = spread_w_out(pieces, arrays[2], arrays[5])
     w_cols_other = take(w_cols, dc=1)
 
     first = seq * row_count + c * half
@@ -303,7 +313,7 @@
 
     squares = sum(jnp.sum(jnp.square(a.astype(jnp.float32)), axis=(0, 2)) for a in arrays)
     row = jnp.concatenate([squares[None, :], gain_send], axis=1)
-    mine, theirs = project(at, row, take(row, dc=1), modality, gain, w, w_other, arrays)
+    mine, theirs = project(at, ys, zs, row, take(row, dc=1), modality, gain, w, w_other, arrays)
     queries, own_keys = finish(mine, take(theirs, dc=1), qk_gain, cosines, sines)
 
     moved = {d: take(own_keys, dx=-d, wrap_x=False) for d in (2, 3, 1)}

time: 160 us -> 159 us (level)
  waiting for transfers between devices: 37 us -> 35.4 us
    all_to_all x1, waiting for transfers between devices: 2.22 us -> 0.01 us  [spread_w_out(): lines = lax.all_to_all(pieces, ('y', 'zl'), 0, 0)]
    unnamed x25 -> x31, local copies, waits for them, and re-layouts: 4.2 us -> 4.27 us
  transfers between devices with their start and end apart: 22 -> 22, of which waited for: 15 -> 13; matrix products, arithmetic and copies ran while one was open for 8% -> 9% of each run, Pallas kernels for 11% -> 11%
where the time goes in v8:
time: 159 us
  starting transfers between devices  47.6 us (30%)
  waiting for transfers between devices  35.4 us (22%)
  Pallas kernels  21.9 us (14%)
  blocking collectives  19.3 us (12%)
  between operations  13.7 us (9%)
  other arithmetic  12.6 us (8%)
  local copies, waits for them, and re-layouts  8.11 us (5%)
    ppermute x10, waiting for transfers between devices, take_by_core(): lax.ppermute(x, AXES, pairs([m and (0, *m, 0) for m in (on_y, on_z)]))  21.2 us
    ppermute x10, starting transfers between devices, take_by_core(): lax.ppermute(x, AXES, pairs([m and (0, *m, 0) for m in (on_y, on_z)]))  21.2 us
    all_to_all x1, blocking collectives, shards(): spread = lax.all_to_all(partial, 'zh', 0, 0)  19.3 us
    ppermute x9, starting transfers between devices, take(): return lax.ppermute(x, AXES, pairs([(dc, dy, dz, dx)] * 2, wrap_x))  18.2 us
    pallas_call x1, Pallas kernels, project(): pl.pallas_call(qkv_kernel, grid_spec=pltpu.PrefetchScalarGridSpec(num_sca...  10.1 us
    all_to_all x1, waiting for transfers between devices, shards(): heads = lax.all_to_all(heads_out, ('y', 'zl'), 0, 0)  8.52 us
    reduce_sum x8, other arithmetic, shards(): jnp.sum(jnp.square(a.astype(jnp.float32)), axis=(0, 2))  7.59 us
    ppermute x9, waiting for transfers between devices, take(): return lax.ppermute(x, AXES, pairs([(dc, dy, dz, dx)] * 2, wrap_x))  5.58 us
  transfers between devices with their start and end apart: 22, of which 13 were waited for; matrix products, arithmetic and copies ran while one was open for 9% of the time, Pallas kernels for 11%

profile of v8, /device:TPU:1, one launch (start us, length us, event | category | flops | bytes accessed | tf_op | source)
XLA Modules:
  0.0 158.6 jit_solution(5284575000605033581)
XLA Ops:
  6.5 6.8 %collective-permute-start = (bf16[512,128]{1,0:T(8,128)(2,1)}, bf16[512,128]{1,0:T(8,128)(2,1)S(1)}, u32[]{:S(2)}, u32[]{:S(2)}) collective-permute-start(bf16[512,128]{1,0:T(8,128)(2,1)} %param.10), channel_id=1, source_target_pairs={{32,0},{33,1},{34,2},{35,3},{36,4},{37,5},{38,6},{39,7},{40,8},{41... | collective-permute-start | bytes 393224 | tf_op jit(solution)/shard_map/ppermute | solution.py:43
  13.4 3.3 %collective-permute-start.2 = (bf16[512,128]{1,0:T(8,128)(2,1)}, bf16[512,128]{1,0:T(8,128)(2,1)S(1)}, u32[]{:S(2)}, u32[]{:S(2)}) collective-permute-start(bf16[512,128]{1,0:T(8,128)(2,1)} %param.10), channel_id=1, source_target_pairs={{64,0},{65,1},{66,2},{67,3},{68,4},{69,5},{70,6},{71,7},{72,8},{73... | collective-permute-start | bytes 393224 | tf_op jit(solution)/shard_map/ppermute | solution.py:43
  17.3 2.6 %shard_map.100 = bf16[8,4,32,256]{3,2,1,0:T(8,128)(2,1)} custom-call(s32[4]{0:T(128)} %pad_add_fusion.at_ref, bf16[128,8192]{1,0:T(8,128)(2,1)} %bitcast.43), custom_call_target="tpu_custom_call" | custom-call | bytes 1048576 | tf_op jit(solution)/shard_map/pallas_call | solution.py:269
  19.8 1.4 collective-permute-done.1
  23.2 2.5 %collective-permute-start.3 = (bf16[4,512,128]{2,1,0:T(8,128)(2,1)S(1)}, bf16[4,512,128]{2,1,0:T(8,128)(2,1)}, u32[]{:S(2)}, u32[]{:S(2)}) collective-permute-start(bf16[4,512,128]{2,1,0:T(8,128)(2,1)S(1)} %get-tuple-element.24.rest_16_), channel_id=1, source_target_pairs={{4,0},{5,1},{6,2},{7,3},{8,4},{9,5},{10,6},{11,7},{12,8},{13,9},{1... | collective-permute-start | bytes 1572872 | tf_op jit(solution)/shard_map/ppermute | solution.py:43
  25.7 1.3 collective-permute-start.5
  27.1 4.7 %all-to-all-start = ((bf16[8,4,32,256]{3,2,1,0:T(8,128)(2,1)}), bf16[8,4,32,256]{3,2,1,0:T(8,128)(2,1)}, u32[]{:S(2)}, u32[]{:S(2)}) async-start(bf16[8,4,32,256]{3,2,1,0:T(8,128)(2,1)} %shard_map.100), calls=%async_computation | async-start | bytes 1048576 | tf_op jit(solution)/shard_map/all_to_all | solution.py:283
  31.7 5.4 %collective-permute-done.3.rest_17_ = bf16[4,512,128]{2,1,0:T(8,128)(2,1)} collective-permute-done((bf16[4,512,128]{2,1,0:T(8,128)(2,1)S(1)}, bf16[4,512,128]{2,1,0:T(8,128)(2,1)}, u32[]{:S(2)}, u32[]{:S(2)}) %collective-permute-start.3) | collective-permute-done | bytes 524320 | tf_op jit(solution)/shard_map/ppermute | solution.py:43
  37.1 3.8 %collective-permute-start.4 = (bf16[4,512,128]{2,1,0:T(8,128)(2,1)}, bf16[4,512,128]{2,1,0:T(8,128)(2,1)}, u32[]{:S(2)}, u32[]{:S(2)}) collective-permute-start(bf16[4,512,128]{2,1,0:T(8,128)(2,1)} %collective-permute-done.3.rest_17_), channel_id=1, source_target_pairs={{4,0},{5,1},{6,2},{7,3},{8,4},{9,5},{10,6},{11,7},{12,8},{13,9},{1... | collective-permute-start | bytes 1572872 | tf_op jit(solution)/shard_map/ppermute | solution.py:43
  41.0 2.1 %constant_dynamic-slice_fusion.2 = bf16[3,1,4,8,128,128]{5,4,3,2,1,0:T(8,128)(2,1)S(1)} fusion(bf16[3,2,4,8,128,128]{5,4,3,2,1,0:T(8,128)(2,1)} %bitcast.34, s32[]{:T(128)S(6)} %select_n.55), kind=kLoop, calls=%fused_computation.20 | loop fusion | bytes 6291460 | tf_op jit(solution)/shard_map/dynamic_slice | solution.py:309
  43.2 4.7 %collective-permute-done.4.rest_18_ = bf16[4,512,128]{2,1,0:T(8,128)(2,1)} collective-permute-done((bf16[4,512,128]{2,1,0:T(8,128)(2,1)}, bf16[4,512,128]{2,1,0:T(8,128)(2,1)}, u32[]{:S(2)}, u32[]{:S(2)}) %collective-permute-start.4) | collective-permute-done | bytes 524320 | tf_op jit(solution)/shard_map/ppermute | solution.py:43
  48.0 2.5 %collective-permute-done.6.rest_21_ = bf16[4,512,128]{2,1,0:T(8,128)(2,1)} collective-permute-done((bf16[4,512,128]{2,1,0:T(8,128)(2,1)}, bf16[4,512,128]{2,1,0:T(8,128)(2,1)}, u32[]{:S(2)}, u32[]{:S(2)}) %collective-permute-start.6) | collective-permute-done | bytes 524320 | tf_op jit(solution)/shard_map/ppermute | solution.py:43
  57.1 3.4 %collective-permute-done.8.rest_20_ = bf16[4,512,128]{2,1,0:T(8,128)(2,1)} collective-permute-done((bf16[4,512,128]{2,1,0:T(8,128)(2,1)}, bf16[4,512,128]{2,1,0:T(8,128)(2,1)}, u32[]{:S(2)}, u32[]{:S(2)}) %collective-permute-start.8) | collective-permute-done | bytes 524320 | tf_op jit(solution)/shard_map/ppermute | solution.py:43
  60.5 1.8 %collective-permute-start.9 = (bf16[4,512,128]{2,1,0:T(8,128)(2,1)}, bf16[4,512,128]{2,1,0:T(8,128)(2,1)S(1)}, u32[]{:S(2)}, u32[]{:S(2)}) collective-permute-start(bf16[4,512,128]{2,1,0:T(8,128)(2,1)} %collective-permute-done.8.rest_20_), channel_id=1, source_target_pairs={{4,0},{5,1},{6,2},{7,3},{8,4},{9,5},{10,6},{11,7},{12,8},{13,9},{1... | collective-permute-start | bytes 1572872 | tf_op jit(solution)/shard_map/ppermute | solution.py:43
  63.5 1.2 multiply_reduce_fusion.5
  64.7 1.2 multiply_reduce_fusion.3
  66.1 3.0 %collective-permute-done.9.rest_22_ = bf16[4,512,128]{2,1,0:T(8,128)(2,1)S(1)} collective-permute-done((bf16[4,512,128]{2,1,0:T(8,128)(2,1)}, bf16[4,512,128]{2,1,0:T(8,128)(2,1)S(1)}, u32[]{:S(2)}, u32[]{:S(2)}) %collective-permute-start.9) | collective-permute-done | bytes 524320 | tf_op jit(solution)/shard_map/ppermute | solution.py:43
  69.4 3.0 %collective-permute-start.11 = (f32[1,4608]{1,0:T(1,128)S(1)}, f32[1,4608]{1,0:T(1,128)S(1)}, u32[]{:S(2)}, u32[]{:S(2)}) collective-permute-start(f32[1,4608]{1,0:T(1,128)S(1)} %pad_maximum_fusion.4.row_ref), channel_id=1, source_target_pairs={{128,0},{129,1},{130,2},{131,3},{132,4},{133,5},{134,6},{135,7},{1... | collective-permute-start | bytes 55304 | tf_op jit(solution)/shard_map/ppermute | solution.py:39
  73.8 10.1 %shard_map.101 = (f32[256,384]{1,0:T(8,128)}, f32[256,384]{1,0:T(8,128)}) custom-call(s32[4]{0:T(128)} %pad_add_fusion.at_ref, s32[32]{0:T(128)} %get-tuple-element.32.y_ref, s32[32]{0:T(128)} %get-tuple-element.33.z_ref, f32[1,4608]{1,0:T(1,128)} %copy-done.7, f32[1,4608]{1,0:T(1,128)} %copy-done.9, s32[1,512]{1,0:T(1,128)} %bitcast.59, ...), custom_call_target="tpu_custom_call" | custom-call | flops 3221225472 | bytes 11534336 | tf_op jit(solution)/shard_map/pallas_call | solution.py:129
  86.7 2.3 %shard_map.102 = (bf16[256,128]{1,0:T(8,128)(2,1)}, bf16[2,256,128]{2,1,0:T(8,128)(2,1)}) custom-call(f32[256,384]{1,0:T(8,128)} %get-tuple-element.19.mine_ref, f32[256,384]{1,0:T(8,128)} %copy-done.6, f32[2,128]{1,0:T(2,128)} %gain_ref.1, f32[256,128]{1,0:T(8,128)} %get-tuple-element.34.cos_ref, f32[256,128]{1,0:T(8,128)} %get-tuple-element.35.sin_ref), custom_call_target="tpu_custom_call" | custom-call | tf_op jit(solution)/shard_map/pallas_call | solution.py:168
  89.0 3.1 %collective-permute-start.14 = (bf16[2,256,128]{2,1,0:T(8,128)(2,1)}, bf16[2,256,128]{2,1,0:T(8,128)(2,1)S(1)}, u32[]{:S(2)}, u32[]{:S(2)}) collective-permute-start(bf16[2,256,128]{2,1,0:T(8,128)(2,1)} %get-tuple-element.22), channel_id=1, source_target_pairs={{0,1},{1,2},{2,3},{4,5},{5,6},{6,7},{8,9},{9,10},{10,11},{12,13},{... | collective-permute-start | bytes 393224 | tf_op jit(solution)/shard_map/ppermute | solution.py:39
  92.1 4.3 %collective-permute-start.15 = (bf16[2,256,128]{2,1,0:T(8,128)(2,1)}, bf16[2,256,128]{2,1,0:T(8,128)(2,1)S(1)}, u32[]{:S(2)}, u32[]{:S(2)}) collective-permute-start(bf16[2,256,128]{2,1,0:T(8,128)(2,1)} %get-tuple-element.22), channel_id=1, source_target_pairs={{0,2},{1,3},{4,6},{5,7},{8,10},{9,11},{12,14},{13,15},{16,18},{17,... | collective-permute-start | bytes 393224 | tf_op jit(solution)/shard_map/ppermute | solution.py:39
  96.4 1.3 collective-permute-start.16
  98.9 1.3 collective-permute-done.16
  101.2 1.6 %collective-permute-start.17 = (bf16[4,2,256,128]{3,2,1,0:T(8,128)(2,1)S(1)}, bf16[4,2,256,128]{3,2,1,0:T(8,128)(2,1)S(1)}, u32[]{:S(2)}, u32[]{:S(2)}) collective-permute-start(bf16[4,2,256,128]{3,2,1,0:T(8,128)(2,1)S(1)} %pad_maximum_fusion.1.rest_0_), channel_id=1, source_target_pairs={{128,0},{129,1},{130,2},{131,3},{132,4},{133,5},{134,6},{135,7},{1... | collective-permute-start | bytes 1572872 | tf_op jit(solution)/shard_map/ppermute | solution.py:39
  102.9 1.5 collective-permute-done.17.rest_1_
  105.2 2.5 %shard_map.103 = bf16[8,256,128]{2,1,0:T(8,128)(2,1)} custom-call(s32[8]{0:T(128)S(1)} %stack.90.base_ref, bf16[256,128]{1,0:T(8,128)(2,1)S(1)} %copy-done, bf16[4,2,256,128]{3,2,1,0:T(8,128)(2,1)S(1)} %pad_maximum_fusion.1.rest_0_, bf16[4,2,256,128]{3,2,1,0:T(8,128)(2,1)S(1)} %collective-permute-done.17.rest_1_), custom_call_target="tpu_custom_call" | custom-call | flops 268435456 | bytes 1048576 | tf_op jit(solution)/shard_map/pallas_call | solution.py:209
  107.7 3.5 %all-to-all-start.1 = ((bf16[8,256,128]{2,1,0:T(8,128)(2,1)}), bf16[8,256,128]{2,1,0:T(8,128)(2,1)S(1)}, u32[]{:S(2)}, u32[]{:S(2)}) async-start(bf16[8,256,128]{2,1,0:T(8,128)(2,1)} %shard_map.103), calls=%async_computation.1 | async-start | bytes 1048576 | tf_op jit(solution)/shard_map/all_to_all | solution.py:327
  111.8 8.5 %all-to-all-done.1.heads_ref = bf16[8,256,128]{2,1,0:T(8,128)(2,1)S(1)} async-done(((bf16[8,256,128]{2,1,0:T(8,128)(2,1)}), bf16[8,256,128]{2,1,0:T(8,128)(2,1)S(1)}, u32[]{:S(2)}, u32[]{:S(2)}) %all-to-all-start.1) | async-done | bytes 524320 | tf_op jit(solution)/shard_map/all_to_all | solution.py:327
  121.9 4.5 %shard_map.104 = bf16[4,256,256]{2,1,0:T(8,128)(2,1)} custom-call(s32[4]{0:T(128)} %pad_add_fusion.at_ref, s32[1,256]{1,0:T(1,128)} %bitcast.60, bf16[4,8,4,32,256]{4,3,2,1,0:T(8,128)(2,1)} %bitcast.45, bf16[4,8,4,32,256]{4,3,2,1,0:T(8,128)(2,1)} %copy-done.5, bf16[8,256,128]{2,1,0:T(8,128)(2,1)} %copy-done.4), custom_call_target="tpu_custom_call" | custom-call | flops 1073741824 | bytes 5242880 | tf_op jit(solution)/shard_map/pallas_call | solution.py:241
  126.4 19.3 %all_to_all.15 = bf16[4,256,256]{2,1,0:T(8,128)(2,1)S(1)} all-to-all(bf16[4,256,256]{2,1,0:T(8,128)(2,1)} %shard_map.104), channel_id=1, replica_groups=mesh['mod'=2,'y'=4,'zh'=4,'zl'=2,'seq'=4] {'zh'}, dimensions={0} | all-to-all | bytes 1048576 | tf_op jit(solution)/shard_map/all_to_all | solution.py:330
  146.0 4.2 %collective-permute-start.18 = (bf16[256,128]{1,0:T(8,128)(2,1)S(1)}, bf16[256,128]{1,0:T(8,128)(2,1)S(1)}, u32[]{:S(2)}, u32[]{:S(2)}) collective-permute-start(bf16[256,128]{1,0:T(8,128)(2,1)S(1)} %bitcast.57), channel_id=1, source_target_pairs={{128,0},{129,1},{130,2},{131,3},{132,4},{133,5},{134,6},{135,7},{1... | collective-permute-start | bytes 196616 | tf_op jit(solution)/shard_map/ppermute | solution.py:39
  (79 shorter events, 22.2 us)
Async XLA Ops:
  6.5 13.3 %collective-permute-start = (bf16[512,128]{1,0:T(8,128)(2,1)}, bf16[512,128]{1,0:T(8,128)(2,1)S(1)}, u32[]{:S(2)}, u32[]{:S(2)}) collective-permute-start(bf16[512,128]{1,0:T(8,128)(2,1)} %param.10), channel_id=1, source_target_pairs={{32,0},{33,1},{34,2},{35,3},{36,4},{37,5},{38,6},{39,7},{40,8},{41... | collective-permute-start | bytes 393224 | tf_op jit(solution)/shard_map/ppermute | solution.py:43
  13.4 7.9 %collective-permute-start.1 = (bf16[512,128]{1,0:T(8,128)(2,1)}, bf16[512,128]{1,0:T(8,128)(2,1)S(1)}, u32[]{:S(2)}, u32[]{:S(2)}) collective-permute-start(bf16[512,128]{1,0:T(8,128)(2,1)} %param.10), channel_id=1, source_target_pairs={{96,0},{97,1},{98,2},{99,3},{100,4},{101,5},{102,6},{103,7},{104,8... | collective-permute-start | bytes 393224 | tf_op jit(solution)/shard_map/ppermute | solution.py:43
  13.4 8.6 %collective-permute-start.2 = (bf16[512,128]{1,0:T(8,128)(2,1)}, bf16[512,128]{1,0:T(8,128)(2,1)S(1)}, u32[]{:S(2)}, u32[]{:S(2)}) collective-permute-start(bf16[512,128]{1,0:T(8,128)(2,1)} %param.10), channel_id=1, source_target_pairs={{64,0},{65,1},{66,2},{67,3},{68,4},{69,5},{70,6},{71,7},{72,8},{73... | collective-permute-start | bytes 393224 | tf_op jit(solution)/shard_map/ppermute | solution.py:43
  23.2 17.8 %copy-start.1 = (bf16[4,512,128]{2,1,0:T(8,128)(2,1)}, bf16[4,512,128]{2,1,0:T(8,128)(2,1)S(1)}, u32[]{:S(2)}) copy-start(bf16[4,512,128]{2,1,0:T(8,128)(2,1)S(1)} %get-tuple-element.24.rest_16_) | copy-start | bytes 1572868
  23.2 14.0 %collective-permute-start.3 = (bf16[4,512,128]{2,1,0:T(8,128)(2,1)S(1)}, bf16[4,512,128]{2,1,0:T(8,128)(2,1)}, u32[]{:S(2)}, u32[]{:S(2)}) collective-permute-start(bf16[4,512,128]{2,1,0:T(8,128)(2,1)S(1)} %get-tuple-element.24.rest_16_), channel_id=1, source_target_pairs={{4,0},{5,1},{6,2},{7,3},{8,4},{9,5},{10,6},{11,7},{12,8},{13,9},{1... | collective-permute-start | bytes 1572872 | tf_op jit(solution)/shard_map/ppermute | solution.py:43
  25.7 15.2 %collective-permute-start.5 = (bf16[4,512,128]{2,1,0:T(8,128)(2,1)S(1)}, bf16[4,512,128]{2,1,0:T(8,128)(2,1)}, u32[]{:S(2)}, u32[]{:S(2)}) collective-permute-start(bf16[4,512,128]{2,1,0:T(8,128)(2,1)S(1)} %get-tuple-element.24.rest_16_), channel_id=1, source_target_pairs={{28,0},{29,1},{30,2},{31,3},{0,4},{1,5},{2,6},{3,7},{4,8},{5,9},{6... | collective-permute-start | bytes 1572872 | tf_op jit(solution)/shard_map/ppermute | solution.py:43
  27.1 16.2 %all-to-all-start = ((bf16[8,4,32,256]{3,2,1,0:T(8,128)(2,1)}), bf16[8,4,32,256]{3,2,1,0:T(8,128)(2,1)}, u32[]{:S(2)}, u32[]{:S(2)}) async-start(bf16[8,4,32,256]{3,2,1,0:T(8,128)(2,1)} %shard_map.100), calls=%async_computation | async-start | bytes 1048576 | tf_op jit(solution)/shard_map/all_to_all | solution.py:283
  31.7 52.7 %all-gather.3.cloned.1.call-start = ((), (), s32[]{:S(2)}) async-start(), calls=%async_computation.3 | async-start | bytes 2621440 | tf_op jit(solution)/shard_map/all_gather | solution.py:285
  37.1 10.8 %collective-permute-start.4 = (bf16[4,512,128]{2,1,0:T(8,128)(2,1)}, bf16[4,512,128]{2,1,0:T(8,128)(2,1)}, u32[]{:S(2)}, u32[]{:S(2)}) collective-permute-start(bf16[4,512,128]{2,1,0:T(8,128)(2,1)} %collective-permute-done.3.rest_17_), channel_id=1, source_target_pairs={{4,0},{5,1},{6,2},{7,3},{8,4},{9,5},{10,6},{11,7},{12,8},{13,9},{1... | collective-permute-start | bytes 1572872 | tf_op jit(solution)/shard_map/ppermute | solution.py:43
  40.9 9.6 %collective-permute-start.6 = (bf16[4,512,128]{2,1,0:T(8,128)(2,1)}, bf16[4,512,128]{2,1,0:T(8,128)(2,1)}, u32[]{:S(2)}, u32[]{:S(2)}) collective-permute-start(bf16[4,512,128]{2,1,0:T(8,128)(2,1)} %collective-permute-done.5.rest_19_), channel_id=1, source_target_pairs={{28,0},{29,1},{30,2},{31,3},{0,4},{1,5},{2,6},{3,7},{4,8},{5,9},{6... | collective-permute-start | bytes 1572872 | tf_op jit(solution)/shard_map/ppermute | solution.py:43
  40.9 10.1 %copy-start.8 = (f32[1,8192]{1,0:T(1,128)S(1)}, f32[1,8192]{1,0:T(1,128)}, u32[]{:S(2)}) copy-start(f32[1,8192]{1,0:T(1,128)} %param.12) | copy-start | bytes 98308
  41.0 12.4 %copy-start.11 = (s32[32]{0:T(128)S(1)}, s32[32]{0:T(128)}, u32[]{:S(2)}) copy-start(s32[32]{0:T(128)} %constant.67.clone) | copy-start | bytes 388
  41.0 12.4 %copy-start.12 = (s32[32]{0:T(128)S(1)}, s32[32]{0:T(128)}, u32[]{:S(2)}) copy-start(s32[32]{0:T(128)} %constant.68.clone) | copy-start | bytes 388
  41.0 12.4 %copy-start.13 = (s32[32]{0:T(128)S(1)}, s32[32]{0:T(128)}, u32[]{:S(2)}) copy-start(s32[32]{0:T(128)} %constant.69.clone) | copy-start | bytes 388
  41.0 12.4 %copy-start.14 = (s32[32]{0:T(128)S(1)}, s32[32]{0:T(128)}, u32[]{:S(2)}) copy-start(s32[32]{0:T(128)} %constant.70.clone) | copy-start | bytes 388
  43.1 30.1 %collective-permute-start.12 = (bf16[3,1,4,8,128,128]{5,4,3,2,1,0:T(8,128)(2,1)S(1)}, bf16[3,1,4,8,128,128]{5,4,3,2,1,0:T(8,128)(2,1)}, u32[]{:S(2)}, u32[]{:S(2)}) collective-permute-start(bf16[3,1,4,8,128,128]{5,4,3,2,1,0:T(8,128)(2,1)S(1)} %constant_dynamic-slice_fusion.2), channel_id=1, source_target_pairs={{128,0},{129,1},{130,2},{131,3},{132,4},{133,5},{134,6},{135,7},{1... | collective-permute-start | bytes 9437192 | tf_op jit(solution)/shard_map/ppermute | solution.py:39
  51.8 8.7 %collective-permute-start.8 = (bf16[4,512,128]{2,1,0:T(8,128)(2,1)}, bf16[4,512,128]{2,1,0:T(8,128)(2,1)}, u32[]{:S(2)}, u32[]{:S(2)}) collective-permute-start(bf16[4,512,128]{2,1,0:T(8,128)(2,1)} %collective-permute-done.4.rest_18_), channel_id=1, source_target_pairs={{4,0},{5,1},{6,2},{7,3},{8,4},{9,5},{10,6},{11,7},{12,8},{13,9},{1... | collective-permute-start | bytes 1572872 | tf_op jit(solution)/shard_map/ppermute | solution.py:43
  55.2 10.8 %collective-permute-start.10 = (bf16[4,512,128]{2,1,0:T(8,128)(2,1)}, bf16[4,512,128]{2,1,0:T(8,128)(2,1)S(1)}, u32[]{:S(2)}, u32[]{:S(2)}) collective-permute-start(bf16[4,512,128]{2,1,0:T(8,128)(2,1)} %collective-permute-done.6.rest_21_), channel_id=1, source_target_pairs={{28,0},{29,1},{30,2},{31,3},{0,4},{1,5},{2,6},{3,7},{4,8},{5,9},{6... | collective-permute-start | bytes 1572872 | tf_op jit(solution)/shard_map/ppermute | solution.py:43
  60.5 8.6 %collective-permute-start.9 = (bf16[4,512,128]{2,1,0:T(8,128)(2,1)}, bf16[4,512,128]{2,1,0:T(8,128)(2,1)S(1)}, u32[]{:S(2)}, u32[]{:S(2)}) collective-permute-start(bf16[4,512,128]{2,1,0:T(8,128)(2,1)} %collective-permute-done.8.rest_20_), channel_id=1, source_target_pairs={{4,0},{5,1},{6,2},{7,3},{8,4},{9,5},{10,6},{11,7},{12,8},{13,9},{1... | collective-permute-start | bytes 1572872 | tf_op jit(solution)/shard_map/ppermute | solution.py:43
  66.0 7.3 %copy-start.2 = (bf16[4,512,128]{2,1,0:T(8,128)(2,1)}, bf16[4,512,128]{2,1,0:T(8,128)(2,1)S(1)}, u32[]{:S(2)}) copy-start(bf16[4,512,128]{2,1,0:T(8,128)(2,1)S(1)} %collective-permute-done.10.rest_23_) | copy-start | bytes 1572868
  69.2 4.1 %copy-start.3 = (bf16[4,512,128]{2,1,0:T(8,128)(2,1)}, bf16[4,512,128]{2,1,0:T(8,128)(2,1)S(1)}, u32[]{:S(2)}) copy-start(bf16[4,512,128]{2,1,0:T(8,128)(2,1)S(1)} %collective-permute-done.9.rest_22_) | copy-start | bytes 1572868
  69.4 3.9 %copy-start.7 = (f32[1,4608]{1,0:T(1,128)}, f32[1,4608]{1,0:T(1,128)S(1)}, u32[]{:S(2)}) copy-start(f32[1,4608]{1,0:T(1,128)S(1)} %pad_maximum_fusion.4.row_ref) | copy-start | bytes 55300
  69.4 3.8 %collective-permute-start.11 = (f32[1,4608]{1,0:T(1,128)S(1)}, f32[1,4608]{1,0:T(1,128)S(1)}, u32[]{:S(2)}, u32[]{:S(2)}) collective-permute-start(f32[1,4608]{1,0:T(1,128)S(1)} %pad_maximum_fusion.4.row_ref), channel_id=1, source_target_pairs={{128,0},{129,1},{130,2},{131,3},{132,4},{133,5},{134,6},{135,7},{1... | collective-permute-start | bytes 55304 | tf_op jit(solution)/shard_map/ppermute | solution.py:39
  83.9 27.2 %copy-start.10 = (s32[512]{0:T(512)S(1)}, s32[512]{0:T(512)}, u32[]{:S(2)}) copy-start(s32[512]{0:T(512)} %param.11) | copy-start | bytes 6148
  83.9 2.0 %collective-permute-start.13 = (f32[256,384]{1,0:T(8,128)}, f32[256,384]{1,0:T(8,128)S(1)}, u32[]{:S(2)}, u32[]{:S(2)}) collective-permute-start(f32[256,384]{1,0:T(8,128)} %get-tuple-element.20), channel_id=1, source_target_pairs={{128,0},{129,1},{130,2},{131,3},{132,4},{133,5},{134,6},{135,7},{1... | collective-permute-start | bytes 1179656 | tf_op jit(solution)/shard_map/ppermute | solution.py:39
  84.4 36.0 %collective-permute-start.7 = (bf16[4,8,4,32,256]{4,3,2,1,0:T(8,128)(2,1)}, bf16[4,8,4,32,256]{4,3,2,1,0:T(8,128)(2,1)S(1)}, u32[]{:S(2)}, u32[]{:S(2)}) collective-permute-start(bf16[4,8,4,32,256]{4,3,2,1,0:T(8,128)(2,1)} %bitcast.44), channel_id=1, source_target_pairs={{128,0},{129,1},{130,2},{131,3},{132,4},{133,5},{134,6},{135,7},{1... | collective-permute-start | bytes 6291464 | tf_op jit(solution)/shard_map/ppermute | solution.py:39
  89.0 8.8 %collective-permute-start.14 = (bf16[2,256,128]{2,1,0:T(8,128)(2,1)}, bf16[2,256,128]{2,1,0:T(8,128)(2,1)S(1)}, u32[]{:S(2)}, u32[]{:S(2)}) collective-permute-start(bf16[2,256,128]{2,1,0:T(8,128)(2,1)} %get-tuple-element.22), channel_id=1, source_target_pairs={{0,1},{1,2},{2,3},{4,5},{5,6},{6,7},{8,9},{9,10},{10,11},{12,13},{... | collective-permute-start | bytes 393224 | tf_op jit(solution)/shard_map/ppermute | solution.py:39
  92.1 6.8 %collective-permute-start.15 = (bf16[2,256,128]{2,1,0:T(8,128)(2,1)}, bf16[2,256,128]{2,1,0:T(8,128)(2,1)S(1)}, u32[]{:S(2)}, u32[]{:S(2)}) collective-permute-start(bf16[2,256,128]{2,1,0:T(8,128)(2,1)} %get-tuple-element.22), channel_id=1, source_target_pairs={{0,2},{1,3},{4,6},{5,7},{8,10},{9,11},{12,14},{13,15},{16,18},{17,... | collective-permute-start | bytes 393224 | tf_op jit(solution)/shard_map/ppermute | solution.py:39
  96.4 3.8 %collective-permute-start.16 = (bf16[2,256,128]{2,1,0:T(8,128)(2,1)}, bf16[2,256,128]{2,1,0:T(8,128)(2,1)S(1)}, u32[]{:S(2)}, u32[]{:S(2)}) collective-permute-start(bf16[2,256,128]{2,1,0:T(8,128)(2,1)} %get-tuple-element.22), channel_id=1, source_target_pairs={{0,3},{4,7},{8,11},{12,15},{16,19},{20,23},{24,27},{28,31},{32,35}... | collective-permute-start | bytes 393224 | tf_op jit(solution)/shard_map/ppermute | solution.py:39
  101.2 3.1 %collective-permute-start.17 = (bf16[4,2,256,128]{3,2,1,0:T(8,128)(2,1)S(1)}, bf16[4,2,256,128]{3,2,1,0:T(8,128)(2,1)S(1)}, u32[]{:S(2)}, u32[]{:S(2)}) collective-permute-start(bf16[4,2,256,128]{3,2,1,0:T(8,128)(2,1)S(1)} %pad_maximum_fusion.1.rest_0_), channel_id=1, source_target_pairs={{128,0},{129,1},{130,2},{131,3},{132,4},{133,5},{134,6},{135,7},{1... | collective-permute-start | bytes 1572872 | tf_op jit(solution)/shard_map/ppermute | solution.py:39
  107.7 12.7 %all-to-all-start.1 = ((bf16[8,256,128]{2,1,0:T(8,128)(2,1)}), bf16[8,256,128]{2,1,0:T(8,128)(2,1)S(1)}, u32[]{:S(2)}, u32[]{:S(2)}) async-start(bf16[8,256,128]{2,1,0:T(8,128)(2,1)} %shard_map.103), calls=%async_computation.1 | async-start | bytes 1048576 | tf_op jit(solution)/shard_map/all_to_all | solution.py:327
  146.0 5.1 %collective-permute-start.18 = (bf16[256,128]{1,0:T(8,128)(2,1)S(1)}, bf16[256,128]{1,0:T(8,128)(2,1)S(1)}, u32[]{:S(2)}, u32[]{:S(2)}) collective-permute-start(bf16[256,128]{1,0:T(8,128)(2,1)S(1)} %bitcast.57), channel_id=1, source_target_pairs={{128,0},{129,1},{130,2},{131,3},{132,4},{133,5},{134,6},{135,7},{1... | collective-permute-start | bytes 196616 | tf_op jit(solution)/shard_map/ppermute | solution.py:39
  (5 other events, 4.5 us)
Sparse Core Ops, SparseCore 0:
  50.6 30.8 all-gather.2

commit v9 on v8

--- a/solution.py
+++ b/solution.py
@@ -254,13 +254,18 @@
     )(at, modality, w, w_other, heads)
 
 
+GROUPS = [[2 * p + (which ^ (p >> 1)) for p in range(NZ // 2)] for which in range(2)]
+
+
 def cut_kernel(at_ref, w_ref, out_ref):
+    upper = (at_ref[2] >> 2) & 1
     for y in range(NY):
         for odd in range(2):
-            for zh in range(NZ // 2):
+            for p in range(NZ // 2):
                 for c in range(2):
-                    first = ((c * NY + y) * NZ + 2 * zh + odd) * HD
-                    out_ref[2 * y + odd, zh, :, c * HD : (c + 1) * HD] = w_ref[:, first : first + HD]
+                    first = (c * NY + y) * NZ + 2 * p + ((odd ^ (p >> 1)) ^ upper)
+                    piece = w_ref[:, pl.ds(pl.multiple_of(first * HD, HD), HD)]
+                    out_ref[2 * y + odd, p, :, c * HD : (c + 1) * HD] = piece
 
 
 def cut_w_out(at, w_out):
@@ -295,7 +300,7 @@
     ys, zs = piece_places(c.astype(jnp.int32), y.astype(jnp.int32), z.astype(jnp.int32))
 
     arrays, pieces = gather(tokens, cut_w_out(at, w_out[0]))
-    w_cols = spread_w_out(pieces, arrays[2], arrays[5])
+    w_cols = spread_w_out(pieces, arrays[2], arrays[3])
     w_cols_other = take(w_cols, dc=1)
 
     first = seq * row_count + c * half
@@ -327,7 +332,7 @@
     heads = lax.all_to_all(heads_out, ("y", "zl"), 0, 0)
     own_half = lax.dynamic_slice_in_dim(modality, c * half, half, axis=1)
     partial = out_part(at, own_half, w_cols, w_cols_other, heads)
-    spread = lax.all_to_all(partial, "zh", 0, 0)
+    spread = lax.all_to_all(partial, ("zh", "zl"), 0, 0, axis_index_groups=GROUPS)
     summed = jnp.sum(spread.astype(jnp.float32), axis=0).astype(jnp.bfloat16).reshape(half, 2, HD)
     keep = lax.dynamic_index_in_dim(summed, c, axis=1, keepdims=False)
     other = take(lax.dynamic_index_in_dim(summed, 1 - c, axis=1, keepdims=False), dc=1)

time: 159 us -> 156 us (0.981)
  blocking collectives: 19.3 us -> 15.4 us
  waiting for transfers between devices: 35.4 us -> 32 us
  starting transfers between devices: 47.6 us -> 50.8 us
    all_to_all x1, blocking collectives: 19.3 us -> 15.4 us  [shards(): lax.all_to_all(partial, ('zh', 'zl'), 0, 0, axis_index_groups=GROUPS)]
    ppermute x10, waiting for transfers between devices: 21.2 us -> 17.7 us  [take_by_core(): lax.ppermute(x, AXES, pairs([m and (0, *m, 0) for m in (on_y, on_z)]))]
    unnamed x31 -> x29, local copies, waits for them, and re-layouts: 4.27 us -> 4.22 us
  transfers between devices with their start and end apart: 22 -> 22, of which waited for: 13 -> 13; matrix products, arithmetic and copies ran while one was open for 9% -> 10% of each run, Pallas kernels for 11% -> 11%
where the time goes in v9:
time: 156 us; the launch traced here: 155 us
  starting transfers between devices  50.8 us (33%)
  waiting for transfers between devices  32 us (21%)
  Pallas kernels  22 us (14%)
  blocking collectives  15.4 us (10%)
  between operations  13.6 us (9%)
  other arithmetic  13.3 us (9%)
  local copies, waits for them, and re-layouts  8.1 us (5%)
    ppermute x10, starting transfers between devices, take_by_core(): lax.ppermute(x, AXES, pairs([m and (0, *m, 0) for m in (on_y, on_z)]))  22.3 us
    ppermute x9, starting transfers between devices, take(): return lax.ppermute(x, AXES, pairs([(dc, dy, dz, dx)] * 2, wrap_x))  19.2 us
    ppermute x10, waiting for transfers between devices, take_by_core(): lax.ppermute(x, AXES, pairs([m and (0, *m, 0) for m in (on_y, on_z)]))  17.7 us
    all_to_all x1, blocking collectives, shards(): lax.all_to_all(partial, ('zh', 'zl'), 0, 0, axis_index_groups=GROUPS)  15.4 us
    pallas_call x1, Pallas kernels, project(): pl.pallas_call(qkv_kernel, grid_spec=pltpu.PrefetchScalarGridSpec(num_sca...  10.1 us
    all_to_all x1, waiting for transfers between devices, shards(): heads = lax.all_to_all(heads_out, ('y', 'zl'), 0, 0)  8.6 us
    reduce_sum x8, other arithmetic, shards(): jnp.sum(jnp.square(a.astype(jnp.float32)), axis=(0, 2))  8.33 us
    ppermute x9, waiting for transfers between devices, take(): return lax.ppermute(x, AXES, pairs([(dc, dy, dz, dx)] * 2, wrap_x))  5.6 us
  transfers between devices with their start and end apart: 22, of which 13 were waited for; matrix products, arithmetic and copies ran while one was open for 10% of the time, Pallas kernels for 11%

profile of v9, /device:TPU:1, one launch (start us, length us, event | category | flops | bytes accessed | tf_op | source)
XLA Modules:
  0.0 155.1 jit_solution(1718742542076758044)
XLA Ops:
  6.5 6.8 %collective-permute-start = (bf16[512,128]{1,0:T(8,128)(2,1)}, bf16[512,128]{1,0:T(8,128)(2,1)S(1)}, u32[]{:S(2)}, u32[]{:S(2)}) collective-permute-start(bf16[512,128]{1,0:T(8,128)(2,1)} %param.10), channel_id=1, source_target_pairs={{32,0},{33,1},{34,2},{35,3},{36,4},{37,5},{38,6},{39,7},{40,8},{41... | collective-permute-start | bytes 393224 | tf_op jit(solution)/shard_map/ppermute | solution.py:43
  13.4 3.3 %collective-permute-start.2 = (bf16[512,128]{1,0:T(8,128)(2,1)}, bf16[512,128]{1,0:T(8,128)(2,1)S(1)}, u32[]{:S(2)}, u32[]{:S(2)}) collective-permute-start(bf16[512,128]{1,0:T(8,128)(2,1)} %param.10), channel_id=1, source_target_pairs={{64,0},{65,1},{66,2},{67,3},{68,4},{69,5},{70,6},{71,7},{72,8},{73... | collective-permute-start | bytes 393224 | tf_op jit(solution)/shard_map/ppermute | solution.py:43
  17.2 2.6 %shard_map.100 = bf16[8,4,32,256]{3,2,1,0:T(8,128)(2,1)} custom-call(s32[4]{0:T(128)} %pad_add_fusion.at_ref, bf16[128,8192]{1,0:T(8,128)(2,1)} %bitcast.43), custom_call_target="tpu_custom_call" | custom-call | bytes 1048576 | tf_op jit(solution)/shard_map/pallas_call | solution.py:274
  19.9 1.4 collective-permute-done.1
  22.0 1.8 %multiply_reduce_fusion.7 = (f32[512]{0:T(512)S(1)}, bf16[4,512,128]{2,1,0:T(8,128)(2,1)}) fusion(bf16[1,512,128]{2,1,0:T(8,128)(2,1)S(1)} %bitcast.51, bf16[1,512,128]{2,1,0:T(8,128)(2,1)S(1)} %bitcast.50, bf16[1,512,128]{2,1,0:T(8,128)(2,1)S(1)} %bitcast.49, bf16[1,512,128]{2,1,0:T(8,128)(2,1)} %bitcast.48), kind=kLoop, calls=%fused_computation.7 | loop fusion | flops 1572352 | bytes 1050624 | tf_op jit(solution)/shard_map/reduce_sum | solution.py:319
  23.8 2.5 %collective-permute-start.3 = (bf16[4,512,128]{2,1,0:T(8,128)(2,1)}, bf16[4,512,128]{2,1,0:T(8,128)(2,1)}, u32[]{:S(2)}, u32[]{:S(2)}) collective-permute-start(bf16[4,512,128]{2,1,0:T(8,128)(2,1)} %get-tuple-element.24.rest_16_), channel_id=1, source_target_pairs={{4,0},{5,1},{6,2},{7,3},{8,4},{9,5},{10,6},{11,7},{12,8},{13,9},{1... | collective-permute-start | bytes 1572872 | tf_op jit(solution)/shard_map/ppermute | solution.py:43
  26.3 5.0 %all-to-all-start = ((bf16[8,4,32,256]{3,2,1,0:T(8,128)(2,1)}), bf16[8,4,32,256]{3,2,1,0:T(8,128)(2,1)}, u32[]{:S(2)}, u32[]{:S(2)}) async-start(bf16[8,4,32,256]{3,2,1,0:T(8,128)(2,1)} %shard_map.100), calls=%async_computation | async-start | bytes 1048576 | tf_op jit(solution)/shard_map/all_to_all | solution.py:288
  31.3 1.4 collective-permute-start.5
  32.8 1.5 collective-permute-done.3.rest_17_
  34.3 2.8 %collective-permute-start.4 = (bf16[4,512,128]{2,1,0:T(8,128)(2,1)}, bf16[4,512,128]{2,1,0:T(8,128)(2,1)}, u32[]{:S(2)}, u32[]{:S(2)}) collective-permute-start(bf16[4,512,128]{2,1,0:T(8,128)(2,1)} %collective-permute-done.3.rest_17_), channel_id=1, source_target_pairs={{4,0},{5,1},{6,2},{7,3},{8,4},{9,5},{10,6},{11,7},{12,8},{13,9},{1... | collective-permute-start | bytes 1572872 | tf_op jit(solution)/shard_map/ppermute | solution.py:43
  37.1 2.2 %constant_dynamic-slice_fusion.2 = bf16[3,1,4,8,128,128]{5,4,3,2,1,0:T(8,128)(2,1)S(1)} fusion(bf16[3,2,4,8,128,128]{5,4,3,2,1,0:T(8,128)(2,1)} %bitcast.34, s32[]{:T(128)S(6)} %select_n.55), kind=kLoop, calls=%fused_computation.20 | loop fusion | bytes 6291460 | tf_op jit(solution)/shard_map/dynamic_slice | solution.py:314
  39.5 6.7 %collective-permute-done.5.rest_19_ = bf16[4,512,128]{2,1,0:T(8,128)(2,1)} collective-permute-done((bf16[4,512,128]{2,1,0:T(8,128)(2,1)}, bf16[4,512,128]{2,1,0:T(8,128)(2,1)}, u32[]{:S(2)}, u32[]{:S(2)}) %collective-permute-start.5) | collective-permute-done | bytes 524320 | tf_op jit(solution)/shard_map/ppermute | solution.py:43
  48.1 2.1 %collective-permute-start.7 = (bf16[4,512,128]{2,1,0:T(8,128)(2,1)}, bf16[4,512,128]{2,1,0:T(8,128)(2,1)}, u32[]{:S(2)}, u32[]{:S(2)}) collective-permute-start(bf16[4,512,128]{2,1,0:T(8,128)(2,1)} %collective-permute-done.4.rest_18_), channel_id=1, source_target_pairs={{4,0},{5,1},{6,2},{7,3},{8,4},{9,5},{10,6},{11,7},{12,8},{13,9},{1... | collective-permute-start | bytes 1572872 | tf_op jit(solution)/shard_map/ppermute | solution.py:43
  52.7 4.7 %collective-permute-done.8.rest_21_ = bf16[4,512,128]{2,1,0:T(8,128)(2,1)} collective-permute-done((bf16[4,512,128]{2,1,0:T(8,128)(2,1)}, bf16[4,512,128]{2,1,0:T(8,128)(2,1)}, u32[]{:S(2)}, u32[]{:S(2)}) %collective-permute-start.8) | collective-permute-done | bytes 524320 | tf_op jit(solution)/shard_map/ppermute | solution.py:43
  57.4 1.3 multiply_reduce_fusion.6
  58.7 2.7 %collective-permute-start.9 = (bf16[4,512,128]{2,1,0:T(8,128)(2,1)}, bf16[4,512,128]{2,1,0:T(8,128)(2,1)S(1)}, u32[]{:S(2)}, u32[]{:S(2)}) collective-permute-start(bf16[4,512,128]{2,1,0:T(8,128)(2,1)} %collective-permute-done.7.rest_20_), channel_id=1, source_target_pairs={{4,0},{5,1},{6,2},{7,3},{8,4},{9,5},{10,6},{11,7},{12,8},{13,9},{1... | collective-permute-start | bytes 1572872 | tf_op jit(solution)/shard_map/ppermute | solution.py:43
  65.1 2.2 %collective-permute-done.10.rest_23_ = bf16[4,512,128]{2,1,0:T(8,128)(2,1)S(1)} collective-permute-done((bf16[4,512,128]{2,1,0:T(8,128)(2,1)}, bf16[4,512,128]{2,1,0:T(8,128)(2,1)S(1)}, u32[]{:S(2)}, u32[]{:S(2)}) %collective-permute-start.10) | collective-permute-done | bytes 524320 | tf_op jit(solution)/shard_map/ppermute | solution.py:43
  68.1 1.9 %collective-permute-start.11 = (f32[1,4608]{1,0:T(1,128)S(1)}, f32[1,4608]{1,0:T(1,128)S(1)}, u32[]{:S(2)}, u32[]{:S(2)}) collective-permute-start(f32[1,4608]{1,0:T(1,128)S(1)} %pad_maximum_fusion.4.row_ref), channel_id=1, source_target_pairs={{128,0},{129,1},{130,2},{131,3},{132,4},{133,5},{134,6},{135,7},{1... | collective-permute-start | bytes 55304 | tf_op jit(solution)/shard_map/ppermute | solution.py:39
  71.4 10.1 %shard_map.101 = (f32[256,384]{1,0:T(8,128)}, f32[256,384]{1,0:T(8,128)}) custom-call(s32[4]{0:T(128)} %pad_add_fusion.at_ref, s32[32]{0:T(128)} %get-tuple-element.32.y_ref, s32[32]{0:T(128)} %get-tuple-element.33.z_ref, f32[1,4608]{1,0:T(1,128)} %copy-done.6, f32[1,4608]{1,0:T(1,128)} %copy-done.8, s32[1,512]{1,0:T(1,128)} %bitcast.59, ...), custom_call_target="tpu_custom_call" | custom-call | flops 3221225472 | bytes 11534336 | tf_op jit(solution)/shard_map/pallas_call | solution.py:129
  84.3 2.3 %shard_map.102 = (bf16[256,128]{1,0:T(8,128)(2,1)}, bf16[2,256,128]{2,1,0:T(8,128)(2,1)}) custom-call(f32[256,384]{1,0:T(8,128)} %get-tuple-element.19.mine_ref, f32[256,384]{1,0:T(8,128)} %copy-done.5, f32[2,128]{1,0:T(2,128)} %gain_ref.1, f32[256,128]{1,0:T(8,128)} %get-tuple-element.34.cos_ref, f32[256,128]{1,0:T(8,128)} %get-tuple-element.35.sin_ref), custom_call_target="tpu_custom_call" | custom-call | tf_op jit(solution)/shard_map/pallas_call | solution.py:168
  86.6 3.1 %collective-permute-start.14 = (bf16[2,256,128]{2,1,0:T(8,128)(2,1)}, bf16[2,256,128]{2,1,0:T(8,128)(2,1)S(1)}, u32[]{:S(2)}, u32[]{:S(2)}) collective-permute-start(bf16[2,256,128]{2,1,0:T(8,128)(2,1)} %get-tuple-element.22), channel_id=1, source_target_pairs={{0,1},{1,2},{2,3},{4,5},{5,6},{6,7},{8,9},{9,10},{10,11},{12,13},{... | collective-permute-start | bytes 393224 | tf_op jit(solution)/shard_map/ppermute | solution.py:39
  89.7 4.3 %collective-permute-start.15 = (bf16[2,256,128]{2,1,0:T(8,128)(2,1)}, bf16[2,256,128]{2,1,0:T(8,128)(2,1)S(1)}, u32[]{:S(2)}, u32[]{:S(2)}) collective-permute-start(bf16[2,256,128]{2,1,0:T(8,128)(2,1)} %get-tuple-element.22), channel_id=1, source_target_pairs={{0,2},{1,3},{4,6},{5,7},{8,10},{9,11},{12,14},{13,15},{16,18},{17,... | collective-permute-start | bytes 393224 | tf_op jit(solution)/shard_map/ppermute | solution.py:39
  94.1 1.3 collective-permute-start.16
  96.6 1.3 collective-permute-done.16
  98.8 1.6 %collective-permute-start.17 = (bf16[4,2,256,128]{3,2,1,0:T(8,128)(2,1)S(1)}, bf16[4,2,256,128]{3,2,1,0:T(8,128)(2,1)S(1)}, u32[]{:S(2)}, u32[]{:S(2)}) collective-permute-start(bf16[4,2,256,128]{3,2,1,0:T(8,128)(2,1)S(1)} %pad_maximum_fusion.1.rest_0_), channel_id=1, source_target_pairs={{128,0},{129,1},{130,2},{131,3},{132,4},{133,5},{134,6},{135,7},{1... | collective-permute-start | bytes 1572872 | tf_op jit(solution)/shard_map/ppermute | solution.py:39
  100.5 1.5 collective-permute-done.17.rest_1_
  102.8 2.5 %shard_map.103 = bf16[8,256,128]{2,1,0:T(8,128)(2,1)} custom-call(s32[8]{0:T(128)S(1)} %stack.90.base_ref, bf16[256,128]{1,0:T(8,128)(2,1)S(1)} %copy-done, bf16[4,2,256,128]{3,2,1,0:T(8,128)(2,1)S(1)} %pad_maximum_fusion.1.rest_0_, bf16[4,2,256,128]{3,2,1,0:T(8,128)(2,1)S(1)} %collective-permute-done.17.rest_1_), custom_call_target="tpu_custom_call" | custom-call | flops 268435456 | bytes 1048576 | tf_op jit(solution)/shard_map/pallas_call | solution.py:209
  105.3 4.3 %all-to-all-start.1 = ((bf16[8,256,128]{2,1,0:T(8,128)(2,1)}), bf16[8,256,128]{2,1,0:T(8,128)(2,1)S(1)}, u32[]{:S(2)}, u32[]{:S(2)}) async-start(bf16[8,256,128]{2,1,0:T(8,128)(2,1)} %shard_map.103), calls=%async_computation.1 | async-start | bytes 1048576 | tf_op jit(solution)/shard_map/all_to_all | solution.py:332
  110.2 8.6 %all-to-all-done.1.heads_ref = bf16[8,256,128]{2,1,0:T(8,128)(2,1)S(1)} async-done(((bf16[8,256,128]{2,1,0:T(8,128)(2,1)}), bf16[8,256,128]{2,1,0:T(8,128)(2,1)S(1)}, u32[]{:S(2)}, u32[]{:S(2)}) %all-to-all-start.1) | async-done | bytes 524320 | tf_op jit(solution)/shard_map/all_to_all | solution.py:332
  120.3 4.5 %shard_map.104 = bf16[4,256,256]{2,1,0:T(8,128)(2,1)} custom-call(s32[4]{0:T(128)} %pad_add_fusion.at_ref, s32[1,256]{1,0:T(1,128)} %bitcast.60, bf16[4,8,4,32,256]{4,3,2,1,0:T(8,128)(2,1)} %bitcast.45, bf16[4,8,4,32,256]{4,3,2,1,0:T(8,128)(2,1)} %copy-done.4, bf16[8,256,128]{2,1,0:T(8,128)(2,1)} %copy-done.3), custom_call_target="tpu_custom_call" | custom-call | flops 1073741824 | bytes 5242880 | tf_op jit(solution)/shard_map/pallas_call | solution.py:241
  124.8 15.4 %all_to_all.15 = bf16[4,256,256]{2,1,0:T(8,128)(2,1)S(1)} all-to-all(bf16[4,256,256]{2,1,0:T(8,128)(2,1)} %shard_map.104), channel_id=1, replica_groups={{0,8,20,28},{4,12,16,24},{1,9,21,29},{5,13,17,25},{2,10,22,30},{6,14,18..., dimensions={0} | all-to-all | bytes 1048576 | tf_op jit(solution)/shard_map/all_to_all | solution.py:335
  140.5 6.1 %collective-permute-start.18 = (bf16[256,128]{1,0:T(8,128)(2,1)S(1)}, bf16[256,128]{1,0:T(8,128)(2,1)S(1)}, u32[]{:S(2)}, u32[]{:S(2)}) collective-permute-start(bf16[256,128]{1,0:T(8,128)(2,1)S(1)} %bitcast.57), channel_id=1, source_target_pairs={{128,0},{129,1},{130,2},{131,3},{132,4},{133,5},{134,6},{135,7},{1... | collective-permute-start | bytes 196616 | tf_op jit(solution)/shard_map/ppermute | solution.py:39
  (77 shorter events, 21.8 us)
Async XLA Ops:
  6.5 13.3 %collective-permute-start = (bf16[512,128]{1,0:T(8,128)(2,1)}, bf16[512,128]{1,0:T(8,128)(2,1)S(1)}, u32[]{:S(2)}, u32[]{:S(2)}) collective-permute-start(bf16[512,128]{1,0:T(8,128)(2,1)} %param.10), channel_id=1, source_target_pairs={{32,0},{33,1},{34,2},{35,3},{36,4},{37,5},{38,6},{39,7},{40,8},{41... | collective-permute-start | bytes 393224 | tf_op jit(solution)/shard_map/ppermute | solution.py:43
  13.4 7.9 %collective-permute-start.1 = (bf16[512,128]{1,0:T(8,128)(2,1)}, bf16[512,128]{1,0:T(8,128)(2,1)S(1)}, u32[]{:S(2)}, u32[]{:S(2)}) collective-permute-start(bf16[512,128]{1,0:T(8,128)(2,1)} %param.10), channel_id=1, source_target_pairs={{96,0},{97,1},{98,2},{99,3},{100,4},{101,5},{102,6},{103,7},{104,8... | collective-permute-start | bytes 393224 | tf_op jit(solution)/shard_map/ppermute | solution.py:43
  13.4 8.6 %collective-permute-start.2 = (bf16[512,128]{1,0:T(8,128)(2,1)}, bf16[512,128]{1,0:T(8,128)(2,1)S(1)}, u32[]{:S(2)}, u32[]{:S(2)}) collective-permute-start(bf16[512,128]{1,0:T(8,128)(2,1)} %param.10), channel_id=1, source_target_pairs={{64,0},{65,1},{66,2},{67,3},{68,4},{69,5},{70,6},{71,7},{72,8},{73... | collective-permute-start | bytes 393224 | tf_op jit(solution)/shard_map/ppermute | solution.py:43
  23.8 10.4 %collective-permute-start.3 = (bf16[4,512,128]{2,1,0:T(8,128)(2,1)}, bf16[4,512,128]{2,1,0:T(8,128)(2,1)}, u32[]{:S(2)}, u32[]{:S(2)}) collective-permute-start(bf16[4,512,128]{2,1,0:T(8,128)(2,1)} %get-tuple-element.24.rest_16_), channel_id=1, source_target_pairs={{4,0},{5,1},{6,2},{7,3},{8,4},{9,5},{10,6},{11,7},{12,8},{13,9},{1... | collective-permute-start | bytes 1572872 | tf_op jit(solution)/shard_map/ppermute | solution.py:43
  26.3 19.9 %all-to-all-start = ((bf16[8,4,32,256]{3,2,1,0:T(8,128)(2,1)}), bf16[8,4,32,256]{3,2,1,0:T(8,128)(2,1)}, u32[]{:S(2)}, u32[]{:S(2)}) async-start(bf16[8,4,32,256]{3,2,1,0:T(8,128)(2,1)} %shard_map.100), calls=%async_computation | async-start | bytes 1048576 | tf_op jit(solution)/shard_map/all_to_all | solution.py:288
  31.3 50.7 %all-gather.3.cloned.1.call-start = ((), (), s32[]{:S(2)}) async-start(), calls=%async_computation.3 | async-start | bytes 2621440 | tf_op jit(solution)/shard_map/all_gather | solution.py:290
  31.3 14.9 %collective-permute-start.5 = (bf16[4,512,128]{2,1,0:T(8,128)(2,1)}, bf16[4,512,128]{2,1,0:T(8,128)(2,1)}, u32[]{:S(2)}, u32[]{:S(2)}) collective-permute-start(bf16[4,512,128]{2,1,0:T(8,128)(2,1)} %get-tuple-element.24.rest_16_), channel_id=1, source_target_pairs={{28,0},{29,1},{30,2},{31,3},{0,4},{1,5},{2,6},{3,7},{4,8},{5,9},{6... | collective-permute-start | bytes 1572872 | tf_op jit(solution)/shard_map/ppermute | solution.py:43
  34.3 12.0 %collective-permute-start.4 = (bf16[4,512,128]{2,1,0:T(8,128)(2,1)}, bf16[4,512,128]{2,1,0:T(8,128)(2,1)}, u32[]{:S(2)}, u32[]{:S(2)}) collective-permute-start(bf16[4,512,128]{2,1,0:T(8,128)(2,1)} %collective-permute-done.3.rest_17_), channel_id=1, source_target_pairs={{4,0},{5,1},{6,2},{7,3},{8,4},{9,5},{10,6},{11,7},{12,8},{13,9},{1... | collective-permute-start | bytes 1572872 | tf_op jit(solution)/shard_map/ppermute | solution.py:43
  37.1 9.7 %copy-start.7 = (f32[1,8192]{1,0:T(1,128)S(1)}, f32[1,8192]{1,0:T(1,128)}, u32[]{:S(2)}) copy-start(f32[1,8192]{1,0:T(1,128)} %param.12) | copy-start | bytes 98308
  37.1 13.8 %copy-start.10 = (s32[32]{0:T(128)S(1)}, s32[32]{0:T(128)}, u32[]{:S(2)}) copy-start(s32[32]{0:T(128)} %constant.67.clone) | copy-start | bytes 388
  37.1 13.8 %copy-start.11 = (s32[32]{0:T(128)S(1)}, s32[32]{0:T(128)}, u32[]{:S(2)}) copy-start(s32[32]{0:T(128)} %constant.68.clone) | copy-start | bytes 388
  37.1 13.8 %copy-start.12 = (s32[32]{0:T(128)S(1)}, s32[32]{0:T(128)}, u32[]{:S(2)}) copy-start(s32[32]{0:T(128)} %constant.69.clone) | copy-start | bytes 388
  37.1 13.8 %copy-start.13 = (s32[32]{0:T(128)S(1)}, s32[32]{0:T(128)}, u32[]{:S(2)}) copy-start(s32[32]{0:T(128)} %constant.70.clone) | copy-start | bytes 388
  39.2 31.6 %collective-permute-start.12 = (bf16[3,1,4,8,128,128]{5,4,3,2,1,0:T(8,128)(2,1)S(1)}, bf16[3,1,4,8,128,128]{5,4,3,2,1,0:T(8,128)(2,1)}, u32[]{:S(2)}, u32[]{:S(2)}) collective-permute-start(bf16[3,1,4,8,128,128]{5,4,3,2,1,0:T(8,128)(2,1)S(1)} %constant_dynamic-slice_fusion.2), channel_id=1, source_target_pairs={{128,0},{129,1},{130,2},{131,3},{132,4},{133,5},{134,6},{135,7},{1... | collective-permute-start | bytes 9437192 | tf_op jit(solution)/shard_map/ppermute | solution.py:39
  47.5 9.9 %collective-permute-start.8 = (bf16[4,512,128]{2,1,0:T(8,128)(2,1)}, bf16[4,512,128]{2,1,0:T(8,128)(2,1)}, u32[]{:S(2)}, u32[]{:S(2)}) collective-permute-start(bf16[4,512,128]{2,1,0:T(8,128)(2,1)} %collective-permute-done.5.rest_19_), channel_id=1, source_target_pairs={{28,0},{29,1},{30,2},{31,3},{0,4},{1,5},{2,6},{3,7},{4,8},{5,9},{6... | collective-permute-start | bytes 1572872 | tf_op jit(solution)/shard_map/ppermute | solution.py:43
  48.1 10.6 %collective-permute-start.7 = (bf16[4,512,128]{2,1,0:T(8,128)(2,1)}, bf16[4,512,128]{2,1,0:T(8,128)(2,1)}, u32[]{:S(2)}, u32[]{:S(2)}) collective-permute-start(bf16[4,512,128]{2,1,0:T(8,128)(2,1)} %collective-permute-done.4.rest_18_), channel_id=1, source_target_pairs={{4,0},{5,1},{6,2},{7,3},{8,4},{9,5},{10,6},{11,7},{12,8},{13,9},{1... | collective-permute-start | bytes 1572872 | tf_op jit(solution)/shard_map/ppermute | solution.py:43
  57.4 9.9 %collective-permute-start.10 = (bf16[4,512,128]{2,1,0:T(8,128)(2,1)}, bf16[4,512,128]{2,1,0:T(8,128)(2,1)S(1)}, u32[]{:S(2)}, u32[]{:S(2)}) collective-permute-start(bf16[4,512,128]{2,1,0:T(8,128)(2,1)} %collective-permute-done.8.rest_21_), channel_id=1, source_target_pairs={{28,0},{29,1},{30,2},{31,3},{0,4},{1,5},{2,6},{3,7},{4,8},{5,9},{6... | collective-permute-start | bytes 1572872 | tf_op jit(solution)/shard_map/ppermute | solution.py:43
  58.7 9.2 %collective-permute-start.9 = (bf16[4,512,128]{2,1,0:T(8,128)(2,1)}, bf16[4,512,128]{2,1,0:T(8,128)(2,1)S(1)}, u32[]{:S(2)}, u32[]{:S(2)}) collective-permute-start(bf16[4,512,128]{2,1,0:T(8,128)(2,1)} %collective-permute-done.7.rest_20_), channel_id=1, source_target_pairs={{4,0},{5,1},{6,2},{7,3},{8,4},{9,5},{10,6},{11,7},{12,8},{13,9},{1... | collective-permute-start | bytes 1572872 | tf_op jit(solution)/shard_map/ppermute | solution.py:43
  67.3 3.6 %copy-start.1 = (bf16[4,512,128]{2,1,0:T(8,128)(2,1)}, bf16[4,512,128]{2,1,0:T(8,128)(2,1)S(1)}, u32[]{:S(2)}) copy-start(bf16[4,512,128]{2,1,0:T(8,128)(2,1)S(1)} %collective-permute-done.10.rest_23_) | copy-start | bytes 1572868
  67.9 3.0 %copy-start.2 = (bf16[4,512,128]{2,1,0:T(8,128)(2,1)}, bf16[4,512,128]{2,1,0:T(8,128)(2,1)S(1)}, u32[]{:S(2)}) copy-start(bf16[4,512,128]{2,1,0:T(8,128)(2,1)S(1)} %collective-permute-done.9.rest_22_) | copy-start | bytes 1572868
  68.1 2.8 %copy-start.6 = (f32[1,4608]{1,0:T(1,128)}, f32[1,4608]{1,0:T(1,128)S(1)}, u32[]{:S(2)}) copy-start(f32[1,4608]{1,0:T(1,128)S(1)} %pad_maximum_fusion.4.row_ref) | copy-start | bytes 55300
  68.1 2.7 %collective-permute-start.11 = (f32[1,4608]{1,0:T(1,128)S(1)}, f32[1,4608]{1,0:T(1,128)S(1)}, u32[]{:S(2)}, u32[]{:S(2)}) collective-permute-start(f32[1,4608]{1,0:T(1,128)S(1)} %pad_maximum_fusion.4.row_ref), channel_id=1, source_target_pairs={{128,0},{129,1},{130,2},{131,3},{132,4},{133,5},{134,6},{135,7},{1... | collective-permute-start | bytes 55304 | tf_op jit(solution)/shard_map/ppermute | solution.py:39
  81.5 28.0 %copy-start.9 = (s32[512]{0:T(512)S(1)}, s32[512]{0:T(512)}, u32[]{:S(2)}) copy-start(s32[512]{0:T(512)} %param.11) | copy-start | bytes 6148
  81.5 2.0 %collective-permute-start.13 = (f32[256,384]{1,0:T(8,128)}, f32[256,384]{1,0:T(8,128)S(1)}, u32[]{:S(2)}, u32[]{:S(2)}) collective-permute-start(f32[256,384]{1,0:T(8,128)} %get-tuple-element.20), channel_id=1, source_target_pairs={{128,0},{129,1},{130,2},{131,3},{132,4},{133,5},{134,6},{135,7},{1... | collective-permute-start | bytes 1179656 | tf_op jit(solution)/shard_map/ppermute | solution.py:39
  82.0 36.8 %collective-permute-start.6 = (bf16[4,8,4,32,256]{4,3,2,1,0:T(8,128)(2,1)}, bf16[4,8,4,32,256]{4,3,2,1,0:T(8,128)(2,1)S(1)}, u32[]{:S(2)}, u32[]{:S(2)}) collective-permute-start(bf16[4,8,4,32,256]{4,3,2,1,0:T(8,128)(2,1)} %bitcast.44), channel_id=1, source_target_pairs={{128,0},{129,1},{130,2},{131,3},{132,4},{133,5},{134,6},{135,7},{1... | collective-permute-start | bytes 6291464 | tf_op jit(solution)/shard_map/ppermute | solution.py:39
  86.6 8.8 %collective-permute-start.14 = (bf16[2,256,128]{2,1,0:T(8,128)(2,1)}, bf16[2,256,128]{2,1,0:T(8,128)(2,1)S(1)}, u32[]{:S(2)}, u32[]{:S(2)}) collective-permute-start(bf16[2,256,128]{2,1,0:T(8,128)(2,1)} %get-tuple-element.22), channel_id=1, source_target_pairs={{0,1},{1,2},{2,3},{4,5},{5,6},{6,7},{8,9},{9,10},{10,11},{12,13},{... | collective-permute-start | bytes 393224 | tf_op jit(solution)/shard_map/ppermute | solution.py:39
  89.7 6.8 %collective-permute-start.15 = (bf16[2,256,128]{2,1,0:T(8,128)(2,1)}, bf16[2,256,128]{2,1,0:T(8,128)(2,1)S(1)}, u32[]{:S(2)}, u32[]{:S(2)}) collective-permute-start(bf16[2,256,128]{2,1,0:T(8,128)(2,1)} %get-tuple-element.22), channel_id=1, source_target_pairs={{0,2},{1,3},{4,6},{5,7},{8,10},{9,11},{12,14},{13,15},{16,18},{17,... | collective-permute-start | bytes 393224 | tf_op jit(solution)/shard_map/ppermute | solution.py:39
  94.1 3.8 %collective-permute-start.16 = (bf16[2,256,128]{2,1,0:T(8,128)(2,1)}, bf16[2,256,128]{2,1,0:T(8,128)(2,1)S(1)}, u32[]{:S(2)}, u32[]{:S(2)}) collective-permute-start(bf16[2,256,128]{2,1,0:T(8,128)(2,1)} %get-tuple-element.22), channel_id=1, source_target_pairs={{0,3},{4,7},{8,11},{12,15},{16,19},{20,23},{24,27},{28,31},{32,35}... | collective-permute-start | bytes 393224 | tf_op jit(solution)/shard_map/ppermute | solution.py:39
  98.8 3.1 %collective-permute-start.17 = (bf16[4,2,256,128]{3,2,1,0:T(8,128)(2,1)S(1)}, bf16[4,2,256,128]{3,2,1,0:T(8,128)(2,1)S(1)}, u32[]{:S(2)}, u32[]{:S(2)}) collective-permute-start(bf16[4,2,256,128]{3,2,1,0:T(8,128)(2,1)S(1)} %pad_maximum_fusion.1.rest_0_), channel_id=1, source_target_pairs={{128,0},{129,1},{130,2},{131,3},{132,4},{133,5},{134,6},{135,7},{1... | collective-permute-start | bytes 1572872 | tf_op jit(solution)/shard_map/ppermute | solution.py:39
  105.3 13.5 %all-to-all-start.1 = ((bf16[8,256,128]{2,1,0:T(8,128)(2,1)}), bf16[8,256,128]{2,1,0:T(8,128)(2,1)S(1)}, u32[]{:S(2)}, u32[]{:S(2)}) async-start(bf16[8,256,128]{2,1,0:T(8,128)(2,1)} %shard_map.103), calls=%async_computation.1 | async-start | bytes 1048576 | tf_op jit(solution)/shard_map/all_to_all | solution.py:332
  118.8 1.5 copy-start.4
  140.5 7.0 %collective-permute-start.18 = (bf16[256,128]{1,0:T(8,128)(2,1)S(1)}, bf16[256,128]{1,0:T(8,128)(2,1)S(1)}, u32[]{:S(2)}, u32[]{:S(2)}) collective-permute-start(bf16[256,128]{1,0:T(8,128)(2,1)S(1)} %bitcast.57), channel_id=1, source_target_pairs={{128,0},{129,1},{130,2},{131,3},{132,4},{133,5},{134,6},{135,7},{1... | collective-permute-start | bytes 196616 | tf_op jit(solution)/shard_map/ppermute | solution.py:39
  (4 other events, 3.0 us)
Sparse Core Ops, SparseCore 0:
  46.4 32.3 all-gather.2

commit v10 on v9

--- a/solution.py
+++ b/solution.py
@@ -158,8 +158,10 @@
         swapped = jnp.concatenate([x[:, half:], x[:, :half]], axis=1)
         turned.append((x * cos_ref[...] + swapped * sin_ref[...]).astype(jnp.bfloat16))
     q_ref[...] = turned[0]
-    kv_ref[0] = turned[1]
-    kv_ref[1] = projected[:, 2 * HD :].astype(jnp.bfloat16)
+    values = projected[:, 2 * HD :].astype(jnp.bfloat16)
+    for x in range(NX):
+        kv_ref[x, 0] = turned[1]
+        kv_ref[x, 1] = values
 
 
 def finish(mine, got, qk_gain, cosines, sines):
@@ -171,7 +173,7 @@
         out_specs=[vmem] * 2,
         out_shape=[
             jax.ShapeDtypeStruct((rows, HD), jnp.bfloat16),
-            jax.ShapeDtypeStruct((2, rows, HD), jnp.bfloat16),
+            jax.ShapeDtypeStruct((NX, 2, rows, HD), jnp.bfloat16),
         ],
     )(mine, got, qk_gain, cosines, sines)
 
@@ -181,7 +183,7 @@
     rows = q_ref.shape[0]
     queries = q_ref[...]
     scale = 1.0 / math.sqrt(HD)
-    row = base_ref[0] + lax.broadcasted_iota(jnp.int32, (rows, rows), 0)
+    row = base_ref[2 * NX] + lax.broadcasted_iota(jnp.int32, (rows, rows), 0)
     column = lax.broadcasted_iota(jnp.int32, (rows, rows), 1)
     blocks = [(ref, i) for ref in key_refs for i in range(ref.shape[0])]
     scores, seen = [], []
@@ -299,7 +301,9 @@
     modality = modality[None, :]
     ys, zs = piece_places(c.astype(jnp.int32), y.astype(jnp.int32), z.astype(jnp.int32))
 
-    arrays, pieces = gather(tokens, cut_w_out(at, w_out[0]))
+    w = w_qkv[0].transpose(1, 0, 2).reshape(3, 2, NY, NZ, HD, HD)
+    w_send = lax.dynamic_slice_in_dim(w, 1 - c, 1, axis=1)
+    arrays, (pieces, w_send) = gather(tokens, (cut_w_out(at, w_out[0]), w_send))
     w_cols = spread_w_out(pieces, arrays[2], arrays[3])
     w_cols_other = take(w_cols, dc=1)
 
@@ -310,8 +314,7 @@
     cosines, sines = jnp.cos(angles), jnp.sin(angles)
     cosines, sines = jnp.concatenate([cosines, cosines], axis=1), jnp.concatenate([-sines, sines], axis=1)
 
-    w = w_qkv[0].transpose(1, 0, 2).reshape(3, 2, NY, NZ, HD, HD)
-    w_other = take(lax.dynamic_slice_in_dim(w, 1 - c, 1, axis=1), dc=1)
+    w_other = take(w_send, dc=1)
     gains = norm_gain.reshape(2, NY * NZ * HD)
     gain_send = lax.dynamic_slice_in_dim(gains, 1 - c, 1, axis=0)
     gain = lax.dynamic_slice_in_dim(gains, c, 1, axis=0).reshape(NY, NZ, HD)
@@ -321,12 +324,10 @@
     mine, theirs = project(at, ys, zs, row, take(row, dc=1), modality, gain, w, w_other, arrays)
     queries, own_keys = finish(mine, take(theirs, dc=1), qk_gain, cosines, sines)
 
-    moved = {d: take(own_keys, dx=-d, wrap_x=False) for d in (2, 3, 1)}
-    got = jnp.stack([own_keys] + [moved[d] for d in (1, 2, 3)])
+    got = lax.all_to_all(own_keys, "seq", 0, 0)
     sibling = take(got, dc=1)
-    never = 1 << 20
-    begin = [jnp.where(seq >= d, (seq - d) * row_count, never) for d in range(NX)]
-    bases = jnp.stack([b + c * half for b in begin] + [b + (1 - c) * half for b in begin]).astype(jnp.int32)
+    starts = jnp.concatenate([jnp.arange(NX) * row_count + part * half for part in (c, 1 - c)])
+    bases = jnp.concatenate([starts, first[None]]).astype(jnp.int32)
     heads_out = attention(bases, queries, [got, sibling])
 
     heads = lax.all_to_all(heads_out, ("y", "zl"), 0, 0)

time: 156 us -> 157 us (level)
  blocking collectives: 15.4 us -> 28 us
  starting transfers between devices: 50.8 us -> 42 us
  waiting for transfers between devices: 32 us -> 29 us
    all_to_all x0 -> x1, blocking collectives: none -> 12.6 us  [shards(): got = lax.all_to_all(own_keys, 'seq', 0, 0)]
    ppermute x9 -> x6, starting transfers between devices: 19.2 us -> 10.5 us  [take(): return lax.ppermute(x, AXES, pairs([(dc, dy, dz, dx)] * 2, wrap_x))]
    ppermute x9 -> x6, waiting for transfers between devices: 5.6 us -> 3.08 us  [take(): return lax.ppermute(x, AXES, pairs([(dc, dy, dz, dx)] * 2, wrap_x))]
    unnamed x29 -> x27, local copies, waits for them, and re-layouts: 4.22 us -> 4.27 us
  transfers between devices with their start and end apart: 22 -> 19, of which waited for: 13 -> 9; matrix products, arithmetic and copies ran while one was open for 10% -> 10% of each run, Pallas kernels for 11% -> 11%
where the time goes in v10:
time: 157 us; the launch traced here: 156 us
  starting transfers between devices  42 us (27%)
  waiting for transfers between devices  29 us (18%)
  blocking collectives  28 us (18%)
  Pallas kernels  22.2 us (14%)
  between operations  13.6 us (9%)
  other arithmetic  13 us (8%)
  local copies, waits for them, and re-layouts  8.06 us (5%)
    ppermute x10, starting transfers between devices, take_by_core(): lax.ppermute(x, AXES, pairs([m and (0, *m, 0) for m in (on_y, on_z)]))  22.2 us
    ppermute x10, waiting for transfers between devices, take_by_core(): lax.ppermute(x, AXES, pairs([m and (0, *m, 0) for m in (on_y, on_z)]))  17.3 us
    all_to_all x1, blocking collectives, shards(): lax.all_to_all(partial, ('zh', 'zl'), 0, 0, axis_index_groups=GROUPS)  15.4 us
    all_to_all x1, blocking collectives, shards(): got = lax.all_to_all(own_keys, 'seq', 0, 0)  12.6 us
    ppermute x6, starting transfers between devices, take(): return lax.ppermute(x, AXES, pairs([(dc, dy, dz, dx)] * 2, wrap_x))  10.5 us
    pallas_call x1, Pallas kernels, project(): pl.pallas_call(qkv_kernel, grid_spec=pltpu.PrefetchScalarGridSpec(num_sca...  10.1 us
    all_to_all x1, waiting for transfers between devices, shards(): heads = lax.all_to_all(heads_out, ('y', 'zl'), 0, 0)  8.6 us
    reduce_sum x8, other arithmetic, shards(): jnp.sum(jnp.square(a.astype(jnp.float32)), axis=(0, 2))  7.43 us
  transfers between devices with their start and end apart: 19, of which 9 were waited for; matrix products, arithmetic and copies ran while one was open for 10% of the time, Pallas kernels for 11%

profile of v10, /device:TPU:1, one launch (start us, length us, event | category | flops | bytes accessed | tf_op | source)
XLA Modules:
  0.0 155.8 jit_solution(2576103734461562785)
XLA Ops:
  6.5 6.8 %collective-permute-start = (bf16[512,128]{1,0:T(8,128)(2,1)}, bf16[512,128]{1,0:T(8,128)(2,1)S(1)}, u32[]{:S(2)}, u32[]{:S(2)}) collective-permute-start(bf16[512,128]{1,0:T(8,128)(2,1)} %param.10), channel_id=1, source_target_pairs={{32,0},{33,1},{34,2},{35,3},{36,4},{37,5},{38,6},{39,7},{40,8},{41... | collective-permute-start | bytes 393224 | tf_op jit(solution)/shard_map/ppermute | solution.py:43
  13.4 3.3 %collective-permute-start.2 = (bf16[512,128]{1,0:T(8,128)(2,1)}, bf16[512,128]{1,0:T(8,128)(2,1)S(1)}, u32[]{:S(2)}, u32[]{:S(2)}) collective-permute-start(bf16[512,128]{1,0:T(8,128)(2,1)} %param.10), channel_id=1, source_target_pairs={{64,0},{65,1},{66,2},{67,3},{68,4},{69,5},{70,6},{71,7},{72,8},{73... | collective-permute-start | bytes 393224 | tf_op jit(solution)/shard_map/ppermute | solution.py:43
  17.3 2.6 %shard_map.100 = bf16[8,4,32,256]{3,2,1,0:T(8,128)(2,1)} custom-call(s32[4]{0:T(128)} %pad_add_fusion.at_ref, bf16[128,8192]{1,0:T(8,128)(2,1)} %bitcast.32), custom_call_target="tpu_custom_call" | custom-call | bytes 1048576 | tf_op jit(solution)/shard_map/pallas_call | solution.py:276
  19.9 2.2 %constant_dynamic-slice_fusion.4 = bf16[3,1,4,8,128,128]{5,4,3,2,1,0:T(8,128)(2,1)S(1)} fusion(bf16[3,2,4,8,128,128]{5,4,3,2,1,0:T(8,128)(2,1)} %bitcast.23, s32[]{:T(128)S(6)} %select_n.35), kind=kLoop, calls=%fused_computation.21 | loop fusion | bytes 6291460 | tf_op jit(solution)/shard_map/dynamic_slice | solution.py:305
  23.0 2.4 %collective-permute-start.3 = (bf16[4,512,128]{2,1,0:T(8,128)(2,1)}, bf16[4,512,128]{2,1,0:T(8,128)(2,1)}, u32[]{:S(2)}, u32[]{:S(2)}) collective-permute-start(bf16[4,512,128]{2,1,0:T(8,128)(2,1)} %get-tuple-element.26.rest_16_), channel_id=1, source_target_pairs={{4,0},{5,1},{6,2},{7,3},{8,4},{9,5},{10,6},{11,7},{12,8},{13,9},{1... | collective-permute-start | bytes 1572872 | tf_op jit(solution)/shard_map/ppermute | solution.py:43
  25.4 5.0 %all-to-all-start = ((bf16[8,4,32,256]{3,2,1,0:T(8,128)(2,1)}), bf16[8,4,32,256]{3,2,1,0:T(8,128)(2,1)}, u32[]{:S(2)}, u32[]{:S(2)}) async-start(bf16[8,4,32,256]{3,2,1,0:T(8,128)(2,1)} %shard_map.100), calls=%async_computation | async-start | bytes 1048576 | tf_op jit(solution)/shard_map/all_to_all | solution.py:290
  30.4 1.4 collective-permute-start.5
  31.9 1.6 %collective-permute-done.3.rest_17_ = bf16[4,512,128]{2,1,0:T(8,128)(2,1)} collective-permute-done((bf16[4,512,128]{2,1,0:T(8,128)(2,1)}, bf16[4,512,128]{2,1,0:T(8,128)(2,1)}, u32[]{:S(2)}, u32[]{:S(2)}) %collective-permute-start.3) | collective-permute-done | bytes 524320 | tf_op jit(solution)/shard_map/ppermute | solution.py:43
  33.4 2.8 %collective-permute-start.4 = (bf16[4,512,128]{2,1,0:T(8,128)(2,1)}, bf16[4,512,128]{2,1,0:T(8,128)(2,1)}, u32[]{:S(2)}, u32[]{:S(2)}) collective-permute-start(bf16[4,512,128]{2,1,0:T(8,128)(2,1)} %collective-permute-done.3.rest_17_), channel_id=1, source_target_pairs={{4,0},{5,1},{6,2},{7,3},{8,4},{9,5},{10,6},{11,7},{12,8},{13,9},{1... | collective-permute-start | bytes 1572872 | tf_op jit(solution)/shard_map/ppermute | solution.py:43
  36.3 9.0 %collective-permute-done.5.rest_19_ = bf16[4,512,128]{2,1,0:T(8,128)(2,1)} collective-permute-done((bf16[4,512,128]{2,1,0:T(8,128)(2,1)}, bf16[4,512,128]{2,1,0:T(8,128)(2,1)}, u32[]{:S(2)}, u32[]{:S(2)}) %collective-permute-start.5) | collective-permute-done | bytes 524320 | tf_op jit(solution)/shard_map/ppermute | solution.py:43
  45.9 1.5 reduce.4
  48.1 2.1 %collective-permute-start.7 = (bf16[4,512,128]{2,1,0:T(8,128)(2,1)}, bf16[4,512,128]{2,1,0:T(8,128)(2,1)}, u32[]{:S(2)}, u32[]{:S(2)}) collective-permute-start(bf16[4,512,128]{2,1,0:T(8,128)(2,1)} %collective-permute-done.4.rest_18_), channel_id=1, source_target_pairs={{4,0},{5,1},{6,2},{7,3},{8,4},{9,5},{10,6},{11,7},{12,8},{13,9},{1... | collective-permute-start | bytes 1572872 | tf_op jit(solution)/shard_map/ppermute | solution.py:43
  52.1 1.2 multiply_reduce_fusion.4
  53.3 4.1 %collective-permute-done.8.rest_21_ = bf16[4,512,128]{2,1,0:T(8,128)(2,1)} collective-permute-done((bf16[4,512,128]{2,1,0:T(8,128)(2,1)}, bf16[4,512,128]{2,1,0:T(8,128)(2,1)}, u32[]{:S(2)}, u32[]{:S(2)}) %collective-permute-start.8) | collective-permute-done | bytes 524320 | tf_op jit(solution)/shard_map/ppermute | solution.py:43
  57.4 1.3 multiply_reduce_fusion.6
  58.7 2.7 %collective-permute-start.9 = (bf16[4,512,128]{2,1,0:T(8,128)(2,1)}, bf16[4,512,128]{2,1,0:T(8,128)(2,1)S(1)}, u32[]{:S(2)}, u32[]{:S(2)}) collective-permute-start(bf16[4,512,128]{2,1,0:T(8,128)(2,1)} %collective-permute-done.7.rest_20_), channel_id=1, source_target_pairs={{4,0},{5,1},{6,2},{7,3},{8,4},{9,5},{10,6},{11,7},{12,8},{13,9},{1... | collective-permute-start | bytes 1572872 | tf_op jit(solution)/shard_map/ppermute | solution.py:43
  61.4 1.2 multiply_reduce_fusion.2
  62.6 1.2 multiply_reduce_fusion.5
  63.9 1.2 multiply_reduce_fusion.3
  65.1 2.2 %collective-permute-done.10.rest_23_ = bf16[4,512,128]{2,1,0:T(8,128)(2,1)S(1)} collective-permute-done((bf16[4,512,128]{2,1,0:T(8,128)(2,1)}, bf16[4,512,128]{2,1,0:T(8,128)(2,1)S(1)}, u32[]{:S(2)}, u32[]{:S(2)}) %collective-permute-start.10) | collective-permute-done | bytes 524320 | tf_op jit(solution)/shard_map/ppermute | solution.py:43
  68.1 1.8 %collective-permute-start.11 = (f32[1,4608]{1,0:T(1,128)S(1)}, f32[1,4608]{1,0:T(1,128)S(1)}, u32[]{:S(2)}, u32[]{:S(2)}) collective-permute-start(f32[1,4608]{1,0:T(1,128)S(1)} %pad_maximum_fusion.3.row_ref), channel_id=1, source_target_pairs={{128,0},{129,1},{130,2},{131,3},{132,4},{133,5},{134,6},{135,7},{1... | collective-permute-start | bytes 55304 | tf_op jit(solution)/shard_map/ppermute | solution.py:39
  71.4 10.1 %shard_map.101 = (f32[256,384]{1,0:T(8,128)}, f32[256,384]{1,0:T(8,128)}) custom-call(s32[4]{0:T(128)} %pad_add_fusion.at_ref, s32[32]{0:T(128)} %get-tuple-element.36.y_ref, s32[32]{0:T(128)} %get-tuple-element.37.z_ref, f32[1,4608]{1,0:T(1,128)} %copy-done.7, f32[1,4608]{1,0:T(1,128)} %copy-done.8, s32[1,512]{1,0:T(1,128)} %bitcast.44, ...), custom_call_target="tpu_custom_call" | custom-call | flops 3221225472 | bytes 11534336 | tf_op jit(solution)/shard_map/pallas_call | solution.py:129
  84.3 2.4 %shard_map.102 = (bf16[256,128]{1,0:T(8,128)(2,1)}, bf16[4,2,256,128]{3,2,1,0:T(8,128)(2,1)}) custom-call(f32[256,384]{1,0:T(8,128)} %get-tuple-element.21.mine_ref, f32[256,384]{1,0:T(8,128)} %copy-done.5, f32[2,128]{1,0:T(2,128)} %gain_ref.1, f32[256,128]{1,0:T(8,128)} %get-tuple-element.38.cos_ref, f32[256,128]{1,0:T(8,128)} %get-tuple-element.39.sin_ref), custom_call_target="tpu_custom_call" | custom-call | tf_op jit(solution)/shard_map/pallas_call | solution.py:170
  86.8 12.6 %all_to_all.20.rest_0_ = bf16[4,2,256,128]{3,2,1,0:T(8,128)(2,1)S(1)} all-to-all(bf16[4,2,256,128]{3,2,1,0:T(8,128)(2,1)} %get-tuple-element.24), channel_id=1, replica_groups=mesh['mod'=2,'y'=4,'zh'=4,'zl'=2,'seq'=4] {'seq'}, dimensions={0} | all-to-all | bytes 1048576 | tf_op jit(solution)/shard_map/all_to_all | solution.py:327
  99.4 1.8 %collective-permute-start.14 = (bf16[4,2,256,128]{3,2,1,0:T(8,128)(2,1)S(1)}, bf16[4,2,256,128]{3,2,1,0:T(8,128)(2,1)S(1)}, u32[]{:S(2)}, u32[]{:S(2)}) collective-permute-start(bf16[4,2,256,128]{3,2,1,0:T(8,128)(2,1)S(1)} %all_to_all.20.rest_0_), channel_id=1, source_target_pairs={{128,0},{129,1},{130,2},{131,3},{132,4},{133,5},{134,6},{135,7},{1... | collective-permute-start | bytes 1572872 | tf_op jit(solution)/shard_map/ppermute | solution.py:39
  101.3 1.5 collective-permute-done.14.rest_1_
  103.6 2.5 %shard_map.103 = bf16[8,256,128]{2,1,0:T(8,128)(2,1)} custom-call(s32[9]{0:T(128)S(1)} %pad_add_fusion.1.base_ref, bf16[256,128]{1,0:T(8,128)(2,1)S(1)} %copy-done, bf16[4,2,256,128]{3,2,1,0:T(8,128)(2,1)S(1)} %all_to_all.20.rest_0_, bf16[4,2,256,128]{3,2,1,0:T(8,128)(2,1)S(1)} %collective-permute-done.14.rest_1_), custom_call_target="tpu_custom_call" | custom-call | flops 268435456 | bytes 1048576 | tf_op jit(solution)/shard_map/pallas_call | solution.py:211
  106.0 4.2 %all-to-all-start.2 = ((bf16[8,256,128]{2,1,0:T(8,128)(2,1)}), bf16[8,256,128]{2,1,0:T(8,128)(2,1)S(1)}, u32[]{:S(2)}, u32[]{:S(2)}) async-start(bf16[8,256,128]{2,1,0:T(8,128)(2,1)} %shard_map.103), calls=%async_computation.2 | async-start | bytes 1048576 | tf_op jit(solution)/shard_map/all_to_all | solution.py:333
  110.9 8.6 %all-to-all-done.2.heads_ref = bf16[8,256,128]{2,1,0:T(8,128)(2,1)S(1)} async-done(((bf16[8,256,128]{2,1,0:T(8,128)(2,1)}), bf16[8,256,128]{2,1,0:T(8,128)(2,1)S(1)}, u32[]{:S(2)}, u32[]{:S(2)}) %all-to-all-start.2) | async-done | bytes 524320 | tf_op jit(solution)/shard_map/all_to_all | solution.py:333
  121.0 4.5 %shard_map.104 = bf16[4,256,256]{2,1,0:T(8,128)(2,1)} custom-call(s32[4]{0:T(128)} %pad_add_fusion.at_ref, s32[1,256]{1,0:T(1,128)} %bitcast.45, bf16[4,8,4,32,256]{4,3,2,1,0:T(8,128)(2,1)} %bitcast.34, bf16[4,8,4,32,256]{4,3,2,1,0:T(8,128)(2,1)} %copy-done.4, bf16[8,256,128]{2,1,0:T(8,128)(2,1)} %copy-done.3), custom_call_target="tpu_custom_call" | custom-call | flops 1073741824 | bytes 5242880 | tf_op jit(solution)/shard_map/pallas_call | solution.py:243
  125.5 15.4 %all_to_all.21 = bf16[4,256,256]{2,1,0:T(8,128)(2,1)S(1)} all-to-all(bf16[4,256,256]{2,1,0:T(8,128)(2,1)} %shard_map.104), channel_id=1, replica_groups={{0,8,20,28},{4,12,16,24},{1,9,21,29},{5,13,17,25},{2,10,22,30},{6,14,18..., dimensions={0} | all-to-all | bytes 1048576 | tf_op jit(solution)/shard_map/all_to_all | solution.py:336
  141.2 6.1 %collective-permute-start.15 = (bf16[256,128]{1,0:T(8,128)(2,1)S(1)}, bf16[256,128]{1,0:T(8,128)(2,1)S(1)}, u32[]{:S(2)}, u32[]{:S(2)}) collective-permute-start(bf16[256,128]{1,0:T(8,128)(2,1)S(1)} %bitcast.42), channel_id=1, source_target_pairs={{128,0},{129,1},{130,2},{131,3},{132,4},{133,5},{134,6},{135,7},{1... | collective-permute-start | bytes 196616 | tf_op jit(solution)/shard_map/ppermute | solution.py:39
  (70 shorter events, 14.9 us)
Async XLA Ops:
  6.5 15.5 %collective-permute-start = (bf16[512,128]{1,0:T(8,128)(2,1)}, bf16[512,128]{1,0:T(8,128)(2,1)S(1)}, u32[]{:S(2)}, u32[]{:S(2)}) collective-permute-start(bf16[512,128]{1,0:T(8,128)(2,1)} %param.10), channel_id=1, source_target_pairs={{32,0},{33,1},{34,2},{35,3},{36,4},{37,5},{38,6},{39,7},{40,8},{41... | collective-permute-start | bytes 393224 | tf_op jit(solution)/shard_map/ppermute | solution.py:43
  13.4 8.7 %collective-permute-start.1 = (bf16[512,128]{1,0:T(8,128)(2,1)}, bf16[512,128]{1,0:T(8,128)(2,1)S(1)}, u32[]{:S(2)}, u32[]{:S(2)}) collective-permute-start(bf16[512,128]{1,0:T(8,128)(2,1)} %param.10), channel_id=1, source_target_pairs={{96,0},{97,1},{98,2},{99,3},{100,4},{101,5},{102,6},{103,7},{104,8... | collective-permute-start | bytes 393224 | tf_op jit(solution)/shard_map/ppermute | solution.py:43
  13.4 8.7 %collective-permute-start.2 = (bf16[512,128]{1,0:T(8,128)(2,1)}, bf16[512,128]{1,0:T(8,128)(2,1)S(1)}, u32[]{:S(2)}, u32[]{:S(2)}) collective-permute-start(bf16[512,128]{1,0:T(8,128)(2,1)} %param.10), channel_id=1, source_target_pairs={{64,0},{65,1},{66,2},{67,3},{68,4},{69,5},{70,6},{71,7},{72,8},{73... | collective-permute-start | bytes 393224 | tf_op jit(solution)/shard_map/ppermute | solution.py:43
  19.9 2.2 %copy-start.6 = (bf16[512,128]{1,0:T(8,128)(2,1)S(1)}, bf16[512,128]{1,0:T(8,128)(2,1)}, u32[]{:S(2)}) copy-start(bf16[512,128]{1,0:T(8,128)(2,1)} %param.10) | copy-start | bytes 393220
  19.9 31.0 %copy-start.10 = (s32[32]{0:T(128)S(1)}, s32[32]{0:T(128)}, u32[]{:S(2)}) copy-start(s32[32]{0:T(128)} %constant.59.clone) | copy-start | bytes 388
  19.9 31.0 %copy-start.11 = (s32[32]{0:T(128)S(1)}, s32[32]{0:T(128)}, u32[]{:S(2)}) copy-start(s32[32]{0:T(128)} %constant.60.clone) | copy-start | bytes 388
  19.9 31.0 %copy-start.12 = (s32[32]{0:T(128)S(1)}, s32[32]{0:T(128)}, u32[]{:S(2)}) copy-start(s32[32]{0:T(128)} %constant.61.clone) | copy-start | bytes 388
  23.0 10.4 %collective-permute-start.3 = (bf16[4,512,128]{2,1,0:T(8,128)(2,1)}, bf16[4,512,128]{2,1,0:T(8,128)(2,1)}, u32[]{:S(2)}, u32[]{:S(2)}) collective-permute-start(bf16[4,512,128]{2,1,0:T(8,128)(2,1)} %get-tuple-element.26.rest_16_), channel_id=1, source_target_pairs={{4,0},{5,1},{6,2},{7,3},{8,4},{9,5},{10,6},{11,7},{12,8},{13,9},{1... | collective-permute-start | bytes 1572872 | tf_op jit(solution)/shard_map/ppermute | solution.py:43
  25.4 19.9 %all-to-all-start = ((bf16[8,4,32,256]{3,2,1,0:T(8,128)(2,1)}), bf16[8,4,32,256]{3,2,1,0:T(8,128)(2,1)}, u32[]{:S(2)}, u32[]{:S(2)}) async-start(bf16[8,4,32,256]{3,2,1,0:T(8,128)(2,1)} %shard_map.100), calls=%async_computation | async-start | bytes 1048576 | tf_op jit(solution)/shard_map/all_to_all | solution.py:290
  30.4 51.5 %all-gather.3.cloned.1.call-start = ((), (), s32[]{:S(2)}) async-start(), calls=%async_computation.4 | async-start | bytes 2621440 | tf_op jit(solution)/shard_map/all_gather | solution.py:292
  30.4 14.9 %collective-permute-start.5 = (bf16[4,512,128]{2,1,0:T(8,128)(2,1)}, bf16[4,512,128]{2,1,0:T(8,128)(2,1)}, u32[]{:S(2)}, u32[]{:S(2)}) collective-permute-start(bf16[4,512,128]{2,1,0:T(8,128)(2,1)} %get-tuple-element.26.rest_16_), channel_id=1, source_target_pairs={{28,0},{29,1},{30,2},{31,3},{0,4},{1,5},{2,6},{3,7},{4,8},{5,9},{6... | collective-permute-start | bytes 1572872 | tf_op jit(solution)/shard_map/ppermute | solution.py:43
  33.4 11.9 %collective-permute-start.4 = (bf16[4,512,128]{2,1,0:T(8,128)(2,1)}, bf16[4,512,128]{2,1,0:T(8,128)(2,1)}, u32[]{:S(2)}, u32[]{:S(2)}) collective-permute-start(bf16[4,512,128]{2,1,0:T(8,128)(2,1)} %collective-permute-done.3.rest_17_), channel_id=1, source_target_pairs={{4,0},{5,1},{6,2},{7,3},{8,4},{9,5},{10,6},{11,7},{12,8},{13,9},{1... | collective-permute-start | bytes 1572872 | tf_op jit(solution)/shard_map/ppermute | solution.py:43
  36.2 34.6 %collective-permute-start.12 = (bf16[3,1,4,8,128,128]{5,4,3,2,1,0:T(8,128)(2,1)S(1)}, bf16[3,1,4,8,128,128]{5,4,3,2,1,0:T(8,128)(2,1)}, u32[]{:S(2)}, u32[]{:S(2)}) collective-permute-start(bf16[3,1,4,8,128,128]{5,4,3,2,1,0:T(8,128)(2,1)S(1)} %constant_dynamic-slice_fusion.4), channel_id=1, source_target_pairs={{128,0},{129,1},{130,2},{131,3},{132,4},{133,5},{134,6},{135,7},{1... | collective-permute-start | bytes 9437192 | tf_op jit(solution)/shard_map/ppermute | solution.py:39
  47.5 9.9 %collective-permute-start.8 = (bf16[4,512,128]{2,1,0:T(8,128)(2,1)}, bf16[4,512,128]{2,1,0:T(8,128)(2,1)}, u32[]{:S(2)}, u32[]{:S(2)}) collective-permute-start(bf16[4,512,128]{2,1,0:T(8,128)(2,1)} %collective-permute-done.5.rest_19_), channel_id=1, source_target_pairs={{28,0},{29,1},{30,2},{31,3},{0,4},{1,5},{2,6},{3,7},{4,8},{5,9},{6... | collective-permute-start | bytes 1572872 | tf_op jit(solution)/shard_map/ppermute | solution.py:43
  48.1 10.6 %collective-permute-start.7 = (bf16[4,512,128]{2,1,0:T(8,128)(2,1)}, bf16[4,512,128]{2,1,0:T(8,128)(2,1)}, u32[]{:S(2)}, u32[]{:S(2)}) collective-permute-start(bf16[4,512,128]{2,1,0:T(8,128)(2,1)} %collective-permute-done.4.rest_18_), channel_id=1, source_target_pairs={{4,0},{5,1},{6,2},{7,3},{8,4},{9,5},{10,6},{11,7},{12,8},{13,9},{1... | collective-permute-start | bytes 1572872 | tf_op jit(solution)/shard_map/ppermute | solution.py:43
  57.4 9.9 %collective-permute-start.10 = (bf16[4,512,128]{2,1,0:T(8,128)(2,1)}, bf16[4,512,128]{2,1,0:T(8,128)(2,1)S(1)}, u32[]{:S(2)}, u32[]{:S(2)}) collective-permute-start(bf16[4,512,128]{2,1,0:T(8,128)(2,1)} %collective-permute-done.8.rest_21_), channel_id=1, source_target_pairs={{28,0},{29,1},{30,2},{31,3},{0,4},{1,5},{2,6},{3,7},{4,8},{5,9},{6... | collective-permute-start | bytes 1572872 | tf_op jit(solution)/shard_map/ppermute | solution.py:43
  58.7 9.2 %collective-permute-start.9 = (bf16[4,512,128]{2,1,0:T(8,128)(2,1)}, bf16[4,512,128]{2,1,0:T(8,128)(2,1)S(1)}, u32[]{:S(2)}, u32[]{:S(2)}) collective-permute-start(bf16[4,512,128]{2,1,0:T(8,128)(2,1)} %collective-permute-done.7.rest_20_), channel_id=1, source_target_pairs={{4,0},{5,1},{6,2},{7,3},{8,4},{9,5},{10,6},{11,7},{12,8},{13,9},{1... | collective-permute-start | bytes 1572872 | tf_op jit(solution)/shard_map/ppermute | solution.py:43
  67.3 3.5 %copy-start.1 = (bf16[4,512,128]{2,1,0:T(8,128)(2,1)}, bf16[4,512,128]{2,1,0:T(8,128)(2,1)S(1)}, u32[]{:S(2)}) copy-start(bf16[4,512,128]{2,1,0:T(8,128)(2,1)S(1)} %collective-permute-done.10.rest_23_) | copy-start | bytes 1572868
  67.9 2.9 %copy-start.2 = (bf16[4,512,128]{2,1,0:T(8,128)(2,1)}, bf16[4,512,128]{2,1,0:T(8,128)(2,1)S(1)}, u32[]{:S(2)}) copy-start(bf16[4,512,128]{2,1,0:T(8,128)(2,1)S(1)} %collective-permute-done.9.rest_22_) | copy-start | bytes 1572868
  68.1 2.7 %copy-start.7 = (f32[1,4608]{1,0:T(1,128)}, f32[1,4608]{1,0:T(1,128)S(1)}, u32[]{:S(2)}) copy-start(f32[1,4608]{1,0:T(1,128)S(1)} %pad_maximum_fusion.3.row_ref) | copy-start | bytes 55300
  68.1 2.7 %collective-permute-start.11 = (f32[1,4608]{1,0:T(1,128)S(1)}, f32[1,4608]{1,0:T(1,128)S(1)}, u32[]{:S(2)}, u32[]{:S(2)}) collective-permute-start(f32[1,4608]{1,0:T(1,128)S(1)} %pad_maximum_fusion.3.row_ref), channel_id=1, source_target_pairs={{128,0},{129,1},{130,2},{131,3},{132,4},{133,5},{134,6},{135,7},{1... | collective-permute-start | bytes 55304 | tf_op jit(solution)/shard_map/ppermute | solution.py:39
  70.8 0.6 copy-start.8
  81.5 28.7 %copy-start.9 = (s32[512]{0:T(512)S(1)}, s32[512]{0:T(512)}, u32[]{:S(2)}) copy-start(s32[512]{0:T(512)} %param.11) | copy-start | bytes 6148
  81.5 2.1 %collective-permute-start.13 = (f32[256,384]{1,0:T(8,128)}, f32[256,384]{1,0:T(8,128)S(1)}, u32[]{:S(2)}, u32[]{:S(2)}) collective-permute-start(f32[256,384]{1,0:T(8,128)} %get-tuple-element.22), channel_id=1, source_target_pairs={{128,0},{129,1},{130,2},{131,3},{132,4},{133,5},{134,6},{135,7},{1... | collective-permute-start | bytes 1179656 | tf_op jit(solution)/shard_map/ppermute | solution.py:39
  81.9 37.5 %collective-permute-start.6 = (bf16[4,8,4,32,256]{4,3,2,1,0:T(8,128)(2,1)}, bf16[4,8,4,32,256]{4,3,2,1,0:T(8,128)(2,1)S(1)}, u32[]{:S(2)}, u32[]{:S(2)}) collective-permute-start(bf16[4,8,4,32,256]{4,3,2,1,0:T(8,128)(2,1)} %bitcast.33), channel_id=1, source_target_pairs={{128,0},{129,1},{130,2},{131,3},{132,4},{133,5},{134,6},{135,7},{1... | collective-permute-start | bytes 6291464 | tf_op jit(solution)/shard_map/ppermute | solution.py:39
  83.6 0.7 copy-start.5
  99.4 3.3 %collective-permute-start.14 = (bf16[4,2,256,128]{3,2,1,0:T(8,128)(2,1)S(1)}, bf16[4,2,256,128]{3,2,1,0:T(8,128)(2,1)S(1)}, u32[]{:S(2)}, u32[]{:S(2)}) collective-permute-start(bf16[4,2,256,128]{3,2,1,0:T(8,128)(2,1)S(1)} %all_to_all.20.rest_0_), channel_id=1, source_target_pairs={{128,0},{129,1},{130,2},{131,3},{132,4},{133,5},{134,6},{135,7},{1... | collective-permute-start | bytes 1572872 | tf_op jit(solution)/shard_map/ppermute | solution.py:39
  102.7 0.8 copy-start
  106.0 13.4 %all-to-all-start.2 = ((bf16[8,256,128]{2,1,0:T(8,128)(2,1)}), bf16[8,256,128]{2,1,0:T(8,128)(2,1)S(1)}, u32[]{:S(2)}, u32[]{:S(2)}) async-start(bf16[8,256,128]{2,1,0:T(8,128)(2,1)} %shard_map.103), calls=%async_computation.2 | async-start | bytes 1048576 | tf_op jit(solution)/shard_map/all_to_all | solution.py:333
  119.5 0.8 copy-start.3
  119.5 1.5 copy-start.4
  141.2 7.0 %collective-permute-start.15 = (bf16[256,128]{1,0:T(8,128)(2,1)S(1)}, bf16[256,128]{1,0:T(8,128)(2,1)S(1)}, u32[]{:S(2)}, u32[]{:S(2)}) collective-permute-start(bf16[256,128]{1,0:T(8,128)(2,1)S(1)} %bitcast.42), channel_id=1, source_target_pairs={{128,0},{129,1},{130,2},{131,3},{132,4},{133,5},{134,6},{135,7},{1... | collective-permute-start | bytes 196616 | tf_op jit(solution)/shard_map/ppermute | solution.py:39
Sparse Core Ops, SparseCore 0:
  45.5 32.4 all-gather.2

commit v11 on v9

--- a/solution.py
+++ b/solution.py
@@ -91,8 +91,9 @@
     normed, right = [], []
     for k, piece in enumerate(pieces):
         yi, zi = y_ref[4 * k + step], z_ref[4 * k + step]
-        first = pl.multiple_of(inv.shape[0] + (yi * NZ + zi) * HD, HD)
-        gain = jnp.where(own_row, gain_ref[yi, pl.ds(zi, 1), :], got_ref[:, pl.ds(first, HD)])
+        at_own = pl.ds(pl.multiple_of((yi * NZ + zi) * HD, HD), HD)
+        at_got = pl.ds(pl.multiple_of(inv.shape[0] + (yi * NZ + zi) * HD, HD), HD)
+        gain = jnp.where(own_row, gain_ref[:, at_own], got_ref[:, at_got])
         normed.append((piece[0].astype(jnp.float32) * inverse * gain).astype(jnp.bfloat16))
         right.append(jnp.concatenate([w[p, 0, 0, 0] for w in (own_ws[k], other_ws[k]) for p in range(3)], axis=1))
     part = jnp.dot(
@@ -131,7 +132,7 @@
         grid_spec=pltpu.PrefetchScalarGridSpec(
             num_scalar_prefetch=3,
             grid=(4,),
-            in_specs=[whole(row.shape), whole(got.shape), whole((1, rows)), whole((NY, NZ, HD))]
+            in_specs=[whole(row.shape), whole(got.shape), whole((1, rows)), whole(gain.shape)]
             + [weights(k, False) for k in range(8)]
             + [weights(k, True) for k in range(8)]
             + [piece] * 8,
@@ -299,7 +300,9 @@
     modality = modality[None, :]
     ys, zs = piece_places(c.astype(jnp.int32), y.astype(jnp.int32), z.astype(jnp.int32))
 
-    arrays, pieces = gather(tokens, cut_w_out(at, w_out[0]))
+    w = w_qkv[0].transpose(1, 0, 2).reshape(3, 2, NY, NZ, HD, HD)
+    w_send = lax.dynamic_slice_in_dim(w, 1 - c, 1, axis=1)
+    arrays, (pieces, w_send) = gather(tokens, (cut_w_out(at, w_out[0]), w_send))
     w_cols = spread_w_out(pieces, arrays[2], arrays[3])
     w_cols_other = take(w_cols, dc=1)
 
@@ -310,11 +313,10 @@
     cosines, sines = jnp.cos(angles), jnp.sin(angles)
     cosines, sines = jnp.concatenate([cosines, cosines], axis=1), jnp.concatenate([-sines, sines], axis=1)
 
-    w = w_qkv[0].transpose(1, 0, 2).reshape(3, 2, NY, NZ, HD, HD)
-    w_other = take(lax.dynamic_slice_in_dim(w, 1 - c, 1, axis=1), dc=1)
-    gains = norm_gain.reshape(2, NY * NZ * HD)
-    gain_send = lax.dynamic_slice_in_dim(gains, 1 - c, 1, axis=0)
-    gain = lax.dynamic_slice_in_dim(gains, c, 1, axis=0).reshape(NY, NZ, HD)
+    w_other = take(w_send, dc=1)
+    width = NY * NZ * HD
+    gain_send = lax.dynamic_slice_in_dim(norm_gain, (1 - c) * width, width, axis=1)
+    gain = lax.dynamic_slice_in_dim(norm_gain, c * width, width, axis=1)
 
     squares = sum(jnp.sum(jnp.square(a.astype(jnp.float32)), axis=(0, 2)) for a in arrays)
     row = jnp.concatenate([squares[None, :], gain_send], axis=1)

time: 156 us -> 154 us (0.987)
  blocking collectives: 15.4 us -> 0 us
  waiting for transfers between devices: 32 us -> 41 us
  starting transfers between devices: 50.8 us -> 55.1 us
    all_to_all x1 -> x0, blocking collectives: 15.4 us -> none  [shards(): lax.all_to_all(partial, ('zh', 'zl'), 0, 0, axis_index_groups=GROUPS)]
    all_to_all x0 -> x1, waiting for transfers between devices: none -> 10.2 us  [shards(): lax.all_to_all(partial, ('zh', 'zl'), 0, 0, axis_index_groups=GROUPS)]
    all_to_all x0 -> x1, starting transfers between devices: none -> 4.91 us  [shards(): lax.all_to_all(partial, ('zh', 'zl'), 0, 0, axis_index_groups=GROUPS)]
    unnamed x29 -> x26, local copies, waits for them, and re-layouts: 4.22 us -> 3.72 us
  transfers between devices with their start and end apart: 22 -> 23, of which waited for: 13 -> 12; matrix products, arithmetic and copies ran while one was open for 10% -> 10% of each run, Pallas kernels for 11% -> 11%
where the time goes in v11:
time: 154 us; the launch traced here: 152 us
  starting transfers between devices  55.1 us (36%)
  waiting for transfers between devices  41 us (27%)
  Pallas kernels  22 us (14%)
  between operations  13.6 us (9%)
  other arithmetic  12.4 us (8%)
  local copies, waits for them, and re-layouts  8.27 us (5%)
    ppermute x10, starting transfers between devices, take_by_core(): lax.ppermute(x, AXES, pairs([m and (0, *m, 0) for m in (on_y, on_z)]))  22.2 us
    ppermute x9, starting transfers between devices, take(): return lax.ppermute(x, AXES, pairs([(dc, dy, dz, dx)] * 2, wrap_x))  18.8 us
    ppermute x10, waiting for transfers between devices, take_by_core(): lax.ppermute(x, AXES, pairs([m and (0, *m, 0) for m in (on_y, on_z)]))  16.6 us
    all_to_all x1, waiting for transfers between devices, shards(): lax.all_to_all(partial, ('zh', 'zl'), 0, 0, axis_index_groups=GROUPS)  10.2 us
    pallas_call x1, Pallas kernels, project(): pl.pallas_call(qkv_kernel, grid_spec=pltpu.PrefetchScalarGridSpec(num_sca...  10.1 us
    all_to_all x1, waiting for transfers between devices, shards(): heads = lax.all_to_all(heads_out, ('y', 'zl'), 0, 0)  8.6 us
    reduce_sum x8, other arithmetic, shards(): jnp.sum(jnp.square(a.astype(jnp.float32)), axis=(0, 2))  7.4 us
    ppermute x9, waiting for transfers between devices, take(): return lax.ppermute(x, AXES, pairs([(dc, dy, dz, dx)] * 2, wrap_x))  5.65 us
  transfers between devices with their start and end apart: 23, of which 12 were waited for; matrix products, arithmetic and copies ran while one was open for 10% of the time, Pallas kernels for 11%

profile of v11, /device:TPU:1, one launch (start us, length us, event | category | flops | bytes accessed | tf_op | source)
XLA Modules:
  0.0 152.4 jit_solution(6403607773278449731)
XLA Ops:
  6.5 6.8 %collective-permute-start = (bf16[512,128]{1,0:T(8,128)(2,1)}, bf16[512,128]{1,0:T(8,128)(2,1)S(1)}, u32[]{:S(2)}, u32[]{:S(2)}) collective-permute-start(bf16[512,128]{1,0:T(8,128)(2,1)} %param.10), channel_id=1, source_target_pairs={{32,0},{33,1},{34,2},{35,3},{36,4},{37,5},{38,6},{39,7},{40,8},{41... | collective-permute-start | bytes 393224 | tf_op jit(solution)/shard_map/ppermute | solution.py:43
  13.4 3.3 %collective-permute-start.2 = (bf16[512,128]{1,0:T(8,128)(2,1)}, bf16[512,128]{1,0:T(8,128)(2,1)S(1)}, u32[]{:S(2)}, u32[]{:S(2)}) collective-permute-start(bf16[512,128]{1,0:T(8,128)(2,1)} %param.10), channel_id=1, source_target_pairs={{64,0},{65,1},{66,2},{67,3},{68,4},{69,5},{70,6},{71,7},{72,8},{73... | collective-permute-start | bytes 393224 | tf_op jit(solution)/shard_map/ppermute | solution.py:43
  17.3 2.6 %shard_map.100 = bf16[8,4,32,256]{3,2,1,0:T(8,128)(2,1)} custom-call(s32[4]{0:T(128)} %pad_add_fusion.at_ref, bf16[128,8192]{1,0:T(8,128)(2,1)} %bitcast.42), custom_call_target="tpu_custom_call" | custom-call | bytes 1048576 | tf_op jit(solution)/shard_map/pallas_call | solution.py:275
  19.9 2.2 %constant_dynamic-slice_fusion.4 = bf16[3,1,4,8,128,128]{5,4,3,2,1,0:T(8,128)(2,1)S(1)} fusion(bf16[3,2,4,8,128,128]{5,4,3,2,1,0:T(8,128)(2,1)} %bitcast.33, s32[]{:T(128)S(6)} %select_n.52), kind=kLoop, calls=%fused_computation.22 | loop fusion | bytes 6291460 | tf_op jit(solution)/shard_map/dynamic_slice | solution.py:304
  23.0 2.4 %collective-permute-start.3 = (bf16[4,512,128]{2,1,0:T(8,128)(2,1)}, bf16[4,512,128]{2,1,0:T(8,128)(2,1)}, u32[]{:S(2)}, u32[]{:S(2)}) collective-permute-start(bf16[4,512,128]{2,1,0:T(8,128)(2,1)} %get-tuple-element.26.rest_16_), channel_id=1, source_target_pairs={{4,0},{5,1},{6,2},{7,3},{8,4},{9,5},{10,6},{11,7},{12,8},{13,9},{1... | collective-permute-start | bytes 1572872 | tf_op jit(solution)/shard_map/ppermute | solution.py:43
  25.4 5.0 %all-to-all-start = ((bf16[8,4,32,256]{3,2,1,0:T(8,128)(2,1)}), bf16[8,4,32,256]{3,2,1,0:T(8,128)(2,1)}, u32[]{:S(2)}, u32[]{:S(2)}) async-start(bf16[8,4,32,256]{3,2,1,0:T(8,128)(2,1)} %shard_map.100), calls=%async_computation | async-start | bytes 1048576 | tf_op jit(solution)/shard_map/all_to_all | solution.py:289
  30.4 1.4 collective-permute-start.5
  31.9 1.6 %collective-permute-done.3.rest_17_ = bf16[4,512,128]{2,1,0:T(8,128)(2,1)} collective-permute-done((bf16[4,512,128]{2,1,0:T(8,128)(2,1)}, bf16[4,512,128]{2,1,0:T(8,128)(2,1)}, u32[]{:S(2)}, u32[]{:S(2)}) %collective-permute-start.3) | collective-permute-done | bytes 524320 | tf_op jit(solution)/shard_map/ppermute | solution.py:43
  33.4 2.8 %collective-permute-start.4 = (bf16[4,512,128]{2,1,0:T(8,128)(2,1)}, bf16[4,512,128]{2,1,0:T(8,128)(2,1)}, u32[]{:S(2)}, u32[]{:S(2)}) collective-permute-start(bf16[4,512,128]{2,1,0:T(8,128)(2,1)} %collective-permute-done.3.rest_17_), channel_id=1, source_target_pairs={{4,0},{5,1},{6,2},{7,3},{8,4},{9,5},{10,6},{11,7},{12,8},{13,9},{1... | collective-permute-start | bytes 1572872 | tf_op jit(solution)/shard_map/ppermute | solution.py:43
  36.3 9.0 %collective-permute-done.5.rest_19_ = bf16[4,512,128]{2,1,0:T(8,128)(2,1)} collective-permute-done((bf16[4,512,128]{2,1,0:T(8,128)(2,1)}, bf16[4,512,128]{2,1,0:T(8,128)(2,1)}, u32[]{:S(2)}, u32[]{:S(2)}) %collective-permute-start.5) | collective-permute-done | bytes 524320 | tf_op jit(solution)/shard_map/ppermute | solution.py:43
  46.0 2.1 %collective-permute-start.7 = (bf16[4,512,128]{2,1,0:T(8,128)(2,1)}, bf16[4,512,128]{2,1,0:T(8,128)(2,1)}, u32[]{:S(2)}, u32[]{:S(2)}) collective-permute-start(bf16[4,512,128]{2,1,0:T(8,128)(2,1)} %collective-permute-done.4.rest_18_), channel_id=1, source_target_pairs={{4,0},{5,1},{6,2},{7,3},{8,4},{9,5},{10,6},{11,7},{12,8},{13,9},{1... | collective-permute-start | bytes 1572872 | tf_op jit(solution)/shard_map/ppermute | solution.py:43
  48.1 1.3 constant_dynamic-slice_fusion.2
  51.9 3.4 %collective-permute-done.8.rest_21_ = bf16[4,512,128]{2,1,0:T(8,128)(2,1)} collective-permute-done((bf16[4,512,128]{2,1,0:T(8,128)(2,1)}, bf16[4,512,128]{2,1,0:T(8,128)(2,1)}, u32[]{:S(2)}, u32[]{:S(2)}) %collective-permute-start.8) | collective-permute-done | bytes 524320 | tf_op jit(solution)/shard_map/ppermute | solution.py:43
  55.3 1.2 multiply_reduce_fusion.6
  56.6 2.8 %collective-permute-start.9 = (bf16[4,512,128]{2,1,0:T(8,128)(2,1)}, bf16[4,512,128]{2,1,0:T(8,128)(2,1)S(1)}, u32[]{:S(2)}, u32[]{:S(2)}) collective-permute-start(bf16[4,512,128]{2,1,0:T(8,128)(2,1)} %collective-permute-done.7.rest_20_), channel_id=1, source_target_pairs={{4,0},{5,1},{6,2},{7,3},{8,4},{9,5},{10,6},{11,7},{12,8},{13,9},{1... | collective-permute-start | bytes 1572872 | tf_op jit(solution)/shard_map/ppermute | solution.py:43
  63.0 2.2 %collective-permute-done.10.rest_23_ = bf16[4,512,128]{2,1,0:T(8,128)(2,1)S(1)} collective-permute-done((bf16[4,512,128]{2,1,0:T(8,128)(2,1)}, bf16[4,512,128]{2,1,0:T(8,128)(2,1)S(1)}, u32[]{:S(2)}, u32[]{:S(2)}) %collective-permute-start.10) | collective-permute-done | bytes 524320 | tf_op jit(solution)/shard_map/ppermute | solution.py:43
  66.0 1.9 %collective-permute-start.11 = (f32[1,4608]{1,0:T(1,128)S(1)}, f32[1,4608]{1,0:T(1,128)S(1)}, u32[]{:S(2)}, u32[]{:S(2)}) collective-permute-start(f32[1,4608]{1,0:T(1,128)S(1)} %pad_maximum_fusion.4.row_ref), channel_id=1, source_target_pairs={{128,0},{129,1},{130,2},{131,3},{132,4},{133,5},{134,6},{135,7},{1... | collective-permute-start | bytes 55304 | tf_op jit(solution)/shard_map/ppermute | solution.py:39
  69.3 10.1 %shard_map.101 = (f32[256,384]{1,0:T(8,128)}, f32[256,384]{1,0:T(8,128)}) custom-call(s32[4]{0:T(128)} %pad_add_fusion.at_ref, s32[32]{0:T(128)} %get-tuple-element.34.y_ref, s32[32]{0:T(128)} %get-tuple-element.35.z_ref, f32[1,4608]{1,0:T(1,128)} %copy-done.7, f32[1,4608]{1,0:T(1,128)} %copy-done.8, s32[1,512]{1,0:T(1,128)} %bitcast.57, ...), custom_call_target="tpu_custom_call" | custom-call | flops 3221225472 | bytes 11534336 | tf_op jit(solution)/shard_map/pallas_call | solution.py:130
  82.2 2.3 %shard_map.102 = (bf16[256,128]{1,0:T(8,128)(2,1)}, bf16[2,256,128]{2,1,0:T(8,128)(2,1)}) custom-call(f32[256,384]{1,0:T(8,128)} %get-tuple-element.21.mine_ref, f32[256,384]{1,0:T(8,128)} %copy-done.5, f32[2,128]{1,0:T(2,128)} %gain_ref.1, f32[256,128]{1,0:T(8,128)} %get-tuple-element.36.cos_ref, f32[256,128]{1,0:T(8,128)} %get-tuple-element.37.sin_ref), custom_call_target="tpu_custom_call" | custom-call | tf_op jit(solution)/shard_map/pallas_call | solution.py:169
  84.5 3.1 %collective-permute-start.14 = (bf16[2,256,128]{2,1,0:T(8,128)(2,1)}, bf16[2,256,128]{2,1,0:T(8,128)(2,1)S(1)}, u32[]{:S(2)}, u32[]{:S(2)}) collective-permute-start(bf16[2,256,128]{2,1,0:T(8,128)(2,1)} %get-tuple-element.24), channel_id=1, source_target_pairs={{0,1},{1,2},{2,3},{4,5},{5,6},{6,7},{8,9},{9,10},{10,11},{12,13},{... | collective-permute-start | bytes 393224 | tf_op jit(solution)/shard_map/ppermute | solution.py:39
  87.6 4.4 %collective-permute-start.15 = (bf16[2,256,128]{2,1,0:T(8,128)(2,1)}, bf16[2,256,128]{2,1,0:T(8,128)(2,1)S(1)}, u32[]{:S(2)}, u32[]{:S(2)}) collective-permute-start(bf16[2,256,128]{2,1,0:T(8,128)(2,1)} %get-tuple-element.24), channel_id=1, source_target_pairs={{0,2},{1,3},{4,6},{5,7},{8,10},{9,11},{12,14},{13,15},{16,18},{17,... | collective-permute-start | bytes 393224 | tf_op jit(solution)/shard_map/ppermute | solution.py:39
  92.0 1.3 collective-permute-start.16
  94.5 1.3 collective-permute-done.16
  96.8 1.5 %collective-permute-start.17 = (bf16[4,2,256,128]{3,2,1,0:T(8,128)(2,1)S(1)}, bf16[4,2,256,128]{3,2,1,0:T(8,128)(2,1)S(1)}, u32[]{:S(2)}, u32[]{:S(2)}) collective-permute-start(bf16[4,2,256,128]{3,2,1,0:T(8,128)(2,1)S(1)} %pad_maximum_fusion.1.rest_0_), channel_id=1, source_target_pairs={{128,0},{129,1},{130,2},{131,3},{132,4},{133,5},{134,6},{135,7},{1... | collective-permute-start | bytes 1572872 | tf_op jit(solution)/shard_map/ppermute | solution.py:39
  98.5 1.5 collective-permute-done.17.rest_1_
  100.7 2.5 %shard_map.103 = bf16[8,256,128]{2,1,0:T(8,128)(2,1)} custom-call(s32[8]{0:T(128)S(1)} %stack.90.base_ref, bf16[256,128]{1,0:T(8,128)(2,1)S(1)} %copy-done, bf16[4,2,256,128]{3,2,1,0:T(8,128)(2,1)S(1)} %pad_maximum_fusion.1.rest_0_, bf16[4,2,256,128]{3,2,1,0:T(8,128)(2,1)S(1)} %collective-permute-done.17.rest_1_), custom_call_target="tpu_custom_call" | custom-call | flops 268435456 | bytes 1048576 | tf_op jit(solution)/shard_map/pallas_call | solution.py:210
  103.2 4.2 %all-to-all-start.1 = ((bf16[8,256,128]{2,1,0:T(8,128)(2,1)}), bf16[8,256,128]{2,1,0:T(8,128)(2,1)S(1)}, u32[]{:S(2)}, u32[]{:S(2)}) async-start(bf16[8,256,128]{2,1,0:T(8,128)(2,1)} %shard_map.103), calls=%async_computation.1 | async-start | bytes 1048576 | tf_op jit(solution)/shard_map/all_to_all | solution.py:334
  108.1 8.6 %all-to-all-done.1.heads_ref = bf16[8,256,128]{2,1,0:T(8,128)(2,1)S(1)} async-done(((bf16[8,256,128]{2,1,0:T(8,128)(2,1)}), bf16[8,256,128]{2,1,0:T(8,128)(2,1)S(1)}, u32[]{:S(2)}, u32[]{:S(2)}) %all-to-all-start.1) | async-done | bytes 524320 | tf_op jit(solution)/shard_map/all_to_all | solution.py:334
  118.2 4.5 %shard_map.104 = bf16[4,256,256]{2,1,0:T(8,128)(2,1)} custom-call(s32[4]{0:T(128)} %pad_add_fusion.at_ref, s32[1,256]{1,0:T(1,128)} %bitcast.58, bf16[4,8,4,32,256]{4,3,2,1,0:T(8,128)(2,1)} %bitcast.44, bf16[4,8,4,32,256]{4,3,2,1,0:T(8,128)(2,1)} %copy-done.4, bf16[8,256,128]{2,1,0:T(8,128)(2,1)} %copy-done.3), custom_call_target="tpu_custom_call" | custom-call | flops 1073741824 | bytes 5242880 | tf_op jit(solution)/shard_map/pallas_call | solution.py:242
  122.7 4.9 %all-to-all-start.2 = ((bf16[4,256,256]{2,1,0:T(8,128)(2,1)}), bf16[4,256,256]{2,1,0:T(8,128)(2,1)S(1)}, u32[]{:S(2)}, u32[]{:S(2)}) async-start(bf16[4,256,256]{2,1,0:T(8,128)(2,1)} %shard_map.104), calls=%async_computation.2 | async-start | bytes 1048576 | tf_op jit(solution)/shard_map/all_to_all | solution.py:337
  127.6 10.2 %all-to-all-done.2 = bf16[4,256,256]{2,1,0:T(8,128)(2,1)S(1)} async-done(((bf16[4,256,256]{2,1,0:T(8,128)(2,1)}), bf16[4,256,256]{2,1,0:T(8,128)(2,1)S(1)}, u32[]{:S(2)}, u32[]{:S(2)}) %all-to-all-start.2) | async-done | bytes 524320 | tf_op jit(solution)/shard_map/all_to_all | solution.py:337
  138.1 5.9 %collective-permute-start.18 = (bf16[256,128]{1,0:T(8,128)(2,1)S(1)}, bf16[256,128]{1,0:T(8,128)(2,1)S(1)}, u32[]{:S(2)}, u32[]{:S(2)}) collective-permute-start(bf16[256,128]{1,0:T(8,128)(2,1)S(1)} %bitcast.55), channel_id=1, source_target_pairs={{128,0},{129,1},{130,2},{131,3},{132,4},{133,5},{134,6},{135,7},{1... | collective-permute-start | bytes 196616 | tf_op jit(solution)/shard_map/ppermute | solution.py:39
  (73 shorter events, 20.7 us)
Async XLA Ops:
  6.5 15.5 %collective-permute-start = (bf16[512,128]{1,0:T(8,128)(2,1)}, bf16[512,128]{1,0:T(8,128)(2,1)S(1)}, u32[]{:S(2)}, u32[]{:S(2)}) collective-permute-start(bf16[512,128]{1,0:T(8,128)(2,1)} %param.10), channel_id=1, source_target_pairs={{32,0},{33,1},{34,2},{35,3},{36,4},{37,5},{38,6},{39,7},{40,8},{41... | collective-permute-start | bytes 393224 | tf_op jit(solution)/shard_map/ppermute | solution.py:43
  13.4 8.7 %collective-permute-start.1 = (bf16[512,128]{1,0:T(8,128)(2,1)}, bf16[512,128]{1,0:T(8,128)(2,1)S(1)}, u32[]{:S(2)}, u32[]{:S(2)}) collective-permute-start(bf16[512,128]{1,0:T(8,128)(2,1)} %param.10), channel_id=1, source_target_pairs={{96,0},{97,1},{98,2},{99,3},{100,4},{101,5},{102,6},{103,7},{104,8... | collective-permute-start | bytes 393224 | tf_op jit(solution)/shard_map/ppermute | solution.py:43
  13.4 8.7 %collective-permute-start.2 = (bf16[512,128]{1,0:T(8,128)(2,1)}, bf16[512,128]{1,0:T(8,128)(2,1)S(1)}, u32[]{:S(2)}, u32[]{:S(2)}) collective-permute-start(bf16[512,128]{1,0:T(8,128)(2,1)} %param.10), channel_id=1, source_target_pairs={{64,0},{65,1},{66,2},{67,3},{68,4},{69,5},{70,6},{71,7},{72,8},{73... | collective-permute-start | bytes 393224 | tf_op jit(solution)/shard_map/ppermute | solution.py:43
  19.9 2.2 %copy-start.6 = (bf16[512,128]{1,0:T(8,128)(2,1)S(1)}, bf16[512,128]{1,0:T(8,128)(2,1)}, u32[]{:S(2)}) copy-start(bf16[512,128]{1,0:T(8,128)(2,1)} %param.10) | copy-start | bytes 393220
  19.9 29.6 %copy-start.10 = (s32[32]{0:T(128)S(1)}, s32[32]{0:T(128)}, u32[]{:S(2)}) copy-start(s32[32]{0:T(128)} %constant.71.clone) | copy-start | bytes 388
  19.9 29.6 %copy-start.11 = (s32[32]{0:T(128)S(1)}, s32[32]{0:T(128)}, u32[]{:S(2)}) copy-start(s32[32]{0:T(128)} %constant.72.clone) | copy-start | bytes 388
  19.9 29.6 %copy-start.12 = (s32[32]{0:T(128)S(1)}, s32[32]{0:T(128)}, u32[]{:S(2)}) copy-start(s32[32]{0:T(128)} %constant.73.clone) | copy-start | bytes 388
  23.0 10.4 %collective-permute-start.3 = (bf16[4,512,128]{2,1,0:T(8,128)(2,1)}, bf16[4,512,128]{2,1,0:T(8,128)(2,1)}, u32[]{:S(2)}, u32[]{:S(2)}) collective-permute-start(bf16[4,512,128]{2,1,0:T(8,128)(2,1)} %get-tuple-element.26.rest_16_), channel_id=1, source_target_pairs={{4,0},{5,1},{6,2},{7,3},{8,4},{9,5},{10,6},{11,7},{12,8},{13,9},{1... | collective-permute-start | bytes 1572872 | tf_op jit(solution)/shard_map/ppermute | solution.py:43
  25.4 19.9 %all-to-all-start = ((bf16[8,4,32,256]{3,2,1,0:T(8,128)(2,1)}), bf16[8,4,32,256]{3,2,1,0:T(8,128)(2,1)}, u32[]{:S(2)}, u32[]{:S(2)}) async-start(bf16[8,4,32,256]{3,2,1,0:T(8,128)(2,1)} %shard_map.100), calls=%async_computation | async-start | bytes 1048576 | tf_op jit(solution)/shard_map/all_to_all | solution.py:289
  30.4 49.5 %all-gather.3.cloned.1.call-start = ((), (), s32[]{:S(2)}) async-start(), calls=%async_computation.3 | async-start | bytes 2621440 | tf_op jit(solution)/shard_map/all_gather | solution.py:291
  30.4 14.9 %collective-permute-start.5 = (bf16[4,512,128]{2,1,0:T(8,128)(2,1)}, bf16[4,512,128]{2,1,0:T(8,128)(2,1)}, u32[]{:S(2)}, u32[]{:S(2)}) collective-permute-start(bf16[4,512,128]{2,1,0:T(8,128)(2,1)} %get-tuple-element.26.rest_16_), channel_id=1, source_target_pairs={{28,0},{29,1},{30,2},{31,3},{0,4},{1,5},{2,6},{3,7},{4,8},{5,9},{6... | collective-permute-start | bytes 1572872 | tf_op jit(solution)/shard_map/ppermute | solution.py:43
  33.4 11.9 %collective-permute-start.4 = (bf16[4,512,128]{2,1,0:T(8,128)(2,1)}, bf16[4,512,128]{2,1,0:T(8,128)(2,1)}, u32[]{:S(2)}, u32[]{:S(2)}) collective-permute-start(bf16[4,512,128]{2,1,0:T(8,128)(2,1)} %collective-permute-done.3.rest_17_), channel_id=1, source_target_pairs={{4,0},{5,1},{6,2},{7,3},{8,4},{9,5},{10,6},{11,7},{12,8},{13,9},{1... | collective-permute-start | bytes 1572872 | tf_op jit(solution)/shard_map/ppermute | solution.py:43
  36.2 32.5 %collective-permute-start.12 = (bf16[3,1,4,8,128,128]{5,4,3,2,1,0:T(8,128)(2,1)S(1)}, bf16[3,1,4,8,128,128]{5,4,3,2,1,0:T(8,128)(2,1)}, u32[]{:S(2)}, u32[]{:S(2)}) collective-permute-start(bf16[3,1,4,8,128,128]{5,4,3,2,1,0:T(8,128)(2,1)S(1)} %constant_dynamic-slice_fusion.4), channel_id=1, source_target_pairs={{128,0},{129,1},{130,2},{131,3},{132,4},{133,5},{134,6},{135,7},{1... | collective-permute-start | bytes 9437192 | tf_op jit(solution)/shard_map/ppermute | solution.py:39
  45.4 9.9 %collective-permute-start.8 = (bf16[4,512,128]{2,1,0:T(8,128)(2,1)}, bf16[4,512,128]{2,1,0:T(8,128)(2,1)}, u32[]{:S(2)}, u32[]{:S(2)}) collective-permute-start(bf16[4,512,128]{2,1,0:T(8,128)(2,1)} %collective-permute-done.5.rest_19_), channel_id=1, source_target_pairs={{28,0},{29,1},{30,2},{31,3},{0,4},{1,5},{2,6},{3,7},{4,8},{5,9},{6... | collective-permute-start | bytes 1572872 | tf_op jit(solution)/shard_map/ppermute | solution.py:43
  46.0 10.5 %collective-permute-start.7 = (bf16[4,512,128]{2,1,0:T(8,128)(2,1)}, bf16[4,512,128]{2,1,0:T(8,128)(2,1)}, u32[]{:S(2)}, u32[]{:S(2)}) collective-permute-start(bf16[4,512,128]{2,1,0:T(8,128)(2,1)} %collective-permute-done.4.rest_18_), channel_id=1, source_target_pairs={{4,0},{5,1},{6,2},{7,3},{8,4},{9,5},{10,6},{11,7},{12,8},{13,9},{1... | collective-permute-start | bytes 1572872 | tf_op jit(solution)/shard_map/ppermute | solution.py:43
  55.3 9.9 %collective-permute-start.10 = (bf16[4,512,128]{2,1,0:T(8,128)(2,1)}, bf16[4,512,128]{2,1,0:T(8,128)(2,1)S(1)}, u32[]{:S(2)}, u32[]{:S(2)}) collective-permute-start(bf16[4,512,128]{2,1,0:T(8,128)(2,1)} %collective-permute-done.8.rest_21_), channel_id=1, source_target_pairs={{28,0},{29,1},{30,2},{31,3},{0,4},{1,5},{2,6},{3,7},{4,8},{5,9},{6... | collective-permute-start | bytes 1572872 | tf_op jit(solution)/shard_map/ppermute | solution.py:43
  56.6 9.2 %collective-permute-start.9 = (bf16[4,512,128]{2,1,0:T(8,128)(2,1)}, bf16[4,512,128]{2,1,0:T(8,128)(2,1)S(1)}, u32[]{:S(2)}, u32[]{:S(2)}) collective-permute-start(bf16[4,512,128]{2,1,0:T(8,128)(2,1)} %collective-permute-done.7.rest_20_), channel_id=1, source_target_pairs={{4,0},{5,1},{6,2},{7,3},{8,4},{9,5},{10,6},{11,7},{12,8},{13,9},{1... | collective-permute-start | bytes 1572872 | tf_op jit(solution)/shard_map/ppermute | solution.py:43
  65.2 3.6 %copy-start.1 = (bf16[4,512,128]{2,1,0:T(8,128)(2,1)}, bf16[4,512,128]{2,1,0:T(8,128)(2,1)S(1)}, u32[]{:S(2)}) copy-start(bf16[4,512,128]{2,1,0:T(8,128)(2,1)S(1)} %collective-permute-done.10.rest_23_) | copy-start | bytes 1572868
  65.8 3.0 %copy-start.2 = (bf16[4,512,128]{2,1,0:T(8,128)(2,1)}, bf16[4,512,128]{2,1,0:T(8,128)(2,1)S(1)}, u32[]{:S(2)}) copy-start(bf16[4,512,128]{2,1,0:T(8,128)(2,1)S(1)} %collective-permute-done.9.rest_22_) | copy-start | bytes 1572868
  66.0 2.7 %copy-start.7 = (f32[1,4608]{1,0:T(1,128)}, f32[1,4608]{1,0:T(1,128)S(1)}, u32[]{:S(2)}) copy-start(f32[1,4608]{1,0:T(1,128)S(1)} %pad_maximum_fusion.4.row_ref) | copy-start | bytes 55300
  66.0 2.7 %collective-permute-start.11 = (f32[1,4608]{1,0:T(1,128)S(1)}, f32[1,4608]{1,0:T(1,128)S(1)}, u32[]{:S(2)}, u32[]{:S(2)}) collective-permute-start(f32[1,4608]{1,0:T(1,128)S(1)} %pad_maximum_fusion.4.row_ref), channel_id=1, source_target_pairs={{128,0},{129,1},{130,2},{131,3},{132,4},{133,5},{134,6},{135,7},{1... | collective-permute-start | bytes 55304 | tf_op jit(solution)/shard_map/ppermute | solution.py:39
  79.4 28.0 %copy-start.9 = (s32[512]{0:T(512)S(1)}, s32[512]{0:T(512)}, u32[]{:S(2)}) copy-start(s32[512]{0:T(512)} %param.11) | copy-start | bytes 6148
  79.4 2.0 %collective-permute-start.13 = (f32[256,384]{1,0:T(8,128)}, f32[256,384]{1,0:T(8,128)S(1)}, u32[]{:S(2)}, u32[]{:S(2)}) collective-permute-start(f32[256,384]{1,0:T(8,128)} %get-tuple-element.22), channel_id=1, source_target_pairs={{128,0},{129,1},{130,2},{131,3},{132,4},{133,5},{134,6},{135,7},{1... | collective-permute-start | bytes 1179656 | tf_op jit(solution)/shard_map/ppermute | solution.py:39
  79.9 36.8 %collective-permute-start.6 = (bf16[4,8,4,32,256]{4,3,2,1,0:T(8,128)(2,1)}, bf16[4,8,4,32,256]{4,3,2,1,0:T(8,128)(2,1)S(1)}, u32[]{:S(2)}, u32[]{:S(2)}) collective-permute-start(bf16[4,8,4,32,256]{4,3,2,1,0:T(8,128)(2,1)} %bitcast.43), channel_id=1, source_target_pairs={{128,0},{129,1},{130,2},{131,3},{132,4},{133,5},{134,6},{135,7},{1... | collective-permute-start | bytes 6291464 | tf_op jit(solution)/shard_map/ppermute | solution.py:39
  84.5 8.8 %collective-permute-start.14 = (bf16[2,256,128]{2,1,0:T(8,128)(2,1)}, bf16[2,256,128]{2,1,0:T(8,128)(2,1)S(1)}, u32[]{:S(2)}, u32[]{:S(2)}) collective-permute-start(bf16[2,256,128]{2,1,0:T(8,128)(2,1)} %get-tuple-element.24), channel_id=1, source_target_pairs={{0,1},{1,2},{2,3},{4,5},{5,6},{6,7},{8,9},{9,10},{10,11},{12,13},{... | collective-permute-start | bytes 393224 | tf_op jit(solution)/shard_map/ppermute | solution.py:39
  87.6 6.9 %collective-permute-start.15 = (bf16[2,256,128]{2,1,0:T(8,128)(2,1)}, bf16[2,256,128]{2,1,0:T(8,128)(2,1)S(1)}, u32[]{:S(2)}, u32[]{:S(2)}) collective-permute-start(bf16[2,256,128]{2,1,0:T(8,128)(2,1)} %get-tuple-element.24), channel_id=1, source_target_pairs={{0,2},{1,3},{4,6},{5,7},{8,10},{9,11},{12,14},{13,15},{16,18},{17,... | collective-permute-start | bytes 393224 | tf_op jit(solution)/shard_map/ppermute | solution.py:39
  92.0 3.8 %collective-permute-start.16 = (bf16[2,256,128]{2,1,0:T(8,128)(2,1)}, bf16[2,256,128]{2,1,0:T(8,128)(2,1)S(1)}, u32[]{:S(2)}, u32[]{:S(2)}) collective-permute-start(bf16[2,256,128]{2,1,0:T(8,128)(2,1)} %get-tuple-element.24), channel_id=1, source_target_pairs={{0,3},{4,7},{8,11},{12,15},{16,19},{20,23},{24,27},{28,31},{32,35}... | collective-permute-start | bytes 393224 | tf_op jit(solution)/shard_map/ppermute | solution.py:39
  96.8 3.1 %collective-permute-start.17 = (bf16[4,2,256,128]{3,2,1,0:T(8,128)(2,1)S(1)}, bf16[4,2,256,128]{3,2,1,0:T(8,128)(2,1)S(1)}, u32[]{:S(2)}, u32[]{:S(2)}) collective-permute-start(bf16[4,2,256,128]{3,2,1,0:T(8,128)(2,1)S(1)} %pad_maximum_fusion.1.rest_0_), channel_id=1, source_target_pairs={{128,0},{129,1},{130,2},{131,3},{132,4},{133,5},{134,6},{135,7},{1... | collective-permute-start | bytes 1572872 | tf_op jit(solution)/shard_map/ppermute | solution.py:39
  103.2 13.4 %all-to-all-start.1 = ((bf16[8,256,128]{2,1,0:T(8,128)(2,1)}), bf16[8,256,128]{2,1,0:T(8,128)(2,1)S(1)}, u32[]{:S(2)}, u32[]{:S(2)}) async-start(bf16[8,256,128]{2,1,0:T(8,128)(2,1)} %shard_map.103), calls=%async_computation.1 | async-start | bytes 1048576 | tf_op jit(solution)/shard_map/all_to_all | solution.py:334
  116.7 1.5 copy-start.4
  122.7 15.1 %all-to-all-start.2 = ((bf16[4,256,256]{2,1,0:T(8,128)(2,1)}), bf16[4,256,256]{2,1,0:T(8,128)(2,1)S(1)}, u32[]{:S(2)}, u32[]{:S(2)}) async-start(bf16[4,256,256]{2,1,0:T(8,128)(2,1)} %shard_map.104), calls=%async_computation.2 | async-start | bytes 1048576 | tf_op jit(solution)/shard_map/all_to_all | solution.py:337
  138.1 6.8 %collective-permute-start.18 = (bf16[256,128]{1,0:T(8,128)(2,1)S(1)}, bf16[256,128]{1,0:T(8,128)(2,1)S(1)}, u32[]{:S(2)}, u32[]{:S(2)}) collective-permute-start(bf16[256,128]{1,0:T(8,128)(2,1)S(1)} %bitcast.55), channel_id=1, source_target_pairs={{128,0},{129,1},{130,2},{131,3},{132,4},{133,5},{134,6},{135,7},{1... | collective-permute-start | bytes 196616 | tf_op jit(solution)/shard_map/ppermute | solution.py:39
  (4 other events, 3.0 us)
Sparse Core Ops, SparseCore 0:
  45.5 32.4 all-gather.2

commit v12 on v11

--- a/solution.py
+++ b/solution.py
@@ -212,7 +212,7 @@
         in_specs=[pl.BlockSpec(memory_space=pltpu.SMEM)] + [vmem] * (1 + len(keys)),
         out_specs=vmem,
         out_shape=jax.ShapeDtypeStruct((2 * NY, *queries.shape), jnp.bfloat16),
-        compiler_params=pltpu.CompilerParams(vmem_limit_bytes=40 * 2**20),
+        compiler_params=pltpu.CompilerParams(vmem_limit_bytes=24 * 2**20),
         cost_estimate=pl.CostEstimate(flops=2**28, bytes_accessed=2**20, transcendentals=2**19),
     )(bases, queries, *keys)
 
@@ -248,7 +248,7 @@
             out_specs=pl.BlockSpec((each, rows, 2 * HD), lambda g, at: (g, 0, 0)),
         ),
         out_shape=jax.ShapeDtypeStruct((NZ // 2, rows, 2 * HD), jnp.bfloat16),
-        compiler_params=pltpu.CompilerParams(vmem_limit_bytes=61 * 2**20),
+        compiler_params=pltpu.CompilerParams(vmem_limit_bytes=20 * 2**20),
         cost_estimate=pl.CostEstimate(
             flops=8 * rows * NY * HD * NZ * HD, bytes_accessed=5 * 2**20, transcendentals=0
         ),

time: 154 us -> 152 us (0.987)
  local copies, waits for them, and re-layouts: 8.27 us -> 6.21 us
  transfers between devices with their start and end apart: 23 -> 23, of which waited for: 12 -> 12; matrix products, arithmetic and copies ran while one was open for 10% -> 10% of each run, Pallas kernels for 11% -> 12%
where the time goes in v12:
time: 152 us; the launch traced here: 150 us
  starting transfers between devices  55.1 us (36%)
  waiting for transfers between devices  41.6 us (27%)
  Pallas kernels  21.5 us (14%)
  between operations  13.6 us (9%)
  other arithmetic  12.4 us (8%)
  local copies, waits for them, and re-layouts  6.21 us (4%)
    ppermute x10, starting transfers between devices, take_by_core(): lax.ppermute(x, AXES, pairs([m and (0, *m, 0) for m in (on_y, on_z)]))  22.2 us
    ppermute x9, starting transfers between devices, take(): return lax.ppermute(x, AXES, pairs([(dc, dy, dz, dx)] * 2, wrap_x))  18.8 us
    ppermute x10, waiting for transfers between devices, take_by_core(): lax.ppermute(x, AXES, pairs([m and (0, *m, 0) for m in (on_y, on_z)]))  16.6 us
    all_to_all x1, waiting for transfers between devices, shards(): lax.all_to_all(partial, ('zh', 'zl'), 0, 0, axis_index_groups=GROUPS)  10.2 us
    pallas_call x1, Pallas kernels, project(): pl.pallas_call(qkv_kernel, grid_spec=pltpu.PrefetchScalarGridSpec(num_sca...  10.1 us
    all_to_all x1, waiting for transfers between devices, shards(): heads = lax.all_to_all(heads_out, ('y', 'zl'), 0, 0)  9.16 us
    reduce_sum x8, other arithmetic, shards(): jnp.sum(jnp.square(a.astype(jnp.float32)), axis=(0, 2))  7.4 us
    ppermute x9, waiting for transfers between devices, take(): return lax.ppermute(x, AXES, pairs([(dc, dy, dz, dx)] * 2, wrap_x))  5.65 us
  transfers between devices with their start and end apart: 23, of which 12 were waited for; matrix products, arithmetic and copies ran while one was open for 10% of the time, Pallas kernels for 12%

profile of v12, /device:TPU:1, one launch (start us, length us, event | category | flops | bytes accessed | tf_op | source)
XLA Modules:
  0.0 150.4 jit_solution(50458163226225669)
XLA Ops:
  6.5 6.8 %collective-permute-start = (bf16[512,128]{1,0:T(8,128)(2,1)}, bf16[512,128]{1,0:T(8,128)(2,1)S(1)}, u32[]{:S(2)}, u32[]{:S(2)}) collective-permute-start(bf16[512,128]{1,0:T(8,128)(2,1)} %param.10), channel_id=1, source_target_pairs={{32,0},{33,1},{34,2},{35,3},{36,4},{37,5},{38,6},{39,7},{40,8},{41... | collective-permute-start | bytes 393224 | tf_op jit(solution)/shard_map/ppermute | solution.py:43
  13.4 3.3 %collective-permute-start.2 = (bf16[512,128]{1,0:T(8,128)(2,1)}, bf16[512,128]{1,0:T(8,128)(2,1)S(1)}, u32[]{:S(2)}, u32[]{:S(2)}) collective-permute-start(bf16[512,128]{1,0:T(8,128)(2,1)} %param.10), channel_id=1, source_target_pairs={{64,0},{65,1},{66,2},{67,3},{68,4},{69,5},{70,6},{71,7},{72,8},{73... | collective-permute-start | bytes 393224 | tf_op jit(solution)/shard_map/ppermute | solution.py:43
  17.3 2.6 %shard_map.100 = bf16[8,4,32,256]{3,2,1,0:T(8,128)(2,1)} custom-call(s32[4]{0:T(128)} %pad_add_fusion.at_ref, bf16[128,8192]{1,0:T(8,128)(2,1)} %bitcast.45), custom_call_target="tpu_custom_call" | custom-call | bytes 1048576 | tf_op jit(solution)/shard_map/pallas_call | solution.py:275
  19.9 2.2 %constant_dynamic-slice_fusion.4 = bf16[3,1,4,8,128,128]{5,4,3,2,1,0:T(8,128)(2,1)S(1)} fusion(bf16[3,2,4,8,128,128]{5,4,3,2,1,0:T(8,128)(2,1)} %bitcast.36, s32[]{:T(128)S(6)} %select_n.52), kind=kLoop, calls=%fused_computation.22 | loop fusion | bytes 6291460 | tf_op jit(solution)/shard_map/dynamic_slice | solution.py:304
  23.0 2.4 %collective-permute-start.3 = (bf16[4,512,128]{2,1,0:T(8,128)(2,1)}, bf16[4,512,128]{2,1,0:T(8,128)(2,1)}, u32[]{:S(2)}, u32[]{:S(2)}) collective-permute-start(bf16[4,512,128]{2,1,0:T(8,128)(2,1)} %get-tuple-element.26.rest_16_), channel_id=1, source_target_pairs={{4,0},{5,1},{6,2},{7,3},{8,4},{9,5},{10,6},{11,7},{12,8},{13,9},{1... | collective-permute-start | bytes 1572872 | tf_op jit(solution)/shard_map/ppermute | solution.py:43
  25.4 5.0 %all-to-all-start = ((bf16[8,4,32,256]{3,2,1,0:T(8,128)(2,1)}), bf16[8,4,32,256]{3,2,1,0:T(8,128)(2,1)}, u32[]{:S(2)}, u32[]{:S(2)}) async-start(bf16[8,4,32,256]{3,2,1,0:T(8,128)(2,1)} %shard_map.100), calls=%async_computation | async-start | bytes 1048576 | tf_op jit(solution)/shard_map/all_to_all | solution.py:289
  30.4 1.4 collective-permute-start.5
  31.9 1.6 %collective-permute-done.3.rest_17_ = bf16[4,512,128]{2,1,0:T(8,128)(2,1)} collective-permute-done((bf16[4,512,128]{2,1,0:T(8,128)(2,1)}, bf16[4,512,128]{2,1,0:T(8,128)(2,1)}, u32[]{:S(2)}, u32[]{:S(2)}) %collective-permute-start.3) | collective-permute-done | bytes 524320 | tf_op jit(solution)/shard_map/ppermute | solution.py:43
  33.4 2.8 %collective-permute-start.4 = (bf16[4,512,128]{2,1,0:T(8,128)(2,1)}, bf16[4,512,128]{2,1,0:T(8,128)(2,1)}, u32[]{:S(2)}, u32[]{:S(2)}) collective-permute-start(bf16[4,512,128]{2,1,0:T(8,128)(2,1)} %collective-permute-done.3.rest_17_), channel_id=1, source_target_pairs={{4,0},{5,1},{6,2},{7,3},{8,4},{9,5},{10,6},{11,7},{12,8},{13,9},{1... | collective-permute-start | bytes 1572872 | tf_op jit(solution)/shard_map/ppermute | solution.py:43
  36.3 9.0 %collective-permute-done.5.rest_19_ = bf16[4,512,128]{2,1,0:T(8,128)(2,1)} collective-permute-done((bf16[4,512,128]{2,1,0:T(8,128)(2,1)}, bf16[4,512,128]{2,1,0:T(8,128)(2,1)}, u32[]{:S(2)}, u32[]{:S(2)}) %collective-permute-start.5) | collective-permute-done | bytes 524320 | tf_op jit(solution)/shard_map/ppermute | solution.py:43
  46.0 2.1 %collective-permute-start.7 = (bf16[4,512,128]{2,1,0:T(8,128)(2,1)}, bf16[4,512,128]{2,1,0:T(8,128)(2,1)}, u32[]{:S(2)}, u32[]{:S(2)}) collective-permute-start(bf16[4,512,128]{2,1,0:T(8,128)(2,1)} %collective-permute-done.4.rest_18_), channel_id=1, source_target_pairs={{4,0},{5,1},{6,2},{7,3},{8,4},{9,5},{10,6},{11,7},{12,8},{13,9},{1... | collective-permute-start | bytes 1572872 | tf_op jit(solution)/shard_map/ppermute | solution.py:43
  48.1 1.3 constant_dynamic-slice_fusion.2
  51.9 3.4 %collective-permute-done.8.rest_21_ = bf16[4,512,128]{2,1,0:T(8,128)(2,1)} collective-permute-done((bf16[4,512,128]{2,1,0:T(8,128)(2,1)}, bf16[4,512,128]{2,1,0:T(8,128)(2,1)}, u32[]{:S(2)}, u32[]{:S(2)}) %collective-permute-start.8) | collective-permute-done | bytes 524320 | tf_op jit(solution)/shard_map/ppermute | solution.py:43
  55.3 1.2 multiply_reduce_fusion.6
  56.6 2.8 %collective-permute-start.9 = (bf16[4,512,128]{2,1,0:T(8,128)(2,1)}, bf16[4,512,128]{2,1,0:T(8,128)(2,1)S(1)}, u32[]{:S(2)}, u32[]{:S(2)}) collective-permute-start(bf16[4,512,128]{2,1,0:T(8,128)(2,1)} %collective-permute-done.7.rest_20_), channel_id=1, source_target_pairs={{4,0},{5,1},{6,2},{7,3},{8,4},{9,5},{10,6},{11,7},{12,8},{13,9},{1... | collective-permute-start | bytes 1572872 | tf_op jit(solution)/shard_map/ppermute | solution.py:43
  63.0 2.2 %collective-permute-done.10.rest_23_ = bf16[4,512,128]{2,1,0:T(8,128)(2,1)S(1)} collective-permute-done((bf16[4,512,128]{2,1,0:T(8,128)(2,1)}, bf16[4,512,128]{2,1,0:T(8,128)(2,1)S(1)}, u32[]{:S(2)}, u32[]{:S(2)}) %collective-permute-start.10) | collective-permute-done | bytes 524320 | tf_op jit(solution)/shard_map/ppermute | solution.py:43
  66.0 1.9 %collective-permute-start.11 = (f32[1,4608]{1,0:T(1,128)S(1)}, f32[1,4608]{1,0:T(1,128)S(1)}, u32[]{:S(2)}, u32[]{:S(2)}) collective-permute-start(f32[1,4608]{1,0:T(1,128)S(1)} %pad_maximum_fusion.4.row_ref), channel_id=1, source_target_pairs={{128,0},{129,1},{130,2},{131,3},{132,4},{133,5},{134,6},{135,7},{1... | collective-permute-start | bytes 55304 | tf_op jit(solution)/shard_map/ppermute | solution.py:39
  69.3 10.1 %shard_map.101 = (f32[256,384]{1,0:T(8,128)}, f32[256,384]{1,0:T(8,128)}) custom-call(s32[4]{0:T(128)} %pad_add_fusion.at_ref, s32[32]{0:T(128)} %get-tuple-element.34.y_ref, s32[32]{0:T(128)} %get-tuple-element.35.z_ref, f32[1,4608]{1,0:T(1,128)} %copy-done.7, f32[1,4608]{1,0:T(1,128)} %copy-done.8, s32[1,512]{1,0:T(1,128)} %bitcast.58, ...), custom_call_target="tpu_custom_call" | custom-call | flops 3221225472 | bytes 11534336 | tf_op jit(solution)/shard_map/pallas_call | solution.py:130
  82.2 2.3 %shard_map.102 = (bf16[256,128]{1,0:T(8,128)(2,1)}, bf16[2,256,128]{2,1,0:T(8,128)(2,1)}) custom-call(f32[256,384]{1,0:T(8,128)} %get-tuple-element.21.mine_ref, f32[256,384]{1,0:T(8,128)} %copy-done.5, f32[2,128]{1,0:T(2,128)} %gain_ref.1, f32[256,128]{1,0:T(8,128)} %get-tuple-element.36.cos_ref, f32[256,128]{1,0:T(8,128)} %get-tuple-element.37.sin_ref), custom_call_target="tpu_custom_call" | custom-call | tf_op jit(solution)/shard_map/pallas_call | solution.py:169
  84.5 3.1 %collective-permute-start.14 = (bf16[2,256,128]{2,1,0:T(8,128)(2,1)}, bf16[2,256,128]{2,1,0:T(8,128)(2,1)S(1)}, u32[]{:S(2)}, u32[]{:S(2)}) collective-permute-start(bf16[2,256,128]{2,1,0:T(8,128)(2,1)} %get-tuple-element.24), channel_id=1, source_target_pairs={{0,1},{1,2},{2,3},{4,5},{5,6},{6,7},{8,9},{9,10},{10,11},{12,13},{... | collective-permute-start | bytes 393224 | tf_op jit(solution)/shard_map/ppermute | solution.py:39
  87.6 4.4 %collective-permute-start.15 = (bf16[2,256,128]{2,1,0:T(8,128)(2,1)}, bf16[2,256,128]{2,1,0:T(8,128)(2,1)S(1)}, u32[]{:S(2)}, u32[]{:S(2)}) collective-permute-start(bf16[2,256,128]{2,1,0:T(8,128)(2,1)} %get-tuple-element.24), channel_id=1, source_target_pairs={{0,2},{1,3},{4,6},{5,7},{8,10},{9,11},{12,14},{13,15},{16,18},{17,... | collective-permute-start | bytes 393224 | tf_op jit(solution)/shard_map/ppermute | solution.py:39
  92.0 1.3 collective-permute-start.16
  94.5 1.3 collective-permute-done.16
  96.8 1.5 %collective-permute-start.17 = (bf16[4,2,256,128]{3,2,1,0:T(8,128)(2,1)S(1)}, bf16[4,2,256,128]{3,2,1,0:T(8,128)(2,1)S(1)}, u32[]{:S(2)}, u32[]{:S(2)}) collective-permute-start(bf16[4,2,256,128]{3,2,1,0:T(8,128)(2,1)S(1)} %pad_maximum_fusion.1.rest_0_), channel_id=1, source_target_pairs={{128,0},{129,1},{130,2},{131,3},{132,4},{133,5},{134,6},{135,7},{1... | collective-permute-start | bytes 1572872 | tf_op jit(solution)/shard_map/ppermute | solution.py:39
  98.5 1.5 collective-permute-done.17.rest_1_
  100.8 2.5 %shard_map.103 = bf16[8,256,128]{2,1,0:T(8,128)(2,1)} custom-call(s32[8]{0:T(128)S(1)} %stack.90.base_ref, bf16[256,128]{1,0:T(8,128)(2,1)S(1)} %copy-done.1, bf16[4,2,256,128]{3,2,1,0:T(8,128)(2,1)S(1)} %pad_maximum_fusion.1.rest_0_, bf16[4,2,256,128]{3,2,1,0:T(8,128)(2,1)S(1)} %collective-permute-done.17.rest_1_), custom_call_target="tpu_custom_call" | custom-call | flops 268435456 | bytes 1048576 | tf_op jit(solution)/shard_map/pallas_call | solution.py:210
  103.2 4.2 %all-to-all-start.1 = ((bf16[8,256,128]{2,1,0:T(8,128)(2,1)}), bf16[8,256,128]{2,1,0:T(8,128)(2,1)S(1)}, u32[]{:S(2)}, u32[]{:S(2)}) async-start(bf16[8,256,128]{2,1,0:T(8,128)(2,1)} %shard_map.103), calls=%async_computation.1 | async-start | bytes 1048576 | tf_op jit(solution)/shard_map/all_to_all | solution.py:334
  107.5 9.2 %all-to-all-done.1.heads_ref = bf16[8,256,128]{2,1,0:T(8,128)(2,1)S(1)} async-done(((bf16[8,256,128]{2,1,0:T(8,128)(2,1)}), bf16[8,256,128]{2,1,0:T(8,128)(2,1)S(1)}, u32[]{:S(2)}, u32[]{:S(2)}) %all-to-all-start.1) | async-done | bytes 524320 | tf_op jit(solution)/shard_map/all_to_all | solution.py:334
  116.7 4.0 %shard_map.104 = bf16[4,256,256]{2,1,0:T(8,128)(2,1)} custom-call(s32[4]{0:T(128)S(1)} %copy-done.2, s32[1,256]{1,0:T(1,128)S(1)} %bitcast.35, bf16[4,8,4,32,256]{4,3,2,1,0:T(8,128)(2,1)S(1)} %bitcast.34, bf16[4,8,4,32,256]{4,3,2,1,0:T(8,128)(2,1)} %collective-permute-done.6.other_ref, bf16[8,256,128]{2,1,0:T(8,128)(2,1)S(1)} %all-to-all-done.1.heads_ref), custom_call_target="tpu_custom_call" | custom-call | flops 1073741824 | bytes 5242880 | tf_op jit(solution)/shard_map/pallas_call | solution.py:242
  120.7 4.9 %all-to-all-start.2 = ((bf16[4,256,256]{2,1,0:T(8,128)(2,1)}), bf16[4,256,256]{2,1,0:T(8,128)(2,1)S(1)}, u32[]{:S(2)}, u32[]{:S(2)}) async-start(bf16[4,256,256]{2,1,0:T(8,128)(2,1)} %shard_map.104), calls=%async_computation.2 | async-start | bytes 1048576 | tf_op jit(solution)/shard_map/all_to_all | solution.py:337
  125.6 10.2 %all-to-all-done.2 = bf16[4,256,256]{2,1,0:T(8,128)(2,1)S(1)} async-done(((bf16[4,256,256]{2,1,0:T(8,128)(2,1)}), bf16[4,256,256]{2,1,0:T(8,128)(2,1)S(1)}, u32[]{:S(2)}, u32[]{:S(2)}) %all-to-all-start.2) | async-done | bytes 524320 | tf_op jit(solution)/shard_map/all_to_all | solution.py:337
  136.1 5.9 %collective-permute-start.18 = (bf16[256,128]{1,0:T(8,128)(2,1)S(1)}, bf16[256,128]{1,0:T(8,128)(2,1)S(1)}, u32[]{:S(2)}, u32[]{:S(2)}) collective-permute-start(bf16[256,128]{1,0:T(8,128)(2,1)S(1)} %bitcast.56), channel_id=1, source_target_pairs={{128,0},{129,1},{130,2},{131,3},{132,4},{133,5},{134,6},{135,7},{1... | collective-permute-start | bytes 196616 | tf_op jit(solution)/shard_map/ppermute | solution.py:39
  (73 shorter events, 18.6 us)
Async XLA Ops:
  6.5 15.5 %collective-permute-start = (bf16[512,128]{1,0:T(8,128)(2,1)}, bf16[512,128]{1,0:T(8,128)(2,1)S(1)}, u32[]{:S(2)}, u32[]{:S(2)}) collective-permute-start(bf16[512,128]{1,0:T(8,128)(2,1)} %param.10), channel_id=1, source_target_pairs={{32,0},{33,1},{34,2},{35,3},{36,4},{37,5},{38,6},{39,7},{40,8},{41... | collective-permute-start | bytes 393224 | tf_op jit(solution)/shard_map/ppermute | solution.py:43
  13.4 8.7 %collective-permute-start.1 = (bf16[512,128]{1,0:T(8,128)(2,1)}, bf16[512,128]{1,0:T(8,128)(2,1)S(1)}, u32[]{:S(2)}, u32[]{:S(2)}) collective-permute-start(bf16[512,128]{1,0:T(8,128)(2,1)} %param.10), channel_id=1, source_target_pairs={{96,0},{97,1},{98,2},{99,3},{100,4},{101,5},{102,6},{103,7},{104,8... | collective-permute-start | bytes 393224 | tf_op jit(solution)/shard_map/ppermute | solution.py:43
  13.4 8.7 %collective-permute-start.2 = (bf16[512,128]{1,0:T(8,128)(2,1)}, bf16[512,128]{1,0:T(8,128)(2,1)S(1)}, u32[]{:S(2)}, u32[]{:S(2)}) collective-permute-start(bf16[512,128]{1,0:T(8,128)(2,1)} %param.10), channel_id=1, source_target_pairs={{64,0},{65,1},{66,2},{67,3},{68,4},{69,5},{70,6},{71,7},{72,8},{73... | collective-permute-start | bytes 393224 | tf_op jit(solution)/shard_map/ppermute | solution.py:43
  19.9 29.6 %copy-start.10 = (s32[32]{0:T(128)S(1)}, s32[32]{0:T(128)}, u32[]{:S(2)}) copy-start(s32[32]{0:T(128)} %constant.71.clone) | copy-start | bytes 388
  19.9 29.6 %copy-start.11 = (s32[32]{0:T(128)S(1)}, s32[32]{0:T(128)}, u32[]{:S(2)}) copy-start(s32[32]{0:T(128)} %constant.72.clone) | copy-start | bytes 388
  19.9 29.6 %copy-start.12 = (s32[32]{0:T(128)S(1)}, s32[32]{0:T(128)}, u32[]{:S(2)}) copy-start(s32[32]{0:T(128)} %constant.73.clone) | copy-start | bytes 388
  23.0 10.4 %collective-permute-start.3 = (bf16[4,512,128]{2,1,0:T(8,128)(2,1)}, bf16[4,512,128]{2,1,0:T(8,128)(2,1)}, u32[]{:S(2)}, u32[]{:S(2)}) collective-permute-start(bf16[4,512,128]{2,1,0:T(8,128)(2,1)} %get-tuple-element.26.rest_16_), channel_id=1, source_target_pairs={{4,0},{5,1},{6,2},{7,3},{8,4},{9,5},{10,6},{11,7},{12,8},{13,9},{1... | collective-permute-start | bytes 1572872 | tf_op jit(solution)/shard_map/ppermute | solution.py:43
  25.4 19.9 %all-to-all-start = ((bf16[8,4,32,256]{3,2,1,0:T(8,128)(2,1)}), bf16[8,4,32,256]{3,2,1,0:T(8,128)(2,1)}, u32[]{:S(2)}, u32[]{:S(2)}) async-start(bf16[8,4,32,256]{3,2,1,0:T(8,128)(2,1)} %shard_map.100), calls=%async_computation | async-start | bytes 1048576 | tf_op jit(solution)/shard_map/all_to_all | solution.py:289
  30.4 49.5 %all-gather.3.cloned.1.call-start = ((), (), s32[]{:S(2)}) async-start(), calls=%async_computation.3 | async-start | bytes 2621440 | tf_op jit(solution)/shard_map/all_gather | solution.py:291
  30.4 14.9 %collective-permute-start.5 = (bf16[4,512,128]{2,1,0:T(8,128)(2,1)}, bf16[4,512,128]{2,1,0:T(8,128)(2,1)}, u32[]{:S(2)}, u32[]{:S(2)}) collective-permute-start(bf16[4,512,128]{2,1,0:T(8,128)(2,1)} %get-tuple-element.26.rest_16_), channel_id=1, source_target_pairs={{28,0},{29,1},{30,2},{31,3},{0,4},{1,5},{2,6},{3,7},{4,8},{5,9},{6... | collective-permute-start | bytes 1572872 | tf_op jit(solution)/shard_map/ppermute | solution.py:43
  33.4 11.9 %collective-permute-start.4 = (bf16[4,512,128]{2,1,0:T(8,128)(2,1)}, bf16[4,512,128]{2,1,0:T(8,128)(2,1)}, u32[]{:S(2)}, u32[]{:S(2)}) collective-permute-start(bf16[4,512,128]{2,1,0:T(8,128)(2,1)} %collective-permute-done.3.rest_17_), channel_id=1, source_target_pairs={{4,0},{5,1},{6,2},{7,3},{8,4},{9,5},{10,6},{11,7},{12,8},{13,9},{1... | collective-permute-start | bytes 1572872 | tf_op jit(solution)/shard_map/ppermute | solution.py:43
  36.2 32.5 %collective-permute-start.12 = (bf16[3,1,4,8,128,128]{5,4,3,2,1,0:T(8,128)(2,1)S(1)}, bf16[3,1,4,8,128,128]{5,4,3,2,1,0:T(8,128)(2,1)}, u32[]{:S(2)}, u32[]{:S(2)}) collective-permute-start(bf16[3,1,4,8,128,128]{5,4,3,2,1,0:T(8,128)(2,1)S(1)} %constant_dynamic-slice_fusion.4), channel_id=1, source_target_pairs={{128,0},{129,1},{130,2},{131,3},{132,4},{133,5},{134,6},{135,7},{1... | collective-permute-start | bytes 9437192 | tf_op jit(solution)/shard_map/ppermute | solution.py:39
  45.4 9.9 %collective-permute-start.8 = (bf16[4,512,128]{2,1,0:T(8,128)(2,1)}, bf16[4,512,128]{2,1,0:T(8,128)(2,1)}, u32[]{:S(2)}, u32[]{:S(2)}) collective-permute-start(bf16[4,512,128]{2,1,0:T(8,128)(2,1)} %collective-permute-done.5.rest_19_), channel_id=1, source_target_pairs={{28,0},{29,1},{30,2},{31,3},{0,4},{1,5},{2,6},{3,7},{4,8},{5,9},{6... | collective-permute-start | bytes 1572872 | tf_op jit(solution)/shard_map/ppermute | solution.py:43
  46.0 10.5 %collective-permute-start.7 = (bf16[4,512,128]{2,1,0:T(8,128)(2,1)}, bf16[4,512,128]{2,1,0:T(8,128)(2,1)}, u32[]{:S(2)}, u32[]{:S(2)}) collective-permute-start(bf16[4,512,128]{2,1,0:T(8,128)(2,1)} %collective-permute-done.4.rest_18_), channel_id=1, source_target_pairs={{4,0},{5,1},{6,2},{7,3},{8,4},{9,5},{10,6},{11,7},{12,8},{13,9},{1... | collective-permute-start | bytes 1572872 | tf_op jit(solution)/shard_map/ppermute | solution.py:43
  55.3 9.9 %collective-permute-start.10 = (bf16[4,512,128]{2,1,0:T(8,128)(2,1)}, bf16[4,512,128]{2,1,0:T(8,128)(2,1)S(1)}, u32[]{:S(2)}, u32[]{:S(2)}) collective-permute-start(bf16[4,512,128]{2,1,0:T(8,128)(2,1)} %collective-permute-done.8.rest_21_), channel_id=1, source_target_pairs={{28,0},{29,1},{30,2},{31,3},{0,4},{1,5},{2,6},{3,7},{4,8},{5,9},{6... | collective-permute-start | bytes 1572872 | tf_op jit(solution)/shard_map/ppermute | solution.py:43
  56.6 9.2 %collective-permute-start.9 = (bf16[4,512,128]{2,1,0:T(8,128)(2,1)}, bf16[4,512,128]{2,1,0:T(8,128)(2,1)S(1)}, u32[]{:S(2)}, u32[]{:S(2)}) collective-permute-start(bf16[4,512,128]{2,1,0:T(8,128)(2,1)} %collective-permute-done.7.rest_20_), channel_id=1, source_target_pairs={{4,0},{5,1},{6,2},{7,3},{8,4},{9,5},{10,6},{11,7},{12,8},{13,9},{1... | collective-permute-start | bytes 1572872 | tf_op jit(solution)/shard_map/ppermute | solution.py:43
  65.2 3.6 %copy-start.3 = (bf16[4,512,128]{2,1,0:T(8,128)(2,1)}, bf16[4,512,128]{2,1,0:T(8,128)(2,1)S(1)}, u32[]{:S(2)}) copy-start(bf16[4,512,128]{2,1,0:T(8,128)(2,1)S(1)} %collective-permute-done.10.rest_23_) | copy-start | bytes 1572868
  65.8 3.0 %copy-start.4 = (bf16[4,512,128]{2,1,0:T(8,128)(2,1)}, bf16[4,512,128]{2,1,0:T(8,128)(2,1)S(1)}, u32[]{:S(2)}) copy-start(bf16[4,512,128]{2,1,0:T(8,128)(2,1)S(1)} %collective-permute-done.9.rest_22_) | copy-start | bytes 1572868
  66.0 2.7 %copy-start.7 = (f32[1,4608]{1,0:T(1,128)}, f32[1,4608]{1,0:T(1,128)S(1)}, u32[]{:S(2)}) copy-start(f32[1,4608]{1,0:T(1,128)S(1)} %pad_maximum_fusion.4.row_ref) | copy-start | bytes 55300
  66.0 2.7 %collective-permute-start.11 = (f32[1,4608]{1,0:T(1,128)S(1)}, f32[1,4608]{1,0:T(1,128)S(1)}, u32[]{:S(2)}, u32[]{:S(2)}) collective-permute-start(f32[1,4608]{1,0:T(1,128)S(1)} %pad_maximum_fusion.4.row_ref), channel_id=1, source_target_pairs={{128,0},{129,1},{130,2},{131,3},{132,4},{133,5},{134,6},{135,7},{1... | collective-permute-start | bytes 55304 | tf_op jit(solution)/shard_map/ppermute | solution.py:39
  79.4 28.0 %copy-start.9 = (s32[512]{0:T(512)S(1)}, s32[512]{0:T(512)}, u32[]{:S(2)}) copy-start(s32[512]{0:T(512)} %param.11) | copy-start | bytes 6148
  79.4 37.2 %copy-start.2 = (s32[4]{0:T(128)S(1)}, s32[4]{0:T(128)}, u32[]{:S(2)}) copy-start(s32[4]{0:T(128)} %pad_add_fusion.at_ref) | copy-start | bytes 52
  79.4 2.0 %collective-permute-start.13 = (f32[256,384]{1,0:T(8,128)}, f32[256,384]{1,0:T(8,128)S(1)}, u32[]{:S(2)}, u32[]{:S(2)}) collective-permute-start(f32[256,384]{1,0:T(8,128)} %get-tuple-element.22), channel_id=1, source_target_pairs={{128,0},{129,1},{130,2},{131,3},{132,4},{133,5},{134,6},{135,7},{1... | collective-permute-start | bytes 1179656 | tf_op jit(solution)/shard_map/ppermute | solution.py:39
  79.9 36.8 %copy-start = (bf16[32,4,32,256]{3,2,1,0:T(8,128)(2,1)S(1)}, bf16[32,4,32,256]{3,2,1,0:T(8,128)(2,1)}, u32[]{:S(2)}) copy-start(bf16[32,4,32,256]{3,2,1,0:T(8,128)(2,1)} %all-gather.3.cloned.1.call-done) | copy-start | bytes 6291460
  79.9 36.8 %collective-permute-start.6 = (bf16[4,8,4,32,256]{4,3,2,1,0:T(8,128)(2,1)}, bf16[4,8,4,32,256]{4,3,2,1,0:T(8,128)(2,1)}, u32[]{:S(2)}, u32[]{:S(2)}) collective-permute-start(bf16[4,8,4,32,256]{4,3,2,1,0:T(8,128)(2,1)} %bitcast.33), channel_id=1, source_target_pairs={{128,0},{129,1},{130,2},{131,3},{132,4},{133,5},{134,6},{135,7},{1... | collective-permute-start | bytes 6291464 | tf_op jit(solution)/shard_map/ppermute | solution.py:39
  84.5 8.8 %collective-permute-start.14 = (bf16[2,256,128]{2,1,0:T(8,128)(2,1)}, bf16[2,256,128]{2,1,0:T(8,128)(2,1)S(1)}, u32[]{:S(2)}, u32[]{:S(2)}) collective-permute-start(bf16[2,256,128]{2,1,0:T(8,128)(2,1)} %get-tuple-element.24), channel_id=1, source_target_pairs={{0,1},{1,2},{2,3},{4,5},{5,6},{6,7},{8,9},{9,10},{10,11},{12,13},{... | collective-permute-start | bytes 393224 | tf_op jit(solution)/shard_map/ppermute | solution.py:39
  87.6 6.9 %collective-permute-start.15 = (bf16[2,256,128]{2,1,0:T(8,128)(2,1)}, bf16[2,256,128]{2,1,0:T(8,128)(2,1)S(1)}, u32[]{:S(2)}, u32[]{:S(2)}) collective-permute-start(bf16[2,256,128]{2,1,0:T(8,128)(2,1)} %get-tuple-element.24), channel_id=1, source_target_pairs={{0,2},{1,3},{4,6},{5,7},{8,10},{9,11},{12,14},{13,15},{16,18},{17,... | collective-permute-start | bytes 393224 | tf_op jit(solution)/shard_map/ppermute | solution.py:39
  92.0 3.8 %collective-permute-start.16 = (bf16[2,256,128]{2,1,0:T(8,128)(2,1)}, bf16[2,256,128]{2,1,0:T(8,128)(2,1)S(1)}, u32[]{:S(2)}, u32[]{:S(2)}) collective-permute-start(bf16[2,256,128]{2,1,0:T(8,128)(2,1)} %get-tuple-element.24), channel_id=1, source_target_pairs={{0,3},{4,7},{8,11},{12,15},{16,19},{20,23},{24,27},{28,31},{32,35}... | collective-permute-start | bytes 393224 | tf_op jit(solution)/shard_map/ppermute | solution.py:39
  96.8 3.1 %collective-permute-start.17 = (bf16[4,2,256,128]{3,2,1,0:T(8,128)(2,1)S(1)}, bf16[4,2,256,128]{3,2,1,0:T(8,128)(2,1)S(1)}, u32[]{:S(2)}, u32[]{:S(2)}) collective-permute-start(bf16[4,2,256,128]{3,2,1,0:T(8,128)(2,1)S(1)} %pad_maximum_fusion.1.rest_0_), channel_id=1, source_target_pairs={{128,0},{129,1},{130,2},{131,3},{132,4},{133,5},{134,6},{135,7},{1... | collective-permute-start | bytes 1572872 | tf_op jit(solution)/shard_map/ppermute | solution.py:39
  103.2 13.4 %all-to-all-start.1 = ((bf16[8,256,128]{2,1,0:T(8,128)(2,1)}), bf16[8,256,128]{2,1,0:T(8,128)(2,1)S(1)}, u32[]{:S(2)}, u32[]{:S(2)}) async-start(bf16[8,256,128]{2,1,0:T(8,128)(2,1)} %shard_map.103), calls=%async_computation.1 | async-start | bytes 1048576 | tf_op jit(solution)/shard_map/all_to_all | solution.py:334
  120.7 15.1 %all-to-all-start.2 = ((bf16[4,256,256]{2,1,0:T(8,128)(2,1)}), bf16[4,256,256]{2,1,0:T(8,128)(2,1)S(1)}, u32[]{:S(2)}, u32[]{:S(2)}) async-start(bf16[4,256,256]{2,1,0:T(8,128)(2,1)} %shard_map.104), calls=%async_computation.2 | async-start | bytes 1048576 | tf_op jit(solution)/shard_map/all_to_all | solution.py:337
  136.1 6.8 %collective-permute-start.18 = (bf16[256,128]{1,0:T(8,128)(2,1)S(1)}, bf16[256,128]{1,0:T(8,128)(2,1)S(1)}, u32[]{:S(2)}, u32[]{:S(2)}) collective-permute-start(bf16[256,128]{1,0:T(8,128)(2,1)S(1)} %bitcast.56), channel_id=1, source_target_pairs={{128,0},{129,1},{130,2},{131,3},{132,4},{133,5},{134,6},{135,7},{1... | collective-permute-start | bytes 196616 | tf_op jit(solution)/shard_map/ppermute | solution.py:39
  (4 other events, 4.4 us)
Sparse Core Ops, SparseCore 0:
  45.5 32.4 all-gather.2

commit v13 on v12

--- a/solution.py
+++ b/solution.py
@@ -140,7 +140,7 @@
             scratch_shapes=[pltpu.VMEM((rows, w), jnp.float32) for w in (6 * HD, HD, HD)],
         ),
         out_shape=[jax.ShapeDtypeStruct((rows // 2, 3 * HD), jnp.float32)] * 2,
-        compiler_params=pltpu.CompilerParams(vmem_limit_bytes=61 * 2**20),
+        compiler_params=pltpu.CompilerParams(vmem_limit_bytes=52 * 2**20),
         cost_estimate=pl.CostEstimate(
             flops=2 * rows * 4096 * 6 * HD, bytes_accessed=11 * 2**20, transcendentals=0
         ),

time: 152 us -> 150 us (0.987)
  other arithmetic: 12.4 us -> 6.35 us
  waiting for transfers between devices: 41.6 us -> 46.2 us
  local copies, waits for them, and re-layouts: 6.21 us -> 7.85 us
    reduce_sum x8, other arithmetic: 7.4 us -> 2.52 us  [shards(): jnp.sum(jnp.square(a.astype(jnp.float32)), axis=(0, 2))]
    ppermute x10, waiting for transfers between devices: 16.6 us -> 21.2 us  [take_by_core(): lax.ppermute(x, AXES, pairs([m and (0, *m, 0) for m in (on_y, on_z)]))]
    dynamic_slice x1, local copies, waits for them, and re-layouts: 2.15 us -> 4.08 us  [shards(): w_send = lax.dynamic_slice_in_dim(w, 1 - c, 1, axis=1)]
    ppermute x10, starting transfers between devices: 22.2 us -> 20.6 us  [take_by_core(): lax.ppermute(x, AXES, pairs([m and (0, *m, 0) for m in (on_y, on_z)]))]
    unnamed x26 -> x36, local copies, waits for them, and re-layouts: 2.22 us -> 3.28 us
  transfers between devices with their start and end apart: 23 -> 23, of which waited for: 12 -> 11; matrix products, arithmetic and copies ran while one was open for 10% -> 7% of each run, Pallas kernels for 12% -> 11%
where the time goes in v13:
time: 150 us; the launch traced here: 149 us
  starting transfers between devices  54 us (36%)
  waiting for transfers between devices  46.2 us (31%)
  Pallas kernels  20.6 us (14%)
  between operations  13.7 us (9%)
  local copies, waits for them, and re-layouts  7.85 us (5%)
  other arithmetic  6.35 us (4%)
    ppermute x10, waiting for transfers between devices, take_by_core(): lax.ppermute(x, AXES, pairs([m and (0, *m, 0) for m in (on_y, on_z)]))  21.2 us
    ppermute x10, starting transfers between devices, take_by_core(): lax.ppermute(x, AXES, pairs([m and (0, *m, 0) for m in (on_y, on_z)]))  20.6 us
    ppermute x9, starting transfers between devices, take(): return lax.ppermute(x, AXES, pairs([(dc, dy, dz, dx)] * 2, wrap_x))  18.5 us
    all_to_all x1, waiting for transfers between devices, shards(): lax.all_to_all(partial, ('zh', 'zl'), 0, 0, axis_index_groups=GROUPS)  10.2 us
    all_to_all x1, waiting for transfers between devices, shards(): heads = lax.all_to_all(heads_out, ('y', 'zl'), 0, 0)  9.18 us
    pallas_call x1, Pallas kernels, project(): pl.pallas_call(qkv_kernel, grid_spec=pltpu.PrefetchScalarGridSpec(num_sca...  9.15 us
    all_to_all x1, starting transfers between devices, spread_w_out(): lines = lax.all_to_all(pieces, ('y', 'zl'), 0, 0)  5.86 us
    ppermute x9, waiting for transfers between devices, take(): return lax.ppermute(x, AXES, pairs([(dc, dy, dz, dx)] * 2, wrap_x))  5.6 us
  transfers between devices with their start and end apart: 23, of which 11 were waited for; matrix products, arithmetic and copies ran while one was open for 7% of the time, Pallas kernels for 11%

profile of v13, /device:TPU:1, one launch (start us, length us, event | category | flops | bytes accessed | tf_op | source)
XLA Modules:
  0.0 148.7 jit_solution(14866800171374865709)
XLA Ops:
  6.5 6.8 %collective-permute-start = (bf16[512,128]{1,0:T(8,128)(2,1)}, bf16[512,128]{1,0:T(8,128)(2,1)S(1)}, u32[]{:S(2)}, u32[]{:S(2)}) collective-permute-start(bf16[512,128]{1,0:T(8,128)(2,1)} %param.10), channel_id=1, source_target_pairs={{32,0},{33,1},{34,2},{35,3},{36,4},{37,5},{38,6},{39,7},{40,8},{41... | collective-permute-start | bytes 393224 | tf_op jit(solution)/shard_map/ppermute | solution.py:43
  13.4 3.3 %collective-permute-start.2 = (bf16[512,128]{1,0:T(8,128)(2,1)}, bf16[512,128]{1,0:T(8,128)(2,1)S(1)}, u32[]{:S(2)}, u32[]{:S(2)}) collective-permute-start(bf16[512,128]{1,0:T(8,128)(2,1)} %param.10), channel_id=1, source_target_pairs={{64,0},{65,1},{66,2},{67,3},{68,4},{69,5},{70,6},{71,7},{72,8},{73... | collective-permute-start | bytes 393224 | tf_op jit(solution)/shard_map/ppermute | solution.py:43
  17.3 2.6 %shard_map.100 = bf16[8,4,32,256]{3,2,1,0:T(8,128)(2,1)} custom-call(s32[4]{0:T(128)} %pad_add_fusion.at_ref, bf16[128,8192]{1,0:T(8,128)(2,1)} %bitcast.46), custom_call_target="tpu_custom_call" | custom-call | bytes 1048576 | tf_op jit(solution)/shard_map/pallas_call | solution.py:275
  20.0 4.1 %constant_dynamic-slice_fusion.4 = bf16[3,1,4,8,128,128]{5,4,3,2,1,0:T(8,128)(2,1)} fusion(bf16[3,2,4,8,128,128]{5,4,3,2,1,0:T(8,128)(2,1)} %bitcast.37, s32[]{:T(128)S(6)} %select_n.52), kind=kLoop, calls=%fused_computation.22 | loop fusion | bytes 6291460 | tf_op jit(solution)/shard_map/dynamic_slice | solution.py:304
  25.2 5.9 %all-to-all-start = ((bf16[8,4,32,256]{3,2,1,0:T(8,128)(2,1)}), bf16[8,4,32,256]{3,2,1,0:T(8,128)(2,1)S(1)}, u32[]{:S(2)}, u32[]{:S(2)}) async-start(bf16[8,4,32,256]{3,2,1,0:T(8,128)(2,1)} %shard_map.100), calls=%async_computation | async-start | bytes 1048576 | tf_op jit(solution)/shard_map/all_to_all | solution.py:289
  31.1 1.4 collective-permute-start.5
  32.5 1.2 collective-permute-done.3.rest_17_
  33.7 2.7 %collective-permute-start.4 = (bf16[4,512,128]{2,1,0:T(8,128)(2,1)S(1)}, bf16[4,512,128]{2,1,0:T(8,128)(2,1)S(1)}, u32[]{:S(2)}, u32[]{:S(2)}) collective-permute-start(bf16[4,512,128]{2,1,0:T(8,128)(2,1)S(1)} %collective-permute-done.3.rest_17_), channel_id=1, source_target_pairs={{4,0},{5,1},{6,2},{7,3},{8,4},{9,5},{10,6},{11,7},{12,8},{13,9},{1... | collective-permute-start | bytes 1572872 | tf_op jit(solution)/shard_map/ppermute | solution.py:43
  36.4 0.9 collective-permute-start.12
  37.3 8.6 %collective-permute-done.5.rest_19_ = bf16[4,512,128]{2,1,0:T(8,128)(2,1)S(1)} collective-permute-done((bf16[4,512,128]{2,1,0:T(8,128)(2,1)S(1)}, bf16[4,512,128]{2,1,0:T(8,128)(2,1)S(1)}, u32[]{:S(2)}, u32[]{:S(2)}) %collective-permute-start.5) | collective-permute-done | bytes 524320 | tf_op jit(solution)/shard_map/ppermute | solution.py:43
  46.9 2.7 %collective-permute-start.7 = (bf16[4,512,128]{2,1,0:T(8,128)(2,1)S(1)}, bf16[4,512,128]{2,1,0:T(8,128)(2,1)}, u32[]{:S(2)}, u32[]{:S(2)}) collective-permute-start(bf16[4,512,128]{2,1,0:T(8,128)(2,1)S(1)} %collective-permute-done.4.rest_18_), channel_id=1, source_target_pairs={{4,0},{5,1},{6,2},{7,3},{8,4},{9,5},{10,6},{11,7},{12,8},{13,9},{1... | collective-permute-start | bytes 1572872 | tf_op jit(solution)/shard_map/ppermute | solution.py:43
  49.8 6.3 %collective-permute-done.8.rest_21_ = bf16[4,512,128]{2,1,0:T(8,128)(2,1)S(1)} collective-permute-done((bf16[4,512,128]{2,1,0:T(8,128)(2,1)S(1)}, bf16[4,512,128]{2,1,0:T(8,128)(2,1)S(1)}, u32[]{:S(2)}, u32[]{:S(2)}) %collective-permute-start.8) | collective-permute-done | bytes 524320 | tf_op jit(solution)/shard_map/ppermute | solution.py:43
  56.3 2.8 %collective-permute-start.9 = (bf16[4,512,128]{2,1,0:T(8,128)(2,1)}, bf16[4,512,128]{2,1,0:T(8,128)(2,1)S(1)}, u32[]{:S(2)}, u32[]{:S(2)}) collective-permute-start(bf16[4,512,128]{2,1,0:T(8,128)(2,1)} %collective-permute-done.7.rest_20_), channel_id=1, source_target_pairs={{4,0},{5,1},{6,2},{7,3},{8,4},{9,5},{10,6},{11,7},{12,8},{13,9},{1... | collective-permute-start | bytes 1572872 | tf_op jit(solution)/shard_map/ppermute | solution.py:43
  59.4 1.2 multiply_reduce_fusion.3
  60.7 5.1 %collective-permute-done.10.rest_23_ = bf16[4,512,128]{2,1,0:T(8,128)(2,1)S(1)} collective-permute-done((bf16[4,512,128]{2,1,0:T(8,128)(2,1)S(1)}, bf16[4,512,128]{2,1,0:T(8,128)(2,1)S(1)}, u32[]{:S(2)}, u32[]{:S(2)}) %collective-permute-start.10) | collective-permute-done | bytes 524320 | tf_op jit(solution)/shard_map/ppermute | solution.py:43
  68.0 9.1 %shard_map.101 = (f32[256,384]{1,0:T(8,128)S(1)}, f32[256,384]{1,0:T(8,128)S(1)}) custom-call(s32[4]{0:T(128)S(1)} %copy-done.3, s32[32]{0:T(128)S(1)} %get-tuple-element.34.y_ref, s32[32]{0:T(128)S(1)} %get-tuple-element.35.z_ref, f32[1,4608]{1,0:T(1,128)S(1)} %pad_maximum_fusion.4.row_ref, f32[1,4608]{1,0:T(1,128)S(1)} %collective-permute-done.11.got_ref, ...), custom_call_target="tpu_custom_call" | custom-call | flops 3221225472 | bytes 11534336 | tf_op jit(solution)/shard_map/pallas_call | solution.py:130
  80.8 2.3 %shard_map.102 = (bf16[256,128]{1,0:T(8,128)(2,1)}, bf16[2,256,128]{2,1,0:T(8,128)(2,1)}) custom-call(f32[256,384]{1,0:T(8,128)} %copy-done.1, f32[256,384]{1,0:T(8,128)} %copy-done.11, f32[2,128]{1,0:T(2,128)} %gain_ref.1, f32[256,128]{1,0:T(8,128)} %get-tuple-element.36.cos_ref, f32[256,128]{1,0:T(8,128)} %get-tuple-element.37.sin_ref), custom_call_target="tpu_custom_call" | custom-call | tf_op jit(solution)/shard_map/pallas_call | solution.py:169
  83.1 2.9 %collective-permute-start.14 = (bf16[2,256,128]{2,1,0:T(8,128)(2,1)}, bf16[2,256,128]{2,1,0:T(8,128)(2,1)S(1)}, u32[]{:S(2)}, u32[]{:S(2)}) collective-permute-start(bf16[2,256,128]{2,1,0:T(8,128)(2,1)} %get-tuple-element.24), channel_id=1, source_target_pairs={{0,1},{1,2},{2,3},{4,5},{5,6},{6,7},{8,9},{9,10},{10,11},{12,13},{... | collective-permute-start | bytes 393224 | tf_op jit(solution)/shard_map/ppermute | solution.py:39
  86.0 4.4 %collective-permute-start.15 = (bf16[2,256,128]{2,1,0:T(8,128)(2,1)}, bf16[2,256,128]{2,1,0:T(8,128)(2,1)S(1)}, u32[]{:S(2)}, u32[]{:S(2)}) collective-permute-start(bf16[2,256,128]{2,1,0:T(8,128)(2,1)} %get-tuple-element.24), channel_id=1, source_target_pairs={{0,2},{1,3},{4,6},{5,7},{8,10},{9,11},{12,14},{13,15},{16,18},{17,... | collective-permute-start | bytes 393224 | tf_op jit(solution)/shard_map/ppermute | solution.py:39
  90.3 1.3 collective-permute-start.16
  91.7 1.2 collective-permute-done.15
  92.9 1.3 collective-permute-done.16
  94.2 1.0 pad_maximum_fusion.1.rest_0_
  95.1 1.6 %collective-permute-start.17 = (bf16[4,2,256,128]{3,2,1,0:T(8,128)(2,1)S(1)}, bf16[4,2,256,128]{3,2,1,0:T(8,128)(2,1)S(1)}, u32[]{:S(2)}, u32[]{:S(2)}) collective-permute-start(bf16[4,2,256,128]{3,2,1,0:T(8,128)(2,1)S(1)} %pad_maximum_fusion.1.rest_0_), channel_id=1, source_target_pairs={{128,0},{129,1},{130,2},{131,3},{132,4},{133,5},{134,6},{135,7},{1... | collective-permute-start | bytes 1572872 | tf_op jit(solution)/shard_map/ppermute | solution.py:39
  96.8 1.5 collective-permute-done.17.rest_1_
  99.1 2.5 %shard_map.103 = bf16[8,256,128]{2,1,0:T(8,128)(2,1)} custom-call(s32[8]{0:T(128)S(1)} %stack.90.base_ref, bf16[256,128]{1,0:T(8,128)(2,1)S(1)} %copy-done.2, bf16[4,2,256,128]{3,2,1,0:T(8,128)(2,1)S(1)} %pad_maximum_fusion.1.rest_0_, bf16[4,2,256,128]{3,2,1,0:T(8,128)(2,1)S(1)} %collective-permute-done.17.rest_1_), custom_call_target="tpu_custom_call" | custom-call | flops 268435456 | bytes 1048576 | tf_op jit(solution)/shard_map/pallas_call | solution.py:210
  101.6 4.9 %all-to-all-start.1 = ((bf16[8,256,128]{2,1,0:T(8,128)(2,1)}), bf16[8,256,128]{2,1,0:T(8,128)(2,1)S(1)}, u32[]{:S(2)}, u32[]{:S(2)}) async-start(bf16[8,256,128]{2,1,0:T(8,128)(2,1)} %shard_map.103), calls=%async_computation.1 | async-start | bytes 1048576 | tf_op jit(solution)/shard_map/all_to_all | solution.py:334
  106.5 9.2 %all-to-all-done.1.heads_ref = bf16[8,256,128]{2,1,0:T(8,128)(2,1)S(1)} async-done(((bf16[8,256,128]{2,1,0:T(8,128)(2,1)}), bf16[8,256,128]{2,1,0:T(8,128)(2,1)S(1)}, u32[]{:S(2)}, u32[]{:S(2)}) %all-to-all-start.1) | async-done | bytes 524320 | tf_op jit(solution)/shard_map/all_to_all | solution.py:334
  115.7 4.0 %shard_map.104 = bf16[4,256,256]{2,1,0:T(8,128)(2,1)} custom-call(s32[4]{0:T(128)S(1)} %copy-done.3, s32[1,256]{1,0:T(1,128)S(1)} %bitcast.36, bf16[4,8,4,32,256]{4,3,2,1,0:T(8,128)(2,1)S(1)} %bitcast.34, bf16[4,8,4,32,256]{4,3,2,1,0:T(8,128)(2,1)} %collective-permute-done.6.other_ref, bf16[8,256,128]{2,1,0:T(8,128)(2,1)S(1)} %all-to-all-done.1.heads_ref), custom_call_target="tpu_custom_call" | custom-call | flops 1073741824 | bytes 5242880 | tf_op jit(solution)/shard_map/pallas_call | solution.py:242
  119.7 4.1 %all-to-all-start.2 = ((bf16[4,256,256]{2,1,0:T(8,128)(2,1)}), bf16[4,256,256]{2,1,0:T(8,128)(2,1)S(1)}, u32[]{:S(2)}, u32[]{:S(2)}) async-start(bf16[4,256,256]{2,1,0:T(8,128)(2,1)} %shard_map.104), calls=%async_computation.2 | async-start | bytes 1048576 | tf_op jit(solution)/shard_map/all_to_all | solution.py:337
  123.9 10.2 %all-to-all-done.2 = bf16[4,256,256]{2,1,0:T(8,128)(2,1)S(1)} async-done(((bf16[4,256,256]{2,1,0:T(8,128)(2,1)}), bf16[4,256,256]{2,1,0:T(8,128)(2,1)S(1)}, u32[]{:S(2)}, u32[]{:S(2)}) %all-to-all-start.2) | async-done | bytes 524320 | tf_op jit(solution)/shard_map/all_to_all | solution.py:337
  134.4 5.9 %collective-permute-start.18 = (bf16[256,128]{1,0:T(8,128)(2,1)S(1)}, bf16[256,128]{1,0:T(8,128)(2,1)S(1)}, u32[]{:S(2)}, u32[]{:S(2)}) collective-permute-start(bf16[256,128]{1,0:T(8,128)(2,1)S(1)} %bitcast.57), channel_id=1, source_target_pairs={{128,0},{129,1},{130,2},{131,3},{132,4},{133,5},{134,6},{135,7},{1... | collective-permute-start | bytes 196616 | tf_op jit(solution)/shard_map/ppermute | solution.py:39
  (83 shorter events, 12.2 us)
Async XLA Ops:
  6.5 17.5 %collective-permute-start = (bf16[512,128]{1,0:T(8,128)(2,1)}, bf16[512,128]{1,0:T(8,128)(2,1)S(1)}, u32[]{:S(2)}, u32[]{:S(2)}) collective-permute-start(bf16[512,128]{1,0:T(8,128)(2,1)} %param.10), channel_id=1, source_target_pairs={{32,0},{33,1},{34,2},{35,3},{36,4},{37,5},{38,6},{39,7},{40,8},{41... | collective-permute-start | bytes 393224 | tf_op jit(solution)/shard_map/ppermute | solution.py:43
  13.4 10.7 %collective-permute-start.1 = (bf16[512,128]{1,0:T(8,128)(2,1)}, bf16[512,128]{1,0:T(8,128)(2,1)S(1)}, u32[]{:S(2)}, u32[]{:S(2)}) collective-permute-start(bf16[512,128]{1,0:T(8,128)(2,1)} %param.10), channel_id=1, source_target_pairs={{96,0},{97,1},{98,2},{99,3},{100,4},{101,5},{102,6},{103,7},{104,8... | collective-permute-start | bytes 393224 | tf_op jit(solution)/shard_map/ppermute | solution.py:43
  13.4 10.7 %collective-permute-start.2 = (bf16[512,128]{1,0:T(8,128)(2,1)}, bf16[512,128]{1,0:T(8,128)(2,1)S(1)}, u32[]{:S(2)}, u32[]{:S(2)}) collective-permute-start(bf16[512,128]{1,0:T(8,128)(2,1)} %param.10), channel_id=1, source_target_pairs={{64,0},{65,1},{66,2},{67,3},{68,4},{69,5},{70,6},{71,7},{72,8},{73... | collective-permute-start | bytes 393224 | tf_op jit(solution)/shard_map/ppermute | solution.py:43
  20.0 29.6 %copy-start.13 = (f32[1,8192]{1,0:T(1,128)S(1)}, f32[1,8192]{1,0:T(1,128)}, u32[]{:S(2)}) copy-start(f32[1,8192]{1,0:T(1,128)} %param.12) | copy-start | bytes 98308
  20.0 29.6 %copy-start.14 = (s32[32]{0:T(128)S(1)}, s32[32]{0:T(128)}, u32[]{:S(2)}) copy-start(s32[32]{0:T(128)} %constant.71.clone) | copy-start | bytes 388
  20.0 29.6 %copy-start.15 = (s32[32]{0:T(128)S(1)}, s32[32]{0:T(128)}, u32[]{:S(2)}) copy-start(s32[32]{0:T(128)} %constant.72.clone) | copy-start | bytes 388
  20.0 29.6 %copy-start.16 = (s32[32]{0:T(128)S(1)}, s32[32]{0:T(128)}, u32[]{:S(2)}) copy-start(s32[32]{0:T(128)} %constant.73.clone) | copy-start | bytes 388
  20.0 29.6 %copy-start.17 = (s32[32]{0:T(128)S(1)}, s32[32]{0:T(128)}, u32[]{:S(2)}) copy-start(s32[32]{0:T(128)} %constant.74.clone) | copy-start | bytes 388
  24.1 43.9 %copy-start.3 = (s32[4]{0:T(128)S(1)}, s32[4]{0:T(128)}, u32[]{:S(2)}) copy-start(s32[4]{0:T(128)} %pad_add_fusion.at_ref) | copy-start | bytes 52
  24.1 43.9 %copy-start.4 = (s32[512]{0:T(512)S(1)}, s32[512]{0:T(512)}, u32[]{:S(2)}) copy-start(s32[512]{0:T(512)} %param.11) | copy-start | bytes 6148
  24.4 9.3 %collective-permute-start.3 = (bf16[4,512,128]{2,1,0:T(8,128)(2,1)S(1)}, bf16[4,512,128]{2,1,0:T(8,128)(2,1)S(1)}, u32[]{:S(2)}, u32[]{:S(2)}) collective-permute-start(bf16[4,512,128]{2,1,0:T(8,128)(2,1)S(1)} %get-tuple-element.26.rest_16_), channel_id=1, source_target_pairs={{4,0},{5,1},{6,2},{7,3},{8,4},{9,5},{10,6},{11,7},{12,8},{13,9},{1... | collective-permute-start | bytes 1572872 | tf_op jit(solution)/shard_map/ppermute | solution.py:43
  25.2 20.7 %all-to-all-start = ((bf16[8,4,32,256]{3,2,1,0:T(8,128)(2,1)}), bf16[8,4,32,256]{3,2,1,0:T(8,128)(2,1)S(1)}, u32[]{:S(2)}, u32[]{:S(2)}) async-start(bf16[8,4,32,256]{3,2,1,0:T(8,128)(2,1)} %shard_map.100), calls=%async_computation | async-start | bytes 1048576 | tf_op jit(solution)/shard_map/all_to_all | solution.py:289
  31.0 47.2 %all-gather.3.cloned.1.call-start = ((), (), s32[]{:S(2)}) async-start(), calls=%async_computation.3 | async-start | bytes 2621440 | tf_op jit(solution)/shard_map/all_gather | solution.py:291
  31.1 14.8 %collective-permute-start.5 = (bf16[4,512,128]{2,1,0:T(8,128)(2,1)S(1)}, bf16[4,512,128]{2,1,0:T(8,128)(2,1)S(1)}, u32[]{:S(2)}, u32[]{:S(2)}) collective-permute-start(bf16[4,512,128]{2,1,0:T(8,128)(2,1)S(1)} %get-tuple-element.26.rest_16_), channel_id=1, source_target_pairs={{28,0},{29,1},{30,2},{31,3},{0,4},{1,5},{2,6},{3,7},{4,8},{5,9},{6... | collective-permute-start | bytes 1572872 | tf_op jit(solution)/shard_map/ppermute | solution.py:43
  33.7 12.2 %collective-permute-start.4 = (bf16[4,512,128]{2,1,0:T(8,128)(2,1)S(1)}, bf16[4,512,128]{2,1,0:T(8,128)(2,1)S(1)}, u32[]{:S(2)}, u32[]{:S(2)}) collective-permute-start(bf16[4,512,128]{2,1,0:T(8,128)(2,1)S(1)} %collective-permute-done.3.rest_17_), channel_id=1, source_target_pairs={{4,0},{5,1},{6,2},{7,3},{8,4},{9,5},{10,6},{11,7},{12,8},{13,9},{1... | collective-permute-start | bytes 1572872 | tf_op jit(solution)/shard_map/ppermute | solution.py:43
  36.4 31.5 %collective-permute-start.12 = (bf16[3,1,4,8,128,128]{5,4,3,2,1,0:T(8,128)(2,1)}, bf16[3,1,4,8,128,128]{5,4,3,2,1,0:T(8,128)(2,1)}, u32[]{:S(2)}, u32[]{:S(2)}) collective-permute-start(bf16[3,1,4,8,128,128]{5,4,3,2,1,0:T(8,128)(2,1)} %constant_dynamic-slice_fusion.4), channel_id=1, source_target_pairs={{128,0},{129,1},{130,2},{131,3},{132,4},{133,5},{134,6},{135,7},{1... | collective-permute-start | bytes 9437192 | tf_op jit(solution)/shard_map/ppermute | solution.py:39
  45.9 22.1 %copy-start.5 = (bf16[4,512,128]{2,1,0:T(8,128)(2,1)}, bf16[4,512,128]{2,1,0:T(8,128)(2,1)S(1)}, u32[]{:S(2)}) copy-start(bf16[4,512,128]{2,1,0:T(8,128)(2,1)S(1)} %collective-permute-done.5.rest_19_) | copy-start | bytes 1572868
  46.8 9.3 %collective-permute-start.8 = (bf16[4,512,128]{2,1,0:T(8,128)(2,1)S(1)}, bf16[4,512,128]{2,1,0:T(8,128)(2,1)S(1)}, u32[]{:S(2)}, u32[]{:S(2)}) collective-permute-start(bf16[4,512,128]{2,1,0:T(8,128)(2,1)S(1)} %collective-permute-done.5.rest_19_), channel_id=1, source_target_pairs={{28,0},{29,1},{30,2},{31,3},{0,4},{1,5},{2,6},{3,7},{4,8},{5,9},{6... | collective-permute-start | bytes 1572872 | tf_op jit(solution)/shard_map/ppermute | solution.py:43
  46.9 9.4 %collective-permute-start.7 = (bf16[4,512,128]{2,1,0:T(8,128)(2,1)S(1)}, bf16[4,512,128]{2,1,0:T(8,128)(2,1)}, u32[]{:S(2)}, u32[]{:S(2)}) collective-permute-start(bf16[4,512,128]{2,1,0:T(8,128)(2,1)S(1)} %collective-permute-done.4.rest_18_), channel_id=1, source_target_pairs={{4,0},{5,1},{6,2},{7,3},{8,4},{9,5},{10,6},{11,7},{12,8},{13,9},{1... | collective-permute-start | bytes 1572872 | tf_op jit(solution)/shard_map/ppermute | solution.py:43
  56.1 9.6 %collective-permute-start.10 = (bf16[4,512,128]{2,1,0:T(8,128)(2,1)S(1)}, bf16[4,512,128]{2,1,0:T(8,128)(2,1)S(1)}, u32[]{:S(2)}, u32[]{:S(2)}) collective-permute-start(bf16[4,512,128]{2,1,0:T(8,128)(2,1)S(1)} %collective-permute-done.8.rest_21_), channel_id=1, source_target_pairs={{28,0},{29,1},{30,2},{31,3},{0,4},{1,5},{2,6},{3,7},{4,8},{5,9},{6... | collective-permute-start | bytes 1572872 | tf_op jit(solution)/shard_map/ppermute | solution.py:43
  56.3 9.6 %collective-permute-start.9 = (bf16[4,512,128]{2,1,0:T(8,128)(2,1)}, bf16[4,512,128]{2,1,0:T(8,128)(2,1)S(1)}, u32[]{:S(2)}, u32[]{:S(2)}) collective-permute-start(bf16[4,512,128]{2,1,0:T(8,128)(2,1)} %collective-permute-done.7.rest_20_), channel_id=1, source_target_pairs={{4,0},{5,1},{6,2},{7,3},{8,4},{9,5},{10,6},{11,7},{12,8},{13,9},{1... | collective-permute-start | bytes 1572872 | tf_op jit(solution)/shard_map/ppermute | solution.py:43
  66.2 1.7 %collective-permute-start.11 = (f32[1,4608]{1,0:T(1,128)S(1)}, f32[1,4608]{1,0:T(1,128)S(1)}, u32[]{:S(2)}, u32[]{:S(2)}) collective-permute-start(f32[1,4608]{1,0:T(1,128)S(1)} %pad_maximum_fusion.4.row_ref), channel_id=1, source_target_pairs={{128,0},{129,1},{130,2},{131,3},{132,4},{133,5},{134,6},{135,7},{1... | collective-permute-start | bytes 55304 | tf_op jit(solution)/shard_map/ppermute | solution.py:39
  77.9 2.2 %collective-permute-start.13 = (f32[256,384]{1,0:T(8,128)S(1)}, f32[256,384]{1,0:T(8,128)S(1)}, u32[]{:S(2)}, u32[]{:S(2)}) collective-permute-start(f32[256,384]{1,0:T(8,128)S(1)} %get-tuple-element.22), channel_id=1, source_target_pairs={{128,0},{129,1},{130,2},{131,3},{132,4},{133,5},{134,6},{135,7},{1... | collective-permute-start | bytes 1179656 | tf_op jit(solution)/shard_map/ppermute | solution.py:39
  78.3 37.4 %copy-start = (bf16[32,4,32,256]{3,2,1,0:T(8,128)(2,1)S(1)}, bf16[32,4,32,256]{3,2,1,0:T(8,128)(2,1)}, u32[]{:S(2)}) copy-start(bf16[32,4,32,256]{3,2,1,0:T(8,128)(2,1)} %all-gather.3.cloned.1.call-done) | copy-start | bytes 6291460
  78.3 37.4 %collective-permute-start.6 = (bf16[4,8,4,32,256]{4,3,2,1,0:T(8,128)(2,1)}, bf16[4,8,4,32,256]{4,3,2,1,0:T(8,128)(2,1)}, u32[]{:S(2)}, u32[]{:S(2)}) collective-permute-start(bf16[4,8,4,32,256]{4,3,2,1,0:T(8,128)(2,1)} %bitcast.33), channel_id=1, source_target_pairs={{128,0},{129,1},{130,2},{131,3},{132,4},{133,5},{134,6},{135,7},{1... | collective-permute-start | bytes 6291464 | tf_op jit(solution)/shard_map/ppermute | solution.py:39
  83.1 8.5 %collective-permute-start.14 = (bf16[2,256,128]{2,1,0:T(8,128)(2,1)}, bf16[2,256,128]{2,1,0:T(8,128)(2,1)S(1)}, u32[]{:S(2)}, u32[]{:S(2)}) collective-permute-start(bf16[2,256,128]{2,1,0:T(8,128)(2,1)} %get-tuple-element.24), channel_id=1, source_target_pairs={{0,1},{1,2},{2,3},{4,5},{5,6},{6,7},{8,9},{9,10},{10,11},{12,13},{... | collective-permute-start | bytes 393224 | tf_op jit(solution)/shard_map/ppermute | solution.py:39
  86.0 6.9 %collective-permute-start.15 = (bf16[2,256,128]{2,1,0:T(8,128)(2,1)}, bf16[2,256,128]{2,1,0:T(8,128)(2,1)S(1)}, u32[]{:S(2)}, u32[]{:S(2)}) collective-permute-start(bf16[2,256,128]{2,1,0:T(8,128)(2,1)} %get-tuple-element.24), channel_id=1, source_target_pairs={{0,2},{1,3},{4,6},{5,7},{8,10},{9,11},{12,14},{13,15},{16,18},{17,... | collective-permute-start | bytes 393224 | tf_op jit(solution)/shard_map/ppermute | solution.py:39
  90.3 3.8 %collective-permute-start.16 = (bf16[2,256,128]{2,1,0:T(8,128)(2,1)}, bf16[2,256,128]{2,1,0:T(8,128)(2,1)S(1)}, u32[]{:S(2)}, u32[]{:S(2)}) collective-permute-start(bf16[2,256,128]{2,1,0:T(8,128)(2,1)} %get-tuple-element.24), channel_id=1, source_target_pairs={{0,3},{4,7},{8,11},{12,15},{16,19},{20,23},{24,27},{28,31},{32,35}... | collective-permute-start | bytes 393224 | tf_op jit(solution)/shard_map/ppermute | solution.py:39
  95.1 3.1 %collective-permute-start.17 = (bf16[4,2,256,128]{3,2,1,0:T(8,128)(2,1)S(1)}, bf16[4,2,256,128]{3,2,1,0:T(8,128)(2,1)S(1)}, u32[]{:S(2)}, u32[]{:S(2)}) collective-permute-start(bf16[4,2,256,128]{3,2,1,0:T(8,128)(2,1)S(1)} %pad_maximum_fusion.1.rest_0_), channel_id=1, source_target_pairs={{128,0},{129,1},{130,2},{131,3},{132,4},{133,5},{134,6},{135,7},{1... | collective-permute-start | bytes 1572872 | tf_op jit(solution)/shard_map/ppermute | solution.py:39
  101.6 14.1 %all-to-all-start.1 = ((bf16[8,256,128]{2,1,0:T(8,128)(2,1)}), bf16[8,256,128]{2,1,0:T(8,128)(2,1)S(1)}, u32[]{:S(2)}, u32[]{:S(2)}) async-start(bf16[8,256,128]{2,1,0:T(8,128)(2,1)} %shard_map.103), calls=%async_computation.1 | async-start | bytes 1048576 | tf_op jit(solution)/shard_map/all_to_all | solution.py:334
  119.7 14.3 %all-to-all-start.2 = ((bf16[4,256,256]{2,1,0:T(8,128)(2,1)}), bf16[4,256,256]{2,1,0:T(8,128)(2,1)S(1)}, u32[]{:S(2)}, u32[]{:S(2)}) async-start(bf16[4,256,256]{2,1,0:T(8,128)(2,1)} %shard_map.104), calls=%async_computation.2 | async-start | bytes 1048576 | tf_op jit(solution)/shard_map/all_to_all | solution.py:337
  134.4 6.8 %collective-permute-start.18 = (bf16[256,128]{1,0:T(8,128)(2,1)S(1)}, bf16[256,128]{1,0:T(8,128)(2,1)S(1)}, u32[]{:S(2)}, u32[]{:S(2)}) collective-permute-start(bf16[256,128]{1,0:T(8,128)(2,1)S(1)} %bitcast.57), channel_id=1, source_target_pairs={{128,0},{129,1},{130,2},{131,3},{132,4},{133,5},{134,6},{135,7},{1... | collective-permute-start | bytes 196616 | tf_op jit(solution)/shard_map/ppermute | solution.py:39
  (9 other events, 45.4 us)
Sparse Core Ops, SparseCore 0:
  46.9 31.0 all-gather.2
